TPU v7x, 256 devices: a whole 4x4x8 slice. The times are simulated.
256 devices in a mesh: seq: 32 (over z_hi, y, core), head: 8 (over z_lo, x).
Axes of the slice: x: 4, y: 4, z: 8 (z_hi: 4, z_lo: 2; z = z_hi * 2 + z_lo), core: 2. Of those that a mesh axis runs over, the one named last changes fastest.
Arguments:
- tokens: bfloat16 [16384, 5120], P(('seq', 'head')), may hold values from -6 to 6
- w_qkv: bfloat16 [3, 5120, 2560], P(None, None, 'head'), may hold values from -0.078125 to 0.078125
- scale_exp: int32 [3, 40, 8], P(None, None, 'head'), may hold values from -2 to 1
- gate_mask: int32 [16384, 8], P('seq', 'head'), may hold values 0 or 1
- rate: float32 [8], P('head'), may hold values from 0.0003125 to 0.0015625
- fast_gate: bfloat16 [8, 320, 640], P('head'), may hold values from -0.3125 to 0.3125
- fast_up: bfloat16 [8, 320, 640], P('head'), may hold values from -0.3125 to 0.3125
- fast_down: bfloat16 [8, 320, 640], P('head'), may hold values from -0.25 to 0.25
Outputs:
- answers: bfloat16 [16384, 2560], P(('seq', 'head'))
All inputs are finite; a program needn't handle non-finite values. No bound on the sum of `gate_mask` on one device may be relied on, other than what follows from the above.
Results may differ from a plain program's by a relative error of at most 0.012.
Values may be sent and summed in bfloat16 or wider, within the bound.
No kernel may reach another device: no remote copies, remote signals or barrier semaphores. Data moves between devices by JAX's collectives and lax.ppermute only.
A program may use at most 64 MiB of HBM per device.

v0:
```python
import jax
import jax.numpy as jnp
from jax import lax
from jax.sharding import PartitionSpec as P


def local_grads(keys, values, weight, old):
    gate = jnp.dot(keys, old[0], preferred_element_type=jnp.float32)
    upper = jnp.dot(keys, old[1], preferred_element_type=jnp.float32)
    sigma = jax.nn.sigmoid(gate)
    active = gate * sigma
    hidden = (active * upper).astype(jnp.bfloat16)
    weighted = (weight[:, None] * values.astype(jnp.float32)).astype(jnp.bfloat16)
    d_hidden = jnp.dot(weighted, old[2], preferred_element_type=jnp.float32)
    d_gate = (d_hidden * upper * sigma * (1.0 + gate * (1.0 - sigma))).astype(jnp.bfloat16)
    d_upper = (d_hidden * active).astype(jnp.bfloat16)
    dims = (((0,), (0,)), ((), ()))
    grad_gate = lax.dot_general(keys, d_gate, dims, preferred_element_type=jnp.float32)
    grad_upper = lax.dot_general(keys, d_upper, dims, preferred_element_type=jnp.float32)
    grad_down = lax.dot_general(weighted, hidden, dims, preferred_element_type=jnp.float32)
    return jnp.stack([grad_gate, grad_upper, grad_down])


def respond(query, renorm):
    gate = jnp.dot(query, renorm[0], preferred_element_type=jnp.float32)
    upper = jnp.dot(query, renorm[1], preferred_element_type=jnp.float32)
    hidden = (jax.nn.silu(gate) * upper).astype(jnp.bfloat16)
    output = lax.dot_general(
        hidden, renorm[2], (((1,), (1,)), ((), ())), preferred_element_type=jnp.float32
    )
    scaled = output * lax.rsqrt(jnp.mean(output * output, axis=-1, keepdims=True) + 1e-05)
    return scaled.astype(jnp.bfloat16)


def body(tokens, w_qkv, scale_exp, gate_mask, rate, fast_gate, fast_up, fast_down):
    factor = jnp.exp2(scale_exp.astype(jnp.float32))[:, :, 0]
    block_rows = w_qkv.shape[1] // factor.shape[1]
    factor = jnp.repeat(factor, block_rows, axis=1)[:, :, None].astype(jnp.bfloat16)
    weff = w_qkv * factor
    triple = jnp.einsum(
        "rd,cdh->rch",
        lax.all_gather(tokens, "head", axis=0, tiled=True),
        weff,
        preferred_element_type=jnp.float32,
    ).astype(jnp.bfloat16)
    query = triple[:, 0]
    keys = triple[:, 1]
    values = triple[:, 2]
    weight = rate[0] * gate_mask[:, 0].astype(jnp.float32)
    old = jnp.stack([fast_gate[0], fast_up[0], fast_down[0]])
    partial_grads = local_grads(keys, values, weight, old)
    old_f = old.astype(jnp.float32)
    old_norm = jnp.sqrt(jnp.sum(old_f * old_f, axis=1))
    total = lax.psum(partial_grads, "seq")
    fresh = old_f + total
    new_sq = jnp.sum(fresh * fresh, axis=1)
    renorm = (fresh * (old_norm / jnp.sqrt(new_sq + 1e-06))[:, None, :]).astype(jnp.bfloat16)
    answer = respond(query, renorm)
    return lax.all_to_all(answer, "head", split_axis=0, concat_axis=1, tiled=True)


def solution(mesh):
    in_specs = (
        P(("seq", "head"), None),
        P(None, None, "head"),
        P(None, None, "head"),
        P("seq", "head"),
        P("head"),
        P("head", None, None),
        P("head", None, None),
        P("head", None, None),
    )
    out_specs = P(("seq", "head"), None)
    return jax.shard_map(body, mesh=mesh, in_specs=in_specs, out_specs=out_specs, check_vma=False)
```

profile of v0, /device:TPU:2, one launch (start us, length us, event | category | flops | bytes accessed | tf_op | source)
XLA Modules:
  0.0 410.4 jit_solution(11649179984776909183)
XLA Ops:
  6.5 0.0 all-gather.2.cloned.1.call-start
  6.5 0.7 all-gather.2.cloned.1.call-update
  7.3 0.0 all-reduce.2.cloned.1.call-start
  7.9 0.7 exponential_convert_fusion
  8.6 0.1 broadcast_bitcast_fusion
  8.8 0.7 convert_multiply_fusion.2
  9.5 65.4 %all-gather.2.cloned.1.call-done = bf16[512,5120]{1,0:T(8,128)(2,1)} async-done(((bf16[64,5120]{1,0:T(8,128)(2,1)}), bf16[512,5120]{1,0:T(8,128)(2,1)}) %all-gather.2.cloned.1.call-update) | async-done | bytes 5242896 | tf_op jit(solution)/shard_map/all_gather | solution.py:42
  74.9 0.0 copy-start.2
  74.9 9.5 %fusion.10 = bf16[512,3,320]{0,2,1:T(8,128)(2,1)S(1)} fusion(bf16[512,5120]{1,0:T(8,128)(2,1)} %all-gather.2.cloned.1.call-done, bf16[3,5120,320]{1,2,0:T(8,128)(2,1)} %param.9, bf16[3,5120]{1,0:T(4,128)(2,1)S(1)} %bitcast.76), kind=kOutput, calls=%fused_computation.12 | convolution fusion | flops 5038571520 | bytes 16087040 | tf_op jit(solution)/shard_map/rd,cdh->rch/dot_general | solution.py:40
  84.4 0.0 copy-done.2
  84.4 0.0 copy-start.1
  84.4 0.6 fusion.23
  85.0 0.4 copy-done.1
  85.4 0.0 copy-start.3
  85.4 0.6 fusion.25
  86.0 0.4 copy-done.3
  86.4 0.6 fusion.27
  87.0 0.6 convolution_bitcast_fusion.1
  87.7 0.8 convolution_bitcast_fusion.2
  88.4 0.6 convolution_bitcast_fusion
  89.1 1.6 pad_maximum_fusion
  90.7 0.0 all-reduce.2.cloned.1.call-update
  90.7 292.7 %all-reduce.2.cloned.1.call-done = f32[3,320,640]{2,1,0:T(8,128)} async-done(((f32[3,320,640]{2,1,0:T(8,128)}), f32[3,320,640]{2,1,0:T(8,128)}) %all-reduce.2.cloned.1.call-update) | async-done | bytes 2457616 | tf_op jit(solution)/shard_map/psum | solution.py:54
  383.4 0.0 copy-start
  383.4 2.4 fusion.4
  385.8 0.1 copy-done
  385.8 0.4 multiply_convert_fusion
  386.2 1.7 fusion.22
  387.9 2.3 multiply_reduce_fusion.1
  390.2 0.1 multiply_convert_fusion.6
  390.3 0.2 copy.11
  390.5 11.8 %all_to_all.19 = bf16[8,64,320]{2,1,0:T(8,128)(2,1)S(1)} all-to-all(bf16[8,64,320]{2,1,0:T(8,128)(2,1)S(1)} %bitcast.75), channel_id=1, replica_groups=mesh['seq'=32,'head'=8] {'head'}, dimensions={0} | all-to-all | bytes 655360 | tf_op jit(solution)/shard_map/all_to_all | solution.py:59
  402.3 0.2 copy.12
  402.6 1.0 all_to_all.17
  (4 shorter events, 0.0 us)
Async XLA Ops:
  6.5 68.4 %all-gather.2.cloned.1.call-start = ((), (), s32[]{:S(2)}) async-start(), calls=%async_computation.1 | async-start | bytes 5898240 | tf_op jit(solution)/shard_map/all_gather | solution.py:42
  7.3 376.1 %all-reduce.2.cloned.1.call-start = ((), (), s32[]{:S(2)}) async-start(), calls=%async_computation.2 | async-start | bytes 4915200 | tf_op jit(solution)/shard_map/psum | solution.py:54
  74.9 9.5 %copy-start.2 = (bf16[1,320,640]{2,1,0:T(8,128)(2,1)S(1)}, bf16[1,320,640]{2,1,0:T(8,128)(2,1)}, u32[]{:S(2)}) copy-start(bf16[1,320,640]{2,1,0:T(8,128)(2,1)} %param.13) | copy-start | bytes 1228804
  84.4 1.0 copy-start.1
  85.4 1.0 copy-start.3
  383.4 2.4 copy-start
Sparse Core Ops, SparseCore 0:
  9.1 65.7 all-gather.1
  90.8 292.5 all-reduce.1
where the time goes:
time: 411 us; the launch traced here: 410 us
  waiting for transfers between devices  359 us (87%)
  matrix products  17.3 us (4%)
  between operations  14.2 us (3%)
  blocking collectives  11.8 us (3%)
  other arithmetic  5.76 us (1%)
    psum x1, waiting for transfers between devices, body(): total = lax.psum(partial_grads, 'seq')  293 us
    all_gather x1, waiting for transfers between devices, body(): lax.all_gather(tokens, 'head', axis=0, tiled=True)  65.4 us
    all_to_all x1, blocking collectives, body(): lax.all_to_all(answer, 'head', split_axis=0, concat_axis=1, tiled=True)  11.8 us
    dot_general x1, matrix products, body(): jnp.einsum('rd,cdh->rch', lax.all_gather(tokens, 'head', axis=0, tiled=Tr...  9.52 us
  transfers between devices with their start and end apart: 2, of which 2 were waited for; matrix products, arithmetic and copies ran while one was open for 0% of the time, Pallas kernels for 0%

commit v1 on v0

v1 whole, which is shorter than its diff:
```python
import jax
import jax.numpy as jnp
from jax import lax
from jax.sharding import PartitionSpec as P

AXES = ("seq", "head")
BF16 = jnp.bfloat16
F32 = jnp.float32


def place(i):
    seq, head = divmod(i, 8)
    return seq // 8, (seq // 2) % 4, seq % 2, head // 4, head % 4


def permute(value, move):
    pairs = []
    for i in range(256):
        z_hi, y, core, z_lo, x = move(*place(i))
        pairs.append((i, ((z_hi % 4) * 8 + (y % 4) * 2 + core) * 8 + z_lo * 4 + x % 4))
    return lax.ppermute(value, AXES, pairs)


def to_core(value):
    return permute(value, lambda h, y, c, l, x: (h, y, 1 - c, l, x))


def to_y(value, d):
    return permute(value, lambda h, y, c, l, x: (h, y + d, c, l, x))


def to_z(value, d):
    return permute(value, lambda h, y, c, l, x: (h + d, y, c, l, x))


def local_grads(keys, values, weight, old):
    gate = jnp.dot(keys, old[0], preferred_element_type=F32)
    upper = jnp.dot(keys, old[1], preferred_element_type=F32)
    sigma = jax.nn.sigmoid(gate)
    active = gate * sigma
    hidden = (active * upper).astype(BF16)
    weighted = (weight[:, None] * values.astype(F32)).astype(BF16)
    d_hidden = jnp.dot(weighted, old[2], preferred_element_type=F32)
    d_gate = (d_hidden * upper * sigma * (1.0 + gate * (1.0 - sigma))).astype(BF16)
    d_upper = (d_hidden * active).astype(BF16)
    dims = (((0,), (0,)), ((), ()))
    return jnp.concatenate(
        [
            lax.dot_general(d_gate, keys, dims, preferred_element_type=F32),
            lax.dot_general(d_upper, keys, dims, preferred_element_type=F32),
            lax.dot_general(hidden, weighted, dims, preferred_element_type=F32),
        ],
        axis=1,
    )


def respond(query, renorm):
    dims = (((1,), (1,)), ((), ()))
    gate = lax.dot_general(query, renorm[:, :320], dims, preferred_element_type=F32)
    upper = lax.dot_general(query, renorm[:, 320:640], dims, preferred_element_type=F32)
    hidden = (jax.nn.silu(gate) * upper).astype(BF16)
    output = jnp.dot(hidden, renorm[:, 640:], preferred_element_type=F32)
    scaled = output * lax.rsqrt(jnp.mean(output * output, axis=-1, keepdims=True) + 1e-05)
    return scaled.astype(BF16)


def rows(value, start, size):
    return lax.dynamic_slice_in_dim(value, start, size, axis=0)


def body(tokens, w_qkv, scale_exp, gate_mask, rate, fast_gate, fast_up, fast_down):
    seq = lax.axis_index("seq")
    core, y = seq % 2, (seq // 2) % 4
    factor = jnp.exp2(scale_exp.astype(F32))[:, :, 0]
    block_rows = w_qkv.shape[1] // factor.shape[1]
    factor = jnp.repeat(factor, block_rows, axis=1)[:, :, None].astype(BF16)
    weff = w_qkv * factor
    triple = jnp.einsum(
        "rd,cdh->rch",
        lax.all_gather(tokens, "head", axis=0, tiled=True),
        weff,
        preferred_element_type=F32,
    ).astype(BF16)
    query, keys, values = triple[:, 0], triple[:, 1], triple[:, 2]
    weight = rate[0] * gate_mask[:, 0].astype(F32)
    old = jnp.stack([fast_gate[0], fast_up[0], fast_down[0]])
    part = local_grads(keys, values, weight, old)

    half = rows(part, core * 320, 320) + to_core(
        rows(part, (1 - core) * 320, 320).astype(BF16)
    ).astype(F32)
    piece = rows(half, y * 80, 80)
    for d in (1, 3, 2):
        piece += to_y(rows(half, (y + d) % 4 * 80, 80).astype(BF16), d).astype(F32)
    small = piece.astype(BF16)
    for d in (1, 3, 2):
        piece += to_z(small, d).astype(F32)

    old_t = jnp.concatenate([fast_gate[0].T, fast_up[0].T, fast_down[0].T], axis=1)
    old_f = rows(old_t, core * 320 + y * 80, 80).astype(F32).reshape(80, 3, 320)
    fresh = old_f + piece.reshape(80, 3, 320)
    old_norm = jnp.sqrt(jnp.sum(old_f * old_f, axis=2, keepdims=True))
    new_sq = jnp.sum(fresh * fresh, axis=2, keepdims=True)
    mine = (fresh * (old_norm / jnp.sqrt(new_sq + 1e-06))).astype(BF16).reshape(80, 960)
    column = jnp.concatenate([mine, to_y(mine, 1), to_y(mine, 3), to_y(mine, 2)], axis=0)
    renorm = jnp.concatenate([column, to_core(column)], axis=0)

    answer = respond(query, renorm)
    return lax.all_to_all(answer, "head", split_axis=0, concat_axis=1, tiled=True)


def solution(mesh):
    in_specs = (
        P(("seq", "head"), None),
        P(None, None, "head"),
        P(None, None, "head"),
        P("seq", "head"),
        P("head"),
        P("head", None, None),
        P("head", None, None),
        P("head", None, None),
    )
    out_specs = P(("seq", "head"), None)
    return jax.shard_map(body, mesh=mesh, in_specs=in_specs, out_specs=out_specs, check_vma=False)
```

time: 411 us -> 173 us (0.42)
  waiting for transfers between devices: 359 us -> 91.6 us
  starting transfers between devices: 0.04 us -> 18.4 us
  blocking collectives: 11.8 us -> 17 us
  local copies, waits for them, and re-layouts: 2.44 us -> 7.59 us
    psum x1 -> x0, waiting for transfers between devices: 293 us -> none  [body(): total = lax.psum(partial_grads, 'seq')]
    ppermute x0 -> x11, waiting for transfers between devices: none -> 25.4 us  [permute(): return lax.ppermute(value, AXES, pairs)]
    ppermute x0 -> x11, starting transfers between devices: none -> 18.4 us  [permute(): return lax.ppermute(value, AXES, pairs)]
    all_to_all x1, blocking collectives: 11.8 us -> 17 us  [body(): lax.all_to_all(answer, 'head', split_axis=0, concat_axis=1, tiled=True)]
  transfers between devices with their start and end apart: 2 -> 12, of which waited for: 2 -> 11; matrix products, arithmetic and copies ran while one was open for 0% -> 2% of each run, Pallas kernels for 0% -> 0%
where the time goes in v1:
time: 173 us; the launch traced here: 172 us
  waiting for transfers between devices  91.6 us (53%)
  starting transfers between devices  18.4 us (11%)
  blocking collectives  17 us (10%)
  matrix products  16.1 us (9%)
  between operations  14.4 us (8%)
  local copies, waits for them, and re-layouts  7.59 us (4%)
  other arithmetic  6.73 us (4%)
    all_gather x1, waiting for transfers between devices, body(): lax.all_gather(tokens, 'head', axis=0, tiled=True)  65.5 us
    ppermute x11, waiting for transfers between devices, permute(): return lax.ppermute(value, AXES, pairs)  25.4 us
    ppermute x11, starting transfers between devices, permute(): return lax.ppermute(value, AXES, pairs)  18.4 us
    all_to_all x1, blocking collectives, body(): lax.all_to_all(answer, 'head', split_axis=0, concat_axis=1, tiled=True)  17 us
    dot_general x1, matrix products, body(): jnp.einsum('rd,cdh->rch', lax.all_gather(tokens, 'head', axis=0, tiled=Tr...  9.52 us
    unnamed x25, local copies, waits for them, and re-layouts  4.23 us
  transfers between devices with their start and end apart: 12, of which 11 were waited for; matrix products, arithmetic and copies ran while one was open for 2% of the time, Pallas kernels for 0%

profile of v1, /device:TPU:2, one launch (start us, length us, event | category | flops | bytes accessed | tf_op | source)
XLA Modules:
  0.0 171.9 jit_solution(1266930908786664186)
XLA Ops:
  6.5 0.7 all-gather.2.cloned.1.call-update
  7.3 0.7 exponential_convert_fusion
  8.0 0.1 broadcast_bitcast_fusion
  8.7 0.7 convert_multiply_fusion.2
  9.4 65.5 %all-gather.2.cloned.1.call-done = bf16[512,5120]{1,0:T(8,128)(2,1)} async-done(((bf16[64,5120]{1,0:T(8,128)(2,1)}), bf16[512,5120]{1,0:T(8,128)(2,1)}) %all-gather.2.cloned.1.call-update) | async-done | bytes 5242896 | tf_op jit(solution)/shard_map/all_gather | solution.py:80
  74.9 9.5 %fusion.9 = bf16[512,3,320]{0,2,1:T(8,128)(2,1)S(1)} fusion(bf16[512,5120]{1,0:T(8,128)(2,1)} %all-gather.2.cloned.1.call-done, bf16[3,5120,320]{1,2,0:T(8,128)(2,1)} %param.9, bf16[3,5120]{1,0:T(4,128)(2,1)S(1)} %bitcast.68), kind=kOutput, calls=%fused_computation.6 | convolution fusion | flops 5038571520 | bytes 16087040 | tf_op jit(solution)/shard_map/rd,cdh->rch/dot_general | solution.py:78
  84.4 0.0 copy-start.4
  84.5 0.6 fusion.31
  85.1 0.7 copy-done.4
  85.7 0.6 fusion.33
  86.3 0.4 copy-done.5
  86.7 0.6 fusion.35
  87.3 0.6 fusion.18
  87.9 0.7 fusion.21
  88.7 0.6 fusion.19
  89.3 0.5 pad_maximum_fusion
  89.8 0.9 dynamic-slice_convert_fusion
  90.7 0.0 collective-permute-start
  90.7 2.4 %collective-permute-done = bf16[320,960]{1,0:T(8,128)(2,1)} collective-permute-done((bf16[320,960]{1,0:T(8,128)(2,1)}, bf16[320,960]{1,0:T(8,128)(2,1)}, u32[]{:S(2)}, u32[]{:S(2)}) %collective-permute-start) | collective-permute-done | bytes 614432 | tf_op jit(solution)/shard_map/ppermute | solution.py:21
  93.2 1.2 convert_add_fusion
  94.4 1.1 copy-done
  95.5 0.1 dynamic-slice_convert_fusion.3
  95.6 1.6 collective-permute-start.1
  97.2 1.8 %collective-permute-start.2 = (bf16[80,960]{1,0:T(8,128)(2,1)S(1)}, bf16[80,960]{1,0:T(8,128)(2,1)S(1)}, u32[]{:S(2)}, u32[]{:S(2)}) collective-permute-start(bf16[80,960]{1,0:T(8,128)(2,1)S(1)} %get-tuple-element.13), channel_id=1, source_target_pairs={{0,48},{1,49},{2,50},{3,51},{4,52},{5,53},{6,54},{7,55},{8,56},{9,... | collective-permute-start | bytes 460808 | tf_op jit(solution)/shard_map/ppermute | solution.py:21
  98.9 1.8 %collective-permute-start.3 = (bf16[80,960]{1,0:T(8,128)(2,1)S(1)}, bf16[80,960]{1,0:T(8,128)(2,1)S(1)}, u32[]{:S(2)}, u32[]{:S(2)}) collective-permute-start(bf16[80,960]{1,0:T(8,128)(2,1)S(1)} %get-tuple-element.12), channel_id=1, source_target_pairs={{0,32},{1,33},{2,34},{3,35},{4,36},{5,37},{6,38},{7,39},{8,40},{9,... | collective-permute-start | bytes 460808 | tf_op jit(solution)/shard_map/ppermute | solution.py:21
  100.7 2.4 %collective-permute-done.1 = bf16[80,960]{1,0:T(8,128)(2,1)S(1)} collective-permute-done((bf16[80,960]{1,0:T(8,128)(2,1)S(1)}, bf16[80,960]{1,0:T(8,128)(2,1)S(1)}, u32[]{:S(2)}, u32[]{:S(2)}) %collective-permute-start.1) | collective-permute-done | bytes 153632 | tf_op jit(solution)/shard_map/ppermute | solution.py:21
  103.1 2.8 %collective-permute-done.2 = bf16[80,960]{1,0:T(8,128)(2,1)S(1)} collective-permute-done((bf16[80,960]{1,0:T(8,128)(2,1)S(1)}, bf16[80,960]{1,0:T(8,128)(2,1)S(1)}, u32[]{:S(2)}, u32[]{:S(2)}) %collective-permute-start.2) | collective-permute-done | bytes 153632 | tf_op jit(solution)/shard_map/ppermute | solution.py:21
  105.9 1.7 collective-permute-done.3
  107.6 1.7 fusion.48
  109.3 2.6 %collective-permute-start.4 = (bf16[80,960]{1,0:T(8,128)(2,1)}, bf16[80,960]{1,0:T(8,128)(2,1)S(1)}, u32[]{:S(2)}, u32[]{:S(2)}) collective-permute-start(bf16[80,960]{1,0:T(8,128)(2,1)} %fusion.48), channel_id=1, source_target_pairs={{0,64},{1,65},{2,66},{3,67},{4,68},{5,69},{6,70},{7,71},{8,72},{9,... | collective-permute-start | bytes 460808 | tf_op jit(solution)/shard_map/ppermute | solution.py:21
  111.9 1.6 collective-permute-start.5
  113.5 5.7 %collective-permute-start.6 = (bf16[80,960]{1,0:T(8,128)(2,1)}, bf16[80,960]{1,0:T(8,128)(2,1)}, u32[]{:S(2)}, u32[]{:S(2)}) collective-permute-start(bf16[80,960]{1,0:T(8,128)(2,1)} %fusion.48), channel_id=1, source_target_pairs={{0,128},{1,129},{2,130},{3,131},{4,132},{5,133},{6,134},{7,135},{8... | collective-permute-start | bytes 460808 | tf_op jit(solution)/shard_map/ppermute | solution.py:21
  119.2 0.3 copy.30
  119.5 0.3 copy.31
  119.7 0.3 copy.32
  120.0 0.1 convert_multiply_fusion.1
  120.1 0.2 mul.135
  120.3 0.2 reduce_sum.27
  120.5 0.0 collective-permute-done.4
  120.5 6.2 %collective-permute-done.5 = bf16[80,960]{1,0:T(8,128)(2,1)S(1)} collective-permute-done((bf16[80,960]{1,0:T(8,128)(2,1)}, bf16[80,960]{1,0:T(8,128)(2,1)S(1)}, u32[]{:S(2)}, u32[]{:S(2)}) %collective-permute-start.5) | collective-permute-done | bytes 153632 | tf_op jit(solution)/shard_map/ppermute | solution.py:21
  126.7 1.1 collective-permute-done.6
  127.8 1.3 fusion.54
  129.1 0.2 mul.137
  129.3 0.2 reduce_sum.28
  129.5 0.1 mul.138
  129.6 0.3 mul.139
  130.0 0.9 collective-permute-start.7
  130.8 2.5 %collective-permute-start.8 = (bf16[80,960]{1,0:T(8,128)(2,1)S(1)}, bf16[80,960]{1,0:T(8,128)(2,1)S(1)}, u32[]{:S(2)}, u32[]{:S(2)}) collective-permute-start(bf16[80,960]{1,0:T(8,128)(2,1)S(1)} %get-tuple-element.6), channel_id=1, source_target_pairs={{0,48},{1,49},{2,50},{3,51},{4,52},{5,53},{6,54},{7,55},{8,56},{9,... | collective-permute-start | bytes 460808 | tf_op jit(solution)/shard_map/ppermute | solution.py:21
  133.3 0.0 collective-permute-start.9
  133.3 5.0 %collective-permute-done.7 = bf16[80,960]{1,0:T(8,128)(2,1)S(1)} collective-permute-done((bf16[80,960]{1,0:T(8,128)(2,1)S(1)}, bf16[80,960]{1,0:T(8,128)(2,1)S(1)}, u32[]{:S(2)}, u32[]{:S(2)}) %collective-permute-start.7) | collective-permute-done | bytes 153632 | tf_op jit(solution)/shard_map/ppermute | solution.py:21
  138.3 0.8 collective-permute-done.8
  139.1 1.0 collective-permute-done.9
  140.1 0.1 pad_maximum_fusion.1
  140.2 0.1 collective-permute-start.10
  140.4 2.0 %collective-permute-done.10 = bf16[320,960]{1,0:T(8,128)(2,1)S(1)} collective-permute-done((bf16[320,960]{1,0:T(8,128)(2,1)S(1)}, bf16[320,960]{1,0:T(8,128)(2,1)S(1)}, u32[]{:S(2)}, u32[]{:S(2)}) %collective-permute-start.10) | collective-permute-done | bytes 614432 | tf_op jit(solution)/shard_map/ppermute | solution.py:21
  142.4 1.1 copy-done.7
  143.5 0.0 copy-done.2
  143.5 0.6 fusion.29
  144.1 2.4 %multiply_reduce_fusion = (f32[512]{0:T(512)S(1)}, f32[512,320]{0,1:T(8,128)S(1)}) fusion(bf16[640,960]{1,0:T(8,128)(2,1)} %copy-done.7, f32[512,640]{1,0:T(8,128)S(1)} %fusion.29, bf16[512,3,320]{0,2,1:T(8,128)(2,1)S(1)} %copy-done.2), kind=kOutput, calls=%fused_computation.27 | convolution fusion | flops 421723648 | bytes 3278848 | tf_op jit(solution)/shard_map/dot_general | solution.py:62
  146.5 0.1 multiply_convert_fusion.6
  146.6 0.2 copy.36
  146.8 17.0 %all_to_all.19 = bf16[8,64,320]{2,1,0:T(8,128)(2,1)S(1)} all-to-all(bf16[8,64,320]{2,1,0:T(8,128)(2,1)S(1)} %bitcast.67), channel_id=1, replica_groups=mesh['seq'=32,'head'=8] {'head'}, dimensions={0} | all-to-all | bytes 655360 | tf_op jit(solution)/shard_map/all_to_all | solution.py:109
  163.8 0.2 copy.37
  164.0 1.0 all_to_all.17
  (20 shorter events, 0.2 us)
Async XLA Ops:
  6.5 68.4 %all-gather.2.cloned.1.call-start = ((), (), s32[]{:S(2)}) async-start(), calls=%async_computation.1 | async-start | bytes 5898240 | tf_op jit(solution)/shard_map/all_gather | solution.py:80
  74.9 9.5 %copy-start.3 = (bf16[1,320,640]{2,1,0:T(8,128)(2,1)S(1)}, bf16[1,320,640]{2,1,0:T(8,128)(2,1)}, u32[]{:S(2)}) copy-start(bf16[1,320,640]{2,1,0:T(8,128)(2,1)} %param.13) | copy-start | bytes 1228804
  84.4 4.2 %copy-start.1 = (bf16[512,3,320]{0,2,1:T(8,128)(2,1)}, bf16[512,3,320]{0,2,1:T(8,128)(2,1)S(1)}, u32[]{:S(2)}) copy-start(bf16[512,3,320]{0,2,1:T(8,128)(2,1)S(1)} %fusion.9) | copy-start | bytes 2949124
  84.4 1.3 copy-start.4
  85.7 1.0 copy-start.5
  90.7 2.4 %collective-permute-start = (bf16[320,960]{1,0:T(8,128)(2,1)}, bf16[320,960]{1,0:T(8,128)(2,1)}, u32[]{:S(2)}, u32[]{:S(2)}) collective-permute-start(bf16[320,960]{1,0:T(8,128)(2,1)} %dynamic-slice_convert_fusion), channel_id=1, source_target_pairs={{0,8},{1,9},{2,10},{3,11},{4,12},{5,13},{6,14},{7,15},{8,0},{9,1},... | collective-permute-start | bytes 1843208 | tf_op jit(solution)/shard_map/ppermute | solution.py:21
  94.4 1.1 copy-start
  95.6 7.5 %collective-permute-start.1 = (bf16[80,960]{1,0:T(8,128)(2,1)S(1)}, bf16[80,960]{1,0:T(8,128)(2,1)S(1)}, u32[]{:S(2)}, u32[]{:S(2)}) collective-permute-start(bf16[80,960]{1,0:T(8,128)(2,1)S(1)} %get-tuple-element.11), channel_id=1, source_target_pairs={{0,16},{1,17},{2,18},{3,19},{4,20},{5,21},{6,22},{7,23},{8,24},{9,... | collective-permute-start | bytes 460808 | tf_op jit(solution)/shard_map/ppermute | solution.py:21
  97.2 8.8 %collective-permute-start.2 = (bf16[80,960]{1,0:T(8,128)(2,1)S(1)}, bf16[80,960]{1,0:T(8,128)(2,1)S(1)}, u32[]{:S(2)}, u32[]{:S(2)}) collective-permute-start(bf16[80,960]{1,0:T(8,128)(2,1)S(1)} %get-tuple-element.13), channel_id=1, source_target_pairs={{0,48},{1,49},{2,50},{3,51},{4,52},{5,53},{6,54},{7,55},{8,56},{9,... | collective-permute-start | bytes 460808 | tf_op jit(solution)/shard_map/ppermute | solution.py:21
  98.9 8.7 %collective-permute-start.3 = (bf16[80,960]{1,0:T(8,128)(2,1)S(1)}, bf16[80,960]{1,0:T(8,128)(2,1)S(1)}, u32[]{:S(2)}, u32[]{:S(2)}) collective-permute-start(bf16[80,960]{1,0:T(8,128)(2,1)S(1)} %get-tuple-element.12), channel_id=1, source_target_pairs={{0,32},{1,33},{2,34},{3,35},{4,36},{5,37},{6,38},{7,39},{8,40},{9,... | collective-permute-start | bytes 460808 | tf_op jit(solution)/shard_map/ppermute | solution.py:21
  100.7 19.0 %copy-start.6 = (bf16[1,320,640]{2,1,0:T(8,128)(2,1)S(1)}, bf16[1,320,640]{2,1,0:T(8,128)(2,1)}, u32[]{:S(2)}) copy-start(bf16[1,320,640]{2,1,0:T(8,128)(2,1)} %param.15) | copy-start | bytes 1228804
  109.3 11.2 %collective-permute-start.4 = (bf16[80,960]{1,0:T(8,128)(2,1)}, bf16[80,960]{1,0:T(8,128)(2,1)S(1)}, u32[]{:S(2)}, u32[]{:S(2)}) collective-permute-start(bf16[80,960]{1,0:T(8,128)(2,1)} %fusion.48), channel_id=1, source_target_pairs={{0,64},{1,65},{2,66},{3,67},{4,68},{5,69},{6,70},{7,71},{8,72},{9,... | collective-permute-start | bytes 460808 | tf_op jit(solution)/shard_map/ppermute | solution.py:21
  111.9 14.9 %collective-permute-start.5 = (bf16[80,960]{1,0:T(8,128)(2,1)}, bf16[80,960]{1,0:T(8,128)(2,1)S(1)}, u32[]{:S(2)}, u32[]{:S(2)}) collective-permute-start(bf16[80,960]{1,0:T(8,128)(2,1)} %fusion.48), channel_id=1, source_target_pairs={{0,192},{1,193},{2,194},{3,195},{4,196},{5,197},{6,198},{7,199},{8... | collective-permute-start | bytes 460808 | tf_op jit(solution)/shard_map/ppermute | solution.py:21
  113.5 14.4 %collective-permute-start.6 = (bf16[80,960]{1,0:T(8,128)(2,1)}, bf16[80,960]{1,0:T(8,128)(2,1)}, u32[]{:S(2)}, u32[]{:S(2)}) collective-permute-start(bf16[80,960]{1,0:T(8,128)(2,1)} %fusion.48), channel_id=1, source_target_pairs={{0,128},{1,129},{2,130},{3,131},{4,132},{5,133},{6,134},{7,135},{8... | collective-permute-start | bytes 460808 | tf_op jit(solution)/shard_map/ppermute | solution.py:21
  130.0 8.4 %collective-permute-start.7 = (bf16[80,960]{1,0:T(8,128)(2,1)S(1)}, bf16[80,960]{1,0:T(8,128)(2,1)S(1)}, u32[]{:S(2)}, u32[]{:S(2)}) collective-permute-start(bf16[80,960]{1,0:T(8,128)(2,1)S(1)} %get-tuple-element.6), channel_id=1, source_target_pairs={{0,16},{1,17},{2,18},{3,19},{4,20},{5,21},{6,22},{7,23},{8,24},{9,... | collective-permute-start | bytes 460808 | tf_op jit(solution)/shard_map/ppermute | solution.py:21
  130.8 8.3 %collective-permute-start.8 = (bf16[80,960]{1,0:T(8,128)(2,1)S(1)}, bf16[80,960]{1,0:T(8,128)(2,1)S(1)}, u32[]{:S(2)}, u32[]{:S(2)}) collective-permute-start(bf16[80,960]{1,0:T(8,128)(2,1)S(1)} %get-tuple-element.6), channel_id=1, source_target_pairs={{0,48},{1,49},{2,50},{3,51},{4,52},{5,53},{6,54},{7,55},{8,56},{9,... | collective-permute-start | bytes 460808 | tf_op jit(solution)/shard_map/ppermute | solution.py:21
  133.3 6.8 %collective-permute-start.9 = (bf16[80,960]{1,0:T(8,128)(2,1)S(1)}, bf16[80,960]{1,0:T(8,128)(2,1)S(1)}, u32[]{:S(2)}, u32[]{:S(2)}) collective-permute-start(bf16[80,960]{1,0:T(8,128)(2,1)S(1)} %get-tuple-element.6), channel_id=1, source_target_pairs={{0,32},{1,33},{2,34},{3,35},{4,36},{5,37},{6,38},{7,39},{8,40},{9,... | collective-permute-start | bytes 460808 | tf_op jit(solution)/shard_map/ppermute | solution.py:21
  140.2 3.3 %copy-start.2 = (bf16[512,3,320]{0,2,1:T(8,128)(2,1)S(1)}, bf16[512,3,320]{0,2,1:T(8,128)(2,1)}, u32[]{:S(2)}) copy-start(bf16[512,3,320]{0,2,1:T(8,128)(2,1)} %copy-done.1) | copy-start | bytes 2949124
  140.2 2.2 %collective-permute-start.10 = (bf16[320,960]{1,0:T(8,128)(2,1)S(1)}, bf16[320,960]{1,0:T(8,128)(2,1)S(1)}, u32[]{:S(2)}, u32[]{:S(2)}) collective-permute-start(bf16[320,960]{1,0:T(8,128)(2,1)S(1)} %pad_maximum_fusion.1), channel_id=1, source_target_pairs={{0,8},{1,9},{2,10},{3,11},{4,12},{5,13},{6,14},{7,15},{8,0},{9,1},... | collective-permute-start | bytes 1843208 | tf_op jit(solution)/shard_map/ppermute | solution.py:21
  142.4 1.1 copy-start.7
Sparse Core Ops, SparseCore 0:
  9.1 65.7 all-gather.1

commit v2 on v1

--- a/solution.py
+++ b/solution.py
@@ -31,6 +31,34 @@
 
 def to_z(value, d):
     return permute(value, lambda h, y, c, l, x: (h + d, y, c, l, x))
+
+
+def near(x):
+    return x ^ 1
+
+
+def far(x):
+    return (x + 1) % 4 if x % 2 else (x - 1) % 4
+
+
+def to_near_x(value):
+    return permute(value, lambda h, y, c, l, x: (h, y, c, l, near(x)))
+
+
+def to_far_x(value):
+    return permute(value, lambda h, y, c, l, x: (h, y, c, l, far(x)))
+
+
+def to_opposite_x(value):
+    return permute(value, lambda h, y, c, l, x: (h, y, c, l, x + 2))
+
+
+def to_near_z(value):
+    return permute(value, lambda h, y, c, l, x: (h, y, c, 1 - l, x))
+
+
+def to_far_z(value):
+    return permute(value, lambda h, y, c, l, x: (h + 1 if l else h - 1, y, c, 1 - l, x))
 
 
 def local_grads(keys, values, weight, old):
@@ -68,21 +96,68 @@
     return lax.dynamic_slice_in_dim(value, start, size, axis=0)
 
 
+def gather(tokens):
+    first, second = tokens[:32], tokens[32:]
+    near_tile, far_tile = to_near_x(tokens), to_far_x(tokens)
+    z1, z2 = to_near_z(first), to_far_z(second)
+    opposite_first = to_far_x(near_tile[:32])
+    opposite_second = to_near_x(far_tile[32:])
+    z3 = to_near_z(jnp.concatenate([near_tile[:32], far_tile[:32]]))
+    z4 = to_far_z(jnp.concatenate([near_tile[32:], far_tile[32:]]))
+    z5, z6 = to_near_z(opposite_first), to_far_z(opposite_second)
+    return (
+        jnp.concatenate([tokens, near_tile, far_tile, opposite_first, opposite_second]),
+        jnp.concatenate([z1, z3, z5, z2, z4, z6]),
+    )
+
+
+def x_order(x):
+    return [x, x ^ 1, (x + jnp.where(x % 2 == 1, 1, 3)) % 4, (x + 2) % 4]
+
+
+def weights_of_rows(weight, z_lo, x):
+    tiles = weight.reshape(8, 64)
+    same = lax.dynamic_slice_in_dim(tiles, z_lo * 4, 4, axis=0)
+    other = lax.dynamic_slice_in_dim(tiles, (1 - z_lo) * 4, 4, axis=0)
+    order = x_order(x)
+    pick = lambda t: jnp.concatenate([lax.dynamic_slice_in_dim(t, i, 1, axis=0) for i in order])
+    same, other = pick(same), pick(other)
+    moved = permute(other[:, 32:], lambda h, y, c, l, x: (h - 1 if l else h + 1, y, c, l, x))
+    return jnp.concatenate([same.reshape(256), other[:, :32].reshape(128), moved.reshape(128)])
+
+
+def send_back(answer, z_lo, x):
+    from_near = to_near_z(answer[256:384]).reshape(4, 32, 320)
+    from_far = to_far_z(answer[384:]).reshape(4, 32, 320)
+    other = jnp.concatenate([from_near, from_far], axis=1)
+    both = jnp.stack([answer[:256].reshape(4, 64, 320), other], axis=1)
+    slots = jnp.stack(
+        [both[0], to_near_x(both[1]), to_far_x(both[2]), to_opposite_x(both[3])]
+    ).reshape(8, 64, 320)
+    out = []
+    for head in range(8):
+        d = (head % 4 - x) % 4
+        at = jnp.where(d == 0, 0, jnp.where(d == 2, 3, jnp.where(head % 4 == x ^ 1, 1, 2)))
+        slot = at * 2 + jnp.where(head // 4 == z_lo, 0, 1)
+        out.append(lax.dynamic_slice_in_dim(slots, slot, 1, axis=0)[0])
+    return jnp.concatenate(out, axis=1)
+
+
 def body(tokens, w_qkv, scale_exp, gate_mask, rate, fast_gate, fast_up, fast_down):
-    seq = lax.axis_index("seq")
+    seq, head = lax.axis_index("seq"), lax.axis_index("head")
     core, y = seq % 2, (seq // 2) % 4
+    z_lo, x = head // 4, head % 4
     factor = jnp.exp2(scale_exp.astype(F32))[:, :, 0]
     block_rows = w_qkv.shape[1] // factor.shape[1]
     factor = jnp.repeat(factor, block_rows, axis=1)[:, :, None].astype(BF16)
-    weff = w_qkv * factor
-    triple = jnp.einsum(
-        "rd,cdh->rch",
-        lax.all_gather(tokens, "head", axis=0, tiled=True),
-        weff,
-        preferred_element_type=F32,
-    ).astype(BF16)
-    query, keys, values = triple[:, 0], triple[:, 1], triple[:, 2]
-    weight = rate[0] * gate_mask[:, 0].astype(F32)
+    weff = lax.optimization_barrier(w_qkv * factor)
+    weight = weights_of_rows(rate[0] * gate_mask[:, 0].astype(F32), z_lo, x)
+    plane, others = gather(tokens)
+    def project(tile, c):
+        return jnp.dot(tile, weff[c], preferred_element_type=F32).astype(BF16)
+    keys = jnp.concatenate([project(plane, 1), project(others, 1)])
+    values = jnp.concatenate([project(plane, 2), project(others, 2)])
+    query = jnp.concatenate([project(plane, 0), project(others, 0)])
     old = jnp.stack([fast_gate[0], fast_up[0], fast_down[0]])
     part = local_grads(keys, values, weight, old)
 
@@ -106,7 +181,7 @@
     renorm = jnp.concatenate([column, to_core(column)], axis=0)
 
     answer = respond(query, renorm)
-    return lax.all_to_all(answer, "head", split_axis=0, concat_axis=1, tiled=True)
+    return send_back(answer, z_lo, x)
 
 
 def solution(mesh):

time: 173 us -> 134 us (0.77)
  waiting for transfers between devices: 91.6 us -> 43.6 us
  starting transfers between devices: 18.4 us -> 40.5 us
  blocking collectives: 17 us -> 0 us
  between operations: 14.4 us -> 1.2 us
  other arithmetic: 6.73 us -> 14.1 us
  local copies, waits for them, and re-layouts: 7.59 us -> 13.1 us
  matrix products: 16.1 us -> 19.4 us
    all_gather x1 -> x0, waiting for transfers between devices: 65.5 us -> none  [body(): lax.all_gather(tokens, 'head', axis=0, tiled=True)]
    ppermute x11 -> x27, starting transfers between devices: 18.4 us -> 40.5 us  [permute(): return lax.ppermute(value, AXES, pairs)]
    ppermute x11 -> x27, waiting for transfers between devices: 25.4 us -> 43.6 us  [permute(): return lax.ppermute(value, AXES, pairs)]
    all_to_all x1 -> x0, blocking collectives: 17 us -> none  [body(): lax.all_to_all(answer, 'head', split_axis=0, concat_axis=1, tiled=True)]
    mul x1 -> x2, other arithmetic: 0.69 us -> 9 us  [the longest x1 8.3 us: body(): weff = lax.optimization_barrier(w_qkv * factor)]
    dot_general x1 -> x6, matrix products: 9.52 us -> 13.1 us  [project(): return jnp.dot(tile, weff[c], preferred_element_type=F32).astype(BF16)]
    unnamed x25 -> x42, local copies, waits for them, and re-layouts: 4.23 us -> 7.44 us
  transfers between devices with their start and end apart: 12 -> 27, of which waited for: 11 -> 17; matrix products, arithmetic and copies ran while one was open for 2% -> 21% of each run, Pallas kernels for 0% -> 0%
where the time goes in v2:
time: 134 us; the launch traced here: 132 us
  waiting for transfers between devices  43.6 us (33%)
  starting transfers between devices  40.5 us (30%)
  matrix products  19.4 us (14%)
  other arithmetic  14.1 us (11%)
  local copies, waits for them, and re-layouts  13.1 us (10%)
    ppermute x27, waiting for transfers between devices, permute(): return lax.ppermute(value, AXES, pairs)  43.6 us
    ppermute x27, starting transfers between devices, permute(): return lax.ppermute(value, AXES, pairs)  40.5 us
    dot_general x6, matrix products, project(): return jnp.dot(tile, weff[c], preferred_element_type=F32).astype(BF16)  13.1 us
    mul x1, other arithmetic, body(): weff = lax.optimization_barrier(w_qkv * factor)  8.3 us
    unnamed x42, local copies, waits for them, and re-layouts  7.44 us
  transfers between devices with their start and end apart: 27, of which 17 were waited for; matrix products, arithmetic and copies ran while one was open for 21% of the time, Pallas kernels for 0%

profile of v2, /device:TPU:2, one launch (start us, length us, event | category | flops | bytes accessed | tf_op | source)
XLA Modules:
  0.0 132.0 jit_solution(16702195692951601896)
XLA Ops:
  0.0 1.5 %collective-permute-start.1 = (bf16[64,5120]{1,0:T(8,128)(2,1)}, bf16[64,5120]{1,0:T(8,128)(2,1)S(1)}, u32[]{:S(2)}, u32[]{:S(2)}) collective-permute-start(bf16[64,5120]{1,0:T(8,128)(2,1)} %param.8), channel_id=1, source_target_pairs={{0,3},{1,2},{2,1},{3,0},{4,7},{5,6},{6,5},{7,4},{8,11},{9,10},{10,... | collective-permute-start | bytes 1966088 | tf_op jit(solution)/shard_map/ppermute | solution.py:21
  1.5 1.8 %collective-permute-start = (bf16[64,5120]{1,0:T(8,128)(2,1)}, bf16[64,5120]{1,0:T(8,128)(2,1)S(1)}, u32[]{:S(2)}, u32[]{:S(2)}) collective-permute-start(bf16[64,5120]{1,0:T(8,128)(2,1)} %param.8), channel_id=1, source_target_pairs={{0,1},{1,0},{2,3},{3,2},{4,5},{5,4},{6,7},{7,6},{8,9},{9,8},{10,11... | collective-permute-start | bytes 1966088 | tf_op jit(solution)/shard_map/ppermute | solution.py:21
  3.9 0.7 multiply_reduce_fusion.1
  4.8 3.3 %collective-permute-start.10 = (f32[4,32]{1,0:T(4,128)S(1)}, f32[4,32]{1,0:T(4,128)S(1)}, u32[]{:S(2)}, u32[]{:S(2)}) collective-permute-start(f32[4,32]{1,0:T(4,128)S(1)} %get-tuple-element.43), channel_id=1, source_target_pairs={{0,64},{1,65},{2,66},{3,67},{4,196},{5,197},{6,198},{7,199},{8,72}... | collective-permute-start | bytes 1544 | tf_op jit(solution)/shard_map/ppermute | solution.py:21
  8.1 1.1 fusion.57
  9.2 4.1 %collective-permute-start.7 = (bf16[32,5120]{1,0:T(8,128)(2,1)S(1)}, bf16[32,5120]{1,0:T(8,128)(2,1)S(1)}, u32[]{:S(2)}, u32[]{:S(2)}) collective-permute-start(bf16[32,5120]{1,0:T(8,128)(2,1)S(1)} %get-tuple-element.18), channel_id=1, source_target_pairs={{0,196},{1,197},{2,198},{3,199},{4,64},{5,65},{6,66},{7,67},{8,204... | collective-permute-start | bytes 983048 | tf_op jit(solution)/shard_map/ppermute | solution.py:21
  13.4 1.0 collective-permute-start.4
  14.5 8.3 %broadcast_multiply_fusion = bf16[3,5120,320]{1,2,0:T(8,128)(2,1)} fusion(bf16[3,5120,320]{1,2,0:T(8,128)(2,1)} %param.9, bf16[3,5120]{1,0:T(4,128)(2,1)S(1)} %bitcast.100), kind=kLoop, calls=%fused_computation | loop fusion | flops 4915200 | bytes 19691520 | tf_op jit(solution)/shard_map/mul | solution.py:153
  22.8 0.9 constant_dynamic-update-slice_fusion.4
  24.5 0.6 collective-permute-start.2
  25.2 1.1 collective-permute-start.5
  26.3 1.6 %collective-permute-start.8 = (bf16[64,5120]{1,0:T(8,128)(2,1)S(1)}, bf16[64,5120]{1,0:T(8,128)(2,1)S(1)}, u32[]{:S(2)}, u32[]{:S(2)}) collective-permute-start(bf16[64,5120]{1,0:T(8,128)(2,1)S(1)} %pad_maximum_fusion.2), channel_id=1, source_target_pairs={{0,196},{1,197},{2,198},{3,199},{4,64},{5,65},{6,66},{7,67},{8,204... | collective-permute-start | bytes 1966088 | tf_op jit(solution)/shard_map/ppermute | solution.py:21
  27.9 0.9 constant_dynamic-update-slice_fusion.3
  28.8 0.9 constant_dynamic-update-slice_fusion.2
  29.7 2.8 %collective-permute-done.2 = bf16[32,5120]{1,0:T(8,128)(2,1)S(1)} collective-permute-done((bf16[32,5120]{1,0:T(8,128)(2,1)S(1)}, bf16[32,5120]{1,0:T(8,128)(2,1)S(1)}, u32[]{:S(2)}, u32[]{:S(2)}) %collective-permute-start.2) | collective-permute-done | bytes 327712 | tf_op jit(solution)/shard_map/ppermute | solution.py:21
  32.5 0.7 constant_dynamic-update-slice_fusion.1
  33.2 0.8 constant_dynamic-update-slice_fusion
  34.0 3.0 %fusion.7 = bf16[256,320]{0,1:T(8,128)(2,1)S(1)} fusion(bf16[256,5120]{1,0:T(8,128)(2,1)} %constant_dynamic-update-slice_fusion, bf16[3,5120,320]{1,2,0:T(8,128)(2,1)S(1)} %copy-done), kind=kOutput, calls=%fused_computation.22 | convolution fusion | flops 838942720 | bytes 6062080 | tf_op jit(solution)/shard_map/dot_general | solution.py:157
  37.0 0.9 collective-permute-start.9
  37.9 1.2 collective-permute-start.6
  39.1 1.0 fusion.9
  40.2 1.1 collective-permute-done.5
  41.3 5.5 %collective-permute-done.6 = bf16[32,5120]{1,0:T(8,128)(2,1)S(1)} collective-permute-done((bf16[32,5120]{1,0:T(8,128)(2,1)S(1)}, bf16[32,5120]{1,0:T(8,128)(2,1)S(1)}, u32[]{:S(2)}, u32[]{:S(2)}) %collective-permute-start.6) | collective-permute-done | bytes 327712 | tf_op jit(solution)/shard_map/ppermute | solution.py:21
  47.0 1.8 %collective-permute-done.9 = bf16[32,5120]{1,0:T(8,128)(2,1)S(1)} collective-permute-done((bf16[32,5120]{1,0:T(8,128)(2,1)S(1)}, bf16[32,5120]{1,0:T(8,128)(2,1)S(1)}, u32[]{:S(2)}, u32[]{:S(2)}) %collective-permute-start.9) | collective-permute-done | bytes 327712 | tf_op jit(solution)/shard_map/ppermute | solution.py:21
  48.8 1.0 fusion.8
  50.3 1.0 fusion.10
  51.4 0.6 fusion.26
  52.4 0.6 fusion.28
  53.4 0.6 fusion.30
  54.0 0.6 fusion.13
  54.6 0.8 fusion.16
  55.4 0.6 fusion.14
  56.5 0.9 dynamic-slice_convert_fusion
  57.5 2.4 %collective-permute-done.11 = bf16[320,960]{1,0:T(8,128)(2,1)} collective-permute-done((bf16[320,960]{1,0:T(8,128)(2,1)}, bf16[320,960]{1,0:T(8,128)(2,1)}, u32[]{:S(2)}, u32[]{:S(2)}) %collective-permute-start.11) | collective-permute-done | bytes 614432 | tf_op jit(solution)/shard_map/ppermute | solution.py:21
  59.9 1.2 convert_add_fusion
  61.2 1.1 copy-done.1
  62.3 1.7 %collective-permute-start.12 = (bf16[80,960]{1,0:T(8,128)(2,1)S(1)}, bf16[80,960]{1,0:T(8,128)(2,1)S(1)}, u32[]{:S(2)}, u32[]{:S(2)}) collective-permute-start(bf16[80,960]{1,0:T(8,128)(2,1)S(1)} %get-tuple-element.11), channel_id=1, source_target_pairs={{0,16},{1,17},{2,18},{3,19},{4,20},{5,21},{6,22},{7,23},{8,24},{9,... | collective-permute-start | bytes 460808 | tf_op jit(solution)/shard_map/ppermute | solution.py:21
  64.0 2.9 %collective-permute-start.14 = (bf16[80,960]{1,0:T(8,128)(2,1)S(1)}, bf16[80,960]{1,0:T(8,128)(2,1)S(1)}, u32[]{:S(2)}, u32[]{:S(2)}) collective-permute-start(bf16[80,960]{1,0:T(8,128)(2,1)S(1)} %get-tuple-element.12), channel_id=1, source_target_pairs={{0,32},{1,33},{2,34},{3,35},{4,36},{5,37},{6,38},{7,39},{8,40},{9,... | collective-permute-start | bytes 460808 | tf_op jit(solution)/shard_map/ppermute | solution.py:21
  66.9 1.3 %collective-permute-start.13 = (bf16[80,960]{1,0:T(8,128)(2,1)S(1)}, bf16[80,960]{1,0:T(8,128)(2,1)S(1)}, u32[]{:S(2)}, u32[]{:S(2)}) collective-permute-start(bf16[80,960]{1,0:T(8,128)(2,1)S(1)} %get-tuple-element.13), channel_id=1, source_target_pairs={{0,48},{1,49},{2,50},{3,51},{4,52},{5,53},{6,54},{7,55},{8,56},{9,... | collective-permute-start | bytes 460808 | tf_op jit(solution)/shard_map/ppermute | solution.py:21
  68.2 1.7 %collective-permute-done.12 = bf16[80,960]{1,0:T(8,128)(2,1)S(1)} collective-permute-done((bf16[80,960]{1,0:T(8,128)(2,1)S(1)}, bf16[80,960]{1,0:T(8,128)(2,1)S(1)}, u32[]{:S(2)}, u32[]{:S(2)}) %collective-permute-start.12) | collective-permute-done | bytes 153632 | tf_op jit(solution)/shard_map/ppermute | solution.py:21
  69.9 4.7 %collective-permute-done.14 = bf16[80,960]{1,0:T(8,128)(2,1)S(1)} collective-permute-done((bf16[80,960]{1,0:T(8,128)(2,1)S(1)}, bf16[80,960]{1,0:T(8,128)(2,1)S(1)}, u32[]{:S(2)}, u32[]{:S(2)}) %collective-permute-start.14) | collective-permute-done | bytes 153632 | tf_op jit(solution)/shard_map/ppermute | solution.py:21
  74.6 1.1 fusion.43
  75.7 3.5 %collective-permute-start.17 = (bf16[80,960]{1,0:T(8,128)(2,1)S(1)}, bf16[80,960]{1,0:T(8,128)(2,1)S(1)}, u32[]{:S(2)}, u32[]{:S(2)}) collective-permute-start(bf16[80,960]{1,0:T(8,128)(2,1)S(1)} %fusion.43), channel_id=1, source_target_pairs={{0,128},{1,129},{2,130},{3,131},{4,132},{5,133},{6,134},{7,135},{8... | collective-permute-start | bytes 460808 | tf_op jit(solution)/shard_map/ppermute | solution.py:21
  79.6 2.6 %collective-permute-start.15 = (bf16[80,960]{1,0:T(8,128)(2,1)S(1)}, bf16[80,960]{1,0:T(8,128)(2,1)}, u32[]{:S(2)}, u32[]{:S(2)}) collective-permute-start(bf16[80,960]{1,0:T(8,128)(2,1)S(1)} %fusion.43), channel_id=1, source_target_pairs={{0,64},{1,65},{2,66},{3,67},{4,68},{5,69},{6,70},{7,71},{8,72},{9,... | collective-permute-start | bytes 460808 | tf_op jit(solution)/shard_map/ppermute | solution.py:21
  83.4 6.3 %collective-permute-done.17 = bf16[80,960]{1,0:T(8,128)(2,1)S(1)} collective-permute-done((bf16[80,960]{1,0:T(8,128)(2,1)S(1)}, bf16[80,960]{1,0:T(8,128)(2,1)S(1)}, u32[]{:S(2)}, u32[]{:S(2)}) %collective-permute-start.17) | collective-permute-done | bytes 153632 | tf_op jit(solution)/shard_map/ppermute | solution.py:21
  89.7 5.2 %collective-permute-done.16 = bf16[80,960]{1,0:T(8,128)(2,1)} collective-permute-done((bf16[80,960]{1,0:T(8,128)(2,1)S(1)}, bf16[80,960]{1,0:T(8,128)(2,1)}, u32[]{:S(2)}, u32[]{:S(2)}) %collective-permute-start.16) | collective-permute-done | bytes 153632 | tf_op jit(solution)/shard_map/ppermute | solution.py:21
  94.9 1.3 %fusion.54 = (f32[80,960]{1,0:T(8,128)S(1)}, f32[80,960]{1,0:T(8,128)S(1)}) fusion(bf16[80,960]{1,0:T(8,128)(2,1)S(1)} %collective-permute-done.17, bf16[80,960]{1,0:T(8,128)(2,1)} %collective-permute-done.16, bf16[80,960]{1,0:T(8,128)(2,1)} %collective-permute-done.15, bf16[80,960]{1,0:T(8,128)(2,1)S(1)} %collective-permute-done.14, ...), kind=kLoop, calls=%fused_computation.127 | loop fusion | flops 1152000 | bytes 1996804 | tf_op jit(solution)/shard_map/mul | solution.py:178
  97.2 2.4 %collective-permute-start.20 = (bf16[80,960]{1,0:T(8,128)(2,1)S(1)}, bf16[80,960]{1,0:T(8,128)(2,1)S(1)}, u32[]{:S(2)}, u32[]{:S(2)}) collective-permute-start(bf16[80,960]{1,0:T(8,128)(2,1)S(1)} %get-tuple-element.6), channel_id=1, source_target_pairs={{0,32},{1,33},{2,34},{3,35},{4,36},{5,37},{6,38},{7,39},{8,40},{9,... | collective-permute-start | bytes 460808 | tf_op jit(solution)/shard_map/ppermute | solution.py:21
  99.6 1.6 %collective-permute-start.19 = (bf16[80,960]{1,0:T(8,128)(2,1)S(1)}, bf16[80,960]{1,0:T(8,128)(2,1)S(1)}, u32[]{:S(2)}, u32[]{:S(2)}) collective-permute-start(bf16[80,960]{1,0:T(8,128)(2,1)S(1)} %get-tuple-element.6), channel_id=1, source_target_pairs={{0,48},{1,49},{2,50},{3,51},{4,52},{5,53},{6,54},{7,55},{8,56},{9,... | collective-permute-start | bytes 460808 | tf_op jit(solution)/shard_map/ppermute | solution.py:21
  101.6 3.9 %fusion.11 = bf16[256,320]{0,1:T(8,128)(2,1)S(1)} fusion(bf16[256,5120]{1,0:T(8,128)(2,1)} %constant_dynamic-update-slice_fusion, bf16[3,5120,320]{1,2,0:T(8,128)(2,1)} %broadcast_multiply_fusion), kind=kOutput, calls=%fused_computation.26 | convolution fusion | flops 838942720 | bytes 6062080 | tf_op jit(solution)/shard_map/dot_general | solution.py:157
  105.8 2.6 %collective-permute-done.19 = bf16[80,960]{1,0:T(8,128)(2,1)S(1)} collective-permute-done((bf16[80,960]{1,0:T(8,128)(2,1)S(1)}, bf16[80,960]{1,0:T(8,128)(2,1)S(1)}, u32[]{:S(2)}, u32[]{:S(2)}) %collective-permute-start.19) | collective-permute-done | bytes 153632 | tf_op jit(solution)/shard_map/ppermute | solution.py:21
  108.8 3.0 %fusion.12 = bf16[256,320]{0,1:T(8,128)(2,1)S(1)} fusion(bf16[256,5120]{1,0:T(8,128)(2,1)S(1)} %copy-done.10, bf16[3,5120,320]{1,2,0:T(8,128)(2,1)} %broadcast_multiply_fusion), kind=kOutput, calls=%fused_computation.27 | convolution fusion | flops 838942720 | bytes 6062080 | tf_op jit(solution)/shard_map/dot_general | solution.py:157
  112.0 0.5 copy-done.7
  112.5 0.6 fusion.24
  113.1 2.0 %multiply_reduce_fusion = (f32[512]{0:T(512)S(1)}, f32[512,320]{0,1:T(8,128)S(1)}) fusion(bf16[640,960]{1,0:T(8,128)(2,1)S(1)} %constant_dynamic-update-slice_fusion.11, f32[512,640]{1,0:T(8,128)S(1)} %fusion.24, bf16[256,320]{0,1:T(8,128)(2,1)} %copy-done.7, bf16[256,320]{0,1:T(8,128)(2,1)S(1)} %fusion.11), kind=kOutput, calls=%fused_computation.34 | convolution fusion | flops 422379008 | bytes 3278848 | tf_op jit(solution)/shard_map/dot_general | solution.py:90
  115.5 2.1 %collective-permute-start.23 = (bf16[128,320]{0,1:T(8,128)(2,1)S(1)}, bf16[128,320]{0,1:T(8,128)(2,1)S(1)}, u32[]{:S(2)}, u32[]{:S(2)}) collective-permute-start(bf16[128,320]{0,1:T(8,128)(2,1)S(1)} %get-tuple-element.33), channel_id=1, source_target_pairs={{0,196},{1,197},{2,198},{3,199},{4,64},{5,65},{6,66},{7,67},{8,204... | collective-permute-start | bytes 245768 | tf_op jit(solution)/shard_map/ppermute | solution.py:21
  117.8 2.4 %collective-permute-done.22 = bf16[128,320]{0,1:T(8,128)(2,1)S(1)} collective-permute-done((bf16[128,320]{0,1:T(8,128)(2,1)S(1)}, bf16[128,320]{0,1:T(8,128)(2,1)S(1)}, u32[]{:S(2)}, u32[]{:S(2)}) %collective-permute-start.22) | collective-permute-done | bytes 81952 | tf_op jit(solution)/shard_map/ppermute | solution.py:21
  120.3 1.2 collective-permute-done.23
  121.8 1.7 %collective-permute-start.24 = (bf16[2,64,320]{2,1,0:T(8,128)(2,1)S(1)}, bf16[2,64,320]{2,1,0:T(8,128)(2,1)S(1)}, u32[]{:S(2)}, u32[]{:S(2)}) collective-permute-start(bf16[2,64,320]{2,1,0:T(8,128)(2,1)S(1)} %get-tuple-element.29), channel_id=1, source_target_pairs={{0,1},{1,0},{2,3},{3,2},{4,5},{5,4},{6,7},{7,6},{8,9},{9,8},{10,11... | collective-permute-start | bytes 245768 | tf_op jit(solution)/shard_map/ppermute | solution.py:21
  123.4 1.7 %collective-permute-start.26 = (bf16[2,64,320]{2,1,0:T(8,128)(2,1)S(1)}, bf16[2,64,320]{2,1,0:T(8,128)(2,1)S(1)}, u32[]{:S(2)}, u32[]{:S(2)}) collective-permute-start(bf16[2,64,320]{2,1,0:T(8,128)(2,1)S(1)} %get-tuple-element.30), channel_id=1, source_target_pairs={{0,2},{1,3},{2,0},{3,1},{4,6},{5,7},{6,4},{7,5},{8,10},{9,11},{10,... | collective-permute-start | bytes 245768 | tf_op jit(solution)/shard_map/ppermute | solution.py:21
  125.6 0.9 collective-permute-done.24
  126.5 3.3 %collective-permute-done.26 = bf16[2,64,320]{2,1,0:T(8,128)(2,1)S(1)} collective-permute-done((bf16[2,64,320]{2,1,0:T(8,128)(2,1)S(1)}, bf16[2,64,320]{2,1,0:T(8,128)(2,1)S(1)}, u32[]{:S(2)}, u32[]{:S(2)}) %collective-permute-start.26) | collective-permute-done | bytes 81952 | tf_op jit(solution)/shard_map/ppermute | solution.py:21
  129.8 1.1 collective-permute-done.25
  131.1 0.9 concatenate.64
  (94 shorter events, 8.4 us)
Async XLA Ops:
  0.0 14.4 %copy-start.11 = (s32[3,40,1]{1,2,0:T(1,128)S(1)}, s32[3,40,1]{1,2,0:T(1,128)}, u32[]{:S(2)}) copy-start(s32[3,40,1]{1,2,0:T(1,128)} %param.10) | copy-start | bytes 1444
  0.0 24.1 %collective-permute-start.1 = (bf16[64,5120]{1,0:T(8,128)(2,1)}, bf16[64,5120]{1,0:T(8,128)(2,1)S(1)}, u32[]{:S(2)}, u32[]{:S(2)}) collective-permute-start(bf16[64,5120]{1,0:T(8,128)(2,1)} %param.8), channel_id=1, source_target_pairs={{0,3},{1,2},{2,1},{3,0},{4,7},{5,6},{6,5},{7,4},{8,11},{9,10},{10,... | collective-permute-start | bytes 1966088 | tf_op jit(solution)/shard_map/ppermute | solution.py:21
  1.5 23.0 %collective-permute-start = (bf16[64,5120]{1,0:T(8,128)(2,1)}, bf16[64,5120]{1,0:T(8,128)(2,1)S(1)}, u32[]{:S(2)}, u32[]{:S(2)}) collective-permute-start(bf16[64,5120]{1,0:T(8,128)(2,1)} %param.8), channel_id=1, source_target_pairs={{0,1},{1,0},{2,3},{3,2},{4,5},{5,4},{6,7},{7,6},{8,9},{9,8},{10,11... | collective-permute-start | bytes 1966088 | tf_op jit(solution)/shard_map/ppermute | solution.py:21
  4.8 19.1 %collective-permute-start.10 = (f32[4,32]{1,0:T(4,128)S(1)}, f32[4,32]{1,0:T(4,128)S(1)}, u32[]{:S(2)}, u32[]{:S(2)}) collective-permute-start(f32[4,32]{1,0:T(4,128)S(1)} %get-tuple-element.43), channel_id=1, source_target_pairs={{0,64},{1,65},{2,66},{3,67},{4,196},{5,197},{6,198},{7,199},{8,72}... | collective-permute-start | bytes 1544 | tf_op jit(solution)/shard_map/ppermute | solution.py:21
  9.2 37.6 %collective-permute-start.7 = (bf16[32,5120]{1,0:T(8,128)(2,1)S(1)}, bf16[32,5120]{1,0:T(8,128)(2,1)S(1)}, u32[]{:S(2)}, u32[]{:S(2)}) collective-permute-start(bf16[32,5120]{1,0:T(8,128)(2,1)S(1)} %get-tuple-element.18), channel_id=1, source_target_pairs={{0,196},{1,197},{2,198},{3,199},{4,64},{5,65},{6,66},{7,67},{8,204... | collective-permute-start | bytes 983048 | tf_op jit(solution)/shard_map/ppermute | solution.py:21
  13.4 10.7 %collective-permute-start.4 = (bf16[32,5120]{1,0:T(8,128)(2,1)S(1)}, bf16[32,5120]{1,0:T(8,128)(2,1)S(1)}, u32[]{:S(2)}, u32[]{:S(2)}) collective-permute-start(bf16[32,5120]{1,0:T(8,128)(2,1)S(1)} %get-tuple-element.19), channel_id=1, source_target_pairs={{0,4},{1,5},{2,6},{3,7},{4,0},{5,1},{6,2},{7,3},{8,12},{9,13},{10,... | collective-permute-start | bytes 983048 | tf_op jit(solution)/shard_map/ppermute | solution.py:21
  14.5 8.3 %copy-start.2 = (bf16[64,5120]{1,0:T(8,128)(2,1)S(1)}, bf16[64,5120]{1,0:T(8,128)(2,1)}, u32[]{:S(2)}) copy-start(bf16[64,5120]{1,0:T(8,128)(2,1)} %param.8) | copy-start | bytes 1966084
  24.0 10.0 %copy-start = (bf16[3,5120,320]{1,2,0:T(8,128)(2,1)S(1)}, bf16[3,5120,320]{1,2,0:T(8,128)(2,1)}, u32[]{:S(2)}) copy-start(bf16[3,5120,320]{1,2,0:T(8,128)(2,1)} %broadcast_multiply_fusion) | copy-start | bytes 29491204
  24.1 9.1 %collective-permute-start.3 = (bf16[32,5120]{1,0:T(8,128)(2,1)S(1)}, bf16[32,5120]{1,0:T(8,128)(2,1)S(1)}, u32[]{:S(2)}, u32[]{:S(2)}) collective-permute-start(bf16[32,5120]{1,0:T(8,128)(2,1)S(1)} %get-tuple-element.16), channel_id=1, source_target_pairs={{0,1},{1,0},{2,3},{3,2},{4,5},{5,4},{6,7},{7,6},{8,9},{9,8},{10,11... | collective-permute-start | bytes 983048 | tf_op jit(solution)/shard_map/ppermute | solution.py:21
  24.5 7.9 %collective-permute-start.2 = (bf16[32,5120]{1,0:T(8,128)(2,1)S(1)}, bf16[32,5120]{1,0:T(8,128)(2,1)S(1)}, u32[]{:S(2)}, u32[]{:S(2)}) collective-permute-start(bf16[32,5120]{1,0:T(8,128)(2,1)S(1)} %get-tuple-element.15), channel_id=1, source_target_pairs={{0,3},{1,2},{2,1},{3,0},{4,7},{5,6},{6,5},{7,4},{8,11},{9,10},{10,... | collective-permute-start | bytes 983048 | tf_op jit(solution)/shard_map/ppermute | solution.py:21
  25.2 16.1 %collective-permute-start.5 = (bf16[64,5120]{1,0:T(8,128)(2,1)S(1)}, bf16[64,5120]{1,0:T(8,128)(2,1)S(1)}, u32[]{:S(2)}, u32[]{:S(2)}) collective-permute-start(bf16[64,5120]{1,0:T(8,128)(2,1)S(1)} %pad_maximum_fusion.1), channel_id=1, source_target_pairs={{0,4},{1,5},{2,6},{3,7},{4,0},{5,1},{6,2},{7,3},{8,12},{9,13},{10,... | collective-permute-start | bytes 1966088 | tf_op jit(solution)/shard_map/ppermute | solution.py:21
  26.3 20.6 %collective-permute-start.8 = (bf16[64,5120]{1,0:T(8,128)(2,1)S(1)}, bf16[64,5120]{1,0:T(8,128)(2,1)S(1)}, u32[]{:S(2)}, u32[]{:S(2)}) collective-permute-start(bf16[64,5120]{1,0:T(8,128)(2,1)S(1)} %pad_maximum_fusion.2), channel_id=1, source_target_pairs={{0,196},{1,197},{2,198},{3,199},{4,64},{5,65},{6,66},{7,67},{8,204... | collective-permute-start | bytes 1966088 | tf_op jit(solution)/shard_map/ppermute | solution.py:21
  34.0 5.1 %copy-start.8 = (bf16[256,5120]{1,0:T(8,128)(2,1)S(1)}, bf16[256,5120]{1,0:T(8,128)(2,1)}, u32[]{:S(2)}) copy-start(bf16[256,5120]{1,0:T(8,128)(2,1)} %constant_dynamic-update-slice_fusion) | copy-start | bytes 7864324
  37.0 11.8 %collective-permute-start.9 = (bf16[32,5120]{1,0:T(8,128)(2,1)S(1)}, bf16[32,5120]{1,0:T(8,128)(2,1)S(1)}, u32[]{:S(2)}, u32[]{:S(2)}) collective-permute-start(bf16[32,5120]{1,0:T(8,128)(2,1)S(1)} %collective-permute-done.3), channel_id=1, source_target_pairs={{0,196},{1,197},{2,198},{3,199},{4,64},{5,65},{6,66},{7,67},{8,204... | collective-permute-start | bytes 983048 | tf_op jit(solution)/shard_map/ppermute | solution.py:21
  37.9 8.9 %collective-permute-start.6 = (bf16[32,5120]{1,0:T(8,128)(2,1)S(1)}, bf16[32,5120]{1,0:T(8,128)(2,1)S(1)}, u32[]{:S(2)}, u32[]{:S(2)}) collective-permute-start(bf16[32,5120]{1,0:T(8,128)(2,1)S(1)} %collective-permute-done.2), channel_id=1, source_target_pairs={{0,4},{1,5},{2,6},{3,7},{4,0},{5,1},{6,2},{7,3},{8,12},{9,13},{10,... | collective-permute-start | bytes 983048 | tf_op jit(solution)/shard_map/ppermute | solution.py:21
  48.8 1.5 %copy-start.9 = (bf16[256,5120]{1,0:T(8,128)(2,1)}, bf16[256,5120]{1,0:T(8,128)(2,1)S(1)}, u32[]{:S(2)}) copy-start(bf16[256,5120]{1,0:T(8,128)(2,1)S(1)} %constant_dynamic-update-slice_fusion.5) | copy-start | bytes 7864324
  50.3 1.1 copy-start.3
  51.4 1.0 copy-start.4
  52.4 1.0 copy-start.5
  57.5 2.4 %collective-permute-start.11 = (bf16[320,960]{1,0:T(8,128)(2,1)}, bf16[320,960]{1,0:T(8,128)(2,1)}, u32[]{:S(2)}, u32[]{:S(2)}) collective-permute-start(bf16[320,960]{1,0:T(8,128)(2,1)} %dynamic-slice_convert_fusion), channel_id=1, source_target_pairs={{0,8},{1,9},{2,10},{3,11},{4,12},{5,13},{6,14},{7,15},{8,0},{9,1},... | collective-permute-start | bytes 1843208 | tf_op jit(solution)/shard_map/ppermute | solution.py:21
  61.2 1.1 copy-start.1
  62.3 7.6 %collective-permute-start.12 = (bf16[80,960]{1,0:T(8,128)(2,1)S(1)}, bf16[80,960]{1,0:T(8,128)(2,1)S(1)}, u32[]{:S(2)}, u32[]{:S(2)}) collective-permute-start(bf16[80,960]{1,0:T(8,128)(2,1)S(1)} %get-tuple-element.11), channel_id=1, source_target_pairs={{0,16},{1,17},{2,18},{3,19},{4,20},{5,21},{6,22},{7,23},{8,24},{9,... | collective-permute-start | bytes 460808 | tf_op jit(solution)/shard_map/ppermute | solution.py:21
  64.0 10.6 %collective-permute-start.14 = (bf16[80,960]{1,0:T(8,128)(2,1)S(1)}, bf16[80,960]{1,0:T(8,128)(2,1)S(1)}, u32[]{:S(2)}, u32[]{:S(2)}) collective-permute-start(bf16[80,960]{1,0:T(8,128)(2,1)S(1)} %get-tuple-element.12), channel_id=1, source_target_pairs={{0,32},{1,33},{2,34},{3,35},{4,36},{5,37},{6,38},{7,39},{8,40},{9,... | collective-permute-start | bytes 460808 | tf_op jit(solution)/shard_map/ppermute | solution.py:21
  66.9 7.7 %collective-permute-start.13 = (bf16[80,960]{1,0:T(8,128)(2,1)S(1)}, bf16[80,960]{1,0:T(8,128)(2,1)S(1)}, u32[]{:S(2)}, u32[]{:S(2)}) collective-permute-start(bf16[80,960]{1,0:T(8,128)(2,1)S(1)} %get-tuple-element.13), channel_id=1, source_target_pairs={{0,48},{1,49},{2,50},{3,51},{4,52},{5,53},{6,54},{7,55},{8,56},{9,... | collective-permute-start | bytes 460808 | tf_op jit(solution)/shard_map/ppermute | solution.py:21
  68.2 14.5 %copy-start.6 = (bf16[1,320,640]{2,1,0:T(8,128)(2,1)S(1)}, bf16[1,320,640]{2,1,0:T(8,128)(2,1)}, u32[]{:S(2)}) copy-start(bf16[1,320,640]{2,1,0:T(8,128)(2,1)} %param.15) | copy-start | bytes 1228804
  75.7 14.1 %collective-permute-start.17 = (bf16[80,960]{1,0:T(8,128)(2,1)S(1)}, bf16[80,960]{1,0:T(8,128)(2,1)S(1)}, u32[]{:S(2)}, u32[]{:S(2)}) collective-permute-start(bf16[80,960]{1,0:T(8,128)(2,1)S(1)} %fusion.43), channel_id=1, source_target_pairs={{0,128},{1,129},{2,130},{3,131},{4,132},{5,133},{6,134},{7,135},{8... | collective-permute-start | bytes 460808 | tf_op jit(solution)/shard_map/ppermute | solution.py:21
  79.2 15.7 %collective-permute-start.16 = (bf16[80,960]{1,0:T(8,128)(2,1)S(1)}, bf16[80,960]{1,0:T(8,128)(2,1)}, u32[]{:S(2)}, u32[]{:S(2)}) collective-permute-start(bf16[80,960]{1,0:T(8,128)(2,1)S(1)} %fusion.43), channel_id=1, source_target_pairs={{0,192},{1,193},{2,194},{3,195},{4,196},{5,197},{6,198},{7,199},{8... | collective-permute-start | bytes 460808 | tf_op jit(solution)/shard_map/ppermute | solution.py:21
  79.6 15.4 %collective-permute-start.15 = (bf16[80,960]{1,0:T(8,128)(2,1)S(1)}, bf16[80,960]{1,0:T(8,128)(2,1)}, u32[]{:S(2)}, u32[]{:S(2)}) collective-permute-start(bf16[80,960]{1,0:T(8,128)(2,1)S(1)} %fusion.43), channel_id=1, source_target_pairs={{0,64},{1,65},{2,66},{3,67},{4,68},{5,69},{6,70},{7,71},{8,72},{9,... | collective-permute-start | bytes 460808 | tf_op jit(solution)/shard_map/ppermute | solution.py:21
  97.2 8.7 %collective-permute-start.20 = (bf16[80,960]{1,0:T(8,128)(2,1)S(1)}, bf16[80,960]{1,0:T(8,128)(2,1)S(1)}, u32[]{:S(2)}, u32[]{:S(2)}) collective-permute-start(bf16[80,960]{1,0:T(8,128)(2,1)S(1)} %get-tuple-element.6), channel_id=1, source_target_pairs={{0,32},{1,33},{2,34},{3,35},{4,36},{5,37},{6,38},{7,39},{8,40},{9,... | collective-permute-start | bytes 460808 | tf_op jit(solution)/shard_map/ppermute | solution.py:21
  99.6 8.8 %collective-permute-start.19 = (bf16[80,960]{1,0:T(8,128)(2,1)S(1)}, bf16[80,960]{1,0:T(8,128)(2,1)S(1)}, u32[]{:S(2)}, u32[]{:S(2)}) collective-permute-start(bf16[80,960]{1,0:T(8,128)(2,1)S(1)} %get-tuple-element.6), channel_id=1, source_target_pairs={{0,48},{1,49},{2,50},{3,51},{4,52},{5,53},{6,54},{7,55},{8,56},{9,... | collective-permute-start | bytes 460808 | tf_op jit(solution)/shard_map/ppermute | solution.py:21
  101.2 7.5 %collective-permute-start.18 = (bf16[80,960]{1,0:T(8,128)(2,1)S(1)}, bf16[80,960]{1,0:T(8,128)(2,1)S(1)}, u32[]{:S(2)}, u32[]{:S(2)}) collective-permute-start(bf16[80,960]{1,0:T(8,128)(2,1)S(1)} %get-tuple-element.6), channel_id=1, source_target_pairs={{0,16},{1,17},{2,18},{3,19},{4,20},{5,21},{6,22},{7,23},{8,24},{9,... | collective-permute-start | bytes 460808 | tf_op jit(solution)/shard_map/ppermute | solution.py:21
  101.6 7.2 %copy-start.10 = (bf16[256,5120]{1,0:T(8,128)(2,1)S(1)}, bf16[256,5120]{1,0:T(8,128)(2,1)}, u32[]{:S(2)}) copy-start(bf16[256,5120]{1,0:T(8,128)(2,1)} %copy-done.9) | copy-start | bytes 7864324
  108.7 3.2 %collective-permute-start.21 = (bf16[320,960]{1,0:T(8,128)(2,1)S(1)}, bf16[320,960]{1,0:T(8,128)(2,1)S(1)}, u32[]{:S(2)}, u32[]{:S(2)}) collective-permute-start(bf16[320,960]{1,0:T(8,128)(2,1)S(1)} %pad_maximum_fusion.3), channel_id=1, source_target_pairs={{0,8},{1,9},{2,10},{3,11},{4,12},{5,13},{6,14},{7,15},{8,0},{9,1},... | collective-permute-start | bytes 1843208 | tf_op jit(solution)/shard_map/ppermute | solution.py:21
  111.9 0.7 copy-start.7
  115.3 4.9 %collective-permute-start.22 = (bf16[128,320]{0,1:T(8,128)(2,1)S(1)}, bf16[128,320]{0,1:T(8,128)(2,1)S(1)}, u32[]{:S(2)}, u32[]{:S(2)}) collective-permute-start(bf16[128,320]{0,1:T(8,128)(2,1)S(1)} %get-tuple-element.32), channel_id=1, source_target_pairs={{0,4},{1,5},{2,6},{3,7},{4,0},{5,1},{6,2},{7,3},{8,12},{9,13},{10,... | collective-permute-start | bytes 245768 | tf_op jit(solution)/shard_map/ppermute | solution.py:21
  115.5 6.0 %collective-permute-start.23 = (bf16[128,320]{0,1:T(8,128)(2,1)S(1)}, bf16[128,320]{0,1:T(8,128)(2,1)S(1)}, u32[]{:S(2)}, u32[]{:S(2)}) collective-permute-start(bf16[128,320]{0,1:T(8,128)(2,1)S(1)} %get-tuple-element.33), channel_id=1, source_target_pairs={{0,196},{1,197},{2,198},{3,199},{4,64},{5,65},{6,66},{7,67},{8,204... | collective-permute-start | bytes 245768 | tf_op jit(solution)/shard_map/ppermute | solution.py:21
  121.8 4.7 %collective-permute-start.24 = (bf16[2,64,320]{2,1,0:T(8,128)(2,1)S(1)}, bf16[2,64,320]{2,1,0:T(8,128)(2,1)S(1)}, u32[]{:S(2)}, u32[]{:S(2)}) collective-permute-start(bf16[2,64,320]{2,1,0:T(8,128)(2,1)S(1)} %get-tuple-element.29), channel_id=1, source_target_pairs={{0,1},{1,0},{2,3},{3,2},{4,5},{5,4},{6,7},{7,6},{8,9},{9,8},{10,11... | collective-permute-start | bytes 245768 | tf_op jit(solution)/shard_map/ppermute | solution.py:21
  123.4 6.4 %collective-permute-start.26 = (bf16[2,64,320]{2,1,0:T(8,128)(2,1)S(1)}, bf16[2,64,320]{2,1,0:T(8,128)(2,1)S(1)}, u32[]{:S(2)}, u32[]{:S(2)}) collective-permute-start(bf16[2,64,320]{2,1,0:T(8,128)(2,1)S(1)} %get-tuple-element.30), channel_id=1, source_target_pairs={{0,2},{1,3},{2,0},{3,1},{4,6},{5,7},{6,4},{7,5},{8,10},{9,11},{10,... | collective-permute-start | bytes 245768 | tf_op jit(solution)/shard_map/ppermute | solution.py:21
  125.1 5.8 %collective-permute-start.25 = (bf16[2,64,320]{2,1,0:T(8,128)(2,1)S(1)}, bf16[2,64,320]{2,1,0:T(8,128)(2,1)S(1)}, u32[]{:S(2)}, u32[]{:S(2)}) collective-permute-start(bf16[2,64,320]{2,1,0:T(8,128)(2,1)S(1)} %get-tuple-element.31), channel_id=1, source_target_pairs={{0,3},{1,2},{2,1},{3,0},{4,7},{5,6},{6,5},{7,4},{8,11},{9,10},{10,... | collective-permute-start | bytes 245768 | tf_op jit(solution)/shard_map/ppermute | solution.py:21

commit v3 on v2

--- a/solution.py
+++ b/solution.py
@@ -106,8 +106,8 @@
     z4 = to_far_z(jnp.concatenate([near_tile[32:], far_tile[32:]]))
     z5, z6 = to_near_z(opposite_first), to_far_z(opposite_second)
     return (
-        jnp.concatenate([tokens, near_tile, far_tile, opposite_first, opposite_second]),
-        jnp.concatenate([z1, z3, z5, z2, z4, z6]),
+        [tokens, near_tile, far_tile, opposite_first, opposite_second],
+        [z1, z3, z5, z2, z4, z6],
     )
 
 
@@ -126,11 +126,11 @@
     return jnp.concatenate([same.reshape(256), other[:, :32].reshape(128), moved.reshape(128)])
 
 
-def send_back(answer, z_lo, x):
-    from_near = to_near_z(answer[256:384]).reshape(4, 32, 320)
-    from_far = to_far_z(answer[384:]).reshape(4, 32, 320)
+def send_back(plane, others, z_lo, x):
+    from_near = to_near_z(others[:128]).reshape(4, 32, 320)
+    from_far = to_far_z(others[128:]).reshape(4, 32, 320)
     other = jnp.concatenate([from_near, from_far], axis=1)
-    both = jnp.stack([answer[:256].reshape(4, 64, 320), other], axis=1)
+    both = jnp.stack([plane.reshape(4, 64, 320), other], axis=1)
     slots = jnp.stack(
         [both[0], to_near_x(both[1]), to_far_x(both[2]), to_opposite_x(both[3])]
     ).reshape(8, 64, 320)
@@ -150,14 +150,21 @@
     factor = jnp.exp2(scale_exp.astype(F32))[:, :, 0]
     block_rows = w_qkv.shape[1] // factor.shape[1]
     factor = jnp.repeat(factor, block_rows, axis=1)[:, :, None].astype(BF16)
-    weff = lax.optimization_barrier(w_qkv * factor)
+    weff_kv = lax.optimization_barrier(w_qkv[1:] * factor[1:])
     weight = weights_of_rows(rate[0] * gate_mask[:, 0].astype(F32), z_lo, x)
     plane, others = gather(tokens)
-    def project(tile, c):
-        return jnp.dot(tile, weff[c], preferred_element_type=F32).astype(BF16)
-    keys = jnp.concatenate([project(plane, 1), project(others, 1)])
-    values = jnp.concatenate([project(plane, 2), project(others, 2)])
-    query = jnp.concatenate([project(plane, 0), project(others, 0)])
+
+    def project(tile, w):
+        return jnp.dot(tile, w, preferred_element_type=F32).astype(BF16)
+
+    plane, others[1], others[4] = lax.optimization_barrier((plane, others[1], others[4]))
+    plane = jnp.concatenate(plane)
+    weff_q = w_qkv[0] * factor[0]
+    ready = project(plane, weff_kv[0]), project(plane, weff_kv[1]), project(plane, weff_q)
+    ready, others = lax.optimization_barrier((ready, others))
+    others = jnp.concatenate(others)
+    keys = jnp.concatenate([ready[0], project(others, weff_kv[0])])
+    values = jnp.concatenate([ready[1], project(others, weff_kv[1])])
     old = jnp.stack([fast_gate[0], fast_up[0], fast_down[0]])
     part = local_grads(keys, values, weight, old)
 
@@ -167,9 +174,12 @@
     piece = rows(half, y * 80, 80)
     for d in (1, 3, 2):
         piece += to_y(rows(half, (y + d) % 4 * 80, 80).astype(BF16), d).astype(F32)
+    others, piece = lax.optimization_barrier((others, piece))
     small = piece.astype(BF16)
-    for d in (1, 3, 2):
-        piece += to_z(small, d).astype(F32)
+    got = to_z(small, 2), to_z(small, 1), to_z(small, 3)
+    query_others, got = lax.optimization_barrier((project(others, weff_q), got))
+    for term in got:
+        piece += term.astype(F32)
 
     old_t = jnp.concatenate([fast_gate[0].T, fast_up[0].T, fast_down[0].T], axis=1)
     old_f = rows(old_t, core * 320 + y * 80, 80).astype(F32).reshape(80, 3, 320)
@@ -180,8 +190,9 @@
     column = jnp.concatenate([mine, to_y(mine, 1), to_y(mine, 3), to_y(mine, 2)], axis=0)
     renorm = jnp.concatenate([column, to_core(column)], axis=0)
 
-    answer = respond(query, renorm)
-    return send_back(answer, z_lo, x)
+    answers = respond(query_others, renorm)
+    query_plane, answers = lax.optimization_barrier((ready[2], answers))
+    return send_back(respond(query_plane, renorm), answers, z_lo, x)
 
 
 def solution(mesh):

time: 134 us -> 137 us (1.022)
  starting transfers between devices: 40.5 us -> 50 us
  waiting for transfers between devices: 43.6 us -> 38.5 us
    ppermute x27, starting transfers between devices: 40.5 us -> 50 us  [permute(): return lax.ppermute(value, AXES, pairs)]
    ppermute x27, waiting for transfers between devices: 43.6 us -> 38.5 us  [permute(): return lax.ppermute(value, AXES, pairs)]
    mul x1, other arithmetic: 8.3 us -> 6.13 us  [body(): weff_kv = lax.optimization_barrier(w_qkv[1:] * factor[1:])]
    unnamed x42 -> x38, local copies, waits for them, and re-layouts: 7.44 us -> 6.68 us
  transfers between devices with their start and end apart: 27 -> 27, of which waited for: 17 -> 20; matrix products, arithmetic and copies ran while one was open for 21% -> 20% of each run, Pallas kernels for 0% -> 0%
where the time goes in v3:
time: 137 us; the launch traced here: 135 us
  starting transfers between devices  50 us (36%)
  waiting for transfers between devices  38.5 us (28%)
  matrix products  20.1 us (15%)
  other arithmetic  13.2 us (10%)
  local copies, waits for them, and re-layouts  12.5 us (9%)
    ppermute x27, starting transfers between devices, permute(): return lax.ppermute(value, AXES, pairs)  50 us
    ppermute x27, waiting for transfers between devices, permute(): return lax.ppermute(value, AXES, pairs)  38.5 us
    dot_general x6, matrix products, project(): return jnp.dot(tile, w, preferred_element_type=F32).astype(BF16)  14 us
    unnamed x38, local copies, waits for them, and re-layouts  6.68 us
    mul x1, other arithmetic, body(): weff_kv = lax.optimization_barrier(w_qkv[1:] * factor[1:])  6.13 us
  transfers between devices with their start and end apart: 27, of which 20 were waited for; matrix products, arithmetic and copies ran while one was open for 20% of the time, Pallas kernels for 0%

profile of v3, /device:TPU:2, one launch (start us, length us, event | category | flops | bytes accessed | tf_op | source)
XLA Modules:
  0.0 135.5 jit_solution(6403094033342943405)
XLA Ops:
  0.0 2.3 %collective-permute-start = (bf16[64,5120]{1,0:T(8,128)(2,1)}, bf16[64,5120]{1,0:T(8,128)(2,1)S(1)}, u32[]{:S(2)}, u32[]{:S(2)}) collective-permute-start(bf16[64,5120]{1,0:T(8,128)(2,1)} %param.8), channel_id=1, source_target_pairs={{0,1},{1,0},{2,3},{3,2},{4,5},{5,4},{6,7},{7,6},{8,9},{9,8},{10,11... | collective-permute-start | bytes 1966088 | tf_op jit(solution)/shard_map/ppermute | solution.py:21
  3.3 0.7 multiply_reduce_fusion.2
  4.2 3.3 %collective-permute-start.10 = (f32[4,32]{1,0:T(4,128)S(1)}, f32[4,32]{1,0:T(4,128)S(1)}, u32[]{:S(2)}, u32[]{:S(2)}) collective-permute-start(f32[4,32]{1,0:T(4,128)S(1)} %get-tuple-element.89), channel_id=1, source_target_pairs={{0,64},{1,65},{2,66},{3,67},{4,196},{5,197},{6,198},{7,199},{8,72}... | collective-permute-start | bytes 1544 | tf_op jit(solution)/shard_map/ppermute | solution.py:21
  7.5 0.7 exponential_convert_fusion
  8.3 6.1 %slice_multiply_fusion = bf16[2,5120,320]{1,2,0:T(8,128)(2,1)} fusion(bf16[3,5120,320]{1,2,0:T(8,128)(2,1)} %param.9, bf16[2,5120]{1,0:T(2,128)(2,1)S(1)} %bitcast.113), kind=kLoop, calls=%fused_computation | loop fusion | flops 3276800 | bytes 13127680 | tf_op jit(solution)/shard_map/mul | solution.py:153
  14.6 0.9 fusion.66
  15.4 1.2 collective-permute-done
  16.7 0.7 collective-permute-done.1
  17.4 0.9 pad_maximum_fusion.1
  18.4 2.2 %collective-permute-start.4 = (bf16[64,5120]{1,0:T(8,128)(2,1)}, bf16[64,5120]{1,0:T(8,128)(2,1)}, u32[]{:S(2)}, u32[]{:S(2)}) collective-permute-start(bf16[64,5120]{1,0:T(8,128)(2,1)} %pad_maximum_fusion.1), channel_id=1, source_target_pairs={{0,4},{1,5},{2,6},{3,7},{4,0},{5,1},{6,2},{7,3},{8,12},{9,13},{10,... | collective-permute-start | bytes 1966088 | tf_op jit(solution)/shard_map/ppermute | solution.py:21
  20.5 0.9 pad_maximum_fusion.2
  21.5 4.7 %collective-permute-start.5 = (bf16[64,5120]{1,0:T(8,128)(2,1)}, bf16[64,5120]{1,0:T(8,128)(2,1)S(1)}, u32[]{:S(2)}, u32[]{:S(2)}) collective-permute-start(bf16[64,5120]{1,0:T(8,128)(2,1)} %pad_maximum_fusion.2), channel_id=1, source_target_pairs={{0,196},{1,197},{2,198},{3,199},{4,64},{5,65},{6,66},{7,67},{8,204... | collective-permute-start | bytes 1966088 | tf_op jit(solution)/shard_map/ppermute | solution.py:21
  26.2 1.8 %collective-permute-start.2 = (bf16[32,5120]{1,0:T(8,128)(2,1)S(1)}, bf16[32,5120]{1,0:T(8,128)(2,1)}, u32[]{:S(2)}, u32[]{:S(2)}) collective-permute-start(bf16[32,5120]{1,0:T(8,128)(2,1)S(1)} %get-tuple-element.63), channel_id=1, source_target_pairs={{0,3},{1,2},{2,1},{3,0},{4,7},{5,6},{6,5},{7,4},{8,11},{9,10},{10,... | collective-permute-start | bytes 983048 | tf_op jit(solution)/shard_map/ppermute | solution.py:21
  28.0 2.6 %collective-permute-start.3 = (bf16[32,5120]{1,0:T(8,128)(2,1)S(1)}, bf16[32,5120]{1,0:T(8,128)(2,1)}, u32[]{:S(2)}, u32[]{:S(2)}) collective-permute-start(bf16[32,5120]{1,0:T(8,128)(2,1)S(1)} %get-tuple-element.65), channel_id=1, source_target_pairs={{0,1},{1,0},{2,3},{3,2},{4,5},{5,4},{6,7},{7,6},{8,9},{9,8},{10,11... | collective-permute-start | bytes 983048 | tf_op jit(solution)/shard_map/ppermute | solution.py:21
  30.9 3.5 %collective-permute-done.2 = bf16[32,5120]{1,0:T(8,128)(2,1)} collective-permute-done((bf16[32,5120]{1,0:T(8,128)(2,1)S(1)}, bf16[32,5120]{1,0:T(8,128)(2,1)}, u32[]{:S(2)}, u32[]{:S(2)}) %collective-permute-start.2) | collective-permute-done | bytes 327712 | tf_op jit(solution)/shard_map/ppermute | solution.py:21
  34.7 1.7 %collective-permute-done.3 = bf16[32,5120]{1,0:T(8,128)(2,1)} collective-permute-done((bf16[32,5120]{1,0:T(8,128)(2,1)S(1)}, bf16[32,5120]{1,0:T(8,128)(2,1)}, u32[]{:S(2)}, u32[]{:S(2)}) %collective-permute-start.3) | collective-permute-done | bytes 327712 | tf_op jit(solution)/shard_map/ppermute | solution.py:21
  36.5 5.7 %collective-permute-start.9 = (bf16[32,5120]{1,0:T(8,128)(2,1)}, bf16[32,5120]{1,0:T(8,128)(2,1)S(1)}, u32[]{:S(2)}, u32[]{:S(2)}) collective-permute-start(bf16[32,5120]{1,0:T(8,128)(2,1)} %collective-permute-done.3), channel_id=1, source_target_pairs={{0,196},{1,197},{2,198},{3,199},{4,64},{5,65},{6,66},{7,67},{8,204... | collective-permute-start | bytes 983048 | tf_op jit(solution)/shard_map/ppermute | solution.py:21
  42.4 1.0 constant_dynamic-update-slice_fusion.1
  43.4 1.0 constant_dynamic-update-slice_fusion
  44.4 3.2 %fusion.13 = bf16[256,320]{0,1:T(8,128)(2,1)S(1)} fusion(bf16[256,5120]{1,0:T(8,128)(2,1)S(1)} %constant_dynamic-update-slice_fusion, bf16[2,5120,320]{1,2,0:T(8,128)(2,1)} %slice_multiply_fusion), kind=kOutput, calls=%fused_computation.27 | convolution fusion | flops 838942720 | bytes 6062080 | tf_op jit(solution)/shard_map/dot_general | solution.py:158
  47.6 3.9 %fusion.9 = bf16[256,320]{0,1:T(8,128)(2,1)} fusion(bf16[256,5120]{1,0:T(8,128)(2,1)S(1)} %constant_dynamic-update-slice_fusion, bf16[3,5120,320]{1,2,0:T(8,128)(2,1)} %param.9, bf16[5120]{0:T(1024)(128)(2,1)S(1)} %broadcast_bitcast_fusion.1), kind=kOutput, calls=%fused_computation.23 | convolution fusion | flops 840581120 | bytes 6072320 | tf_op jit(solution)/shard_map/dot_general | solution.py:158
  51.4 1.0 fusion.11
  52.5 1.5 %collective-permute-done.9 = bf16[32,5120]{1,0:T(8,128)(2,1)S(1)} collective-permute-done((bf16[32,5120]{1,0:T(8,128)(2,1)}, bf16[32,5120]{1,0:T(8,128)(2,1)S(1)}, u32[]{:S(2)}, u32[]{:S(2)}) %collective-permute-start.9) | collective-permute-done | bytes 327712 | tf_op jit(solution)/shard_map/ppermute | solution.py:21
  54.0 1.0 constant_dynamic-update-slice_fusion.10
  55.0 1.1 constant_dynamic-update-slice_fusion.9
  56.3 1.0 fusion.14
  57.8 1.0 fusion.12
  58.8 0.6 fusion.40
  60.8 0.6 fusion.42
  61.4 0.6 fusion.16
  62.0 0.6 fusion.15
  62.6 0.7 fusion.17
  63.9 1.0 dynamic-slice_convert_fusion
  64.9 2.4 %collective-permute-done.11 = bf16[320,960]{1,0:T(8,128)(2,1)} collective-permute-done((bf16[320,960]{1,0:T(8,128)(2,1)}, bf16[320,960]{1,0:T(8,128)(2,1)}, u32[]{:S(2)}, u32[]{:S(2)}) %collective-permute-start.11) | collective-permute-done | bytes 614432 | tf_op jit(solution)/shard_map/ppermute | solution.py:21
  67.3 1.2 convert_add_fusion
  68.6 1.1 copy-done
  69.7 3.3 %collective-permute-start.14 = (bf16[80,960]{1,0:T(8,128)(2,1)S(1)}, bf16[80,960]{1,0:T(8,128)(2,1)S(1)}, u32[]{:S(2)}, u32[]{:S(2)}) collective-permute-start(bf16[80,960]{1,0:T(8,128)(2,1)S(1)} %get-tuple-element.58), channel_id=1, source_target_pairs={{0,32},{1,33},{2,34},{3,35},{4,36},{5,37},{6,38},{7,39},{8,40},{9,... | collective-permute-start | bytes 460808 | tf_op jit(solution)/shard_map/ppermute | solution.py:21
  73.0 1.1 collective-permute-start.13
  74.0 1.0 collective-permute-start.12
  76.3 2.0 %collective-permute-done.14 = bf16[80,960]{1,0:T(8,128)(2,1)S(1)} collective-permute-done((bf16[80,960]{1,0:T(8,128)(2,1)S(1)}, bf16[80,960]{1,0:T(8,128)(2,1)S(1)}, u32[]{:S(2)}, u32[]{:S(2)}) %collective-permute-start.14) | collective-permute-done | bytes 153632 | tf_op jit(solution)/shard_map/ppermute | solution.py:21
  78.3 3.1 %collective-permute-done.13 = bf16[80,960]{1,0:T(8,128)(2,1)S(1)} collective-permute-done((bf16[80,960]{1,0:T(8,128)(2,1)S(1)}, bf16[80,960]{1,0:T(8,128)(2,1)S(1)}, u32[]{:S(2)}, u32[]{:S(2)}) %collective-permute-start.13) | collective-permute-done | bytes 153632 | tf_op jit(solution)/shard_map/ppermute | solution.py:21
  81.4 1.0 convert_add_fusion.2
  82.5 4.4 %collective-permute-start.15 = (bf16[80,960]{1,0:T(8,128)(2,1)S(1)}, bf16[80,960]{1,0:T(8,128)(2,1)S(1)}, u32[]{:S(2)}, u32[]{:S(2)}) collective-permute-start(bf16[80,960]{1,0:T(8,128)(2,1)S(1)} %convert_element_type.132), channel_id=1, source_target_pairs={{0,128},{1,129},{2,130},{3,131},{4,132},{5,133},{6,134},{7,135},{8... | collective-permute-start | bytes 460808 | tf_op jit(solution)/shard_map/ppermute | solution.py:21
  87.2 3.9 %collective-permute-start.17 = (bf16[80,960]{1,0:T(8,128)(2,1)S(1)}, bf16[80,960]{1,0:T(8,128)(2,1)S(1)}, u32[]{:S(2)}, u32[]{:S(2)}) collective-permute-start(bf16[80,960]{1,0:T(8,128)(2,1)S(1)} %convert_element_type.132), channel_id=1, source_target_pairs={{0,192},{1,193},{2,194},{3,195},{4,196},{5,197},{6,198},{7,199},{8... | collective-permute-start | bytes 460808 | tf_op jit(solution)/shard_map/ppermute | solution.py:21
  91.0 3.8 %fusion.10 = bf16[256,320]{0,1:T(8,128)(2,1)S(1)} fusion(bf16[256,5120]{1,0:T(8,128)(2,1)} %copy-done.7, bf16[3,5120,320]{1,2,0:T(8,128)(2,1)} %param.9, bf16[5120]{0:T(1024)(128)(2,1)S(1)} %broadcast_bitcast_fusion.1), kind=kOutput, calls=%fused_computation.24 | convolution fusion | flops 840581120 | bytes 6072320 | tf_op jit(solution)/shard_map/dot_general | solution.py:158
  94.8 2.0 %collective-permute-done.15 = bf16[80,960]{1,0:T(8,128)(2,1)S(1)} collective-permute-done((bf16[80,960]{1,0:T(8,128)(2,1)S(1)}, bf16[80,960]{1,0:T(8,128)(2,1)S(1)}, u32[]{:S(2)}, u32[]{:S(2)}) %collective-permute-start.15) | collective-permute-done | bytes 153632 | tf_op jit(solution)/shard_map/ppermute | solution.py:21
  96.8 4.0 %collective-permute-done.17 = bf16[80,960]{1,0:T(8,128)(2,1)S(1)} collective-permute-done((bf16[80,960]{1,0:T(8,128)(2,1)S(1)}, bf16[80,960]{1,0:T(8,128)(2,1)S(1)}, u32[]{:S(2)}, u32[]{:S(2)}) %collective-permute-start.17) | collective-permute-done | bytes 153632 | tf_op jit(solution)/shard_map/ppermute | solution.py:21
  101.9 2.0 %collective-permute-start.18 = (bf16[80,960]{1,0:T(8,128)(2,1)S(1)}, bf16[80,960]{1,0:T(8,128)(2,1)S(1)}, u32[]{:S(2)}, u32[]{:S(2)}) collective-permute-start(bf16[80,960]{1,0:T(8,128)(2,1)S(1)} %get-tuple-element.54), channel_id=1, source_target_pairs={{0,16},{1,17},{2,18},{3,19},{4,20},{5,21},{6,22},{7,23},{8,24},{9,... | collective-permute-start | bytes 460808 | tf_op jit(solution)/shard_map/ppermute | solution.py:21
  103.9 1.5 %collective-permute-start.19 = (bf16[80,960]{1,0:T(8,128)(2,1)S(1)}, bf16[80,960]{1,0:T(8,128)(2,1)S(1)}, u32[]{:S(2)}, u32[]{:S(2)}) collective-permute-start(bf16[80,960]{1,0:T(8,128)(2,1)S(1)} %get-tuple-element.54), channel_id=1, source_target_pairs={{0,48},{1,49},{2,50},{3,51},{4,52},{5,53},{6,54},{7,55},{8,56},{9,... | collective-permute-start | bytes 460808 | tf_op jit(solution)/shard_map/ppermute | solution.py:21
  105.4 2.1 %collective-permute-start.20 = (bf16[80,960]{1,0:T(8,128)(2,1)S(1)}, bf16[80,960]{1,0:T(8,128)(2,1)S(1)}, u32[]{:S(2)}, u32[]{:S(2)}) collective-permute-start(bf16[80,960]{1,0:T(8,128)(2,1)S(1)} %get-tuple-element.54), channel_id=1, source_target_pairs={{0,32},{1,33},{2,34},{3,35},{4,36},{5,37},{6,38},{7,39},{8,40},{9,... | collective-permute-start | bytes 460808 | tf_op jit(solution)/shard_map/ppermute | solution.py:21
  107.5 2.2 %collective-permute-done.18 = bf16[80,960]{1,0:T(8,128)(2,1)S(1)} collective-permute-done((bf16[80,960]{1,0:T(8,128)(2,1)S(1)}, bf16[80,960]{1,0:T(8,128)(2,1)S(1)}, u32[]{:S(2)}, u32[]{:S(2)}) %collective-permute-start.18) | collective-permute-done | bytes 153632 | tf_op jit(solution)/shard_map/ppermute | solution.py:21
  109.7 2.9 %collective-permute-done.19 = bf16[80,960]{1,0:T(8,128)(2,1)S(1)} collective-permute-done((bf16[80,960]{1,0:T(8,128)(2,1)S(1)}, bf16[80,960]{1,0:T(8,128)(2,1)S(1)}, u32[]{:S(2)}, u32[]{:S(2)}) %collective-permute-start.19) | collective-permute-done | bytes 153632 | tf_op jit(solution)/shard_map/ppermute | solution.py:21
  112.6 1.8 %collective-permute-done.20 = bf16[80,960]{1,0:T(8,128)(2,1)S(1)} collective-permute-done((bf16[80,960]{1,0:T(8,128)(2,1)S(1)}, bf16[80,960]{1,0:T(8,128)(2,1)S(1)}, u32[]{:S(2)}, u32[]{:S(2)}) %collective-permute-start.20) | collective-permute-done | bytes 153632 | tf_op jit(solution)/shard_map/ppermute | solution.py:21
  114.6 2.0 %collective-permute-done.21 = bf16[320,960]{1,0:T(8,128)(2,1)S(1)} collective-permute-done((bf16[320,960]{1,0:T(8,128)(2,1)S(1)}, bf16[320,960]{1,0:T(8,128)(2,1)S(1)}, u32[]{:S(2)}, u32[]{:S(2)}) %collective-permute-start.21) | collective-permute-done | bytes 614432 | tf_op jit(solution)/shard_map/ppermute | solution.py:21
  117.1 0.8 multiply_reduce_fusion.1
  118.4 0.8 multiply_reduce_fusion
  119.3 2.4 %collective-permute-start.23 = (bf16[128,320]{0,1:T(8,128)(2,1)S(1)}, bf16[128,320]{0,1:T(8,128)(2,1)S(1)}, u32[]{:S(2)}, u32[]{:S(2)}) collective-permute-start(bf16[128,320]{0,1:T(8,128)(2,1)S(1)} %get-tuple-element.79), channel_id=1, source_target_pairs={{0,196},{1,197},{2,198},{3,199},{4,64},{5,65},{6,66},{7,67},{8,204... | collective-permute-start | bytes 245768 | tf_op jit(solution)/shard_map/ppermute | solution.py:21
  121.8 3.2 %collective-permute-done.23 = bf16[128,320]{0,1:T(8,128)(2,1)S(1)} collective-permute-done((bf16[128,320]{0,1:T(8,128)(2,1)S(1)}, bf16[128,320]{0,1:T(8,128)(2,1)S(1)}, u32[]{:S(2)}, u32[]{:S(2)}) %collective-permute-start.23) | collective-permute-done | bytes 81952 | tf_op jit(solution)/shard_map/ppermute | solution.py:21
  125.2 0.9 collective-permute-done.22
  126.3 3.0 %collective-permute-start.26 = (bf16[2,64,320]{2,1,0:T(8,128)(2,1)S(1)}, bf16[2,64,320]{2,1,0:T(8,128)(2,1)S(1)}, u32[]{:S(2)}, u32[]{:S(2)}) collective-permute-start(bf16[2,64,320]{2,1,0:T(8,128)(2,1)S(1)} %get-tuple-element.76), channel_id=1, source_target_pairs={{0,2},{1,3},{2,0},{3,1},{4,6},{5,7},{6,4},{7,5},{8,10},{9,11},{10,... | collective-permute-start | bytes 245768 | tf_op jit(solution)/shard_map/ppermute | solution.py:21
  129.8 1.3 collective-permute-start.24
  131.1 2.2 %collective-permute-done.26 = bf16[2,64,320]{2,1,0:T(8,128)(2,1)S(1)} collective-permute-done((bf16[2,64,320]{2,1,0:T(8,128)(2,1)S(1)}, bf16[2,64,320]{2,1,0:T(8,128)(2,1)S(1)}, u32[]{:S(2)}, u32[]{:S(2)}) %collective-permute-start.26) | collective-permute-done | bytes 81952 | tf_op jit(solution)/shard_map/ppermute | solution.py:21
  133.3 0.8 collective-permute-done.25
  134.6 0.9 concatenate.60
  (98 shorter events, 9.6 us)
Async XLA Ops:
  0.0 16.7 %collective-permute-start = (bf16[64,5120]{1,0:T(8,128)(2,1)}, bf16[64,5120]{1,0:T(8,128)(2,1)S(1)}, u32[]{:S(2)}, u32[]{:S(2)}) collective-permute-start(bf16[64,5120]{1,0:T(8,128)(2,1)} %param.8), channel_id=1, source_target_pairs={{0,1},{1,0},{2,3},{3,2},{4,5},{5,4},{6,7},{7,6},{8,9},{9,8},{10,11... | collective-permute-start | bytes 1966088 | tf_op jit(solution)/shard_map/ppermute | solution.py:21
  2.3 15.1 %collective-permute-start.1 = (bf16[64,5120]{1,0:T(8,128)(2,1)}, bf16[64,5120]{1,0:T(8,128)(2,1)S(1)}, u32[]{:S(2)}, u32[]{:S(2)}) collective-permute-start(bf16[64,5120]{1,0:T(8,128)(2,1)} %param.8), channel_id=1, source_target_pairs={{0,3},{1,2},{2,1},{3,0},{4,7},{5,6},{6,5},{7,4},{8,11},{9,10},{10,... | collective-permute-start | bytes 1966088 | tf_op jit(solution)/shard_map/ppermute | solution.py:21
  4.2 26.5 %collective-permute-start.10 = (f32[4,32]{1,0:T(4,128)S(1)}, f32[4,32]{1,0:T(4,128)S(1)}, u32[]{:S(2)}, u32[]{:S(2)}) collective-permute-start(f32[4,32]{1,0:T(4,128)S(1)} %get-tuple-element.89), channel_id=1, source_target_pairs={{0,64},{1,65},{2,66},{3,67},{4,196},{5,197},{6,198},{7,199},{8,72}... | collective-permute-start | bytes 1544 | tf_op jit(solution)/shard_map/ppermute | solution.py:21
  8.3 6.2 %copy-start.1 = (bf16[64,5120]{1,0:T(8,128)(2,1)S(1)}, bf16[64,5120]{1,0:T(8,128)(2,1)}, u32[]{:S(2)}) copy-start(bf16[64,5120]{1,0:T(8,128)(2,1)} %param.8) | copy-start | bytes 1966084
  18.4 18.1 %collective-permute-start.4 = (bf16[64,5120]{1,0:T(8,128)(2,1)}, bf16[64,5120]{1,0:T(8,128)(2,1)}, u32[]{:S(2)}, u32[]{:S(2)}) collective-permute-start(bf16[64,5120]{1,0:T(8,128)(2,1)} %pad_maximum_fusion.1), channel_id=1, source_target_pairs={{0,4},{1,5},{2,6},{3,7},{4,0},{5,1},{6,2},{7,3},{8,12},{9,13},{10,... | collective-permute-start | bytes 1966088 | tf_op jit(solution)/shard_map/ppermute | solution.py:21
  21.5 20.7 %collective-permute-start.5 = (bf16[64,5120]{1,0:T(8,128)(2,1)}, bf16[64,5120]{1,0:T(8,128)(2,1)S(1)}, u32[]{:S(2)}, u32[]{:S(2)}) collective-permute-start(bf16[64,5120]{1,0:T(8,128)(2,1)} %pad_maximum_fusion.2), channel_id=1, source_target_pairs={{0,196},{1,197},{2,198},{3,199},{4,64},{5,65},{6,66},{7,67},{8,204... | collective-permute-start | bytes 1966088 | tf_op jit(solution)/shard_map/ppermute | solution.py:21
  26.2 8.2 %collective-permute-start.2 = (bf16[32,5120]{1,0:T(8,128)(2,1)S(1)}, bf16[32,5120]{1,0:T(8,128)(2,1)}, u32[]{:S(2)}, u32[]{:S(2)}) collective-permute-start(bf16[32,5120]{1,0:T(8,128)(2,1)S(1)} %get-tuple-element.63), channel_id=1, source_target_pairs={{0,3},{1,2},{2,1},{3,0},{4,7},{5,6},{6,5},{7,4},{8,11},{9,10},{10,... | collective-permute-start | bytes 983048 | tf_op jit(solution)/shard_map/ppermute | solution.py:21
  28.0 8.4 %collective-permute-start.3 = (bf16[32,5120]{1,0:T(8,128)(2,1)S(1)}, bf16[32,5120]{1,0:T(8,128)(2,1)}, u32[]{:S(2)}, u32[]{:S(2)}) collective-permute-start(bf16[32,5120]{1,0:T(8,128)(2,1)S(1)} %get-tuple-element.65), channel_id=1, source_target_pairs={{0,1},{1,0},{2,3},{3,2},{4,5},{5,4},{6,7},{7,6},{8,9},{9,8},{10,11... | collective-permute-start | bytes 983048 | tf_op jit(solution)/shard_map/ppermute | solution.py:21
  30.8 21.7 %collective-permute-start.6 = (bf16[32,5120]{1,0:T(8,128)(2,1)}, bf16[32,5120]{1,0:T(8,128)(2,1)}, u32[]{:S(2)}, u32[]{:S(2)}) collective-permute-start(bf16[32,5120]{1,0:T(8,128)(2,1)} %get-tuple-element.61), channel_id=1, source_target_pairs={{0,4},{1,5},{2,6},{3,7},{4,0},{5,1},{6,2},{7,3},{8,12},{9,13},{10,... | collective-permute-start | bytes 983048 | tf_op jit(solution)/shard_map/ppermute | solution.py:21
  34.4 18.1 %collective-permute-start.8 = (bf16[32,5120]{1,0:T(8,128)(2,1)}, bf16[32,5120]{1,0:T(8,128)(2,1)S(1)}, u32[]{:S(2)}, u32[]{:S(2)}) collective-permute-start(bf16[32,5120]{1,0:T(8,128)(2,1)} %get-tuple-element.60), channel_id=1, source_target_pairs={{0,196},{1,197},{2,198},{3,199},{4,64},{5,65},{6,66},{7,67},{8,204... | collective-permute-start | bytes 983048 | tf_op jit(solution)/shard_map/ppermute | solution.py:21
  36.4 16.1 %collective-permute-start.7 = (bf16[32,5120]{1,0:T(8,128)(2,1)}, bf16[32,5120]{1,0:T(8,128)(2,1)S(1)}, u32[]{:S(2)}, u32[]{:S(2)}) collective-permute-start(bf16[32,5120]{1,0:T(8,128)(2,1)} %collective-permute-done.2), channel_id=1, source_target_pairs={{0,4},{1,5},{2,6},{3,7},{4,0},{5,1},{6,2},{7,3},{8,12},{9,13},{10,... | collective-permute-start | bytes 983048 | tf_op jit(solution)/shard_map/ppermute | solution.py:21
  36.5 17.5 %collective-permute-start.9 = (bf16[32,5120]{1,0:T(8,128)(2,1)}, bf16[32,5120]{1,0:T(8,128)(2,1)S(1)}, u32[]{:S(2)}, u32[]{:S(2)}) collective-permute-start(bf16[32,5120]{1,0:T(8,128)(2,1)} %collective-permute-done.3), channel_id=1, source_target_pairs={{0,196},{1,197},{2,198},{3,199},{4,64},{5,65},{6,66},{7,67},{8,204... | collective-permute-start | bytes 983048 | tf_op jit(solution)/shard_map/ppermute | solution.py:21
  44.4 7.1 %slice-start = ((s8[6553600]{0:T(1024)(128)(4,1)}), s8[4194304]{0:T(1024)(128)(4,1)S(1)}, s32[]{:S(2)}) async-start(s8[6553600]{0:T(1024)(128)(4,1)} %bitcast.101), calls=%async_computation | async-start | bytes 8388608
  47.6 3.9 %slice-start.1 = ((s8[6553600]{0:T(1024)(128)(4,1)}), s8[2359296]{0:T(1024)(128)(4,1)S(1)}, s32[]{:S(2)}) async-start(s8[6553600]{0:T(1024)(128)(4,1)} %bitcast.101), calls=%async_computation.1 | async-start | bytes 4718592
  56.3 1.5 %copy-start.7 = (bf16[256,5120]{1,0:T(8,128)(2,1)}, bf16[256,5120]{1,0:T(8,128)(2,1)S(1)}, u32[]{:S(2)}) copy-start(bf16[256,5120]{1,0:T(8,128)(2,1)S(1)} %constant_dynamic-update-slice_fusion.5) | copy-start | bytes 7864324
  57.8 1.1 copy-start.3
  58.8 1.0 copy-start.4
  59.8 1.0 copy-start.2
  64.9 2.4 %collective-permute-start.11 = (bf16[320,960]{1,0:T(8,128)(2,1)}, bf16[320,960]{1,0:T(8,128)(2,1)}, u32[]{:S(2)}, u32[]{:S(2)}) collective-permute-start(bf16[320,960]{1,0:T(8,128)(2,1)} %dynamic-slice_convert_fusion), channel_id=1, source_target_pairs={{0,8},{1,9},{2,10},{3,11},{4,12},{5,13},{6,14},{7,15},{8,0},{9,1},... | collective-permute-start | bytes 1843208 | tf_op jit(solution)/shard_map/ppermute | solution.py:21
  68.6 1.1 copy-start
  69.6 5.9 %copy-start.5 = (bf16[1,320,640]{2,1,0:T(8,128)(2,1)S(1)}, bf16[1,320,640]{2,1,0:T(8,128)(2,1)}, u32[]{:S(2)}) copy-start(bf16[1,320,640]{2,1,0:T(8,128)(2,1)} %param.13) | copy-start | bytes 1228804
  69.7 8.6 %collective-permute-start.14 = (bf16[80,960]{1,0:T(8,128)(2,1)S(1)}, bf16[80,960]{1,0:T(8,128)(2,1)S(1)}, u32[]{:S(2)}, u32[]{:S(2)}) collective-permute-start(bf16[80,960]{1,0:T(8,128)(2,1)S(1)} %get-tuple-element.58), channel_id=1, source_target_pairs={{0,32},{1,33},{2,34},{3,35},{4,36},{5,37},{6,38},{7,39},{8,40},{9,... | collective-permute-start | bytes 460808 | tf_op jit(solution)/shard_map/ppermute | solution.py:21
  73.0 8.4 %collective-permute-start.13 = (bf16[80,960]{1,0:T(8,128)(2,1)S(1)}, bf16[80,960]{1,0:T(8,128)(2,1)S(1)}, u32[]{:S(2)}, u32[]{:S(2)}) collective-permute-start(bf16[80,960]{1,0:T(8,128)(2,1)S(1)} %get-tuple-element.59), channel_id=1, source_target_pairs={{0,48},{1,49},{2,50},{3,51},{4,52},{5,53},{6,54},{7,55},{8,56},{9,... | collective-permute-start | bytes 460808 | tf_op jit(solution)/shard_map/ppermute | solution.py:21
  74.0 7.4 %collective-permute-start.12 = (bf16[80,960]{1,0:T(8,128)(2,1)S(1)}, bf16[80,960]{1,0:T(8,128)(2,1)S(1)}, u32[]{:S(2)}, u32[]{:S(2)}) collective-permute-start(bf16[80,960]{1,0:T(8,128)(2,1)S(1)} %get-tuple-element.57), channel_id=1, source_target_pairs={{0,16},{1,17},{2,18},{3,19},{4,20},{5,21},{6,22},{7,23},{8,24},{9,... | collective-permute-start | bytes 460808 | tf_op jit(solution)/shard_map/ppermute | solution.py:21
  82.5 14.3 %collective-permute-start.15 = (bf16[80,960]{1,0:T(8,128)(2,1)S(1)}, bf16[80,960]{1,0:T(8,128)(2,1)S(1)}, u32[]{:S(2)}, u32[]{:S(2)}) collective-permute-start(bf16[80,960]{1,0:T(8,128)(2,1)S(1)} %convert_element_type.132), channel_id=1, source_target_pairs={{0,128},{1,129},{2,130},{3,131},{4,132},{5,133},{6,134},{7,135},{8... | collective-permute-start | bytes 460808 | tf_op jit(solution)/shard_map/ppermute | solution.py:21
  86.9 9.9 %collective-permute-start.16 = (bf16[80,960]{1,0:T(8,128)(2,1)S(1)}, bf16[80,960]{1,0:T(8,128)(2,1)S(1)}, u32[]{:S(2)}, u32[]{:S(2)}) collective-permute-start(bf16[80,960]{1,0:T(8,128)(2,1)S(1)} %convert_element_type.132), channel_id=1, source_target_pairs={{0,64},{1,65},{2,66},{3,67},{4,68},{5,69},{6,70},{7,71},{8,72},{9,... | collective-permute-start | bytes 460808 | tf_op jit(solution)/shard_map/ppermute | solution.py:21
  87.2 13.6 %collective-permute-start.17 = (bf16[80,960]{1,0:T(8,128)(2,1)S(1)}, bf16[80,960]{1,0:T(8,128)(2,1)S(1)}, u32[]{:S(2)}, u32[]{:S(2)}) collective-permute-start(bf16[80,960]{1,0:T(8,128)(2,1)S(1)} %convert_element_type.132), channel_id=1, source_target_pairs={{0,192},{1,193},{2,194},{3,195},{4,196},{5,197},{6,198},{7,199},{8... | collective-permute-start | bytes 460808 | tf_op jit(solution)/shard_map/ppermute | solution.py:21
  101.9 7.8 %collective-permute-start.18 = (bf16[80,960]{1,0:T(8,128)(2,1)S(1)}, bf16[80,960]{1,0:T(8,128)(2,1)S(1)}, u32[]{:S(2)}, u32[]{:S(2)}) collective-permute-start(bf16[80,960]{1,0:T(8,128)(2,1)S(1)} %get-tuple-element.54), channel_id=1, source_target_pairs={{0,16},{1,17},{2,18},{3,19},{4,20},{5,21},{6,22},{7,23},{8,24},{9,... | collective-permute-start | bytes 460808 | tf_op jit(solution)/shard_map/ppermute | solution.py:21
  103.9 8.7 %collective-permute-start.19 = (bf16[80,960]{1,0:T(8,128)(2,1)S(1)}, bf16[80,960]{1,0:T(8,128)(2,1)S(1)}, u32[]{:S(2)}, u32[]{:S(2)}) collective-permute-start(bf16[80,960]{1,0:T(8,128)(2,1)S(1)} %get-tuple-element.54), channel_id=1, source_target_pairs={{0,48},{1,49},{2,50},{3,51},{4,52},{5,53},{6,54},{7,55},{8,56},{9,... | collective-permute-start | bytes 460808 | tf_op jit(solution)/shard_map/ppermute | solution.py:21
  105.4 9.0 %collective-permute-start.20 = (bf16[80,960]{1,0:T(8,128)(2,1)S(1)}, bf16[80,960]{1,0:T(8,128)(2,1)S(1)}, u32[]{:S(2)}, u32[]{:S(2)}) collective-permute-start(bf16[80,960]{1,0:T(8,128)(2,1)S(1)} %get-tuple-element.54), channel_id=1, source_target_pairs={{0,32},{1,33},{2,34},{3,35},{4,36},{5,37},{6,38},{7,39},{8,40},{9,... | collective-permute-start | bytes 460808 | tf_op jit(solution)/shard_map/ppermute | solution.py:21
  114.5 2.2 %collective-permute-start.21 = (bf16[320,960]{1,0:T(8,128)(2,1)S(1)}, bf16[320,960]{1,0:T(8,128)(2,1)S(1)}, u32[]{:S(2)}, u32[]{:S(2)}) collective-permute-start(bf16[320,960]{1,0:T(8,128)(2,1)S(1)} %pad_maximum_fusion.3), channel_id=1, source_target_pairs={{0,8},{1,9},{2,10},{3,11},{4,12},{5,13},{6,14},{7,15},{8,0},{9,1},... | collective-permute-start | bytes 1843208 | tf_op jit(solution)/shard_map/ppermute | solution.py:21
  117.1 0.9 copy-start.6
  119.3 5.8 %collective-permute-start.23 = (bf16[128,320]{0,1:T(8,128)(2,1)S(1)}, bf16[128,320]{0,1:T(8,128)(2,1)S(1)}, u32[]{:S(2)}, u32[]{:S(2)}) collective-permute-start(bf16[128,320]{0,1:T(8,128)(2,1)S(1)} %get-tuple-element.79), channel_id=1, source_target_pairs={{0,196},{1,197},{2,198},{3,199},{4,64},{5,65},{6,66},{7,67},{8,204... | collective-permute-start | bytes 245768 | tf_op jit(solution)/shard_map/ppermute | solution.py:21
  121.6 4.4 %collective-permute-start.22 = (bf16[128,320]{0,1:T(8,128)(2,1)S(1)}, bf16[128,320]{0,1:T(8,128)(2,1)S(1)}, u32[]{:S(2)}, u32[]{:S(2)}) collective-permute-start(bf16[128,320]{0,1:T(8,128)(2,1)S(1)} %get-tuple-element.78), channel_id=1, source_target_pairs={{0,4},{1,5},{2,6},{3,7},{4,0},{5,1},{6,2},{7,3},{8,12},{9,13},{10,... | collective-permute-start | bytes 245768 | tf_op jit(solution)/shard_map/ppermute | solution.py:21
  126.3 7.0 %collective-permute-start.26 = (bf16[2,64,320]{2,1,0:T(8,128)(2,1)S(1)}, bf16[2,64,320]{2,1,0:T(8,128)(2,1)S(1)}, u32[]{:S(2)}, u32[]{:S(2)}) collective-permute-start(bf16[2,64,320]{2,1,0:T(8,128)(2,1)S(1)} %get-tuple-element.76), channel_id=1, source_target_pairs={{0,2},{1,3},{2,0},{3,1},{4,6},{5,7},{6,4},{7,5},{8,10},{9,11},{10,... | collective-permute-start | bytes 245768 | tf_op jit(solution)/shard_map/ppermute | solution.py:21
  129.3 4.8 %collective-permute-start.25 = (bf16[2,64,320]{2,1,0:T(8,128)(2,1)S(1)}, bf16[2,64,320]{2,1,0:T(8,128)(2,1)S(1)}, u32[]{:S(2)}, u32[]{:S(2)}) collective-permute-start(bf16[2,64,320]{2,1,0:T(8,128)(2,1)S(1)} %get-tuple-element.77), channel_id=1, source_target_pairs={{0,3},{1,2},{2,1},{3,0},{4,7},{5,6},{6,5},{7,4},{8,11},{9,10},{10,... | collective-permute-start | bytes 245768 | tf_op jit(solution)/shard_map/ppermute | solution.py:21
  129.8 4.6 %collective-permute-start.24 = (bf16[2,64,320]{2,1,0:T(8,128)(2,1)S(1)}, bf16[2,64,320]{2,1,0:T(8,128)(2,1)S(1)}, u32[]{:S(2)}, u32[]{:S(2)}) collective-permute-start(bf16[2,64,320]{2,1,0:T(8,128)(2,1)S(1)} %get-tuple-element.75), channel_id=1, source_target_pairs={{0,1},{1,0},{2,3},{3,2},{4,5},{5,4},{6,7},{7,6},{8,9},{9,8},{10,11... | collective-permute-start | bytes 245768 | tf_op jit(solution)/shard_map/ppermute | solution.py:21

commit v4 on v2

v4 whole, which is shorter than its diff:
```python
import functools

import jax
import jax.numpy as jnp
from jax import lax
from jax.experimental import pallas as pl
from jax.experimental.pallas import tpu as pltpu
from jax.sharding import PartitionSpec as P

AXES = ("seq", "head")
BF16 = jnp.bfloat16
F32 = jnp.float32


def place(i):
    seq, head = divmod(i, 8)
    return seq // 8, (seq // 2) % 4, seq % 2, head // 4, head % 4


def permute(value, move):
    pairs = []
    for i in range(256):
        z_hi, y, core, z_lo, x = move(*place(i))
        pairs.append((i, ((z_hi % 4) * 8 + (y % 4) * 2 + core) * 8 + z_lo * 4 + x % 4))
    return lax.ppermute(value, AXES, pairs)


def to_core(value):
    return permute(value, lambda h, y, c, l, x: (h, y, 1 - c, l, x))


def to_y(value, d):
    return permute(value, lambda h, y, c, l, x: (h, y + d, c, l, x))


def to_z(value, d):
    return permute(value, lambda h, y, c, l, x: (h + d, y, c, l, x))


def near(x):
    return x ^ 1


def far(x):
    return (x + 1) % 4 if x % 2 else (x - 1) % 4


def to_near_x(value):
    return permute(value, lambda h, y, c, l, x: (h, y, c, l, near(x)))


def to_far_x(value):
    return permute(value, lambda h, y, c, l, x: (h, y, c, l, far(x)))


def to_opposite_x(value):
    return permute(value, lambda h, y, c, l, x: (h, y, c, l, x + 2))


def to_near_z(value):
    return permute(value, lambda h, y, c, l, x: (h, y, c, 1 - l, x))


def to_far_z(value):
    return permute(value, lambda h, y, c, l, x: (h + 1 if l else h - 1, y, c, 1 - l, x))


VMEM = pl.BlockSpec(memory_space=pltpu.VMEM)
SMEM = pl.BlockSpec(memory_space=pltpu.SMEM)
SMALL = pl.CostEstimate(flops=1000, bytes_accessed=1000, transcendentals=0)
PARAMS = pltpu.CompilerParams(vmem_limit_bytes=40 * 1024 * 1024)
BY_ROW = (((1,), (1,)), ((), ()))
BY_TOKEN = (((0,), (0,)), ((), ()))


def like(shape, dtype=BF16):
    return jax.ShapeDtypeStruct(shape, dtype)


def call(kernel, out_shape, *args, scalars=0):
    return pl.pallas_call(
        kernel,
        out_shape=out_shape,
        in_specs=[SMEM] * scalars + [VMEM] * (len(args) - scalars),
        out_specs=jax.tree.map(lambda _: VMEM, out_shape),
        compiler_params=PARAMS,
        cost_estimate=SMALL,
    )(*args)


def project_kernel(n_tiles, n_out, steps, *refs):
    tiles, (w_ref, f_ref), refs = refs[:n_tiles], refs[n_tiles : n_tiles + 2], refs[n_tiles + 2 :]
    outs, acc = refs[:n_out], refs[n_out]
    step = pl.program_id(0)
    tile = jnp.concatenate([t[...] for t in tiles], axis=0)
    for c in range(n_out):
        part = lax.dot_general(tile, w_ref[c] * f_ref[c], BY_ROW, preferred_element_type=F32)

        @pl.when(step == 0)
        def _():
            acc[c] = part

        @pl.when(step > 0)
        def _():
            acc[c] += part

        @pl.when(step == steps - 1)
        def _():
            outs[c][...] = acc[c].astype(BF16)


def project(tiles, w_t, factor, depth=1024):
    n, width, total = w_t.shape
    rows_ = sum(t.shape[0] for t in tiles)
    steps = total // depth
    return pl.pallas_call(
        functools.partial(project_kernel, len(tiles), n, steps),
        grid=(steps,),
        out_shape=[like((rows_, width))] * n,
        in_specs=[pl.BlockSpec((t.shape[0], depth), lambda k: (0, k)) for t in tiles]
        + [
            pl.BlockSpec((n, width, depth), lambda k: (0, 0, k)),
            pl.BlockSpec((n, 1, depth), lambda k: (0, 0, k)),
        ],
        out_specs=[pl.BlockSpec((rows_, width), lambda k: (0, 0))] * n,
        scratch_shapes=[pltpu.VMEM((n, rows_, width), F32)],
        compiler_params=PARAMS,
        cost_estimate=SMALL,
    )(*tiles, w_t, factor)


def grads_kernel(k1, k2, v1, v2, weight, gate_w, up_w, down_w, out):
    keys = jnp.concatenate([k1[...], k2[...]], axis=0)
    values = jnp.concatenate([v1[...], v2[...]], axis=0)
    gate = jnp.dot(keys, gate_w[...], preferred_element_type=F32)
    upper = jnp.dot(keys, up_w[...], preferred_element_type=F32)
    sigma = jax.nn.sigmoid(gate)
    active = gate * sigma
    hidden = (active * upper).astype(BF16)
    weighted = (weight[...] * values.astype(F32)).astype(BF16)
    d_hidden = jnp.dot(weighted, down_w[...], preferred_element_type=F32)
    d_gate = (d_hidden * upper * sigma * (1.0 + gate * (1.0 - sigma))).astype(BF16)
    d_upper = (d_hidden * active).astype(BF16)
    pairs = ((d_gate, keys), (d_upper, keys), (hidden, weighted))
    for i, (left, right) in enumerate(pairs):
        grad = lax.dot_general(left, right, BY_TOKEN, preferred_element_type=F32)
        out[:, i * 320 : (i + 1) * 320] = grad.astype(out.dtype)


def halves_kernel(y, own, got, to1, to2, to3, mine):
    for d, out in ((1, to1), (2, to2), (3, to3), (0, mine)):
        at = pl.ds(pl.multiple_of(lax.rem(y[0] + d, 4) * 80, 16), 80)
        out[...] = (own[at, :] + got[at, :].astype(F32)).astype(out.dtype)


def sum_kernel(mine, a, b, c, total, rounded):
    result = mine[...] + a[...].astype(F32) + b[...].astype(F32) + c[...].astype(F32)
    total[...] = result
    rounded[...] = result.astype(BF16)


def renorm_kernel(mine, a, b, c, old, out):
    total = mine[...] + a[...].astype(F32) + b[...].astype(F32) + c[...].astype(F32)
    before = old[...]
    fresh = before + total
    for i in range(3):
        at = slice(i * 320, (i + 1) * 320)
        old_norm = jnp.sqrt(jnp.sum(before[:, at] * before[:, at], axis=1, keepdims=True))
        new_sq = jnp.sum(fresh[:, at] * fresh[:, at], axis=1, keepdims=True)
        out[:, at] = (fresh[:, at] * (old_norm / jnp.sqrt(new_sq + 1e-06))).astype(BF16)


def respond_kernel(query_ref, column, other, *outs):
    renorm = jnp.concatenate([column[...], other[...]], axis=0)
    query = query_ref[...]
    gate = lax.dot_general(query, renorm[:, :320], BY_ROW, preferred_element_type=F32)
    upper = lax.dot_general(query, renorm[:, 320:640], BY_ROW, preferred_element_type=F32)
    hidden = (gate * jax.nn.sigmoid(gate) * upper).astype(BF16)
    output = jnp.dot(hidden, renorm[:, 640:], preferred_element_type=F32)
    scaled = output * lax.rsqrt(jnp.mean(output * output, axis=-1, keepdims=True) + 1e-05)
    answer = scaled.astype(BF16)
    at = 0
    for out in outs:
        out[...] = answer[at : at + out.shape[0]]
        at += out.shape[0]


def rows(value, start, size):
    return lax.dynamic_slice_in_dim(value, start, size, axis=0)


def gather(tokens):
    first, second = tokens[:32], tokens[32:]
    near_tile, far_tile = to_near_x(tokens), to_far_x(tokens)
    z1, z2 = to_near_z(first), to_far_z(second)
    opposite_first = to_far_x(near_tile[:32])
    opposite_second = to_near_x(far_tile[32:])
    z3 = to_near_z(jnp.concatenate([near_tile[:32], far_tile[:32]]))
    z4 = to_far_z(jnp.concatenate([near_tile[32:], far_tile[32:]]))
    z5, z6 = to_near_z(opposite_first), to_far_z(opposite_second)
    return (
        [tokens, near_tile, far_tile, opposite_first, opposite_second],
        [z1, z3, z5, z2, z4, z6],
    )


def x_order(x):
    return [x, x ^ 1, (x + jnp.where(x % 2 == 1, 1, 3)) % 4, (x + 2) % 4]


def weights_of_rows(weight, z_lo, x):
    tiles = weight.reshape(8, 64)
    same = lax.dynamic_slice_in_dim(tiles, z_lo * 4, 4, axis=0)
    other = lax.dynamic_slice_in_dim(tiles, (1 - z_lo) * 4, 4, axis=0)
    order = x_order(x)
    pick = lambda t: jnp.concatenate([lax.dynamic_slice_in_dim(t, i, 1, axis=0) for i in order])
    same, other = pick(same), pick(other)
    moved = permute(other[:, 32:], lambda h, y, c, l, x: (h - 1 if l else h + 1, y, c, l, x))
    return jnp.concatenate([same.reshape(256), other[:, :32].reshape(128), moved.reshape(128)])


def send_back(plane, for_near, for_far, z_lo, x):
    from_near = to_near_z(for_near).reshape(4, 32, 320)
    from_far = to_far_z(for_far).reshape(4, 32, 320)
    other = jnp.concatenate([from_near, from_far], axis=1)
    both = jnp.stack([plane.reshape(4, 64, 320), other], axis=1)
    slots = jnp.stack(
        [both[0], to_near_x(both[1]), to_far_x(both[2]), to_opposite_x(both[3])]
    ).reshape(8, 64, 320)
    out = []
    for head in range(8):
        d = (head % 4 - x) % 4
        at = jnp.where(d == 0, 0, jnp.where(d == 2, 3, jnp.where(head % 4 == x ^ 1, 1, 2)))
        slot = at * 2 + jnp.where(head // 4 == z_lo, 0, 1)
        out.append(lax.dynamic_slice_in_dim(slots, slot, 1, axis=0)[0])
    return jnp.concatenate(out, axis=1)


def body(tokens, w_qkv, scale_exp, gate_mask, rate, fast_gate, fast_up, fast_down):
    seq, head = lax.axis_index("seq"), lax.axis_index("head")
    core, y = seq % 2, (seq // 2) % 4
    z_lo, x = head // 4, head % 4
    factor = jnp.exp2(scale_exp.astype(F32)).astype(BF16)[:, :, 0]
    factor = jnp.repeat(factor, w_qkv.shape[1] // factor.shape[1], axis=1)[:, None, :]
    w_t = jnp.transpose(w_qkv, (0, 2, 1))
    weight = weights_of_rows(rate[0] * gate_mask[:, 0].astype(F32), z_lo, x)[:, None]
    old = (fast_gate[0], fast_up[0], fast_down[0])
    own_w = [lax.dynamic_slice_in_dim(w, core * 320, 320, axis=1) for w in old]
    other_w = [lax.dynamic_slice_in_dim(w, (1 - core) * 320, 320, axis=1) for w in old]
    old_t = rows(jnp.concatenate([w.T for w in own_w], axis=1), y * 80, 80).astype(F32)
    plane, others = gather(tokens)

    prepared = (weight, own_w, other_w, old_t, factor)
    plane, others[1], others[4], prepared = lax.optimization_barrier(
        (plane, others[1], others[4], prepared)
    )
    weight, own_w, other_w, old_t, factor = prepared
    ready = project(plane, w_t, factor)
    ready, others = lax.optimization_barrier((ready, others))
    keys, values = project(others, w_t[1:], factor[1:])

    inputs = (ready[1], keys, ready[2], values, weight)
    sent = call(grads_kernel, like((320, 960)), *inputs, *other_w)
    inputs, sent = lax.optimization_barrier((inputs, sent))
    got = to_core(sent)
    own = call(grads_kernel, like((320, 960), F32), *inputs, *own_w)
    own, got = lax.optimization_barrier((own, got))
    to1, to2, to3, mine = call(
        halves_kernel,
        [like((80, 960))] * 3 + [like((80, 960), F32)],
        y.astype(jnp.int32).reshape(1),
        own,
        got,
        scalars=1,
    )
    got = to_y(to2, 2), to_y(to1, 1), to_y(to3, 3)
    mine, small = call(sum_kernel, [like((80, 960), F32), like((80, 960))], mine, *got)

    others, small = lax.optimization_barrier((others, small))
    got = to_z(small, 2), to_z(small, 1), to_z(small, 3)
    (query_others,) = project(others, w_t[:1], factor[:1])
    query_others, got = lax.optimization_barrier((query_others, got))
    block = call(renorm_kernel, like((80, 960)), mine, *got, old_t)
    column = jnp.concatenate([block, to_y(block, 2), to_y(block, 1), to_y(block, 3)], axis=0)
    other = to_core(column)

    for_near, for_far = call(respond_kernel, [like((128, 320))] * 2, query_others, column, other)
    query_plane, for_near, for_far = lax.optimization_barrier((ready[0], for_near, for_far))
    (plane,) = call(respond_kernel, [like((256, 320))], query_plane, column, other)
    return send_back(plane, for_near, for_far, z_lo, x)


def solution(mesh):
    in_specs = (
        P(("seq", "head"), None),
        P(None, None, "head"),
        P(None, None, "head"),
        P("seq", "head"),
        P("head"),
        P("head", None, None),
        P("head", None, None),
        P("head", None, None),
    )
    out_specs = P(("seq", "head"), None)
    return jax.shard_map(body, mesh=mesh, in_specs=in_specs, out_specs=out_specs, check_vma=False)
```

time: 134 us -> 151 us (1.13)
  Pallas kernels: 0 us -> 27.7 us
  local copies, waits for them, and re-layouts: 13.1 us -> 34.9 us
  matrix products: 19.4 us -> 0 us
  waiting for transfers between devices: 43.6 us -> 29.9 us
  starting transfers between devices: 40.5 us -> 49.1 us
  other arithmetic: 14.1 us -> 6.5 us
    pallas_call x0 -> x10, Pallas kernels: none -> 27.7 us  [the longest x3 20.2 us: project(): pl.pallas_call(functools.partial(project_kernel, len(tiles), n, steps), g...]
    dot_general x14 -> x0, matrix products: 19.4 us -> none  [the longest x6 13.1 us: project(): return jnp.dot(tile, weff[c], preferred_element_type=F32).astype(BF16)]
    ppermute x27, waiting for transfers between devices: 43.6 us -> 29.9 us  [permute(): return lax.ppermute(value, AXES, pairs)]
    mul x4 -> x1, other arithmetic: 10.4 us -> 0.7 us  [body(): rate[0] * gate_mask[:, 0].astype(F32)]
    slice x4 -> x5, local copies, waits for them, and re-layouts: 0.23 us -> 9.72 us  [the longest x2 6.05 us: body(): keys, values = project(others, w_t[1:], factor[1:])]
    dynamic_slice x0 -> x5, local copies, waits for them, and re-layouts: none -> 8.96 us  [the longest x3 5.39 us: body(): own_w = [lax.dynamic_slice_in_dim(w, core * 320, 320, axis=1) for w in old]]
    ppermute x27, starting transfers between devices: 40.5 us -> 49.1 us  [permute(): return lax.ppermute(value, AXES, pairs)]
    optimization_barrier x0 -> x6, local copies, waits for them, and re-layouts: none -> 2.64 us  [the longest x5 2.5 us: body(): lax.optimization_barrier((plane, others[1], others[4], prepared))]
  transfers between devices with their start and end apart: 27 -> 27, of which waited for: 17 -> 15; matrix products, arithmetic and copies ran while one was open for 21% -> 21% of each run, Pallas kernels for 0% -> 11%
where the time goes in v4:
time: 151 us; the launch traced here: 149 us
  starting transfers between devices  49.1 us (33%)
  local copies, waits for them, and re-layouts  34.9 us (23%)
  waiting for transfers between devices  29.9 us (20%)
  Pallas kernels  27.7 us (18%)
  other arithmetic  6.5 us (4%)
    ppermute x27, starting transfers between devices, permute(): return lax.ppermute(value, AXES, pairs)  49.1 us
    ppermute x27, waiting for transfers between devices, permute(): return lax.ppermute(value, AXES, pairs)  29.9 us
    pallas_call x3, Pallas kernels, project(): pl.pallas_call(functools.partial(project_kernel, len(tiles), n, steps), g...  20.2 us
    unnamed x43, local copies, waits for them, and re-layouts  8.71 us
    pallas_call x7, Pallas kernels, call(): pl.pallas_call(kernel, out_shape=out_shape, in_specs=[SMEM] * scalars + [...  7.49 us
    slice x2, local copies, waits for them, and re-layouts, body(): keys, values = project(others, w_t[1:], factor[1:])  6.05 us
    dynamic_slice x3, local copies, waits for them, and re-layouts, body(): own_w = [lax.dynamic_slice_in_dim(w, core * 320, 320, axis=1) for w in old]  5.39 us
    dynamic_slice x2, local copies, waits for them, and re-layouts, body(): lax.dynamic_slice_in_dim(w, (1 - core) * 320, 320, axis=1)  3.57 us
  transfers between devices with their start and end apart: 27, of which 15 were waited for; matrix products, arithmetic and copies ran while one was open for 21% of the time, Pallas kernels for 11%

profile of v4, /device:TPU:2, one launch (start us, length us, event | category | flops | bytes accessed | tf_op | source)
XLA Modules:
  0.0 149.2 jit_solution(3709585440662972459)
XLA Ops:
  0.0 2.3 %collective-permute-start = (bf16[64,5120]{1,0:T(8,128)(2,1)}, bf16[64,5120]{1,0:T(8,128)(2,1)S(1)}, u32[]{:S(2)}, u32[]{:S(2)}) collective-permute-start(bf16[64,5120]{1,0:T(8,128)(2,1)} %refs_0_), channel_id=1, source_target_pairs={{0,1},{1,0},{2,3},{3,2},{4,5},{5,4},{6,7},{7,6},{8,9},{9,8},{10,11... | collective-permute-start | bytes 1966088 | tf_op jit(solution)/shard_map/ppermute | solution.py:25
  3.3 0.7 multiply_reduce_fusion
  4.2 3.3 %collective-permute-start.6 = (f32[4,32]{1,0:T(4,128)S(1)}, f32[4,32]{1,0:T(4,128)S(1)}, u32[]{:S(2)}, u32[]{:S(2)}) collective-permute-start(f32[4,32]{1,0:T(4,128)S(1)} %get-tuple-element.158), channel_id=1, source_target_pairs={{0,64},{1,65},{2,66},{3,67},{4,196},{5,197},{6,198},{7,199},{8,72}... | collective-permute-start | bytes 1544 | tf_op jit(solution)/shard_map/ppermute | solution.py:25
  7.5 2.5 %dynamic-slice_bitcast_fusion = (bf16[320,320]{1,0:T(8,128)(2,1)S(1)}, bf16[1,320,320]{2,1,0:T(8,128)(2,1)}, bf16[1,320,320]{2,1,0:T(8,128)(2,1)}, bf16[320,320]{1,0:T(8,128)(2,1)}) fusion(bf16[1,320,640]{2,1,0:T(8,128)(2,1)} %param.15, s32[]{:T(128)S(6)} %select_n.214, s32[]{:T(128)S(6)} %select_n.213, bf16[1,320,640]{2,1,0:T(8,128)(2,1)} %param.14), kind=kLoop, calls=%fused_computation.13 | loop fusion | bytes 1638408 | tf_op jit(solution)/shard_map/dynamic_slice | solution.py:249
  10.1 0.9 fusion.10
  11.0 5.7 %collective-permute-done.refs_1_ = bf16[64,5120]{1,0:T(8,128)(2,1)S(1)} collective-permute-done((bf16[64,5120]{1,0:T(8,128)(2,1)}, bf16[64,5120]{1,0:T(8,128)(2,1)S(1)}, u32[]{:S(2)}, u32[]{:S(2)}) %collective-permute-start) | collective-permute-done | bytes 655392 | tf_op jit(solution)/shard_map/ppermute | solution.py:25
  16.7 0.8 fusion.11
  17.5 1.5 collective-permute-start.2
  18.9 0.8 fusion.12
  19.7 1.9 %pad_maximum_fusion = bf16[64,5120]{1,0:T(8,128)(2,1)} fusion(bf16[32,5120]{1,0:T(8,128)(2,1)S(1)} %get-tuple-element.129, bf16[32,5120]{1,0:T(8,128)(2,1)} %get-tuple-element.128), kind=kLoop, calls=%fused_computation | loop fusion | flops 1310720 | bytes 1310720 | tf_op jit(solution)/shard_map/concatenate | solution.py:198
  21.7 1.9 %collective-permute-start.4 = (bf16[64,5120]{1,0:T(8,128)(2,1)}, bf16[64,5120]{1,0:T(8,128)(2,1)S(1)}, u32[]{:S(2)}, u32[]{:S(2)}) collective-permute-start(bf16[64,5120]{1,0:T(8,128)(2,1)} %pad_maximum_fusion), channel_id=1, source_target_pairs={{0,4},{1,5},{2,6},{3,7},{4,0},{5,1},{6,2},{7,3},{8,12},{9,13},{10,... | collective-permute-start | bytes 1966088 | tf_op jit(solution)/shard_map/ppermute | solution.py:25
  23.6 1.8 %collective-permute-start.3 = (bf16[32,5120]{1,0:T(8,128)(2,1)}, bf16[32,5120]{1,0:T(8,128)(2,1)}, u32[]{:S(2)}, u32[]{:S(2)}) collective-permute-start(bf16[32,5120]{1,0:T(8,128)(2,1)} %get-tuple-element.130), channel_id=1, source_target_pairs={{0,1},{1,0},{2,3},{3,2},{4,5},{5,4},{6,7},{7,6},{8,9},{9,8},{10,11... | collective-permute-start | bytes 983048 | tf_op jit(solution)/shard_map/ppermute | solution.py:25
  25.4 1.9 %pad_maximum_fusion.1 = bf16[64,5120]{1,0:T(8,128)(2,1)} fusion(bf16[32,5120]{1,0:T(8,128)(2,1)} %get-tuple-element.130, bf16[32,5120]{1,0:T(8,128)(2,1)S(1)} %get-tuple-element.127), kind=kLoop, calls=%fused_computation.1 | loop fusion | flops 1310720 | bytes 1310720 | tf_op jit(solution)/shard_map/concatenate | solution.py:199
  27.3 4.9 %collective-permute-start.5 = (bf16[64,5120]{1,0:T(8,128)(2,1)}, bf16[64,5120]{1,0:T(8,128)(2,1)S(1)}, u32[]{:S(2)}, u32[]{:S(2)}) collective-permute-start(bf16[64,5120]{1,0:T(8,128)(2,1)} %pad_maximum_fusion.1), channel_id=1, source_target_pairs={{0,196},{1,197},{2,198},{3,199},{4,64},{5,65},{6,66},{7,67},{8,204... | collective-permute-start | bytes 1966088 | tf_op jit(solution)/shard_map/ppermute | solution.py:25
  32.2 1.0 dynamic-slice_bitcast_fusion.2
  33.3 1.8 %copy.20 = bf16[1,320,320]{1,2,0:T(8,128)(2,1)} copy(bf16[1,320,320]{2,1,0:T(8,128)(2,1)} %get-tuple-element.132) | data formatting | bytes 409600 | tf_op jit(solution)/shard_map/dynamic_slice | solution.py:248
  35.1 1.8 %copy.19 = bf16[1,320,320]{1,2,0:T(8,128)(2,1)} copy(bf16[1,320,320]{2,1,0:T(8,128)(2,1)} %get-tuple-element.159) | data formatting | bytes 409600 | tf_op jit(solution)/shard_map/dynamic_slice | solution.py:248
  36.9 1.8 %copy.18 = bf16[1,320,320]{1,2,0:T(8,128)(2,1)} copy(bf16[1,320,320]{2,1,0:T(8,128)(2,1)} %get-tuple-element.136) | data formatting | bytes 409600 | tf_op jit(solution)/shard_map/dynamic_slice | solution.py:248
  38.7 2.0 %collective-permute-start.9 = (bf16[32,5120]{1,0:T(8,128)(2,1)}, bf16[32,5120]{1,0:T(8,128)(2,1)}, u32[]{:S(2)}, u32[]{:S(2)}) collective-permute-start(bf16[32,5120]{1,0:T(8,128)(2,1)} %get-tuple-element.125), channel_id=1, source_target_pairs={{0,196},{1,197},{2,198},{3,199},{4,64},{5,65},{6,66},{7,67},{8,204... | collective-permute-start | bytes 983048 | tf_op jit(solution)/shard_map/ppermute | solution.py:25
  40.7 1.3 collective-permute-start.10
  42.0 0.7 collective-permute-start.8
  42.7 0.7 reshape.32
  44.8 6.0 %slice.70.refs_6_ = bf16[2,320,5120]{2,1,0:T(8,128)(2,1)} slice(bf16[3,320,5120]{2,1,0:T(8,128)(2,1)} %bitcast.60), slice={[1:3], [0:320], [0:5120]} | slice | bytes 13107200 | tf_op jit(solution)/shard_map/slice | solution.py:260
  50.8 1.7 %fusion.2.old = f32[80,960]{1,0:T(8,128)} fusion(s32[]{:T(128)S(6)} %select_n.217, bf16[320,320]{1,0:T(8,128)(2,1)} %bitcast.68, bf16[320,320]{1,0:T(8,128)(2,1)} %bitcast.66, bf16[320,320]{1,0:T(8,128)(2,1)} %bitcast.64), kind=kLoop, calls=%fused_computation.19 | loop fusion | flops 460800 | bytes 921604 | tf_op jit(solution)/shard_map/convert_element_type | solution.py:250
  52.6 0.8 copy.21.refs_6_
  53.4 3.8 %copy-done = bf16[3,5120,320]{1,2,0:T(8,128)(2,1)S(1)} copy-done((bf16[3,5120,320]{1,2,0:T(8,128)(2,1)S(1)}, bf16[3,5120,320]{1,2,0:T(8,128)(2,1)}, u32[]{:S(2)}) %copy-start) | copy-done | bytes 9830424
  57.2 9.1 %shard_map.82 = (bf16[256,320]{1,0:T(8,128)(2,1)S(1)}, bf16[256,320]{1,0:T(8,128)(2,1)S(1)}, bf16[256,320]{1,0:T(8,128)(2,1)S(1)}) custom-call(bf16[64,5120]{1,0:T(8,128)(2,1)S(1)} %copy-done.2, bf16[64,5120]{1,0:T(8,128)(2,1)S(1)} %collective-permute-done.refs_1_, bf16[64,5120]{1,0:T(8,128)(2,1)S(1)} %collective-permute-done.1.refs_2_, ...), custom_call_target="tpu_custom_call" | custom-call | flops 1000 | bytes 1000 | tf_op jit(solution)/shard_map/pallas_call | solution.py:116
  66.4 0.7 copy-done.6
  67.0 0.7 copy-done.8
  67.7 0.7 copy-done.11
  68.6 2.9 %copy-done.1 = bf16[2,320,5120]{2,1,0:T(8,128)(2,1)S(1)} copy-done((bf16[2,320,5120]{2,1,0:T(8,128)(2,1)S(1)}, bf16[2,320,5120]{2,1,0:T(8,128)(2,1)}, u32[]{:S(2)}) %copy-start.1) | copy-done | bytes 6553624
  71.5 6.6 %shard_map.83 = (bf16[256,320]{1,0:T(8,128)(2,1)S(1)}, bf16[256,320]{1,0:T(8,128)(2,1)S(1)}) custom-call(bf16[32,5120]{1,0:T(8,128)(2,1)} %collective-permute-done.7.refs_0_, bf16[64,5120]{1,0:T(8,128)(2,1)S(1)} %collective-permute-done.4.refs_1_, bf16[32,5120]{1,0:T(8,128)(2,1)} %collective-permute-done.8.refs_2_, ...), custom_call_target="tpu_custom_call" | custom-call | flops 1000 | bytes 1000 | tf_op jit(solution)/shard_map/pallas_call | solution.py:116
  78.2 2.5 %shard_map.84 = bf16[320,960]{1,0:T(8,128)(2,1)} custom-call(bf16[256,320]{1,0:T(8,128)(2,1)S(1)} %copy-done.7, bf16[256,320]{1,0:T(8,128)(2,1)S(1)} %get-tuple-element.92.k2, bf16[256,320]{1,0:T(8,128)(2,1)S(1)} %copy-done.9, bf16[256,320]{1,0:T(8,128)(2,1)S(1)} %get-tuple-element.94.v2, f32[512,1]{1,0:T(8,128)S(1)} %copy.23.weight, ...), custom_call_target="tpu_custom_call" | custom-call | flops 1000 | bytes 1000 | tf_op jit(solution)/shard_map/pallas_call | solution.py:81
  81.0 1.1 copy.26.up_w
  82.4 1.6 %shard_map.85.own = f32[320,960]{1,0:T(8,128)S(1)} custom-call(bf16[256,320]{1,0:T(8,128)(2,1)S(1)} %copy-done.7, bf16[256,320]{1,0:T(8,128)(2,1)S(1)} %get-tuple-element.92.k2, bf16[256,320]{1,0:T(8,128)(2,1)S(1)} %copy-done.9, bf16[256,320]{1,0:T(8,128)(2,1)S(1)} %get-tuple-element.94.v2, f32[512,1]{1,0:T(8,128)S(1)} %copy.24.weight, ...), custom_call_target="tpu_custom_call" | custom-call | flops 1000 | bytes 1000 | tf_op jit(solution)/shard_map/pallas_call | solution.py:81
  84.0 1.2 shard_map.86
  85.2 3.3 %collective-permute-start.12 = (bf16[80,960]{1,0:T(8,128)(2,1)S(1)}, bf16[80,960]{1,0:T(8,128)(2,1)S(1)}, u32[]{:S(2)}, u32[]{:S(2)}) collective-permute-start(bf16[80,960]{1,0:T(8,128)(2,1)S(1)} %get-tuple-element.103), channel_id=1, source_target_pairs={{0,32},{1,33},{2,34},{3,35},{4,36},{5,37},{6,38},{7,39},{8,40},{9,... | collective-permute-start | bytes 460808 | tf_op jit(solution)/shard_map/ppermute | solution.py:25
  88.5 0.7 collective-permute-start.13
  89.2 2.6 %collective-permute-start.14 = (bf16[80,960]{1,0:T(8,128)(2,1)S(1)}, bf16[80,960]{1,0:T(8,128)(2,1)S(1)}, u32[]{:S(2)}, u32[]{:S(2)}) collective-permute-start(bf16[80,960]{1,0:T(8,128)(2,1)S(1)} %get-tuple-element.105), channel_id=1, source_target_pairs={{0,48},{1,49},{2,50},{3,51},{4,52},{5,53},{6,54},{7,55},{8,56},{9,... | collective-permute-start | bytes 460808 | tf_op jit(solution)/shard_map/ppermute | solution.py:25
  91.7 2.1 %collective-permute-done.12.a = bf16[80,960]{1,0:T(8,128)(2,1)S(1)} collective-permute-done((bf16[80,960]{1,0:T(8,128)(2,1)S(1)}, bf16[80,960]{1,0:T(8,128)(2,1)S(1)}, u32[]{:S(2)}, u32[]{:S(2)}) %collective-permute-start.12) | collective-permute-done | bytes 153632 | tf_op jit(solution)/shard_map/ppermute | solution.py:25
  93.8 3.1 %collective-permute-done.13.b = bf16[80,960]{1,0:T(8,128)(2,1)S(1)} collective-permute-done((bf16[80,960]{1,0:T(8,128)(2,1)S(1)}, bf16[80,960]{1,0:T(8,128)(2,1)S(1)}, u32[]{:S(2)}, u32[]{:S(2)}) %collective-permute-start.13) | collective-permute-done | bytes 153632 | tf_op jit(solution)/shard_map/ppermute | solution.py:25
  97.3 5.1 %collective-permute-start.15 = (bf16[80,960]{1,0:T(8,128)(2,1)S(1)}, bf16[80,960]{1,0:T(8,128)(2,1)S(1)}, u32[]{:S(2)}, u32[]{:S(2)}) collective-permute-start(bf16[80,960]{1,0:T(8,128)(2,1)S(1)} %get-tuple-element.113), channel_id=1, source_target_pairs={{0,128},{1,129},{2,130},{3,131},{4,132},{5,133},{6,134},{7,135},{8... | collective-permute-start | bytes 460808 | tf_op jit(solution)/shard_map/ppermute | solution.py:25
  102.4 1.5 collective-permute-start.16
  103.9 2.7 %collective-permute-start.17 = (bf16[80,960]{1,0:T(8,128)(2,1)S(1)}, bf16[80,960]{1,0:T(8,128)(2,1)S(1)}, u32[]{:S(2)}, u32[]{:S(2)}) collective-permute-start(bf16[80,960]{1,0:T(8,128)(2,1)S(1)} %get-tuple-element.113), channel_id=1, source_target_pairs={{0,192},{1,193},{2,194},{3,195},{4,196},{5,197},{6,198},{7,199},{8... | collective-permute-start | bytes 460808 | tf_op jit(solution)/shard_map/ppermute | solution.py:25
  106.6 2.1 %slice.72.refs_6_ = bf16[1,320,5120]{2,1,0:T(8,128)(2,1)S(1)} slice(bf16[3,320,5120]{2,1,0:T(8,128)(2,1)} %bitcast.61), slice={[0:1], [0:320], [0:5120]} | slice | bytes 6553600 | tf_op jit(solution)/shard_map/slice | solution.py:281
  108.7 0.8 slice.73.refs_7_
  109.5 4.4 %shard_map.88.query_ref = bf16[256,320]{1,0:T(8,128)(2,1)S(1)} custom-call(bf16[32,5120]{1,0:T(8,128)(2,1)} %collective-permute-done.7.refs_0_, bf16[64,5120]{1,0:T(8,128)(2,1)S(1)} %collective-permute-done.4.refs_1_, bf16[32,5120]{1,0:T(8,128)(2,1)} %collective-permute-done.8.refs_2_, bf16[32,5120]{1,0:T(8,128)(2,1)} %collective-permute-done.9.refs_3_, ...), custom_call_target="tpu_custom_call" | custom-call | flops 1000 | bytes 1000 | tf_op jit(solution)/shard_map/pallas_call | solution.py:116
  113.9 0.7 collective-permute-done.16.b
  114.6 3.9 %collective-permute-done.17.c = bf16[80,960]{1,0:T(8,128)(2,1)S(1)} collective-permute-done((bf16[80,960]{1,0:T(8,128)(2,1)S(1)}, bf16[80,960]{1,0:T(8,128)(2,1)S(1)}, u32[]{:S(2)}, u32[]{:S(2)}) %collective-permute-start.17) | collective-permute-done | bytes 153632 | tf_op jit(solution)/shard_map/ppermute | solution.py:25
  118.9 2.2 %collective-permute-start.18 = (bf16[80,960]{1,0:T(8,128)(2,1)S(1)}, bf16[80,960]{1,0:T(8,128)(2,1)S(1)}, u32[]{:S(2)}, u32[]{:S(2)}) collective-permute-start(bf16[80,960]{1,0:T(8,128)(2,1)S(1)} %shard_map.89), channel_id=1, source_target_pairs={{0,32},{1,33},{2,34},{3,35},{4,36},{5,37},{6,38},{7,39},{8,40},{9,... | collective-permute-start | bytes 460808 | tf_op jit(solution)/shard_map/ppermute | solution.py:25
  121.0 1.6 %collective-permute-start.19 = (bf16[80,960]{1,0:T(8,128)(2,1)S(1)}, bf16[80,960]{1,0:T(8,128)(2,1)S(1)}, u32[]{:S(2)}, u32[]{:S(2)}) collective-permute-start(bf16[80,960]{1,0:T(8,128)(2,1)S(1)} %shard_map.89), channel_id=1, source_target_pairs={{0,16},{1,17},{2,18},{3,19},{4,20},{5,21},{6,22},{7,23},{8,24},{9,... | collective-permute-start | bytes 460808 | tf_op jit(solution)/shard_map/ppermute | solution.py:25
  122.6 1.6 %collective-permute-start.20 = (bf16[80,960]{1,0:T(8,128)(2,1)S(1)}, bf16[80,960]{1,0:T(8,128)(2,1)S(1)}, u32[]{:S(2)}, u32[]{:S(2)}) collective-permute-start(bf16[80,960]{1,0:T(8,128)(2,1)S(1)} %shard_map.89), channel_id=1, source_target_pairs={{0,48},{1,49},{2,50},{3,51},{4,52},{5,53},{6,54},{7,55},{8,56},{9,... | collective-permute-start | bytes 460808 | tf_op jit(solution)/shard_map/ppermute | solution.py:25
  124.3 3.3 %collective-permute-done.18 = bf16[80,960]{1,0:T(8,128)(2,1)S(1)} collective-permute-done((bf16[80,960]{1,0:T(8,128)(2,1)S(1)}, bf16[80,960]{1,0:T(8,128)(2,1)S(1)}, u32[]{:S(2)}, u32[]{:S(2)}) %collective-permute-start.18) | collective-permute-done | bytes 153632 | tf_op jit(solution)/shard_map/ppermute | solution.py:25
  127.5 2.6 %collective-permute-done.19 = bf16[80,960]{1,0:T(8,128)(2,1)S(1)} collective-permute-done((bf16[80,960]{1,0:T(8,128)(2,1)S(1)}, bf16[80,960]{1,0:T(8,128)(2,1)S(1)}, u32[]{:S(2)}, u32[]{:S(2)}) %collective-permute-start.19) | collective-permute-done | bytes 153632 | tf_op jit(solution)/shard_map/ppermute | solution.py:25
  130.4 2.1 %collective-permute-done.21.other = bf16[320,960]{1,0:T(8,128)(2,1)S(1)} collective-permute-done((bf16[320,960]{1,0:T(8,128)(2,1)S(1)}, bf16[320,960]{1,0:T(8,128)(2,1)S(1)}, u32[]{:S(2)}, u32[]{:S(2)}) %collective-permute-start.21) | collective-permute-done | bytes 614432 | tf_op jit(solution)/shard_map/ppermute | solution.py:25
  132.5 0.9 shard_map.90
  133.5 3.4 %collective-permute-start.23 = (bf16[128,320]{1,0:T(8,128)(2,1)S(1)}, bf16[128,320]{1,0:T(8,128)(2,1)S(1)}, u32[]{:S(2)}, u32[]{:S(2)}) collective-permute-start(bf16[128,320]{1,0:T(8,128)(2,1)S(1)} %get-tuple-element.124), channel_id=1, source_target_pairs={{0,196},{1,197},{2,198},{3,199},{4,64},{5,65},{6,66},{7,67},{8,204... | collective-permute-start | bytes 245768 | tf_op jit(solution)/shard_map/ppermute | solution.py:25
  136.9 0.9 shard_map.91
  138.3 1.4 collective-permute-done.23
  139.8 1.8 %collective-permute-start.24 = (bf16[2,64,320]{2,1,0:T(8,128)(2,1)S(1)}, bf16[2,64,320]{2,1,0:T(8,128)(2,1)S(1)}, u32[]{:S(2)}, u32[]{:S(2)}) collective-permute-start(bf16[2,64,320]{2,1,0:T(8,128)(2,1)S(1)} %get-tuple-element.146), channel_id=1, source_target_pairs={{0,1},{1,0},{2,3},{3,2},{4,5},{5,4},{6,7},{7,6},{8,9},{9,8},{10,11... | collective-permute-start | bytes 245768 | tf_op jit(solution)/shard_map/ppermute | solution.py:25
  142.0 2.0 %collective-permute-start.26 = (bf16[2,64,320]{2,1,0:T(8,128)(2,1)S(1)}, bf16[2,64,320]{2,1,0:T(8,128)(2,1)S(1)}, u32[]{:S(2)}, u32[]{:S(2)}) collective-permute-start(bf16[2,64,320]{2,1,0:T(8,128)(2,1)S(1)} %get-tuple-element.147), channel_id=1, source_target_pairs={{0,2},{1,3},{2,0},{3,1},{4,6},{5,7},{6,4},{7,5},{8,10},{9,11},{10,... | collective-permute-start | bytes 245768 | tf_op jit(solution)/shard_map/ppermute | solution.py:25
  144.6 2.4 %collective-permute-done.25 = bf16[2,64,320]{2,1,0:T(8,128)(2,1)S(1)} collective-permute-done((bf16[2,64,320]{2,1,0:T(8,128)(2,1)S(1)}, bf16[2,64,320]{2,1,0:T(8,128)(2,1)S(1)}, u32[]{:S(2)}, u32[]{:S(2)}) %collective-permute-start.25) | collective-permute-done | bytes 81952 | tf_op jit(solution)/shard_map/ppermute | solution.py:25
  146.9 1.2 collective-permute-done.26
  148.3 0.9 concatenate.35
  (83 shorter events, 5.7 us)
Async XLA Ops:
  0.0 10.1 %copy-start.2 = (bf16[64,5120]{1,0:T(8,128)(2,1)S(1)}, bf16[64,5120]{1,0:T(8,128)(2,1)}, u32[]{:S(2)}) copy-start(bf16[64,5120]{1,0:T(8,128)(2,1)} %refs_0_) | copy-start | bytes 1966084
  0.0 16.7 %collective-permute-start = (bf16[64,5120]{1,0:T(8,128)(2,1)}, bf16[64,5120]{1,0:T(8,128)(2,1)S(1)}, u32[]{:S(2)}, u32[]{:S(2)}) collective-permute-start(bf16[64,5120]{1,0:T(8,128)(2,1)} %refs_0_), channel_id=1, source_target_pairs={{0,1},{1,0},{2,3},{3,2},{4,5},{5,4},{6,7},{7,6},{8,9},{9,8},{10,11... | collective-permute-start | bytes 1966088 | tf_op jit(solution)/shard_map/ppermute | solution.py:25
  2.3 16.7 %collective-permute-start.1 = (bf16[64,5120]{1,0:T(8,128)(2,1)}, bf16[64,5120]{1,0:T(8,128)(2,1)S(1)}, u32[]{:S(2)}, u32[]{:S(2)}) collective-permute-start(bf16[64,5120]{1,0:T(8,128)(2,1)} %refs_0_), channel_id=1, source_target_pairs={{0,3},{1,2},{2,1},{3,0},{4,7},{5,6},{6,5},{7,4},{8,11},{9,10},{10,... | collective-permute-start | bytes 1966088 | tf_op jit(solution)/shard_map/ppermute | solution.py:25
  4.2 34.4 %collective-permute-start.6 = (f32[4,32]{1,0:T(4,128)S(1)}, f32[4,32]{1,0:T(4,128)S(1)}, u32[]{:S(2)}, u32[]{:S(2)}) collective-permute-start(f32[4,32]{1,0:T(4,128)S(1)} %get-tuple-element.158), channel_id=1, source_target_pairs={{0,64},{1,65},{2,66},{3,67},{4,196},{5,197},{6,198},{7,199},{8,72}... | collective-permute-start | bytes 1544 | tf_op jit(solution)/shard_map/ppermute | solution.py:25
  17.5 21.2 %collective-permute-start.2 = (bf16[32,5120]{1,0:T(8,128)(2,1)}, bf16[32,5120]{1,0:T(8,128)(2,1)}, u32[]{:S(2)}, u32[]{:S(2)}) collective-permute-start(bf16[32,5120]{1,0:T(8,128)(2,1)} %get-tuple-element.128), channel_id=1, source_target_pairs={{0,3},{1,2},{2,1},{3,0},{4,7},{5,6},{6,5},{7,4},{8,11},{9,10},{10,... | collective-permute-start | bytes 983048 | tf_op jit(solution)/shard_map/ppermute | solution.py:25
  19.7 12.5 %copy-start.15 = (bf16[1,320,640]{2,1,0:T(8,128)(2,1)S(1)}, bf16[1,320,640]{2,1,0:T(8,128)(2,1)}, u32[]{:S(2)}) copy-start(bf16[1,320,640]{2,1,0:T(8,128)(2,1)} %param.13) | copy-start | bytes 1228804
  21.7 11.6 %copy-start.20 = (s32[3,40,1]{1,2,0:T(1,128)S(1)}, s32[3,40,1]{1,2,0:T(1,128)}, u32[]{:S(2)}) copy-start(s32[3,40,1]{1,2,0:T(1,128)} %param.10) | copy-start | bytes 1444
  21.7 20.4 %collective-permute-start.4 = (bf16[64,5120]{1,0:T(8,128)(2,1)}, bf16[64,5120]{1,0:T(8,128)(2,1)S(1)}, u32[]{:S(2)}, u32[]{:S(2)}) collective-permute-start(bf16[64,5120]{1,0:T(8,128)(2,1)} %pad_maximum_fusion), channel_id=1, source_target_pairs={{0,4},{1,5},{2,6},{3,7},{4,0},{5,1},{6,2},{7,3},{8,12},{9,13},{10,... | collective-permute-start | bytes 1966088 | tf_op jit(solution)/shard_map/ppermute | solution.py:25
  23.6 17.1 %collective-permute-start.3 = (bf16[32,5120]{1,0:T(8,128)(2,1)}, bf16[32,5120]{1,0:T(8,128)(2,1)}, u32[]{:S(2)}, u32[]{:S(2)}) collective-permute-start(bf16[32,5120]{1,0:T(8,128)(2,1)} %get-tuple-element.130), channel_id=1, source_target_pairs={{0,1},{1,0},{2,3},{3,2},{4,5},{5,4},{6,7},{7,6},{8,9},{9,8},{10,11... | collective-permute-start | bytes 983048 | tf_op jit(solution)/shard_map/ppermute | solution.py:25
  27.3 25.3 %collective-permute-start.5 = (bf16[64,5120]{1,0:T(8,128)(2,1)}, bf16[64,5120]{1,0:T(8,128)(2,1)S(1)}, u32[]{:S(2)}, u32[]{:S(2)}) collective-permute-start(bf16[64,5120]{1,0:T(8,128)(2,1)} %pad_maximum_fusion.1), channel_id=1, source_target_pairs={{0,196},{1,197},{2,198},{3,199},{4,64},{5,65},{6,66},{7,67},{8,204... | collective-permute-start | bytes 1966088 | tf_op jit(solution)/shard_map/ppermute | solution.py:25
  38.7 4.1 %copy-start.17 = (f32[4,32]{1,0:T(4,128)}, f32[4,32]{1,0:T(4,128)S(1)}, u32[]{:S(2)}) copy-start(f32[4,32]{1,0:T(4,128)S(1)} %collective-permute-done.6) | copy-start | bytes 1540
  38.7 29.8 %collective-permute-start.7 = (bf16[32,5120]{1,0:T(8,128)(2,1)}, bf16[32,5120]{1,0:T(8,128)(2,1)}, u32[]{:S(2)}, u32[]{:S(2)}) collective-permute-start(bf16[32,5120]{1,0:T(8,128)(2,1)} %get-tuple-element.126), channel_id=1, source_target_pairs={{0,4},{1,5},{2,6},{3,7},{4,0},{5,1},{6,2},{7,3},{8,12},{9,13},{10,... | collective-permute-start | bytes 983048 | tf_op jit(solution)/shard_map/ppermute | solution.py:25
  38.7 29.8 %collective-permute-start.9 = (bf16[32,5120]{1,0:T(8,128)(2,1)}, bf16[32,5120]{1,0:T(8,128)(2,1)}, u32[]{:S(2)}, u32[]{:S(2)}) collective-permute-start(bf16[32,5120]{1,0:T(8,128)(2,1)} %get-tuple-element.125), channel_id=1, source_target_pairs={{0,196},{1,197},{2,198},{3,199},{4,64},{5,65},{6,66},{7,67},{8,204... | collective-permute-start | bytes 983048 | tf_op jit(solution)/shard_map/ppermute | solution.py:25
  40.7 27.8 %collective-permute-start.10 = (bf16[32,5120]{1,0:T(8,128)(2,1)}, bf16[32,5120]{1,0:T(8,128)(2,1)}, u32[]{:S(2)}, u32[]{:S(2)}) collective-permute-start(bf16[32,5120]{1,0:T(8,128)(2,1)} %collective-permute-done.3.refs_4_), channel_id=1, source_target_pairs={{0,196},{1,197},{2,198},{3,199},{4,64},{5,65},{6,66},{7,67},{8,204... | collective-permute-start | bytes 983048 | tf_op jit(solution)/shard_map/ppermute | solution.py:25
  42.0 26.4 %collective-permute-start.8 = (bf16[32,5120]{1,0:T(8,128)(2,1)}, bf16[32,5120]{1,0:T(8,128)(2,1)}, u32[]{:S(2)}, u32[]{:S(2)}) collective-permute-start(bf16[32,5120]{1,0:T(8,128)(2,1)} %collective-permute-done.2.refs_3_), channel_id=1, source_target_pairs={{0,4},{1,5},{2,6},{3,7},{4,0},{5,1},{6,2},{7,3},{8,12},{9,13},{10,... | collective-permute-start | bytes 983048 | tf_op jit(solution)/shard_map/ppermute | solution.py:25
  44.7 7.7 %copy-start.18 = (f32[4,32]{1,0:T(4,128)S(1)}, f32[4,32]{1,0:T(4,128)}, u32[]{:S(2)}) copy-start(f32[4,32]{1,0:T(4,128)} %copy-done.17) | copy-start | bytes 1540
  44.7 7.8 %copy-start.16 = (f32[256]{0:T(256)S(1)}, f32[256]{0:T(256)}, u32[]{:S(2)}) copy-start(f32[256]{0:T(256)} %reshape.32) | copy-start | bytes 3076
  44.8 7.8 %copy-start.19 = (f32[128]{0:T(128)S(1)}, f32[128]{0:T(128)}, u32[]{:S(2)}) copy-start(f32[128]{0:T(128)} %reshape.33) | copy-start | bytes 1540
  53.4 3.8 %copy-start = (bf16[3,5120,320]{1,2,0:T(8,128)(2,1)S(1)}, bf16[3,5120,320]{1,2,0:T(8,128)(2,1)}, u32[]{:S(2)}) copy-start(bf16[3,5120,320]{1,2,0:T(8,128)(2,1)} %param.9) | copy-start | bytes 29491204
  57.2 9.1 %copy-start.10 = (bf16[3,1,5120]{2,1,0:T(2,128)(2,1)}, bf16[3,1,5120]{2,1,0:T(2,128)(2,1)S(1)}, u32[]{:S(2)}) copy-start(bf16[3,1,5120]{2,1,0:T(2,128)(2,1)S(1)} %copy.21.refs_6_) | copy-start | bytes 92164
  66.4 0.7 copy-start.6
  67.0 0.7 copy-start.8
  67.7 0.7 copy-start.11
  68.6 2.9 %copy-start.1 = (bf16[2,320,5120]{2,1,0:T(8,128)(2,1)S(1)}, bf16[2,320,5120]{2,1,0:T(8,128)(2,1)}, u32[]{:S(2)}) copy-start(bf16[2,320,5120]{2,1,0:T(8,128)(2,1)} %slice.70.refs_6_) | copy-start | bytes 19660804
  71.5 6.6 %copy-start.4 = (bf16[320,320]{1,0:T(8,128)(2,1)S(1)}, bf16[320,320]{1,0:T(8,128)(2,1)}, u32[]{:S(2)}) copy-start(bf16[320,320]{1,0:T(8,128)(2,1)} %get-tuple-element.89.up_w) | copy-start | bytes 614404
  71.5 6.7 %copy-start.5 = (bf16[320,320]{1,0:T(8,128)(2,1)S(1)}, bf16[320,320]{1,0:T(8,128)(2,1)}, u32[]{:S(2)}) copy-start(bf16[320,320]{1,0:T(8,128)(2,1)} %get-tuple-element.88.gate_w) | copy-start | bytes 614404
  71.5 6.7 %copy-start.7 = (bf16[256,320]{1,0:T(8,128)(2,1)S(1)}, bf16[256,320]{1,0:T(8,128)(2,1)}, u32[]{:S(2)}) copy-start(bf16[256,320]{1,0:T(8,128)(2,1)} %copy-done.6) | copy-start | bytes 491524
  71.5 6.7 %copy-start.9 = (bf16[256,320]{1,0:T(8,128)(2,1)S(1)}, bf16[256,320]{1,0:T(8,128)(2,1)}, u32[]{:S(2)}) copy-start(bf16[256,320]{1,0:T(8,128)(2,1)} %copy-done.8) | copy-start | bytes 491524
  78.2 2.6 %copy-start.14 = (bf16[1,320,320]{1,2,0:T(8,128)(2,1)S(1)}, bf16[1,320,320]{1,2,0:T(8,128)(2,1)}, u32[]{:S(2)}) copy-start(bf16[1,320,320]{1,2,0:T(8,128)(2,1)} %copy.18) | copy-start | bytes 614404
  80.6 1.5 %copy-start.13 = (bf16[1,320,320]{1,2,0:T(8,128)(2,1)S(1)}, bf16[1,320,320]{1,2,0:T(8,128)(2,1)}, u32[]{:S(2)}) copy-start(bf16[1,320,320]{1,2,0:T(8,128)(2,1)} %copy.20) | copy-start | bytes 614404
  80.7 3.3 %collective-permute-start.11 = (bf16[320,960]{1,0:T(8,128)(2,1)}, bf16[320,960]{1,0:T(8,128)(2,1)}, u32[]{:S(2)}, u32[]{:S(2)}) collective-permute-start(bf16[320,960]{1,0:T(8,128)(2,1)} %shard_map.84), channel_id=1, source_target_pairs={{0,8},{1,9},{2,10},{3,11},{4,12},{5,13},{6,14},{7,15},{8,0},{9,1},... | collective-permute-start | bytes 1843208 | tf_op jit(solution)/shard_map/ppermute | solution.py:25
  85.2 8.6 %collective-permute-start.12 = (bf16[80,960]{1,0:T(8,128)(2,1)S(1)}, bf16[80,960]{1,0:T(8,128)(2,1)S(1)}, u32[]{:S(2)}, u32[]{:S(2)}) collective-permute-start(bf16[80,960]{1,0:T(8,128)(2,1)S(1)} %get-tuple-element.103), channel_id=1, source_target_pairs={{0,32},{1,33},{2,34},{3,35},{4,36},{5,37},{6,38},{7,39},{8,40},{9,... | collective-permute-start | bytes 460808 | tf_op jit(solution)/shard_map/ppermute | solution.py:25
  88.5 8.4 %collective-permute-start.13 = (bf16[80,960]{1,0:T(8,128)(2,1)S(1)}, bf16[80,960]{1,0:T(8,128)(2,1)S(1)}, u32[]{:S(2)}, u32[]{:S(2)}) collective-permute-start(bf16[80,960]{1,0:T(8,128)(2,1)S(1)} %get-tuple-element.104), channel_id=1, source_target_pairs={{0,16},{1,17},{2,18},{3,19},{4,20},{5,21},{6,22},{7,23},{8,24},{9,... | collective-permute-start | bytes 460808 | tf_op jit(solution)/shard_map/ppermute | solution.py:25
  89.2 8.1 %collective-permute-start.14 = (bf16[80,960]{1,0:T(8,128)(2,1)S(1)}, bf16[80,960]{1,0:T(8,128)(2,1)S(1)}, u32[]{:S(2)}, u32[]{:S(2)}) collective-permute-start(bf16[80,960]{1,0:T(8,128)(2,1)S(1)} %get-tuple-element.105), channel_id=1, source_target_pairs={{0,48},{1,49},{2,50},{3,51},{4,52},{5,53},{6,54},{7,55},{8,56},{9,... | collective-permute-start | bytes 460808 | tf_op jit(solution)/shard_map/ppermute | solution.py:25
  97.3 16.6 %collective-permute-start.15 = (bf16[80,960]{1,0:T(8,128)(2,1)S(1)}, bf16[80,960]{1,0:T(8,128)(2,1)S(1)}, u32[]{:S(2)}, u32[]{:S(2)}) collective-permute-start(bf16[80,960]{1,0:T(8,128)(2,1)S(1)} %get-tuple-element.113), channel_id=1, source_target_pairs={{0,128},{1,129},{2,130},{3,131},{4,132},{5,133},{6,134},{7,135},{8... | collective-permute-start | bytes 460808 | tf_op jit(solution)/shard_map/ppermute | solution.py:25
  102.4 12.2 %collective-permute-start.16 = (bf16[80,960]{1,0:T(8,128)(2,1)S(1)}, bf16[80,960]{1,0:T(8,128)(2,1)S(1)}, u32[]{:S(2)}, u32[]{:S(2)}) collective-permute-start(bf16[80,960]{1,0:T(8,128)(2,1)S(1)} %get-tuple-element.113), channel_id=1, source_target_pairs={{0,64},{1,65},{2,66},{3,67},{4,68},{5,69},{6,70},{7,71},{8,72},{9,... | collective-permute-start | bytes 460808 | tf_op jit(solution)/shard_map/ppermute | solution.py:25
  103.9 14.6 %collective-permute-start.17 = (bf16[80,960]{1,0:T(8,128)(2,1)S(1)}, bf16[80,960]{1,0:T(8,128)(2,1)S(1)}, u32[]{:S(2)}, u32[]{:S(2)}) collective-permute-start(bf16[80,960]{1,0:T(8,128)(2,1)S(1)} %get-tuple-element.113), channel_id=1, source_target_pairs={{0,192},{1,193},{2,194},{3,195},{4,196},{5,197},{6,198},{7,199},{8... | collective-permute-start | bytes 460808 | tf_op jit(solution)/shard_map/ppermute | solution.py:25
  109.5 9.0 %copy-start.3 = (f32[80,960]{1,0:T(8,128)S(1)}, f32[80,960]{1,0:T(8,128)}, u32[]{:S(2)}) copy-start(f32[80,960]{1,0:T(8,128)} %fusion.2.old) | copy-start | bytes 921604
  118.8 18.1 %copy-start.12 = (bf16[256,320]{1,0:T(8,128)(2,1)S(1)}, bf16[256,320]{1,0:T(8,128)(2,1)}, u32[]{:S(2)}) copy-start(bf16[256,320]{1,0:T(8,128)(2,1)} %copy-done.11) | copy-start | bytes 491524
  118.9 8.7 %collective-permute-start.18 = (bf16[80,960]{1,0:T(8,128)(2,1)S(1)}, bf16[80,960]{1,0:T(8,128)(2,1)S(1)}, u32[]{:S(2)}, u32[]{:S(2)}) collective-permute-start(bf16[80,960]{1,0:T(8,128)(2,1)S(1)} %shard_map.89), channel_id=1, source_target_pairs={{0,32},{1,33},{2,34},{3,35},{4,36},{5,37},{6,38},{7,39},{8,40},{9,... | collective-permute-start | bytes 460808 | tf_op jit(solution)/shard_map/ppermute | solution.py:25
  121.0 9.1 %collective-permute-start.19 = (bf16[80,960]{1,0:T(8,128)(2,1)S(1)}, bf16[80,960]{1,0:T(8,128)(2,1)S(1)}, u32[]{:S(2)}, u32[]{:S(2)}) collective-permute-start(bf16[80,960]{1,0:T(8,128)(2,1)S(1)} %shard_map.89), channel_id=1, source_target_pairs={{0,16},{1,17},{2,18},{3,19},{4,20},{5,21},{6,22},{7,23},{8,24},{9,... | collective-permute-start | bytes 460808 | tf_op jit(solution)/shard_map/ppermute | solution.py:25
  122.6 7.6 %collective-permute-start.20 = (bf16[80,960]{1,0:T(8,128)(2,1)S(1)}, bf16[80,960]{1,0:T(8,128)(2,1)S(1)}, u32[]{:S(2)}, u32[]{:S(2)}) collective-permute-start(bf16[80,960]{1,0:T(8,128)(2,1)S(1)} %shard_map.89), channel_id=1, source_target_pairs={{0,48},{1,49},{2,50},{3,51},{4,52},{5,53},{6,54},{7,55},{8,56},{9,... | collective-permute-start | bytes 460808 | tf_op jit(solution)/shard_map/ppermute | solution.py:25
  130.3 2.2 %collective-permute-start.21 = (bf16[320,960]{1,0:T(8,128)(2,1)S(1)}, bf16[320,960]{1,0:T(8,128)(2,1)S(1)}, u32[]{:S(2)}, u32[]{:S(2)}) collective-permute-start(bf16[320,960]{1,0:T(8,128)(2,1)S(1)} %pad_maximum_fusion.2.column), channel_id=1, source_target_pairs={{0,8},{1,9},{2,10},{3,11},{4,12},{5,13},{6,14},{7,15},{8,0},{9,1},... | collective-permute-start | bytes 1843208 | tf_op jit(solution)/shard_map/ppermute | solution.py:25
  133.4 4.9 %collective-permute-start.22 = (bf16[128,320]{1,0:T(8,128)(2,1)S(1)}, bf16[128,320]{1,0:T(8,128)(2,1)S(1)}, u32[]{:S(2)}, u32[]{:S(2)}) collective-permute-start(bf16[128,320]{1,0:T(8,128)(2,1)S(1)} %get-tuple-element.123), channel_id=1, source_target_pairs={{0,4},{1,5},{2,6},{3,7},{4,0},{5,1},{6,2},{7,3},{8,12},{9,13},{10,... | collective-permute-start | bytes 245768 | tf_op jit(solution)/shard_map/ppermute | solution.py:25
  133.5 6.2 %collective-permute-start.23 = (bf16[128,320]{1,0:T(8,128)(2,1)S(1)}, bf16[128,320]{1,0:T(8,128)(2,1)S(1)}, u32[]{:S(2)}, u32[]{:S(2)}) collective-permute-start(bf16[128,320]{1,0:T(8,128)(2,1)S(1)} %get-tuple-element.124), channel_id=1, source_target_pairs={{0,196},{1,197},{2,198},{3,199},{4,64},{5,65},{6,66},{7,67},{8,204... | collective-permute-start | bytes 245768 | tf_op jit(solution)/shard_map/ppermute | solution.py:25
  139.8 4.7 %collective-permute-start.24 = (bf16[2,64,320]{2,1,0:T(8,128)(2,1)S(1)}, bf16[2,64,320]{2,1,0:T(8,128)(2,1)S(1)}, u32[]{:S(2)}, u32[]{:S(2)}) collective-permute-start(bf16[2,64,320]{2,1,0:T(8,128)(2,1)S(1)} %get-tuple-element.146), channel_id=1, source_target_pairs={{0,1},{1,0},{2,3},{3,2},{4,5},{5,4},{6,7},{7,6},{8,9},{9,8},{10,11... | collective-permute-start | bytes 245768 | tf_op jit(solution)/shard_map/ppermute | solution.py:25
  141.6 5.3 %collective-permute-start.25 = (bf16[2,64,320]{2,1,0:T(8,128)(2,1)S(1)}, bf16[2,64,320]{2,1,0:T(8,128)(2,1)S(1)}, u32[]{:S(2)}, u32[]{:S(2)}) collective-permute-start(bf16[2,64,320]{2,1,0:T(8,128)(2,1)S(1)} %get-tuple-element.148), channel_id=1, source_target_pairs={{0,3},{1,2},{2,1},{3,0},{4,7},{5,6},{6,5},{7,4},{8,11},{9,10},{10,... | collective-permute-start | bytes 245768 | tf_op jit(solution)/shard_map/ppermute | solution.py:25
  142.0 6.1 %collective-permute-start.26 = (bf16[2,64,320]{2,1,0:T(8,128)(2,1)S(1)}, bf16[2,64,320]{2,1,0:T(8,128)(2,1)S(1)}, u32[]{:S(2)}, u32[]{:S(2)}) collective-permute-start(bf16[2,64,320]{2,1,0:T(8,128)(2,1)S(1)} %get-tuple-element.147), channel_id=1, source_target_pairs={{0,2},{1,3},{2,0},{3,1},{4,6},{5,7},{6,4},{7,5},{8,10},{9,11},{10,... | collective-permute-start | bytes 245768 | tf_op jit(solution)/shard_map/ppermute | solution.py:25

commit v5 on v1

v5 whole, which is shorter than its diff:
```python
import functools

import jax
import jax.numpy as jnp
import numpy as np
from jax import lax
from jax.experimental import pallas as pl
from jax.experimental.pallas import tpu as pltpu
from jax.sharding import PartitionSpec as P

AXES = ("seq", "head")
BF16 = jnp.bfloat16
F32 = jnp.float32


def place(i):
    seq, head = divmod(i, 8)
    return seq // 8, (seq // 2) % 4, seq % 2, head // 4, head % 4


def permute(value, move):
    pairs = []
    for i in range(256):
        z_hi, y, core, z_lo, x = move(*place(i))
        pairs.append((i, ((z_hi % 4) * 8 + (y % 4) * 2 + core) * 8 + z_lo * 4 + x % 4))
    return lax.ppermute(value, AXES, pairs)


def to_core(value):
    return permute(value, lambda h, y, c, l, x: (h, y, 1 - c, l, x))


def to_y(value, d):
    return permute(value, lambda h, y, c, l, x: (h, y + d, c, l, x))


def to_z(value, d):
    return permute(value, lambda h, y, c, l, x: (h + d, y, c, l, x))


def near(x):
    return x ^ 1


def far(x):
    return (x + 1) % 4 if x % 2 else (x - 1) % 4


def to_near_x(value):
    return permute(value, lambda h, y, c, l, x: (h, y, c, l, near(x)))


def to_far_x(value):
    return permute(value, lambda h, y, c, l, x: (h, y, c, l, far(x)))


def to_opposite_x(value):
    return permute(value, lambda h, y, c, l, x: (h, y, c, l, x + 2))


def to_near_z(value):
    return permute(value, lambda h, y, c, l, x: (h, y, c, 1 - l, x))


def to_far_z(value):
    return permute(value, lambda h, y, c, l, x: (h + 1 if l else h - 1, y, c, 1 - l, x))


VMEM = pl.BlockSpec(memory_space=pltpu.VMEM)
SMEM = pl.BlockSpec(memory_space=pltpu.SMEM)
SMALL = pl.CostEstimate(flops=1000, bytes_accessed=1000, transcendentals=0)
PARAMS = pltpu.CompilerParams(vmem_limit_bytes=14 * 1024 * 1024)
BY_ROW = (((1,), (1,)), ((), ()))
BY_TOKEN = (((0,), (0,)), ((), ()))


def like(shape, dtype=BF16):
    return jax.ShapeDtypeStruct(shape, dtype)


def call(kernel, out_shape, *args, scalars=0, after=(), scratch=()):
    n, skip = len(args), len(args) + len(after)

    def run(*refs):
        kernel(*refs[:n], *refs[skip:])

    return pl.pallas_call(
        run,
        out_shape=out_shape,
        in_specs=[SMEM] * scalars + [VMEM] * (n - scalars) + [VMEM] * len(after),
        out_specs=jax.tree.map(lambda _: VMEM, out_shape),
        scratch_shapes=list(scratch),
        compiler_params=PARAMS,
        cost_estimate=SMALL,
    )(*args, *after)


def split_kernel(near_tile, far_tile, near_first, far_second, first, second):
    near_first[...] = near_tile[:32, :]
    far_second[...] = far_tile[32:, :]
    first[:32, :] = near_tile[:32, :]
    first[32:, :] = far_tile[:32, :]
    second[:32, :] = near_tile[32:, :]
    second[32:, :] = far_tile[32:, :]


def project_kernel(n_tiles, *refs):
    tile = jnp.concatenate([t[...] for t in refs[:n_tiles]], axis=0)
    w_ref, out = refs[n_tiles:]
    for c in range(w_ref.shape[0]):
        part = lax.dot_general(w_ref[c], tile, BY_ROW, preferred_element_type=F32)
        out[c * 320 : (c + 1) * 320, :] = part.astype(BF16)


def project(tiles, weff, after=()):
    shape = (weff.shape[0] * weff.shape[1], sum(t.shape[0] for t in tiles))
    return call(
        functools.partial(project_kernel, len(tiles)), like(shape), *tiles, weff, after=after
    )


def grads_kernel(which, my, kv1, kv2, weight, moved, gate_t, up_t, down_t, out):
    half = pl.ds(pl.multiple_of(my[which], 16), 320)
    weight = jnp.concatenate([weight[...], moved[...]], axis=1)
    keys = jnp.concatenate([kv1[:320, :], kv2[:320, :]], axis=1)
    values = jnp.concatenate([kv1[320:, :], kv2[320:, :]], axis=1)
    gate = jnp.dot(gate_t[half, :], keys, preferred_element_type=F32)
    upper = jnp.dot(up_t[half, :], keys, preferred_element_type=F32)
    sigma = jax.nn.sigmoid(gate)
    active = gate * sigma
    hidden = (active * upper).astype(BF16)
    weighted = (weight * values.astype(F32)).astype(BF16)
    d_hidden = jnp.dot(down_t[half, :], weighted, preferred_element_type=F32)
    d_gate = (d_hidden * upper * sigma * (1.0 + gate * (1.0 - sigma))).astype(BF16)
    d_upper = (d_hidden * active).astype(BF16)
    pairs = ((d_gate, keys), (d_upper, keys), (hidden, weighted))
    for i, (left, right) in enumerate(pairs):
        grad = lax.dot_general(left, right, BY_ROW, preferred_element_type=F32)
        out[:, i * 320 : (i + 1) * 320] = grad.astype(out.dtype)


def halves_kernel(my, own, got, to1, to2, to3, mine):
    for d, out in ((1, to1), (2, to2), (3, to3), (0, mine)):
        at = pl.ds(pl.multiple_of(lax.rem(my[Y] + d, 4) * 80, 16), 80)
        out[...] = (own[at, :] + got[at, :].astype(F32)).astype(out.dtype)


def sum_kernel(mine, a, b, c, total, rounded):
    result = mine[...] + a[...].astype(F32) + b[...].astype(F32) + c[...].astype(F32)
    total[...] = result
    rounded[...] = result.astype(BF16)


def renorm_kernel(my, mine, a, b, c, gate_t, up_t, down_t, out):
    total = mine[...] + a[...].astype(F32) + b[...].astype(F32) + c[...].astype(F32)
    mine_rows = pl.ds(pl.multiple_of(my[BLOCK], 16), 80)
    for i, old in enumerate((gate_t, up_t, down_t)):
        at = slice(i * 320, (i + 1) * 320)
        before = old[mine_rows, :].astype(F32)
        fresh = before + total[:, at]
        old_norm = jnp.sqrt(jnp.sum(before * before, axis=1, keepdims=True))
        new_sq = jnp.sum(fresh * fresh, axis=1, keepdims=True)
        out[:, at] = (fresh * (old_norm / jnp.sqrt(new_sq + 1e-06))).astype(BF16)


def respond_kernel(start, query_ref, column, other, *outs):
    renorm = jnp.concatenate([column[...], other[...]], axis=0)
    query = query_ref[:, start : start + 256]
    gate = jnp.dot(renorm[:, :320], query, preferred_element_type=F32)
    upper = jnp.dot(renorm[:, 320:640], query, preferred_element_type=F32)
    hidden = (gate * jax.nn.sigmoid(gate) * upper).astype(BF16)
    output = lax.dot_general(hidden, renorm[:, 640:], BY_TOKEN, preferred_element_type=F32)
    scaled = output * lax.rsqrt(jnp.mean(output * output, axis=-1, keepdims=True) + 1e-05)
    answer = scaled.astype(BF16)
    at = 0
    for out in outs:
        out[...] = answer[at : at + out.shape[0]]
        at += out.shape[0]


def gather(tokens, work):
    near_tile, far_tile = to_near_x(tokens), to_far_x(tokens)
    z1, z2 = to_near_z(tokens[:32]), to_far_z(tokens[32:])
    near_first, far_second, first, second = call(
        split_kernel,
        [like((32, 5120)), like((32, 5120)), like((64, 5120)), like((64, 5120))],
        near_tile,
        far_tile,
        after=(z1, z2, *work),
    )
    opposite_first, opposite_second = to_far_x(near_first), to_near_x(far_second)
    z3, z4 = to_near_z(first), to_far_z(second)
    z5, z6 = to_near_z(opposite_first), to_far_z(opposite_second)
    return (
        [tokens, near_tile, far_tile, opposite_first, opposite_second],
        [z1, z3, z5, z2, z4, z6],
    )


OWN_HALF, OTHER_HALF, Y, BLOCK, SAME, OTHER, SLOT = 0, 1, 2, 3, 4, 8, 12


def table():
    lines = np.zeros((256, 32), np.int32)
    for i in range(256):
        _, y, core, z_lo, x = place(i)
        order = [x, near(x), far(x), (x + 2) % 4]
        lines[i, :4] = core * 320, 320 - core * 320, y, core * 320 + y * 80
        lines[i, SAME : SAME + 4] = [z_lo * 4 + t for t in order]
        lines[i, OTHER : OTHER + 4] = [(1 - z_lo) * 4 + t for t in order]
        lines[i, SLOT : SLOT + 8] = [order.index(h % 4) * 2 + (h // 4 != z_lo) for h in range(8)]
    return lines


def weights_kernel(my, rate, mask, weight, sent):
    for i in range(4):
        same = mask[pl.ds(my[SAME + i], 1), :].astype(F32) * rate[0]
        other = mask[pl.ds(my[OTHER + i], 1), :].astype(F32) * rate[0]
        weight[:, i * 64 : (i + 1) * 64] = same
        weight[:, 256 + i * 32 : 288 + i * 32] = other[:, :32]
        sent[:, i * 32 : (i + 1) * 32] = other[:, 32:]


def pieces_kernel(plane, from_near, from_far, *outs):
    for i, out in enumerate(outs):
        out[0] = plane[i * 64 : (i + 1) * 64, :]
        out[1, :32] = from_near[i * 32 : (i + 1) * 32, :]
        out[1, 32:] = from_far[i * 32 : (i + 1) * 32, :]


def place_kernel(my, a, b, c, d, out, slots):
    for i, piece in enumerate((a, b, c, d)):
        slots[2 * i : 2 * i + 2] = piece[...]
    for head in range(8):
        out[:, head * 320 : (head + 1) * 320] = slots[my[SLOT + head]]


def send_back(my, plane, for_near, for_far):
    pieces = call(
        pieces_kernel, [like((2, 64, 320))] * 4, plane, to_near_z(for_near), to_far_z(for_far)
    )
    opposite = to_opposite_x(pieces[3])
    pieces = pieces[0], to_near_x(pieces[1]), to_far_x(pieces[2]), opposite
    return call(
        place_kernel,
        like((64, 2560)),
        my,
        *pieces,
        scalars=1,
        scratch=[pltpu.VMEM((8, 64, 320), BF16)],
    )


def body(tokens, w_qkv, scale_exp, gate_mask, rate, fast_gate, fast_up, fast_down):
    at = lax.axis_index("seq") * 8 + lax.axis_index("head")
    my = lax.dynamic_slice_in_dim(jnp.asarray(table()), at, 1, axis=0).reshape(32)
    tokens, my = lax.optimization_barrier((tokens, my))
    factor = jnp.exp2(scale_exp.astype(F32)).astype(BF16)[:, :, 0]
    factor = jnp.repeat(factor, w_qkv.shape[1] // factor.shape[1], axis=1)[:, None, :]
    w_t = jnp.transpose(w_qkv, (0, 2, 1))
    weight, sent = call(
        weights_kernel,
        [like((1, 384), F32), like((1, 128), F32)],
        my,
        rate,
        gate_mask.reshape(8, 64),
        scalars=2,
    )
    moved = permute(sent, lambda h, y, c, l, x: (h - 1 if l else h + 1, y, c, l, x))
    old_t = [w[0].T for w in (fast_gate, fast_up, fast_down)]
    weff_kv, weff_q = w_t[1:] * factor[1:], w_t[:1] * factor[:1]
    plane, others = gather(tokens, (weff_kv[0, :8, :128], weight, *old_t))
    kv1 = project(plane, weff_kv, after=(others[1], others[4]))
    kv2 = project(others, weff_kv, after=(kv1,))

    grads = (my, kv1, kv2, weight, moved, *old_t)
    sent = call(
        functools.partial(grads_kernel, OTHER_HALF), like((320, 960)), *grads, scalars=1
    )
    got = to_core(sent)
    own = call(
        functools.partial(grads_kernel, OWN_HALF),
        like((320, 960), F32),
        *grads,
        scalars=1,
        after=(sent,),
    )
    to1, to2, to3, mine = call(
        halves_kernel, [like((80, 960))] * 3 + [like((80, 960), F32)], my, own, got, scalars=1
    )
    got = to_y(to2, 2), to_y(to1, 1), to_y(to3, 3)
    mine, small = call(sum_kernel, [like((80, 960), F32), like((80, 960))], mine, *got)

    got = to_z(small, 2), to_z(small, 1), to_z(small, 3)
    query = project(plane + others, weff_q, after=(small,))
    block = call(
        renorm_kernel,
        like((80, 960)),
        my,
        mine,
        *got,
        *old_t,
        scalars=1,
        after=(query,),
    )
    column = jnp.concatenate([block, to_y(block, 2), to_y(block, 1), to_y(block, 3)], axis=0)
    other = to_core(column)

    for_near, for_far = call(
        functools.partial(respond_kernel, 256), [like((128, 320))] * 2, query, column, other
    )
    (answers,) = call(
        functools.partial(respond_kernel, 0),
        [like((256, 320))],
        query,
        column,
        other,
        after=(for_near,),
    )
    return send_back(my, answers, for_near, for_far)


def solution(mesh):
    in_specs = (
        P(("seq", "head"), None),
        P(None, None, "head"),
        P(None, None, "head"),
        P("seq", "head"),
        P("head"),
        P("head", None, None),
        P("head", None, None),
        P("head", None, None),
    )
    out_specs = P(("seq", "head"), None)
    return jax.shard_map(body, mesh=mesh, in_specs=in_specs, out_specs=out_specs, check_vma=False)
```

time: 173 us -> 122 us (0.71)
  waiting for transfers between devices: 91.6 us -> 39.4 us
  starting transfers between devices: 18.4 us -> 43.6 us
  Pallas kernels: 0 us -> 18.4 us
  blocking collectives: 17 us -> 0 us
  matrix products: 16.1 us -> 0 us
  between operations: 14.4 us -> 0.9 us
  other arithmetic: 6.73 us -> 9.6 us
    all_gather x1 -> x0, waiting for transfers between devices: 65.5 us -> none  [body(): lax.all_gather(tokens, 'head', axis=0, tiled=True)]
    ppermute x11 -> x27, starting transfers between devices: 18.4 us -> 43.6 us  [permute(): return lax.ppermute(value, AXES, pairs)]
    pallas_call x0 -> x14, Pallas kernels: none -> 18.4 us  [call(): pl.pallas_call(run, out_shape=out_shape, in_specs=[SMEM] * scalars + [VME...]
    all_to_all x1 -> x0, blocking collectives: 17 us -> none  [body(): lax.all_to_all(answer, 'head', split_axis=0, concat_axis=1, tiled=True)]
    dot_general x9 -> x0, matrix products: 16.1 us -> none  [the longest x1 9.52 us: body(): jnp.einsum('rd,cdh->rch', lax.all_gather(tokens, 'head', axis=0, tiled=Tr...]
    ppermute x11 -> x27, waiting for transfers between devices: 25.4 us -> 39.4 us  [permute(): return lax.ppermute(value, AXES, pairs)]
    mul x3 -> x2, other arithmetic: 2.05 us -> 8.27 us  [body(): weff_kv, weff_q = (w_t[1:] * factor[1:], w_t[:1] * factor[:1])]
    slice x0 -> x3, local copies, waits for them, and re-layouts: none -> 1.95 us  [the longest x1 1.94 us: gather(): z1, z2 = (to_near_z(tokens[:32]), to_far_z(tokens[32:]))]
  transfers between devices with their start and end apart: 12 -> 27, of which waited for: 11 -> 19; matrix products, arithmetic and copies ran while one was open for 2% -> 12% of each run, Pallas kernels for 0% -> 9%
where the time goes in v5:
time: 122 us; the launch traced here: 121 us
  starting transfers between devices  43.6 us (36%)
  waiting for transfers between devices  39.4 us (32%)
  Pallas kernels  18.4 us (15%)
  other arithmetic  9.6 us (8%)
  local copies, waits for them, and re-layouts  8.77 us (7%)
    ppermute x27, starting transfers between devices, permute(): return lax.ppermute(value, AXES, pairs)  43.6 us
    ppermute x27, waiting for transfers between devices, permute(): return lax.ppermute(value, AXES, pairs)  39.4 us
    pallas_call x14, Pallas kernels, call(): pl.pallas_call(run, out_shape=out_shape, in_specs=[SMEM] * scalars + [VME...  18.4 us
    mul x2, other arithmetic, body(): weff_kv, weff_q = (w_t[1:] * factor[1:], w_t[:1] * factor[:1])  8.27 us
    unnamed x17, local copies, waits for them, and re-layouts  5.29 us
  transfers between devices with their start and end apart: 27, of which 19 were waited for; matrix products, arithmetic and copies ran while one was open for 12% of the time, Pallas kernels for 9%

profile of v5, /device:TPU:2, one launch (start us, length us, event | category | flops | bytes accessed | tf_op | source)
XLA Modules:
  0.0 120.6 jit_solution(4842716217612513538)
XLA Ops:
  0.0 0.7 dynamic-slice_bitcast_fusion.refs_0_
  0.7 2.3 %collective-permute-start = (bf16[64,5120]{1,0:T(8,128)(2,1)}, bf16[64,5120]{1,0:T(8,128)(2,1)S(1)}, u32[]{:S(2)}, u32[]{:S(2)}) collective-permute-start(bf16[64,5120]{1,0:T(8,128)(2,1)} %refs_0_.1), channel_id=1, source_target_pairs={{0,1},{1,0},{2,3},{3,2},{4,5},{5,4},{6,7},{7,6},{8,9},{9,8},{10,11... | collective-permute-start | bytes 1966088 | tf_op jit(solution)/shard_map/ppermute | solution.py:26
  3.0 0.4 collective-permute-start.1
  3.4 1.9 %fusion = (bf16[32,5120]{1,0:T(8,128)(2,1)}, bf16[32,5120]{1,0:T(8,128)(2,1)}) fusion(bf16[64,5120]{1,0:T(8,128)(2,1)} %refs_0_.1), kind=kLoop, calls=%fused_computation.11 | loop fusion | bytes 1310720 | tf_op jit(solution)/shard_map/slice | solution.py:183
  5.3 1.9 %collective-permute-start.2 = (bf16[32,5120]{1,0:T(8,128)(2,1)}, bf16[32,5120]{1,0:T(8,128)(2,1)}, u32[]{:S(2)}, u32[]{:S(2)}) collective-permute-start(bf16[32,5120]{1,0:T(8,128)(2,1)} %get-tuple-element.46), channel_id=1, source_target_pairs={{0,4},{1,5},{2,6},{3,7},{4,0},{5,1},{6,2},{7,3},{8,12},{9,13},{10,... | collective-permute-start | bytes 983048 | tf_op jit(solution)/shard_map/ppermute | solution.py:26
  7.2 4.9 %collective-permute-start.3 = (bf16[32,5120]{1,0:T(8,128)(2,1)}, bf16[32,5120]{1,0:T(8,128)(2,1)}, u32[]{:S(2)}, u32[]{:S(2)}) collective-permute-start(bf16[32,5120]{1,0:T(8,128)(2,1)} %get-tuple-element.45), channel_id=1, source_target_pairs={{0,196},{1,197},{2,198},{3,199},{4,64},{5,65},{6,66},{7,67},{8,204... | collective-permute-start | bytes 983048 | tf_op jit(solution)/shard_map/ppermute | solution.py:26
  12.2 0.7 exponential_convert_fusion
  13.0 6.1 %slice_multiply_fusion.refs_5_.refs_6_ = bf16[2,320,5120]{2,1,0:T(8,128)(2,1)} fusion(bf16[3,320,5120]{2,1,0:T(8,128)(2,1)} %bitcast.39, bf16[2,5120]{1,0:T(2,128)(2,1)S(1)} %bitcast.41), kind=kLoop, calls=%fused_computation | loop fusion | flops 3276800 | bytes 13127680 | tf_op jit(solution)/shard_map/mul | solution.py:271
  19.2 0.5 broadcast.8
  19.7 0.6 reduce.3
  21.0 0.6 shard_map.91
  21.6 0.3 copy.10
  22.2 1.3 %copy.12 = bf16[1,320,640]{1,2,0:T(8,128)(2,1)S(1)} copy(bf16[1,320,640]{2,1,0:T(8,128)(2,1)} %param.16) | data formatting | bytes 819200 | tf_op args[7]
  23.4 0.7 slice_bitcast_fusion.refs_4_
  24.1 1.2 shard_map.92
  25.5 2.0 %collective-permute-start.8 = (bf16[64,5120]{1,0:T(8,128)(2,1)S(1)}, bf16[64,5120]{1,0:T(8,128)(2,1)S(1)}, u32[]{:S(2)}, u32[]{:S(2)}) collective-permute-start(bf16[64,5120]{1,0:T(8,128)(2,1)S(1)} %get-tuple-element.31), channel_id=1, source_target_pairs={{0,196},{1,197},{2,198},{3,199},{4,64},{5,65},{6,66},{7,67},{8,204... | collective-permute-start | bytes 1966088 | tf_op jit(solution)/shard_map/ppermute | solution.py:26
  27.5 0.5 collective-permute-start.4
  27.9 2.6 %collective-permute-start.5 = (bf16[32,5120]{1,0:T(8,128)(2,1)S(1)}, bf16[32,5120]{1,0:T(8,128)(2,1)S(1)}, u32[]{:S(2)}, u32[]{:S(2)}) collective-permute-start(bf16[32,5120]{1,0:T(8,128)(2,1)S(1)} %get-tuple-element.29), channel_id=1, source_target_pairs={{0,1},{1,0},{2,3},{3,2},{4,5},{5,4},{6,7},{7,6},{8,9},{9,8},{10,11... | collective-permute-start | bytes 983048 | tf_op jit(solution)/shard_map/ppermute | solution.py:26
  30.6 4.6 %collective-permute-done.4.refs_3_ = bf16[32,5120]{1,0:T(8,128)(2,1)S(1)} collective-permute-done((bf16[32,5120]{1,0:T(8,128)(2,1)S(1)}, bf16[32,5120]{1,0:T(8,128)(2,1)S(1)}, u32[]{:S(2)}, u32[]{:S(2)}) %collective-permute-start.4) | collective-permute-done | bytes 327712 | tf_op jit(solution)/shard_map/ppermute | solution.py:26
  35.2 1.0 collective-permute-start.7
  36.3 1.1 collective-permute-start.9
  37.4 1.3 %collective-permute-start.10 = (f32[1,128]{1,0:T(1,128)S(1)}, f32[1,128]{1,0:T(1,128)S(1)}, u32[]{:S(2)}, u32[]{:S(2)}) collective-permute-start(f32[1,128]{1,0:T(1,128)S(1)} %get-tuple-element.32), channel_id=1, source_target_pairs={{0,64},{1,65},{2,66},{3,67},{4,196},{5,197},{6,198},{7,199},{8,72}... | collective-permute-start | bytes 1544 | tf_op jit(solution)/shard_map/ppermute | solution.py:26
  38.7 4.4 %collective-permute-done.6.refs_6_.refs_1_ = bf16[64,5120]{1,0:T(8,128)(2,1)S(1)} collective-permute-done((bf16[64,5120]{1,0:T(8,128)(2,1)S(1)}, bf16[64,5120]{1,0:T(8,128)(2,1)S(1)}, u32[]{:S(2)}, u32[]{:S(2)}) %collective-permute-start.6) | collective-permute-done | bytes 655392 | tf_op jit(solution)/shard_map/ppermute | solution.py:26
  43.1 1.3 %collective-permute-done.8.refs_7_.refs_4_.refs_9_ = bf16[64,5120]{1,0:T(8,128)(2,1)S(1)} collective-permute-done((bf16[64,5120]{1,0:T(8,128)(2,1)S(1)}, bf16[64,5120]{1,0:T(8,128)(2,1)S(1)}, u32[]{:S(2)}, u32[]{:S(2)}) %collective-permute-start.8) | collective-permute-done | bytes 655392 | tf_op jit(solution)/shard_map/ppermute | solution.py:26
  44.4 2.9 %copy-done = bf16[2,320,5120]{2,1,0:T(8,128)(2,1)S(1)} copy-done((bf16[2,320,5120]{2,1,0:T(8,128)(2,1)S(1)}, bf16[2,320,5120]{2,1,0:T(8,128)(2,1)}, u32[]{:S(2)}) %copy-start) | copy-done | bytes 6553624
  47.3 1.9 %shard_map.93.refs_7_.refs_1_ = bf16[640,256]{1,0:T(8,128)(2,1)S(1)} custom-call(bf16[64,5120]{1,0:T(8,128)(2,1)S(1)} %copy-done.1, bf16[64,5120]{1,0:T(8,128)(2,1)S(1)} %collective-permute-done.refs_0_.refs_1_, bf16[64,5120]{1,0:T(8,128)(2,1)S(1)} %collective-permute-done.1.refs_1_.refs_2_, bf16[32,5120]{1,0:T(8,128)(2,1)S(1)} %collective-permute-done.4.refs_3_, ...), custom_call_target="tpu_custom_call" | custom-call | flops 1000 | bytes 1000 | tf_op jit(solution)/shard_map/pallas_call | solution.py:87
  49.2 3.0 %shard_map.94.refs_2_ = bf16[640,256]{1,0:T(8,128)(2,1)S(1)} custom-call(bf16[32,5120]{1,0:T(8,128)(2,1)} %collective-permute-done.2.refs_2_.refs_0_.refs_5_, bf16[64,5120]{1,0:T(8,128)(2,1)S(1)} %collective-permute-done.6.refs_6_.refs_1_, bf16[32,5120]{1,0:T(8,128)(2,1)S(1)} %collective-permute-done.7.refs_2_.refs_7_, ...), custom_call_target="tpu_custom_call" | custom-call | flops 1000 | bytes 1000 | tf_op jit(solution)/shard_map/pallas_call | solution.py:87
  52.2 1.9 %shard_map.95.refs_8_ = bf16[320,960]{1,0:T(8,128)(2,1)S(1)} custom-call(s32[32]{0:T(128)S(1)} %dynamic-slice_bitcast_fusion.refs_0_, bf16[640,256]{1,0:T(8,128)(2,1)S(1)} %shard_map.93.refs_7_.refs_1_, bf16[640,256]{1,0:T(8,128)(2,1)S(1)} %shard_map.94.refs_2_, f32[1,384]{1,0:T(1,128)S(1)} %get-tuple-element.27.refs_5_.refs_3_, ...), custom_call_target="tpu_custom_call" | custom-call | flops 1000 | bytes 1000 | tf_op jit(solution)/shard_map/pallas_call | solution.py:87
  54.1 0.3 collective-permute-start.11
  54.4 1.9 %shard_map.96.refs_1_ = f32[320,960]{1,0:T(8,128)S(1)} custom-call(s32[32]{0:T(128)S(1)} %dynamic-slice_bitcast_fusion.refs_0_, bf16[640,256]{1,0:T(8,128)(2,1)S(1)} %shard_map.93.refs_7_.refs_1_, bf16[640,256]{1,0:T(8,128)(2,1)S(1)} %shard_map.94.refs_2_, f32[1,384]{1,0:T(1,128)S(1)} %get-tuple-element.27.refs_5_.refs_3_, ...), custom_call_target="tpu_custom_call" | custom-call | flops 1000 | bytes 1000 | tf_op jit(solution)/shard_map/pallas_call | solution.py:87
  56.5 0.7 shard_map.97
  57.2 3.3 %collective-permute-start.12 = (bf16[80,960]{1,0:T(8,128)(2,1)S(1)}, bf16[80,960]{1,0:T(8,128)(2,1)S(1)}, u32[]{:S(2)}, u32[]{:S(2)}) collective-permute-start(bf16[80,960]{1,0:T(8,128)(2,1)S(1)} %get-tuple-element.34), channel_id=1, source_target_pairs={{0,32},{1,33},{2,34},{3,35},{4,36},{5,37},{6,38},{7,39},{8,40},{9,... | collective-permute-start | bytes 460808 | tf_op jit(solution)/shard_map/ppermute | solution.py:26
  60.4 0.7 collective-permute-start.13
  61.1 2.6 %collective-permute-start.14 = (bf16[80,960]{1,0:T(8,128)(2,1)S(1)}, bf16[80,960]{1,0:T(8,128)(2,1)S(1)}, u32[]{:S(2)}, u32[]{:S(2)}) collective-permute-start(bf16[80,960]{1,0:T(8,128)(2,1)S(1)} %get-tuple-element.36), channel_id=1, source_target_pairs={{0,48},{1,49},{2,50},{3,51},{4,52},{5,53},{6,54},{7,55},{8,56},{9,... | collective-permute-start | bytes 460808 | tf_op jit(solution)/shard_map/ppermute | solution.py:26
  63.8 2.0 %collective-permute-done.12.refs_1_ = bf16[80,960]{1,0:T(8,128)(2,1)S(1)} collective-permute-done((bf16[80,960]{1,0:T(8,128)(2,1)S(1)}, bf16[80,960]{1,0:T(8,128)(2,1)S(1)}, u32[]{:S(2)}, u32[]{:S(2)}) %collective-permute-start.12) | collective-permute-done | bytes 153632 | tf_op jit(solution)/shard_map/ppermute | solution.py:26
  65.8 2.9 %collective-permute-done.13.refs_2_ = bf16[80,960]{1,0:T(8,128)(2,1)S(1)} collective-permute-done((bf16[80,960]{1,0:T(8,128)(2,1)S(1)}, bf16[80,960]{1,0:T(8,128)(2,1)S(1)}, u32[]{:S(2)}, u32[]{:S(2)}) %collective-permute-start.13) | collective-permute-done | bytes 153632 | tf_op jit(solution)/shard_map/ppermute | solution.py:26
  68.7 0.3 collective-permute-done.14.refs_3_
  69.1 3.4 %collective-permute-start.15 = (bf16[80,960]{1,0:T(8,128)(2,1)S(1)}, bf16[80,960]{1,0:T(8,128)(2,1)S(1)}, u32[]{:S(2)}, u32[]{:S(2)}) collective-permute-start(bf16[80,960]{1,0:T(8,128)(2,1)S(1)} %get-tuple-element.37.refs_12_), channel_id=1, source_target_pairs={{0,128},{1,129},{2,130},{3,131},{4,132},{5,133},{6,134},{7,135},{8... | collective-permute-start | bytes 460808 | tf_op jit(solution)/shard_map/ppermute | solution.py:26
  72.5 4.1 %collective-permute-start.17 = (bf16[80,960]{1,0:T(8,128)(2,1)S(1)}, bf16[80,960]{1,0:T(8,128)(2,1)S(1)}, u32[]{:S(2)}, u32[]{:S(2)}) collective-permute-start(bf16[80,960]{1,0:T(8,128)(2,1)S(1)} %get-tuple-element.37.refs_12_), channel_id=1, source_target_pairs={{0,192},{1,193},{2,194},{3,195},{4,196},{5,197},{6,198},{7,199},{8... | collective-permute-start | bytes 460808 | tf_op jit(solution)/shard_map/ppermute | solution.py:26
  76.6 2.1 %slice_multiply_fusion.1.refs_11_ = bf16[1,320,5120]{2,1,0:T(8,128)(2,1)S(1)} fusion(bf16[3,320,5120]{2,1,0:T(8,128)(2,1)} %bitcast.40, bf16[5120]{0:T(1024)(128)(2,1)S(1)} %broadcast_bitcast_fusion.1), kind=kLoop, calls=%fused_computation.1 | loop fusion | flops 1638400 | bytes 6563840 | tf_op jit(solution)/shard_map/mul | solution.py:271
  78.8 3.0 %shard_map.99.refs_8_.refs_0_ = bf16[320,512]{1,0:T(8,128)(2,1)S(1)} custom-call(bf16[64,5120]{1,0:T(8,128)(2,1)S(1)} %copy-done.1, bf16[64,5120]{1,0:T(8,128)(2,1)S(1)} %collective-permute-done.refs_0_.refs_1_, bf16[64,5120]{1,0:T(8,128)(2,1)S(1)} %collective-permute-done.1.refs_1_.refs_2_, bf16[32,5120]{1,0:T(8,128)(2,1)S(1)} %collective-permute-done.4.refs_3_, ...), custom_call_target="tpu_custom_call" | custom-call | flops 1000 | bytes 1000 | tf_op jit(solution)/shard_map/pallas_call | solution.py:87
  81.8 0.6 collective-permute-done.15.refs_2_
  82.3 2.7 %collective-permute-done.16.refs_3_ = bf16[80,960]{1,0:T(8,128)(2,1)S(1)} collective-permute-done((bf16[80,960]{1,0:T(8,128)(2,1)S(1)}, bf16[80,960]{1,0:T(8,128)(2,1)S(1)}, u32[]{:S(2)}, u32[]{:S(2)}) %collective-permute-start.16) | collective-permute-done | bytes 153632 | tf_op jit(solution)/shard_map/ppermute | solution.py:26
  85.0 3.5 %collective-permute-done.17.refs_4_ = bf16[80,960]{1,0:T(8,128)(2,1)S(1)} collective-permute-done((bf16[80,960]{1,0:T(8,128)(2,1)S(1)}, bf16[80,960]{1,0:T(8,128)(2,1)S(1)}, u32[]{:S(2)}, u32[]{:S(2)}) %collective-permute-start.17) | collective-permute-done | bytes 153632 | tf_op jit(solution)/shard_map/ppermute | solution.py:26
  88.6 0.9 shard_map.100
  89.5 2.2 %collective-permute-start.18 = (bf16[80,960]{1,0:T(8,128)(2,1)S(1)}, bf16[80,960]{1,0:T(8,128)(2,1)S(1)}, u32[]{:S(2)}, u32[]{:S(2)}) collective-permute-start(bf16[80,960]{1,0:T(8,128)(2,1)S(1)} %shard_map.100), channel_id=1, source_target_pairs={{0,32},{1,33},{2,34},{3,35},{4,36},{5,37},{6,38},{7,39},{8,40},{9,... | collective-permute-start | bytes 460808 | tf_op jit(solution)/shard_map/ppermute | solution.py:26
  91.6 1.6 %collective-permute-start.19 = (bf16[80,960]{1,0:T(8,128)(2,1)S(1)}, bf16[80,960]{1,0:T(8,128)(2,1)S(1)}, u32[]{:S(2)}, u32[]{:S(2)}) collective-permute-start(bf16[80,960]{1,0:T(8,128)(2,1)S(1)} %shard_map.100), channel_id=1, source_target_pairs={{0,16},{1,17},{2,18},{3,19},{4,20},{5,21},{6,22},{7,23},{8,24},{9,... | collective-permute-start | bytes 460808 | tf_op jit(solution)/shard_map/ppermute | solution.py:26
  93.2 1.6 %collective-permute-start.20 = (bf16[80,960]{1,0:T(8,128)(2,1)S(1)}, bf16[80,960]{1,0:T(8,128)(2,1)S(1)}, u32[]{:S(2)}, u32[]{:S(2)}) collective-permute-start(bf16[80,960]{1,0:T(8,128)(2,1)S(1)} %shard_map.100), channel_id=1, source_target_pairs={{0,48},{1,49},{2,50},{3,51},{4,52},{5,53},{6,54},{7,55},{8,56},{9,... | collective-permute-start | bytes 460808 | tf_op jit(solution)/shard_map/ppermute | solution.py:26
  94.9 3.3 %collective-permute-done.18 = bf16[80,960]{1,0:T(8,128)(2,1)S(1)} collective-permute-done((bf16[80,960]{1,0:T(8,128)(2,1)S(1)}, bf16[80,960]{1,0:T(8,128)(2,1)S(1)}, u32[]{:S(2)}, u32[]{:S(2)}) %collective-permute-start.18) | collective-permute-done | bytes 153632 | tf_op jit(solution)/shard_map/ppermute | solution.py:26
  98.1 2.6 %collective-permute-done.19 = bf16[80,960]{1,0:T(8,128)(2,1)S(1)} collective-permute-done((bf16[80,960]{1,0:T(8,128)(2,1)S(1)}, bf16[80,960]{1,0:T(8,128)(2,1)S(1)}, u32[]{:S(2)}, u32[]{:S(2)}) %collective-permute-start.19) | collective-permute-done | bytes 153632 | tf_op jit(solution)/shard_map/ppermute | solution.py:26
  101.0 2.1 %collective-permute-done.21.refs_2_ = bf16[320,960]{1,0:T(8,128)(2,1)S(1)} collective-permute-done((bf16[320,960]{1,0:T(8,128)(2,1)S(1)}, bf16[320,960]{1,0:T(8,128)(2,1)S(1)}, u32[]{:S(2)}, u32[]{:S(2)}) %collective-permute-start.21) | collective-permute-done | bytes 614432 | tf_op jit(solution)/shard_map/ppermute | solution.py:26
  103.1 0.9 shard_map.101
  104.0 0.8 collective-permute-start.22
  104.8 0.6 collective-permute-start.23
  105.4 0.9 shard_map.102.refs_0_
  106.3 2.6 %collective-permute-done.22.refs_1_ = bf16[128,320]{1,0:T(8,128)(2,1)S(1)} collective-permute-done((bf16[128,320]{1,0:T(8,128)(2,1)S(1)}, bf16[128,320]{1,0:T(8,128)(2,1)S(1)}, u32[]{:S(2)}, u32[]{:S(2)}) %collective-permute-start.22) | collective-permute-done | bytes 81952 | tf_op jit(solution)/shard_map/ppermute | solution.py:26
  108.9 1.7 %collective-permute-done.23.refs_2_ = bf16[128,320]{1,0:T(8,128)(2,1)S(1)} collective-permute-done((bf16[128,320]{1,0:T(8,128)(2,1)S(1)}, bf16[128,320]{1,0:T(8,128)(2,1)S(1)}, u32[]{:S(2)}, u32[]{:S(2)}) %collective-permute-start.23) | collective-permute-done | bytes 81952 | tf_op jit(solution)/shard_map/ppermute | solution.py:26
  110.6 1.8 %collective-permute-start.24 = (bf16[2,64,320]{2,1,0:T(8,128)(2,1)S(1)}, bf16[2,64,320]{2,1,0:T(8,128)(2,1)S(1)}, u32[]{:S(2)}, u32[]{:S(2)}) collective-permute-start(bf16[2,64,320]{2,1,0:T(8,128)(2,1)S(1)} %get-tuple-element.42), channel_id=1, source_target_pairs={{0,1},{1,0},{2,3},{3,2},{4,5},{5,4},{6,7},{7,6},{8,9},{9,8},{10,11... | collective-permute-start | bytes 245768 | tf_op jit(solution)/shard_map/ppermute | solution.py:26
  112.5 0.6 collective-permute-start.25
  113.1 1.8 %collective-permute-start.26 = (bf16[2,64,320]{2,1,0:T(8,128)(2,1)S(1)}, bf16[2,64,320]{2,1,0:T(8,128)(2,1)S(1)}, u32[]{:S(2)}, u32[]{:S(2)}) collective-permute-start(bf16[2,64,320]{2,1,0:T(8,128)(2,1)S(1)} %get-tuple-element.44), channel_id=1, source_target_pairs={{0,2},{1,3},{2,0},{3,1},{4,6},{5,7},{6,4},{7,5},{8,10},{9,11},{10,... | collective-permute-start | bytes 245768 | tf_op jit(solution)/shard_map/ppermute | solution.py:26
  114.8 0.6 collective-permute-done.24.refs_2_
  115.4 2.4 %collective-permute-done.25.refs_3_ = bf16[2,64,320]{2,1,0:T(8,128)(2,1)S(1)} collective-permute-done((bf16[2,64,320]{2,1,0:T(8,128)(2,1)S(1)}, bf16[2,64,320]{2,1,0:T(8,128)(2,1)S(1)}, u32[]{:S(2)}, u32[]{:S(2)}) %collective-permute-start.25) | collective-permute-done | bytes 81952 | tf_op jit(solution)/shard_map/ppermute | solution.py:26
  117.8 1.3 %collective-permute-done.26.refs_4_ = bf16[2,64,320]{2,1,0:T(8,128)(2,1)S(1)} collective-permute-done((bf16[2,64,320]{2,1,0:T(8,128)(2,1)S(1)}, bf16[2,64,320]{2,1,0:T(8,128)(2,1)S(1)}, u32[]{:S(2)}, u32[]{:S(2)}) %collective-permute-start.26) | collective-permute-done | bytes 81952 | tf_op jit(solution)/shard_map/ppermute | solution.py:26
  119.2 1.4 %shard_map.104 = bf16[64,2560]{1,0:T(8,128)(2,1)} custom-call(s32[32]{0:T(128)S(1)} %dynamic-slice_bitcast_fusion.refs_0_, bf16[2,64,320]{2,1,0:T(8,128)(2,1)S(1)} %get-tuple-element.41.refs_1_, bf16[2,64,320]{2,1,0:T(8,128)(2,1)S(1)} %collective-permute-done.24.refs_2_, bf16[2,64,320]{2,1,0:T(8,128)(2,1)S(1)} %collective-permute-done.25.refs_3_, ...), custom_call_target="tpu_custom_call" | custom-call | flops 1000 | bytes 1000 | tf_op jit(solution)/shard_map/pallas_call | solution.py:87
  (33 shorter events, 1.2 us)
Async XLA Ops:
  0.7 23.4 %collective-permute-start = (bf16[64,5120]{1,0:T(8,128)(2,1)}, bf16[64,5120]{1,0:T(8,128)(2,1)S(1)}, u32[]{:S(2)}, u32[]{:S(2)}) collective-permute-start(bf16[64,5120]{1,0:T(8,128)(2,1)} %refs_0_.1), channel_id=1, source_target_pairs={{0,1},{1,0},{2,3},{3,2},{4,5},{5,4},{6,7},{7,6},{8,9},{9,8},{10,11... | collective-permute-start | bytes 1966088 | tf_op jit(solution)/shard_map/ppermute | solution.py:26
  3.0 21.2 %collective-permute-start.1 = (bf16[64,5120]{1,0:T(8,128)(2,1)}, bf16[64,5120]{1,0:T(8,128)(2,1)S(1)}, u32[]{:S(2)}, u32[]{:S(2)}) collective-permute-start(bf16[64,5120]{1,0:T(8,128)(2,1)} %refs_0_.1), channel_id=1, source_target_pairs={{0,3},{1,2},{2,1},{3,0},{4,7},{5,6},{6,5},{7,4},{8,11},{9,10},{10,... | collective-permute-start | bytes 1966088 | tf_op jit(solution)/shard_map/ppermute | solution.py:26
  5.3 18.8 %collective-permute-start.2 = (bf16[32,5120]{1,0:T(8,128)(2,1)}, bf16[32,5120]{1,0:T(8,128)(2,1)}, u32[]{:S(2)}, u32[]{:S(2)}) collective-permute-start(bf16[32,5120]{1,0:T(8,128)(2,1)} %get-tuple-element.46), channel_id=1, source_target_pairs={{0,4},{1,5},{2,6},{3,7},{4,0},{5,1},{6,2},{7,3},{8,12},{9,13},{10,... | collective-permute-start | bytes 983048 | tf_op jit(solution)/shard_map/ppermute | solution.py:26
  7.2 16.9 %collective-permute-start.3 = (bf16[32,5120]{1,0:T(8,128)(2,1)}, bf16[32,5120]{1,0:T(8,128)(2,1)}, u32[]{:S(2)}, u32[]{:S(2)}) collective-permute-start(bf16[32,5120]{1,0:T(8,128)(2,1)} %get-tuple-element.45), channel_id=1, source_target_pairs={{0,196},{1,197},{2,198},{3,199},{4,64},{5,65},{6,66},{7,67},{8,204... | collective-permute-start | bytes 983048 | tf_op jit(solution)/shard_map/ppermute | solution.py:26
  13.0 6.7 %copy-start.4 = (s32[512,1]{0,1:T(1,128)S(1)}, s32[512,1]{0,1:T(1,128)}, u32[]{:S(2)}) copy-start(s32[512,1]{0,1:T(1,128)} %param.12) | copy-start | bytes 6148
  13.0 8.6 %copy-start.2 = (bf16[1,320,640]{2,1,0:T(8,128)(2,1)S(1)}, bf16[1,320,640]{2,1,0:T(8,128)(2,1)}, u32[]{:S(2)}) copy-start(bf16[1,320,640]{2,1,0:T(8,128)(2,1)} %param.14) | copy-start | bytes 1228804
  13.0 8.9 %copy-start.3 = (bf16[1,320,640]{2,1,0:T(8,128)(2,1)S(1)}, bf16[1,320,640]{2,1,0:T(8,128)(2,1)}, u32[]{:S(2)}) copy-start(bf16[1,320,640]{2,1,0:T(8,128)(2,1)} %param.15) | copy-start | bytes 1228804
  19.2 25.3 %copy-start.1 = (bf16[64,5120]{1,0:T(8,128)(2,1)S(1)}, bf16[64,5120]{1,0:T(8,128)(2,1)}, u32[]{:S(2)}) copy-start(bf16[64,5120]{1,0:T(8,128)(2,1)} %refs_0_.1) | copy-start | bytes 1966084
  25.4 17.8 %collective-permute-start.6 = (bf16[64,5120]{1,0:T(8,128)(2,1)S(1)}, bf16[64,5120]{1,0:T(8,128)(2,1)S(1)}, u32[]{:S(2)}, u32[]{:S(2)}) collective-permute-start(bf16[64,5120]{1,0:T(8,128)(2,1)S(1)} %get-tuple-element.30), channel_id=1, source_target_pairs={{0,4},{1,5},{2,6},{3,7},{4,0},{5,1},{6,2},{7,3},{8,12},{9,13},{10,... | collective-permute-start | bytes 1966088 | tf_op jit(solution)/shard_map/ppermute | solution.py:26
  25.5 19.0 %collective-permute-start.8 = (bf16[64,5120]{1,0:T(8,128)(2,1)S(1)}, bf16[64,5120]{1,0:T(8,128)(2,1)S(1)}, u32[]{:S(2)}, u32[]{:S(2)}) collective-permute-start(bf16[64,5120]{1,0:T(8,128)(2,1)S(1)} %get-tuple-element.31), channel_id=1, source_target_pairs={{0,196},{1,197},{2,198},{3,199},{4,64},{5,65},{6,66},{7,67},{8,204... | collective-permute-start | bytes 1966088 | tf_op jit(solution)/shard_map/ppermute | solution.py:26
  27.5 7.8 %collective-permute-start.4 = (bf16[32,5120]{1,0:T(8,128)(2,1)S(1)}, bf16[32,5120]{1,0:T(8,128)(2,1)S(1)}, u32[]{:S(2)}, u32[]{:S(2)}) collective-permute-start(bf16[32,5120]{1,0:T(8,128)(2,1)S(1)} %get-tuple-element.28), channel_id=1, source_target_pairs={{0,3},{1,2},{2,1},{3,0},{4,7},{5,6},{6,5},{7,4},{8,11},{9,10},{10,... | collective-permute-start | bytes 983048 | tf_op jit(solution)/shard_map/ppermute | solution.py:26
  27.9 8.3 %collective-permute-start.5 = (bf16[32,5120]{1,0:T(8,128)(2,1)S(1)}, bf16[32,5120]{1,0:T(8,128)(2,1)S(1)}, u32[]{:S(2)}, u32[]{:S(2)}) collective-permute-start(bf16[32,5120]{1,0:T(8,128)(2,1)S(1)} %get-tuple-element.29), channel_id=1, source_target_pairs={{0,1},{1,0},{2,3},{3,2},{4,5},{5,4},{6,7},{7,6},{8,9},{9,8},{10,11... | collective-permute-start | bytes 983048 | tf_op jit(solution)/shard_map/ppermute | solution.py:26
  35.2 14.0 %collective-permute-start.7 = (bf16[32,5120]{1,0:T(8,128)(2,1)S(1)}, bf16[32,5120]{1,0:T(8,128)(2,1)S(1)}, u32[]{:S(2)}, u32[]{:S(2)}) collective-permute-start(bf16[32,5120]{1,0:T(8,128)(2,1)S(1)} %collective-permute-done.4.refs_3_), channel_id=1, source_target_pairs={{0,4},{1,5},{2,6},{3,7},{4,0},{5,1},{6,2},{7,3},{8,12},{9,13},{10,... | collective-permute-start | bytes 983048 | tf_op jit(solution)/shard_map/ppermute | solution.py:26
  36.3 13.0 %collective-permute-start.9 = (bf16[32,5120]{1,0:T(8,128)(2,1)S(1)}, bf16[32,5120]{1,0:T(8,128)(2,1)S(1)}, u32[]{:S(2)}, u32[]{:S(2)}) collective-permute-start(bf16[32,5120]{1,0:T(8,128)(2,1)S(1)} %collective-permute-done.5.refs_4_), channel_id=1, source_target_pairs={{0,196},{1,197},{2,198},{3,199},{4,64},{5,65},{6,66},{7,67},{8,204... | collective-permute-start | bytes 983048 | tf_op jit(solution)/shard_map/ppermute | solution.py:26
  37.4 14.8 %collective-permute-start.10 = (f32[1,128]{1,0:T(1,128)S(1)}, f32[1,128]{1,0:T(1,128)S(1)}, u32[]{:S(2)}, u32[]{:S(2)}) collective-permute-start(f32[1,128]{1,0:T(1,128)S(1)} %get-tuple-element.32), channel_id=1, source_target_pairs={{0,64},{1,65},{2,66},{3,67},{4,196},{5,197},{6,198},{7,199},{8,72}... | collective-permute-start | bytes 1544 | tf_op jit(solution)/shard_map/ppermute | solution.py:26
  44.4 2.9 %copy-start = (bf16[2,320,5120]{2,1,0:T(8,128)(2,1)S(1)}, bf16[2,320,5120]{2,1,0:T(8,128)(2,1)}, u32[]{:S(2)}) copy-start(bf16[2,320,5120]{2,1,0:T(8,128)(2,1)} %slice_multiply_fusion.refs_5_.refs_6_) | copy-start | bytes 19660804
  54.1 2.4 %collective-permute-start.11 = (bf16[320,960]{1,0:T(8,128)(2,1)S(1)}, bf16[320,960]{1,0:T(8,128)(2,1)S(1)}, u32[]{:S(2)}, u32[]{:S(2)}) collective-permute-start(bf16[320,960]{1,0:T(8,128)(2,1)S(1)} %shard_map.95.refs_8_), channel_id=1, source_target_pairs={{0,8},{1,9},{2,10},{3,11},{4,12},{5,13},{6,14},{7,15},{8,0},{9,1},... | collective-permute-start | bytes 1843208 | tf_op jit(solution)/shard_map/ppermute | solution.py:26
  57.2 8.6 %collective-permute-start.12 = (bf16[80,960]{1,0:T(8,128)(2,1)S(1)}, bf16[80,960]{1,0:T(8,128)(2,1)S(1)}, u32[]{:S(2)}, u32[]{:S(2)}) collective-permute-start(bf16[80,960]{1,0:T(8,128)(2,1)S(1)} %get-tuple-element.34), channel_id=1, source_target_pairs={{0,32},{1,33},{2,34},{3,35},{4,36},{5,37},{6,38},{7,39},{8,40},{9,... | collective-permute-start | bytes 460808 | tf_op jit(solution)/shard_map/ppermute | solution.py:26
  60.4 8.3 %collective-permute-start.13 = (bf16[80,960]{1,0:T(8,128)(2,1)S(1)}, bf16[80,960]{1,0:T(8,128)(2,1)S(1)}, u32[]{:S(2)}, u32[]{:S(2)}) collective-permute-start(bf16[80,960]{1,0:T(8,128)(2,1)S(1)} %get-tuple-element.35), channel_id=1, source_target_pairs={{0,16},{1,17},{2,18},{3,19},{4,20},{5,21},{6,22},{7,23},{8,24},{9,... | collective-permute-start | bytes 460808 | tf_op jit(solution)/shard_map/ppermute | solution.py:26
  61.1 7.9 %collective-permute-start.14 = (bf16[80,960]{1,0:T(8,128)(2,1)S(1)}, bf16[80,960]{1,0:T(8,128)(2,1)S(1)}, u32[]{:S(2)}, u32[]{:S(2)}) collective-permute-start(bf16[80,960]{1,0:T(8,128)(2,1)S(1)} %get-tuple-element.36), channel_id=1, source_target_pairs={{0,48},{1,49},{2,50},{3,51},{4,52},{5,53},{6,54},{7,55},{8,56},{9,... | collective-permute-start | bytes 460808 | tf_op jit(solution)/shard_map/ppermute | solution.py:26
  69.1 13.2 %collective-permute-start.15 = (bf16[80,960]{1,0:T(8,128)(2,1)S(1)}, bf16[80,960]{1,0:T(8,128)(2,1)S(1)}, u32[]{:S(2)}, u32[]{:S(2)}) collective-permute-start(bf16[80,960]{1,0:T(8,128)(2,1)S(1)} %get-tuple-element.37.refs_12_), channel_id=1, source_target_pairs={{0,128},{1,129},{2,130},{3,131},{4,132},{5,133},{6,134},{7,135},{8... | collective-permute-start | bytes 460808 | tf_op jit(solution)/shard_map/ppermute | solution.py:26
  72.5 12.5 %collective-permute-start.16 = (bf16[80,960]{1,0:T(8,128)(2,1)S(1)}, bf16[80,960]{1,0:T(8,128)(2,1)S(1)}, u32[]{:S(2)}, u32[]{:S(2)}) collective-permute-start(bf16[80,960]{1,0:T(8,128)(2,1)S(1)} %get-tuple-element.37.refs_12_), channel_id=1, source_target_pairs={{0,64},{1,65},{2,66},{3,67},{4,68},{5,69},{6,70},{7,71},{8,72},{9,... | collective-permute-start | bytes 460808 | tf_op jit(solution)/shard_map/ppermute | solution.py:26
  72.5 16.1 %collective-permute-start.17 = (bf16[80,960]{1,0:T(8,128)(2,1)S(1)}, bf16[80,960]{1,0:T(8,128)(2,1)S(1)}, u32[]{:S(2)}, u32[]{:S(2)}) collective-permute-start(bf16[80,960]{1,0:T(8,128)(2,1)S(1)} %get-tuple-element.37.refs_12_), channel_id=1, source_target_pairs={{0,192},{1,193},{2,194},{3,195},{4,196},{5,197},{6,198},{7,199},{8... | collective-permute-start | bytes 460808 | tf_op jit(solution)/shard_map/ppermute | solution.py:26
  89.5 8.7 %collective-permute-start.18 = (bf16[80,960]{1,0:T(8,128)(2,1)S(1)}, bf16[80,960]{1,0:T(8,128)(2,1)S(1)}, u32[]{:S(2)}, u32[]{:S(2)}) collective-permute-start(bf16[80,960]{1,0:T(8,128)(2,1)S(1)} %shard_map.100), channel_id=1, source_target_pairs={{0,32},{1,33},{2,34},{3,35},{4,36},{5,37},{6,38},{7,39},{8,40},{9,... | collective-permute-start | bytes 460808 | tf_op jit(solution)/shard_map/ppermute | solution.py:26
  91.6 9.1 %collective-permute-start.19 = (bf16[80,960]{1,0:T(8,128)(2,1)S(1)}, bf16[80,960]{1,0:T(8,128)(2,1)S(1)}, u32[]{:S(2)}, u32[]{:S(2)}) collective-permute-start(bf16[80,960]{1,0:T(8,128)(2,1)S(1)} %shard_map.100), channel_id=1, source_target_pairs={{0,16},{1,17},{2,18},{3,19},{4,20},{5,21},{6,22},{7,23},{8,24},{9,... | collective-permute-start | bytes 460808 | tf_op jit(solution)/shard_map/ppermute | solution.py:26
  93.2 7.6 %collective-permute-start.20 = (bf16[80,960]{1,0:T(8,128)(2,1)S(1)}, bf16[80,960]{1,0:T(8,128)(2,1)S(1)}, u32[]{:S(2)}, u32[]{:S(2)}) collective-permute-start(bf16[80,960]{1,0:T(8,128)(2,1)S(1)} %shard_map.100), channel_id=1, source_target_pairs={{0,48},{1,49},{2,50},{3,51},{4,52},{5,53},{6,54},{7,55},{8,56},{9,... | collective-permute-start | bytes 460808 | tf_op jit(solution)/shard_map/ppermute | solution.py:26
  100.9 2.2 %collective-permute-start.21 = (bf16[320,960]{1,0:T(8,128)(2,1)S(1)}, bf16[320,960]{1,0:T(8,128)(2,1)S(1)}, u32[]{:S(2)}, u32[]{:S(2)}) collective-permute-start(bf16[320,960]{1,0:T(8,128)(2,1)S(1)} %pad_maximum_fusion.refs_1_), channel_id=1, source_target_pairs={{0,8},{1,9},{2,10},{3,11},{4,12},{5,13},{6,14},{7,15},{8,0},{9,1},... | collective-permute-start | bytes 1843208 | tf_op jit(solution)/shard_map/ppermute | solution.py:26
  104.0 4.9 %collective-permute-start.22 = (bf16[128,320]{1,0:T(8,128)(2,1)S(1)}, bf16[128,320]{1,0:T(8,128)(2,1)S(1)}, u32[]{:S(2)}, u32[]{:S(2)}) collective-permute-start(bf16[128,320]{1,0:T(8,128)(2,1)S(1)} %get-tuple-element.39.refs_3_), channel_id=1, source_target_pairs={{0,4},{1,5},{2,6},{3,7},{4,0},{5,1},{6,2},{7,3},{8,12},{9,13},{10,... | collective-permute-start | bytes 245768 | tf_op jit(solution)/shard_map/ppermute | solution.py:26
  104.8 5.8 %collective-permute-start.23 = (bf16[128,320]{1,0:T(8,128)(2,1)S(1)}, bf16[128,320]{1,0:T(8,128)(2,1)S(1)}, u32[]{:S(2)}, u32[]{:S(2)}) collective-permute-start(bf16[128,320]{1,0:T(8,128)(2,1)S(1)} %get-tuple-element.40), channel_id=1, source_target_pairs={{0,196},{1,197},{2,198},{3,199},{4,64},{5,65},{6,66},{7,67},{8,204... | collective-permute-start | bytes 245768 | tf_op jit(solution)/shard_map/ppermute | solution.py:26
  110.6 4.8 %collective-permute-start.24 = (bf16[2,64,320]{2,1,0:T(8,128)(2,1)S(1)}, bf16[2,64,320]{2,1,0:T(8,128)(2,1)S(1)}, u32[]{:S(2)}, u32[]{:S(2)}) collective-permute-start(bf16[2,64,320]{2,1,0:T(8,128)(2,1)S(1)} %get-tuple-element.42), channel_id=1, source_target_pairs={{0,1},{1,0},{2,3},{3,2},{4,5},{5,4},{6,7},{7,6},{8,9},{9,8},{10,11... | collective-permute-start | bytes 245768 | tf_op jit(solution)/shard_map/ppermute | solution.py:26
  112.5 5.4 %collective-permute-start.25 = (bf16[2,64,320]{2,1,0:T(8,128)(2,1)S(1)}, bf16[2,64,320]{2,1,0:T(8,128)(2,1)S(1)}, u32[]{:S(2)}, u32[]{:S(2)}) collective-permute-start(bf16[2,64,320]{2,1,0:T(8,128)(2,1)S(1)} %get-tuple-element.43), channel_id=1, source_target_pairs={{0,3},{1,2},{2,1},{3,0},{4,7},{5,6},{6,5},{7,4},{8,11},{9,10},{10,... | collective-permute-start | bytes 245768 | tf_op jit(solution)/shard_map/ppermute | solution.py:26
  113.1 6.1 %collective-permute-start.26 = (bf16[2,64,320]{2,1,0:T(8,128)(2,1)S(1)}, bf16[2,64,320]{2,1,0:T(8,128)(2,1)S(1)}, u32[]{:S(2)}, u32[]{:S(2)}) collective-permute-start(bf16[2,64,320]{2,1,0:T(8,128)(2,1)S(1)} %get-tuple-element.44), channel_id=1, source_target_pairs={{0,2},{1,3},{2,0},{3,1},{4,6},{5,7},{6,4},{7,5},{8,10},{9,11},{10,... | collective-permute-start | bytes 245768 | tf_op jit(solution)/shard_map/ppermute | solution.py:26

commit v6 on v5

--- a/solution.py
+++ b/solution.py
@@ -69,7 +69,7 @@
 VMEM = pl.BlockSpec(memory_space=pltpu.VMEM)
 SMEM = pl.BlockSpec(memory_space=pltpu.SMEM)
 SMALL = pl.CostEstimate(flops=1000, bytes_accessed=1000, transcendentals=0)
-PARAMS = pltpu.CompilerParams(vmem_limit_bytes=14 * 1024 * 1024)
+PARAMS = pltpu.CompilerParams(vmem_limit_bytes=20 * 1024 * 1024)
 BY_ROW = (((1,), (1,)), ((), ()))
 BY_TOKEN = (((0,), (0,)), ((), ()))
 
@@ -95,28 +95,30 @@
     )(*args, *after)
 
 
-def split_kernel(near_tile, far_tile, near_first, far_second, first, second):
+def split_kernel(near_tile, far_tile, z1, z2, near_first, far_second, first, second, both):
     near_first[...] = near_tile[:32, :]
     far_second[...] = far_tile[32:, :]
-    first[:32, :] = near_tile[:32, :]
-    first[32:, :] = far_tile[:32, :]
-    second[:32, :] = near_tile[32:, :]
-    second[32:, :] = far_tile[32:, :]
-
-
-def project_kernel(n_tiles, *refs):
-    tile = jnp.concatenate([t[...] for t in refs[:n_tiles]], axis=0)
-    w_ref, out = refs[n_tiles:]
-    for c in range(w_ref.shape[0]):
-        part = lax.dot_general(w_ref[c], tile, BY_ROW, preferred_element_type=F32)
+    first[:16, :] = near_tile[16:32, :]
+    first[16:, :] = far_tile[16:32, :]
+    second[:16, :] = near_tile[48:, :]
+    second[16:, :] = far_tile[48:, :]
+    both[:16, :] = z1[:16, :]
+    both[16:, :] = z2[:16, :]
+
+
+def project_kernel(cuts, first, count, *refs):
+    tiles, (w_ref, f_ref, out) = refs[:-3], refs[-3:]
+    tile = jnp.concatenate([tiles[i][lo:hi, :] for i, lo, hi in cuts], axis=0)
+    for c in range(count):
+        weff = w_ref[first + c] * f_ref[first + c]
+        part = lax.dot_general(weff, tile, BY_ROW, preferred_element_type=F32)
         out[c * 320 : (c + 1) * 320, :] = part.astype(BF16)
 
 
-def project(tiles, weff, after=()):
-    shape = (weff.shape[0] * weff.shape[1], sum(t.shape[0] for t in tiles))
-    return call(
-        functools.partial(project_kernel, len(tiles)), like(shape), *tiles, weff, after=after
-    )
+def project(tiles, cuts, w_t, factor, first, count, after=()):
+    shape = (count * w_t.shape[1], sum(hi - lo for _, lo, hi in cuts))
+    kernel = functools.partial(project_kernel, cuts, first, count)
+    return call(kernel, like(shape), *tiles, w_t, factor, after=after)
 
 
 def grads_kernel(which, my, kv1, kv2, weight, moved, gate_t, up_t, down_t, out):
@@ -178,22 +180,24 @@
         at += out.shape[0]
 
 
+PLANE = [(0, 0, 64), (1, 0, 64), (2, 0, 64), (3, 0, 32), (4, 0, 32)]
+OTHERS = [(0, 0, 32), (2, 0, 16), (4, 0, 16), (3, 0, 16), (4, 16, 32), (6, 0, 32)]
+OTHERS += [(1, 0, 32), (2, 16, 32), (5, 0, 16), (3, 16, 32), (5, 16, 32), (7, 0, 32)]
+
+
 def gather(tokens, work):
     near_tile, far_tile = to_near_x(tokens), to_far_x(tokens)
     z1, z2 = to_near_z(tokens[:32]), to_far_z(tokens[32:])
-    near_first, far_second, first, second = call(
-        split_kernel,
-        [like((32, 5120)), like((32, 5120)), like((64, 5120)), like((64, 5120))],
-        near_tile,
-        far_tile,
-        after=(z1, z2, *work),
+    near_first, far_second, first, second, both = call(
+        split_kernel, [like((32, 5120))] * 5, near_tile, far_tile, z1, z2, after=work
     )
     opposite_first, opposite_second = to_far_x(near_first), to_near_x(far_second)
     z3, z4 = to_near_z(first), to_far_z(second)
+    near_both, far_both = to_near_x(both), to_far_x(both)
     z5, z6 = to_near_z(opposite_first), to_far_z(opposite_second)
     return (
         [tokens, near_tile, far_tile, opposite_first, opposite_second],
-        [z1, z3, z5, z2, z4, z6],
+        [z1, z2, near_both, far_both, z3, z4, z5, z6],
     )
 
 
@@ -268,10 +272,9 @@
     )
     moved = permute(sent, lambda h, y, c, l, x: (h - 1 if l else h + 1, y, c, l, x))
     old_t = [w[0].T for w in (fast_gate, fast_up, fast_down)]
-    weff_kv, weff_q = w_t[1:] * factor[1:], w_t[:1] * factor[:1]
-    plane, others = gather(tokens, (weff_kv[0, :8, :128], weight, *old_t))
-    kv1 = project(plane, weff_kv, after=(others[1], others[4]))
-    kv2 = project(others, weff_kv, after=(kv1,))
+    plane, others = gather(tokens, (factor, weight, *old_t))
+    kv1 = project(plane, PLANE, w_t, factor, 1, 2, after=others[2:6])
+    kv2 = project(others, OTHERS, w_t, factor, 1, 2, after=(kv1,))
 
     grads = (my, kv1, kv2, weight, moved, *old_t)
     sent = call(
@@ -292,7 +295,8 @@
     mine, small = call(sum_kernel, [like((80, 960), F32), like((80, 960))], mine, *got)
 
     got = to_z(small, 2), to_z(small, 1), to_z(small, 3)
-    query = project(plane + others, weff_q, after=(small,))
+    cuts = PLANE + [(len(plane) + i, lo, hi) for i, lo, hi in OTHERS]
+    query = project(plane + others, cuts, w_t, factor, 0, 1, after=(small,))
     block = call(
         renorm_kernel,
         like((80, 960)),

time: 122 us -> 121 us (level); the launches traced: 121 us -> 121 us
  starting transfers between devices: 43.6 us -> 59 us
  other arithmetic: 9.6 us -> 0.64 us
  waiting for transfers between devices: 39.4 us -> 34.3 us
  Pallas kernels: 18.4 us -> 15.1 us
  local copies, waits for them, and re-layouts: 8.77 us -> 10.9 us
    ppermute x27 -> x29, starting transfers between devices: 43.6 us -> 59 us  [permute(): return lax.ppermute(value, AXES, pairs)]
    mul x2 -> x0, other arithmetic: 8.27 us -> none  [body(): weff_kv, weff_q = (w_t[1:] * factor[1:], w_t[:1] * factor[:1])]
    ppermute x27 -> x29, waiting for transfers between devices: 39.4 us -> 34.3 us  [permute(): return lax.ppermute(value, AXES, pairs)]
    pallas_call x14, Pallas kernels: 18.4 us -> 15.1 us  [call(): pl.pallas_call(run, out_shape=out_shape, in_specs=[SMEM] * scalars + [VME...]
    unnamed x17 -> x19, local copies, waits for them, and re-layouts: 5.29 us -> 7.96 us
  transfers between devices with their start and end apart: 27 -> 29, of which waited for: 19 -> 16; matrix products, arithmetic and copies ran while one was open for 12% -> 4% of each run, Pallas kernels for 9% -> 8%
where the time goes in v6:
time: 121 us
  starting transfers between devices  59 us (49%)
  waiting for transfers between devices  34.3 us (28%)
  Pallas kernels  15.1 us (12%)
  local copies, waits for them, and re-layouts  10.9 us (9%)
    ppermute x29, starting transfers between devices, permute(): return lax.ppermute(value, AXES, pairs)  59 us
    ppermute x29, waiting for transfers between devices, permute(): return lax.ppermute(value, AXES, pairs)  34.3 us
    pallas_call x14, Pallas kernels, call(): pl.pallas_call(run, out_shape=out_shape, in_specs=[SMEM] * scalars + [VME...  15.1 us
    unnamed x19, local copies, waits for them, and re-layouts  7.96 us
  transfers between devices with their start and end apart: 29, of which 16 were waited for; matrix products, arithmetic and copies ran while one was open for 4% of the time, Pallas kernels for 8%

profile of v6, /device:TPU:2, one launch (start us, length us, event | category | flops | bytes accessed | tf_op | source)
XLA Modules:
  0.0 120.9 jit_solution(9825229270782796326)
XLA Ops:
  0.0 0.8 dynamic-slice_bitcast_fusion.refs_0_
  0.8 1.5 %collective-permute-start.1 = (bf16[64,5120]{1,0:T(8,128)(2,1)}, bf16[64,5120]{1,0:T(8,128)(2,1)S(1)}, u32[]{:S(2)}, u32[]{:S(2)}) collective-permute-start(bf16[64,5120]{1,0:T(8,128)(2,1)} %refs_0_.1), channel_id=1, source_target_pairs={{0,3},{1,2},{2,1},{3,0},{4,7},{5,6},{6,5},{7,4},{8,11},{9,10},{10,... | collective-permute-start | bytes 1966088 | tf_op jit(solution)/shard_map/ppermute | solution.py:26
  2.3 1.8 %collective-permute-start = (bf16[64,5120]{1,0:T(8,128)(2,1)}, bf16[64,5120]{1,0:T(8,128)(2,1)S(1)}, u32[]{:S(2)}, u32[]{:S(2)}) collective-permute-start(bf16[64,5120]{1,0:T(8,128)(2,1)} %refs_0_.1), channel_id=1, source_target_pairs={{0,1},{1,0},{2,3},{3,2},{4,5},{5,4},{6,7},{7,6},{8,9},{9,8},{10,11... | collective-permute-start | bytes 1966088 | tf_op jit(solution)/shard_map/ppermute | solution.py:26
  4.1 1.9 %fusion = (bf16[32,5120]{1,0:T(8,128)(2,1)}, bf16[32,5120]{1,0:T(8,128)(2,1)}) fusion(bf16[64,5120]{1,0:T(8,128)(2,1)} %refs_0_.1), kind=kLoop, calls=%fused_computation.4 | loop fusion | bytes 1310720 | tf_op jit(solution)/shard_map/slice | solution.py:190
  6.0 5.9 %collective-permute-start.3 = (bf16[32,5120]{1,0:T(8,128)(2,1)}, bf16[32,5120]{1,0:T(8,128)(2,1)S(1)}, u32[]{:S(2)}, u32[]{:S(2)}) collective-permute-start(bf16[32,5120]{1,0:T(8,128)(2,1)} %get-tuple-element.47), channel_id=1, source_target_pairs={{0,196},{1,197},{2,198},{3,199},{4,64},{5,65},{6,66},{7,67},{8,204... | collective-permute-start | bytes 983048 | tf_op jit(solution)/shard_map/ppermute | solution.py:26
  12.6 0.5 broadcast.3
  13.0 0.6 reduce.3
  13.6 0.1 reshape.7.refs_2_
  13.7 0.6 shard_map.91
  14.3 0.1 broadcast_in_dim.3
  14.5 0.3 copy.13
  14.7 0.3 copy.14
  15.0 1.3 %copy.15 = bf16[1,320,640]{1,2,0:T(8,128)(2,1)S(1)} copy(bf16[1,320,640]{2,1,0:T(8,128)(2,1)} %param.16) | data formatting | bytes 819200 | tf_op args[7]
  16.3 3.0 %collective-permute-done.3.refs_3_.refs_1_.refs_6_ = bf16[32,5120]{1,0:T(8,128)(2,1)S(1)} collective-permute-done((bf16[32,5120]{1,0:T(8,128)(2,1)}, bf16[32,5120]{1,0:T(8,128)(2,1)S(1)}, u32[]{:S(2)}, u32[]{:S(2)}) %collective-permute-start.3) | collective-permute-done | bytes 327712 | tf_op jit(solution)/shard_map/ppermute | solution.py:26
  19.3 1.5 %collective-permute-done.2.refs_2_.refs_0_.refs_5_ = bf16[32,5120]{1,0:T(8,128)(2,1)S(1)} collective-permute-done((bf16[32,5120]{1,0:T(8,128)(2,1)}, bf16[32,5120]{1,0:T(8,128)(2,1)S(1)}, u32[]{:S(2)}, u32[]{:S(2)}) %collective-permute-start.2) | collective-permute-done | bytes 327712 | tf_op jit(solution)/shard_map/ppermute | solution.py:26
  20.7 0.1 shard_map.92
  20.9 0.1 collective-permute-start.4
  21.0 1.4 %collective-permute-start.5 = (bf16[32,5120]{1,0:T(8,128)(2,1)S(1)}, bf16[32,5120]{1,0:T(8,128)(2,1)S(1)}, u32[]{:S(2)}, u32[]{:S(2)}) collective-permute-start(bf16[32,5120]{1,0:T(8,128)(2,1)S(1)} %get-tuple-element.30), channel_id=1, source_target_pairs={{0,1},{1,0},{2,3},{3,2},{4,5},{5,4},{6,7},{7,6},{8,9},{9,8},{10,11... | collective-permute-start | bytes 983048 | tf_op jit(solution)/shard_map/ppermute | solution.py:26
  22.3 1.8 %collective-permute-start.8 = (bf16[32,5120]{1,0:T(8,128)(2,1)S(1)}, bf16[32,5120]{1,0:T(8,128)(2,1)S(1)}, u32[]{:S(2)}, u32[]{:S(2)}) collective-permute-start(bf16[32,5120]{1,0:T(8,128)(2,1)S(1)} %get-tuple-element.32), channel_id=1, source_target_pairs={{0,4},{1,5},{2,6},{3,7},{4,0},{5,1},{6,2},{7,3},{8,12},{9,13},{10,... | collective-permute-start | bytes 983048 | tf_op jit(solution)/shard_map/ppermute | solution.py:26
  24.1 4.9 %collective-permute-start.9 = (bf16[32,5120]{1,0:T(8,128)(2,1)S(1)}, bf16[32,5120]{1,0:T(8,128)(2,1)S(1)}, u32[]{:S(2)}, u32[]{:S(2)}) collective-permute-start(bf16[32,5120]{1,0:T(8,128)(2,1)S(1)} %get-tuple-element.33), channel_id=1, source_target_pairs={{0,196},{1,197},{2,198},{3,199},{4,64},{5,65},{6,66},{7,67},{8,204... | collective-permute-start | bytes 983048 | tf_op jit(solution)/shard_map/ppermute | solution.py:26
  29.1 1.1 collective-permute-start.7
  30.2 0.6 collective-permute-start.6
  30.8 3.4 %collective-permute-start.10 = (bf16[32,5120]{1,0:T(8,128)(2,1)S(1)}, bf16[32,5120]{1,0:T(8,128)(2,1)S(1)}, u32[]{:S(2)}, u32[]{:S(2)}) collective-permute-start(bf16[32,5120]{1,0:T(8,128)(2,1)S(1)} %collective-permute-done.4.refs_3_), channel_id=1, source_target_pairs={{0,4},{1,5},{2,6},{3,7},{4,0},{5,1},{6,2},{7,3},{8,12},{9,13},{10,... | collective-permute-start | bytes 983048 | tf_op jit(solution)/shard_map/ppermute | solution.py:26
  34.2 5.2 %collective-permute-start.11 = (bf16[32,5120]{1,0:T(8,128)(2,1)S(1)}, bf16[32,5120]{1,0:T(8,128)(2,1)S(1)}, u32[]{:S(2)}, u32[]{:S(2)}) collective-permute-start(bf16[32,5120]{1,0:T(8,128)(2,1)S(1)} %collective-permute-done.5.refs_4_), channel_id=1, source_target_pairs={{0,196},{1,197},{2,198},{3,199},{4,64},{5,65},{6,66},{7,67},{8,204... | collective-permute-start | bytes 983048 | tf_op jit(solution)/shard_map/ppermute | solution.py:26
  39.5 3.8 %copy-done = bf16[3,5120,320]{1,2,0:T(8,128)(2,1)S(1)} copy-done((bf16[3,5120,320]{1,2,0:T(8,128)(2,1)S(1)}, bf16[3,5120,320]{1,2,0:T(8,128)(2,1)}, u32[]{:S(2)}) %copy-start) | copy-done | bytes 9830424
  43.3 1.9 %shard_map.93.refs_10_.refs_1_ = bf16[640,256]{1,0:T(8,128)(2,1)S(1)} custom-call(bf16[64,5120]{1,0:T(8,128)(2,1)S(1)} %copy-done.2, bf16[64,5120]{1,0:T(8,128)(2,1)S(1)} %collective-permute-done.refs_0_.refs_1_, bf16[64,5120]{1,0:T(8,128)(2,1)S(1)} %collective-permute-done.1.refs_1_.refs_2_, bf16[32,5120]{1,0:T(8,128)(2,1)S(1)} %collective-permute-done.4.refs_3_, ...), custom_call_target="tpu_custom_call" | custom-call | flops 1000 | bytes 1000 | tf_op jit(solution)/shard_map/pallas_call | solution.py:87
  45.2 1.9 %copy-done.1 = bf16[3,5120,320]{1,2,0:T(8,128)(2,1)S(1)} copy-done((bf16[3,5120,320]{1,2,0:T(8,128)(2,1)S(1)}, bf16[3,5120,320]{1,2,0:T(8,128)(2,1)}, u32[]{:S(2)}) %copy-start.1) | copy-done | bytes 9830424
  47.1 1.9 %shard_map.94.refs_2_ = bf16[640,256]{1,0:T(8,128)(2,1)S(1)} custom-call(bf16[32,5120]{1,0:T(8,128)(2,1)S(1)} %collective-permute-done.2.refs_2_.refs_0_.refs_5_, bf16[32,5120]{1,0:T(8,128)(2,1)S(1)} %collective-permute-done.3.refs_3_.refs_1_.refs_6_, bf16[32,5120]{1,0:T(8,128)(2,1)S(1)} %collective-permute-done.6.refs_7_.refs_2_, ...), custom_call_target="tpu_custom_call" | custom-call | flops 1000 | bytes 1000 | tf_op jit(solution)/shard_map/pallas_call | solution.py:87
  49.0 1.9 %shard_map.95.refs_8_ = bf16[320,960]{1,0:T(8,128)(2,1)S(1)} custom-call(s32[32]{0:T(128)S(1)} %dynamic-slice_bitcast_fusion.refs_0_, bf16[640,256]{1,0:T(8,128)(2,1)S(1)} %shard_map.93.refs_10_.refs_1_, bf16[640,256]{1,0:T(8,128)(2,1)S(1)} %shard_map.94.refs_2_, f32[1,384]{1,0:T(1,128)S(1)} %get-tuple-element.28.refs_5_.refs_3_, ...), custom_call_target="tpu_custom_call" | custom-call | flops 1000 | bytes 1000 | tf_op jit(solution)/shard_map/pallas_call | solution.py:87
  50.9 0.1 collective-permute-start.13
  51.0 1.9 %shard_map.96.refs_1_ = f32[320,960]{1,0:T(8,128)S(1)} custom-call(s32[32]{0:T(128)S(1)} %dynamic-slice_bitcast_fusion.refs_0_, bf16[640,256]{1,0:T(8,128)(2,1)S(1)} %shard_map.93.refs_10_.refs_1_, bf16[640,256]{1,0:T(8,128)(2,1)S(1)} %shard_map.94.refs_2_, f32[1,384]{1,0:T(1,128)S(1)} %get-tuple-element.28.refs_5_.refs_3_, ...), custom_call_target="tpu_custom_call" | custom-call | flops 1000 | bytes 1000 | tf_op jit(solution)/shard_map/pallas_call | solution.py:87
  52.9 0.2 collective-permute-done.13.refs_2_
  53.1 0.7 shard_map.97
  53.7 3.3 %collective-permute-start.14 = (bf16[80,960]{1,0:T(8,128)(2,1)S(1)}, bf16[80,960]{1,0:T(8,128)(2,1)S(1)}, u32[]{:S(2)}, u32[]{:S(2)}) collective-permute-start(bf16[80,960]{1,0:T(8,128)(2,1)S(1)} %get-tuple-element.36), channel_id=1, source_target_pairs={{0,32},{1,33},{2,34},{3,35},{4,36},{5,37},{6,38},{7,39},{8,40},{9,... | collective-permute-start | bytes 460808 | tf_op jit(solution)/shard_map/ppermute | solution.py:26
  57.0 0.7 collective-permute-start.15
  57.7 2.6 %collective-permute-start.16 = (bf16[80,960]{1,0:T(8,128)(2,1)S(1)}, bf16[80,960]{1,0:T(8,128)(2,1)S(1)}, u32[]{:S(2)}, u32[]{:S(2)}) collective-permute-start(bf16[80,960]{1,0:T(8,128)(2,1)S(1)} %get-tuple-element.38), channel_id=1, source_target_pairs={{0,48},{1,49},{2,50},{3,51},{4,52},{5,53},{6,54},{7,55},{8,56},{9,... | collective-permute-start | bytes 460808 | tf_op jit(solution)/shard_map/ppermute | solution.py:26
  60.3 2.1 %collective-permute-done.14.refs_1_ = bf16[80,960]{1,0:T(8,128)(2,1)S(1)} collective-permute-done((bf16[80,960]{1,0:T(8,128)(2,1)S(1)}, bf16[80,960]{1,0:T(8,128)(2,1)S(1)}, u32[]{:S(2)}, u32[]{:S(2)}) %collective-permute-start.14) | collective-permute-done | bytes 153632 | tf_op jit(solution)/shard_map/ppermute | solution.py:26
  62.4 2.9 %collective-permute-done.15.refs_2_ = bf16[80,960]{1,0:T(8,128)(2,1)S(1)} collective-permute-done((bf16[80,960]{1,0:T(8,128)(2,1)S(1)}, bf16[80,960]{1,0:T(8,128)(2,1)S(1)}, u32[]{:S(2)}, u32[]{:S(2)}) %collective-permute-start.15) | collective-permute-done | bytes 153632 | tf_op jit(solution)/shard_map/ppermute | solution.py:26
  65.3 0.3 collective-permute-done.16.refs_3_
  65.7 4.5 %collective-permute-start.19 = (bf16[80,960]{1,0:T(8,128)(2,1)S(1)}, bf16[80,960]{1,0:T(8,128)(2,1)S(1)}, u32[]{:S(2)}, u32[]{:S(2)}) collective-permute-start(bf16[80,960]{1,0:T(8,128)(2,1)S(1)} %get-tuple-element.39.refs_15_), channel_id=1, source_target_pairs={{0,192},{1,193},{2,194},{3,195},{4,196},{5,197},{6,198},{7,199},{8... | collective-permute-start | bytes 460808 | tf_op jit(solution)/shard_map/ppermute | solution.py:26
  70.2 3.8 %collective-permute-start.17 = (bf16[80,960]{1,0:T(8,128)(2,1)S(1)}, bf16[80,960]{1,0:T(8,128)(2,1)S(1)}, u32[]{:S(2)}, u32[]{:S(2)}) collective-permute-start(bf16[80,960]{1,0:T(8,128)(2,1)S(1)} %get-tuple-element.39.refs_15_), channel_id=1, source_target_pairs={{0,128},{1,129},{2,130},{3,131},{4,132},{5,133},{6,134},{7,135},{8... | collective-permute-start | bytes 460808 | tf_op jit(solution)/shard_map/ppermute | solution.py:26
  74.1 1.9 %shard_map.99.refs_8_.refs_0_ = bf16[320,512]{1,0:T(8,128)(2,1)S(1)} custom-call(bf16[64,5120]{1,0:T(8,128)(2,1)S(1)} %copy-done.2, bf16[64,5120]{1,0:T(8,128)(2,1)S(1)} %collective-permute-done.refs_0_.refs_1_, bf16[64,5120]{1,0:T(8,128)(2,1)S(1)} %collective-permute-done.1.refs_1_.refs_2_, bf16[32,5120]{1,0:T(8,128)(2,1)S(1)} %collective-permute-done.4.refs_3_, ...), custom_call_target="tpu_custom_call" | custom-call | flops 1000 | bytes 1000 | tf_op jit(solution)/shard_map/pallas_call | solution.py:87
  76.0 6.9 %collective-permute-done.19.refs_4_ = bf16[80,960]{1,0:T(8,128)(2,1)S(1)} collective-permute-done((bf16[80,960]{1,0:T(8,128)(2,1)S(1)}, bf16[80,960]{1,0:T(8,128)(2,1)S(1)}, u32[]{:S(2)}, u32[]{:S(2)}) %collective-permute-start.19) | collective-permute-done | bytes 153632 | tf_op jit(solution)/shard_map/ppermute | solution.py:26
  82.9 2.2 %collective-permute-done.18.refs_3_ = bf16[80,960]{1,0:T(8,128)(2,1)S(1)} collective-permute-done((bf16[80,960]{1,0:T(8,128)(2,1)S(1)}, bf16[80,960]{1,0:T(8,128)(2,1)S(1)}, u32[]{:S(2)}, u32[]{:S(2)}) %collective-permute-start.18) | collective-permute-done | bytes 153632 | tf_op jit(solution)/shard_map/ppermute | solution.py:26
  85.1 0.9 shard_map.100
  86.0 3.1 %collective-permute-start.22 = (bf16[80,960]{1,0:T(8,128)(2,1)S(1)}, bf16[80,960]{1,0:T(8,128)(2,1)S(1)}, u32[]{:S(2)}, u32[]{:S(2)}) collective-permute-start(bf16[80,960]{1,0:T(8,128)(2,1)S(1)} %shard_map.100), channel_id=1, source_target_pairs={{0,48},{1,49},{2,50},{3,51},{4,52},{5,53},{6,54},{7,55},{8,56},{9,... | collective-permute-start | bytes 460808 | tf_op jit(solution)/shard_map/ppermute | solution.py:26
  89.1 1.6 %collective-permute-start.20 = (bf16[80,960]{1,0:T(8,128)(2,1)S(1)}, bf16[80,960]{1,0:T(8,128)(2,1)S(1)}, u32[]{:S(2)}, u32[]{:S(2)}) collective-permute-start(bf16[80,960]{1,0:T(8,128)(2,1)S(1)} %shard_map.100), channel_id=1, source_target_pairs={{0,32},{1,33},{2,34},{3,35},{4,36},{5,37},{6,38},{7,39},{8,40},{9,... | collective-permute-start | bytes 460808 | tf_op jit(solution)/shard_map/ppermute | solution.py:26
  90.6 2.8 %collective-permute-done.22 = bf16[80,960]{1,0:T(8,128)(2,1)S(1)} collective-permute-done((bf16[80,960]{1,0:T(8,128)(2,1)S(1)}, bf16[80,960]{1,0:T(8,128)(2,1)S(1)}, u32[]{:S(2)}, u32[]{:S(2)}) %collective-permute-start.22) | collective-permute-done | bytes 153632 | tf_op jit(solution)/shard_map/ppermute | solution.py:26
  93.5 3.9 %collective-permute-done.21 = bf16[80,960]{1,0:T(8,128)(2,1)S(1)} collective-permute-done((bf16[80,960]{1,0:T(8,128)(2,1)S(1)}, bf16[80,960]{1,0:T(8,128)(2,1)S(1)}, u32[]{:S(2)}, u32[]{:S(2)}) %collective-permute-start.21) | collective-permute-done | bytes 153632 | tf_op jit(solution)/shard_map/ppermute | solution.py:26
  97.4 0.1 collective-permute-start.23
  97.5 2.1 %collective-permute-done.23.refs_2_ = bf16[320,960]{1,0:T(8,128)(2,1)S(1)} collective-permute-done((bf16[320,960]{1,0:T(8,128)(2,1)S(1)}, bf16[320,960]{1,0:T(8,128)(2,1)S(1)}, u32[]{:S(2)}, u32[]{:S(2)}) %collective-permute-start.23) | collective-permute-done | bytes 614432 | tf_op jit(solution)/shard_map/ppermute | solution.py:26
  99.6 0.9 shard_map.101
  100.5 5.1 %collective-permute-start.25 = (bf16[128,320]{1,0:T(8,128)(2,1)S(1)}, bf16[128,320]{1,0:T(8,128)(2,1)S(1)}, u32[]{:S(2)}, u32[]{:S(2)}) collective-permute-start(bf16[128,320]{1,0:T(8,128)(2,1)S(1)} %get-tuple-element.42), channel_id=1, source_target_pairs={{0,196},{1,197},{2,198},{3,199},{4,64},{5,65},{6,66},{7,67},{8,204... | collective-permute-start | bytes 245768 | tf_op jit(solution)/shard_map/ppermute | solution.py:26
  105.6 2.0 %collective-permute-start.24 = (bf16[128,320]{1,0:T(8,128)(2,1)S(1)}, bf16[128,320]{1,0:T(8,128)(2,1)S(1)}, u32[]{:S(2)}, u32[]{:S(2)}) collective-permute-start(bf16[128,320]{1,0:T(8,128)(2,1)S(1)} %get-tuple-element.41.refs_3_), channel_id=1, source_target_pairs={{0,4},{1,5},{2,6},{3,7},{4,0},{5,1},{6,2},{7,3},{8,12},{9,13},{10,... | collective-permute-start | bytes 245768 | tf_op jit(solution)/shard_map/ppermute | solution.py:26
  107.7 0.9 shard_map.102.refs_0_
  108.6 0.2 collective-permute-done.25.refs_2_
  108.7 1.7 %collective-permute-done.24.refs_1_ = bf16[128,320]{1,0:T(8,128)(2,1)S(1)} collective-permute-done((bf16[128,320]{1,0:T(8,128)(2,1)S(1)}, bf16[128,320]{1,0:T(8,128)(2,1)S(1)}, u32[]{:S(2)}, u32[]{:S(2)}) %collective-permute-start.24) | collective-permute-done | bytes 81952 | tf_op jit(solution)/shard_map/ppermute | solution.py:26
  110.5 2.3 %collective-permute-start.26 = (bf16[2,64,320]{2,1,0:T(8,128)(2,1)S(1)}, bf16[2,64,320]{2,1,0:T(8,128)(2,1)S(1)}, u32[]{:S(2)}, u32[]{:S(2)}) collective-permute-start(bf16[2,64,320]{2,1,0:T(8,128)(2,1)S(1)} %get-tuple-element.44), channel_id=1, source_target_pairs={{0,1},{1,0},{2,3},{3,2},{4,5},{5,4},{6,7},{7,6},{8,9},{9,8},{10,11... | collective-permute-start | bytes 245768 | tf_op jit(solution)/shard_map/ppermute | solution.py:26
  112.8 0.5 collective-permute-start.27
  113.3 1.7 %collective-permute-start.28 = (bf16[2,64,320]{2,1,0:T(8,128)(2,1)S(1)}, bf16[2,64,320]{2,1,0:T(8,128)(2,1)S(1)}, u32[]{:S(2)}, u32[]{:S(2)}) collective-permute-start(bf16[2,64,320]{2,1,0:T(8,128)(2,1)S(1)} %get-tuple-element.46), channel_id=1, source_target_pairs={{0,2},{1,3},{2,0},{3,1},{4,6},{5,7},{6,4},{7,5},{8,10},{9,11},{10,... | collective-permute-start | bytes 245768 | tf_op jit(solution)/shard_map/ppermute | solution.py:26
  115.0 0.6 collective-permute-done.26.refs_2_
  115.6 2.6 %collective-permute-done.27.refs_3_ = bf16[2,64,320]{2,1,0:T(8,128)(2,1)S(1)} collective-permute-done((bf16[2,64,320]{2,1,0:T(8,128)(2,1)S(1)}, bf16[2,64,320]{2,1,0:T(8,128)(2,1)S(1)}, u32[]{:S(2)}, u32[]{:S(2)}) %collective-permute-start.27) | collective-permute-done | bytes 81952 | tf_op jit(solution)/shard_map/ppermute | solution.py:26
  118.3 1.2 collective-permute-done.28.refs_4_
  119.4 1.4 %shard_map.104 = bf16[64,2560]{1,0:T(8,128)(2,1)} custom-call(s32[32]{0:T(128)S(1)} %dynamic-slice_bitcast_fusion.refs_0_, bf16[2,64,320]{2,1,0:T(8,128)(2,1)S(1)} %get-tuple-element.43.refs_1_, bf16[2,64,320]{2,1,0:T(8,128)(2,1)S(1)} %collective-permute-done.26.refs_2_, bf16[2,64,320]{2,1,0:T(8,128)(2,1)S(1)} %collective-permute-done.27.refs_3_, ...), custom_call_target="tpu_custom_call" | custom-call | flops 1000 | bytes 1000 | tf_op jit(solution)/shard_map/pallas_call | solution.py:87
  (35 shorter events, 0.3 us)
Async XLA Ops:
  0.0 13.0 %copy-start.5 = (s32[512,1]{0,1:T(1,128)S(1)}, s32[512,1]{0,1:T(1,128)}, u32[]{:S(2)}) copy-start(s32[512,1]{0,1:T(1,128)} %param.12) | copy-start | bytes 6148
  0.0 14.3 %copy-start.6 = (s32[3,40,1]{1,2,0:T(1,128)S(1)}, s32[3,40,1]{1,2,0:T(1,128)}, u32[]{:S(2)}) copy-start(s32[3,40,1]{1,2,0:T(1,128)} %param.11) | copy-start | bytes 1444
  0.0 14.5 %copy-start.3 = (bf16[1,320,640]{2,1,0:T(8,128)(2,1)S(1)}, bf16[1,320,640]{2,1,0:T(8,128)(2,1)}, u32[]{:S(2)}) copy-start(bf16[1,320,640]{2,1,0:T(8,128)(2,1)} %param.14) | copy-start | bytes 1228804
  0.0 14.7 %copy-start.4 = (bf16[1,320,640]{2,1,0:T(8,128)(2,1)S(1)}, bf16[1,320,640]{2,1,0:T(8,128)(2,1)}, u32[]{:S(2)}) copy-start(bf16[1,320,640]{2,1,0:T(8,128)(2,1)} %param.15) | copy-start | bytes 1228804
  0.8 19.9 %collective-permute-start.1 = (bf16[64,5120]{1,0:T(8,128)(2,1)}, bf16[64,5120]{1,0:T(8,128)(2,1)S(1)}, u32[]{:S(2)}, u32[]{:S(2)}) collective-permute-start(bf16[64,5120]{1,0:T(8,128)(2,1)} %refs_0_.1), channel_id=1, source_target_pairs={{0,3},{1,2},{2,1},{3,0},{4,7},{5,6},{6,5},{7,4},{8,11},{9,10},{10,... | collective-permute-start | bytes 1966088 | tf_op jit(solution)/shard_map/ppermute | solution.py:26
  2.3 18.4 %collective-permute-start = (bf16[64,5120]{1,0:T(8,128)(2,1)}, bf16[64,5120]{1,0:T(8,128)(2,1)S(1)}, u32[]{:S(2)}, u32[]{:S(2)}) collective-permute-start(bf16[64,5120]{1,0:T(8,128)(2,1)} %refs_0_.1), channel_id=1, source_target_pairs={{0,1},{1,0},{2,3},{3,2},{4,5},{5,4},{6,7},{7,6},{8,9},{9,8},{10,11... | collective-permute-start | bytes 1966088 | tf_op jit(solution)/shard_map/ppermute | solution.py:26
  6.0 13.2 %collective-permute-start.3 = (bf16[32,5120]{1,0:T(8,128)(2,1)}, bf16[32,5120]{1,0:T(8,128)(2,1)S(1)}, u32[]{:S(2)}, u32[]{:S(2)}) collective-permute-start(bf16[32,5120]{1,0:T(8,128)(2,1)} %get-tuple-element.47), channel_id=1, source_target_pairs={{0,196},{1,197},{2,198},{3,199},{4,64},{5,65},{6,66},{7,67},{8,204... | collective-permute-start | bytes 983048 | tf_op jit(solution)/shard_map/ppermute | solution.py:26
  11.9 8.8 %collective-permute-start.2 = (bf16[32,5120]{1,0:T(8,128)(2,1)}, bf16[32,5120]{1,0:T(8,128)(2,1)S(1)}, u32[]{:S(2)}, u32[]{:S(2)}) collective-permute-start(bf16[32,5120]{1,0:T(8,128)(2,1)} %get-tuple-element.48), channel_id=1, source_target_pairs={{0,4},{1,5},{2,6},{3,7},{4,0},{5,1},{6,2},{7,3},{8,12},{9,13},{10,... | collective-permute-start | bytes 983048 | tf_op jit(solution)/shard_map/ppermute | solution.py:26
  20.7 18.7 %copy-start.2 = (bf16[64,5120]{1,0:T(8,128)(2,1)S(1)}, bf16[64,5120]{1,0:T(8,128)(2,1)}, u32[]{:S(2)}) copy-start(bf16[64,5120]{1,0:T(8,128)(2,1)} %refs_0_.1) | copy-start | bytes 1966084
  20.9 9.3 %collective-permute-start.4 = (bf16[32,5120]{1,0:T(8,128)(2,1)S(1)}, bf16[32,5120]{1,0:T(8,128)(2,1)S(1)}, u32[]{:S(2)}, u32[]{:S(2)}) collective-permute-start(bf16[32,5120]{1,0:T(8,128)(2,1)S(1)} %get-tuple-element.29), channel_id=1, source_target_pairs={{0,3},{1,2},{2,1},{3,0},{4,7},{5,6},{6,5},{7,4},{8,11},{9,10},{10,... | collective-permute-start | bytes 983048 | tf_op jit(solution)/shard_map/ppermute | solution.py:26
  21.0 9.9 %collective-permute-start.5 = (bf16[32,5120]{1,0:T(8,128)(2,1)S(1)}, bf16[32,5120]{1,0:T(8,128)(2,1)S(1)}, u32[]{:S(2)}, u32[]{:S(2)}) collective-permute-start(bf16[32,5120]{1,0:T(8,128)(2,1)S(1)} %get-tuple-element.30), channel_id=1, source_target_pairs={{0,1},{1,0},{2,3},{3,2},{4,5},{5,4},{6,7},{7,6},{8,9},{9,8},{10,11... | collective-permute-start | bytes 983048 | tf_op jit(solution)/shard_map/ppermute | solution.py:26
  22.3 11.9 %collective-permute-start.8 = (bf16[32,5120]{1,0:T(8,128)(2,1)S(1)}, bf16[32,5120]{1,0:T(8,128)(2,1)S(1)}, u32[]{:S(2)}, u32[]{:S(2)}) collective-permute-start(bf16[32,5120]{1,0:T(8,128)(2,1)S(1)} %get-tuple-element.32), channel_id=1, source_target_pairs={{0,4},{1,5},{2,6},{3,7},{4,0},{5,1},{6,2},{7,3},{8,12},{9,13},{10,... | collective-permute-start | bytes 983048 | tf_op jit(solution)/shard_map/ppermute | solution.py:26
  24.1 15.3 %collective-permute-start.9 = (bf16[32,5120]{1,0:T(8,128)(2,1)S(1)}, bf16[32,5120]{1,0:T(8,128)(2,1)S(1)}, u32[]{:S(2)}, u32[]{:S(2)}) collective-permute-start(bf16[32,5120]{1,0:T(8,128)(2,1)S(1)} %get-tuple-element.33), channel_id=1, source_target_pairs={{0,196},{1,197},{2,198},{3,199},{4,64},{5,65},{6,66},{7,67},{8,204... | collective-permute-start | bytes 983048 | tf_op jit(solution)/shard_map/ppermute | solution.py:26
  29.1 10.4 %collective-permute-start.7 = (bf16[32,5120]{1,0:T(8,128)(2,1)S(1)}, bf16[32,5120]{1,0:T(8,128)(2,1)S(1)}, u32[]{:S(2)}, u32[]{:S(2)}) collective-permute-start(bf16[32,5120]{1,0:T(8,128)(2,1)S(1)} %get-tuple-element.31), channel_id=1, source_target_pairs={{0,3},{1,2},{2,1},{3,0},{4,7},{5,6},{6,5},{7,4},{8,11},{9,10},{10,... | collective-permute-start | bytes 983048 | tf_op jit(solution)/shard_map/ppermute | solution.py:26
  30.2 9.2 %collective-permute-start.6 = (bf16[32,5120]{1,0:T(8,128)(2,1)S(1)}, bf16[32,5120]{1,0:T(8,128)(2,1)S(1)}, u32[]{:S(2)}, u32[]{:S(2)}) collective-permute-start(bf16[32,5120]{1,0:T(8,128)(2,1)S(1)} %get-tuple-element.31), channel_id=1, source_target_pairs={{0,1},{1,0},{2,3},{3,2},{4,5},{5,4},{6,7},{7,6},{8,9},{9,8},{10,11... | collective-permute-start | bytes 983048 | tf_op jit(solution)/shard_map/ppermute | solution.py:26
  30.8 14.4 %collective-permute-start.10 = (bf16[32,5120]{1,0:T(8,128)(2,1)S(1)}, bf16[32,5120]{1,0:T(8,128)(2,1)S(1)}, u32[]{:S(2)}, u32[]{:S(2)}) collective-permute-start(bf16[32,5120]{1,0:T(8,128)(2,1)S(1)} %collective-permute-done.4.refs_3_), channel_id=1, source_target_pairs={{0,4},{1,5},{2,6},{3,7},{4,0},{5,1},{6,2},{7,3},{8,12},{9,13},{10,... | collective-permute-start | bytes 983048 | tf_op jit(solution)/shard_map/ppermute | solution.py:26
  34.2 11.0 %collective-permute-start.11 = (bf16[32,5120]{1,0:T(8,128)(2,1)S(1)}, bf16[32,5120]{1,0:T(8,128)(2,1)S(1)}, u32[]{:S(2)}, u32[]{:S(2)}) collective-permute-start(bf16[32,5120]{1,0:T(8,128)(2,1)S(1)} %collective-permute-done.5.refs_4_), channel_id=1, source_target_pairs={{0,196},{1,197},{2,198},{3,199},{4,64},{5,65},{6,66},{7,67},{8,204... | collective-permute-start | bytes 983048 | tf_op jit(solution)/shard_map/ppermute | solution.py:26
  39.4 9.5 %collective-permute-start.12 = (f32[1,128]{1,0:T(1,128)S(1)}, f32[1,128]{1,0:T(1,128)S(1)}, u32[]{:S(2)}, u32[]{:S(2)}) collective-permute-start(f32[1,128]{1,0:T(1,128)S(1)} %get-tuple-element.34), channel_id=1, source_target_pairs={{0,64},{1,65},{2,66},{3,67},{4,196},{5,197},{6,198},{7,199},{8,72}... | collective-permute-start | bytes 1544 | tf_op jit(solution)/shard_map/ppermute | solution.py:26
  39.5 3.8 %copy-start = (bf16[3,5120,320]{1,2,0:T(8,128)(2,1)S(1)}, bf16[3,5120,320]{1,2,0:T(8,128)(2,1)}, u32[]{:S(2)}) copy-start(bf16[3,5120,320]{1,2,0:T(8,128)(2,1)} %param.10) | copy-start | bytes 29491204
  43.3 3.8 %copy-start.1 = (bf16[3,5120,320]{1,2,0:T(8,128)(2,1)S(1)}, bf16[3,5120,320]{1,2,0:T(8,128)(2,1)}, u32[]{:S(2)}) copy-start(bf16[3,5120,320]{1,2,0:T(8,128)(2,1)} %param.10) | copy-start | bytes 29491204
  50.9 2.2 %collective-permute-start.13 = (bf16[320,960]{1,0:T(8,128)(2,1)S(1)}, bf16[320,960]{1,0:T(8,128)(2,1)S(1)}, u32[]{:S(2)}, u32[]{:S(2)}) collective-permute-start(bf16[320,960]{1,0:T(8,128)(2,1)S(1)} %shard_map.95.refs_8_), channel_id=1, source_target_pairs={{0,8},{1,9},{2,10},{3,11},{4,12},{5,13},{6,14},{7,15},{8,0},{9,1},... | collective-permute-start | bytes 1843208 | tf_op jit(solution)/shard_map/ppermute | solution.py:26
  53.7 8.6 %collective-permute-start.14 = (bf16[80,960]{1,0:T(8,128)(2,1)S(1)}, bf16[80,960]{1,0:T(8,128)(2,1)S(1)}, u32[]{:S(2)}, u32[]{:S(2)}) collective-permute-start(bf16[80,960]{1,0:T(8,128)(2,1)S(1)} %get-tuple-element.36), channel_id=1, source_target_pairs={{0,32},{1,33},{2,34},{3,35},{4,36},{5,37},{6,38},{7,39},{8,40},{9,... | collective-permute-start | bytes 460808 | tf_op jit(solution)/shard_map/ppermute | solution.py:26
  57.0 8.3 %collective-permute-start.15 = (bf16[80,960]{1,0:T(8,128)(2,1)S(1)}, bf16[80,960]{1,0:T(8,128)(2,1)S(1)}, u32[]{:S(2)}, u32[]{:S(2)}) collective-permute-start(bf16[80,960]{1,0:T(8,128)(2,1)S(1)} %get-tuple-element.37), channel_id=1, source_target_pairs={{0,16},{1,17},{2,18},{3,19},{4,20},{5,21},{6,22},{7,23},{8,24},{9,... | collective-permute-start | bytes 460808 | tf_op jit(solution)/shard_map/ppermute | solution.py:26
  57.7 7.9 %collective-permute-start.16 = (bf16[80,960]{1,0:T(8,128)(2,1)S(1)}, bf16[80,960]{1,0:T(8,128)(2,1)S(1)}, u32[]{:S(2)}, u32[]{:S(2)}) collective-permute-start(bf16[80,960]{1,0:T(8,128)(2,1)S(1)} %get-tuple-element.38), channel_id=1, source_target_pairs={{0,48},{1,49},{2,50},{3,51},{4,52},{5,53},{6,54},{7,55},{8,56},{9,... | collective-permute-start | bytes 460808 | tf_op jit(solution)/shard_map/ppermute | solution.py:26
  65.7 17.2 %collective-permute-start.19 = (bf16[80,960]{1,0:T(8,128)(2,1)S(1)}, bf16[80,960]{1,0:T(8,128)(2,1)S(1)}, u32[]{:S(2)}, u32[]{:S(2)}) collective-permute-start(bf16[80,960]{1,0:T(8,128)(2,1)S(1)} %get-tuple-element.39.refs_15_), channel_id=1, source_target_pairs={{0,192},{1,193},{2,194},{3,195},{4,196},{5,197},{6,198},{7,199},{8... | collective-permute-start | bytes 460808 | tf_op jit(solution)/shard_map/ppermute | solution.py:26
  70.2 14.8 %collective-permute-start.18 = (bf16[80,960]{1,0:T(8,128)(2,1)S(1)}, bf16[80,960]{1,0:T(8,128)(2,1)S(1)}, u32[]{:S(2)}, u32[]{:S(2)}) collective-permute-start(bf16[80,960]{1,0:T(8,128)(2,1)S(1)} %get-tuple-element.39.refs_15_), channel_id=1, source_target_pairs={{0,64},{1,65},{2,66},{3,67},{4,68},{5,69},{6,70},{7,71},{8,72},{9,... | collective-permute-start | bytes 460808 | tf_op jit(solution)/shard_map/ppermute | solution.py:26
  70.2 14.8 %collective-permute-start.17 = (bf16[80,960]{1,0:T(8,128)(2,1)S(1)}, bf16[80,960]{1,0:T(8,128)(2,1)S(1)}, u32[]{:S(2)}, u32[]{:S(2)}) collective-permute-start(bf16[80,960]{1,0:T(8,128)(2,1)S(1)} %get-tuple-element.39.refs_15_), channel_id=1, source_target_pairs={{0,128},{1,129},{2,130},{3,131},{4,132},{5,133},{6,134},{7,135},{8... | collective-permute-start | bytes 460808 | tf_op jit(solution)/shard_map/ppermute | solution.py:26
  86.0 7.5 %collective-permute-start.22 = (bf16[80,960]{1,0:T(8,128)(2,1)S(1)}, bf16[80,960]{1,0:T(8,128)(2,1)S(1)}, u32[]{:S(2)}, u32[]{:S(2)}) collective-permute-start(bf16[80,960]{1,0:T(8,128)(2,1)S(1)} %shard_map.100), channel_id=1, source_target_pairs={{0,48},{1,49},{2,50},{3,51},{4,52},{5,53},{6,54},{7,55},{8,56},{9,... | collective-permute-start | bytes 460808 | tf_op jit(solution)/shard_map/ppermute | solution.py:26
  89.1 8.3 %collective-permute-start.21 = (bf16[80,960]{1,0:T(8,128)(2,1)S(1)}, bf16[80,960]{1,0:T(8,128)(2,1)S(1)}, u32[]{:S(2)}, u32[]{:S(2)}) collective-permute-start(bf16[80,960]{1,0:T(8,128)(2,1)S(1)} %shard_map.100), channel_id=1, source_target_pairs={{0,16},{1,17},{2,18},{3,19},{4,20},{5,21},{6,22},{7,23},{8,24},{9,... | collective-permute-start | bytes 460808 | tf_op jit(solution)/shard_map/ppermute | solution.py:26
  89.1 8.3 %collective-permute-start.20 = (bf16[80,960]{1,0:T(8,128)(2,1)S(1)}, bf16[80,960]{1,0:T(8,128)(2,1)S(1)}, u32[]{:S(2)}, u32[]{:S(2)}) collective-permute-start(bf16[80,960]{1,0:T(8,128)(2,1)S(1)} %shard_map.100), channel_id=1, source_target_pairs={{0,32},{1,33},{2,34},{3,35},{4,36},{5,37},{6,38},{7,39},{8,40},{9,... | collective-permute-start | bytes 460808 | tf_op jit(solution)/shard_map/ppermute | solution.py:26
  97.4 2.2 %collective-permute-start.23 = (bf16[320,960]{1,0:T(8,128)(2,1)S(1)}, bf16[320,960]{1,0:T(8,128)(2,1)S(1)}, u32[]{:S(2)}, u32[]{:S(2)}) collective-permute-start(bf16[320,960]{1,0:T(8,128)(2,1)S(1)} %pad_maximum_fusion.refs_1_), channel_id=1, source_target_pairs={{0,8},{1,9},{2,10},{3,11},{4,12},{5,13},{6,14},{7,15},{8,0},{9,1},... | collective-permute-start | bytes 1843208 | tf_op jit(solution)/shard_map/ppermute | solution.py:26
  100.5 8.2 %collective-permute-start.25 = (bf16[128,320]{1,0:T(8,128)(2,1)S(1)}, bf16[128,320]{1,0:T(8,128)(2,1)S(1)}, u32[]{:S(2)}, u32[]{:S(2)}) collective-permute-start(bf16[128,320]{1,0:T(8,128)(2,1)S(1)} %get-tuple-element.42), channel_id=1, source_target_pairs={{0,196},{1,197},{2,198},{3,199},{4,64},{5,65},{6,66},{7,67},{8,204... | collective-permute-start | bytes 245768 | tf_op jit(solution)/shard_map/ppermute | solution.py:26
  105.6 4.8 %collective-permute-start.24 = (bf16[128,320]{1,0:T(8,128)(2,1)S(1)}, bf16[128,320]{1,0:T(8,128)(2,1)S(1)}, u32[]{:S(2)}, u32[]{:S(2)}) collective-permute-start(bf16[128,320]{1,0:T(8,128)(2,1)S(1)} %get-tuple-element.41.refs_3_), channel_id=1, source_target_pairs={{0,4},{1,5},{2,6},{3,7},{4,0},{5,1},{6,2},{7,3},{8,12},{9,13},{10,... | collective-permute-start | bytes 245768 | tf_op jit(solution)/shard_map/ppermute | solution.py:26
  110.5 5.1 %collective-permute-start.26 = (bf16[2,64,320]{2,1,0:T(8,128)(2,1)S(1)}, bf16[2,64,320]{2,1,0:T(8,128)(2,1)S(1)}, u32[]{:S(2)}, u32[]{:S(2)}) collective-permute-start(bf16[2,64,320]{2,1,0:T(8,128)(2,1)S(1)} %get-tuple-element.44), channel_id=1, source_target_pairs={{0,1},{1,0},{2,3},{3,2},{4,5},{5,4},{6,7},{7,6},{8,9},{9,8},{10,11... | collective-permute-start | bytes 245768 | tf_op jit(solution)/shard_map/ppermute | solution.py:26
  112.8 5.4 %collective-permute-start.27 = (bf16[2,64,320]{2,1,0:T(8,128)(2,1)S(1)}, bf16[2,64,320]{2,1,0:T(8,128)(2,1)S(1)}, u32[]{:S(2)}, u32[]{:S(2)}) collective-permute-start(bf16[2,64,320]{2,1,0:T(8,128)(2,1)S(1)} %get-tuple-element.45), channel_id=1, source_target_pairs={{0,3},{1,2},{2,1},{3,0},{4,7},{5,6},{6,5},{7,4},{8,11},{9,10},{10,... | collective-permute-start | bytes 245768 | tf_op jit(solution)/shard_map/ppermute | solution.py:26
  113.3 6.1 %collective-permute-start.28 = (bf16[2,64,320]{2,1,0:T(8,128)(2,1)S(1)}, bf16[2,64,320]{2,1,0:T(8,128)(2,1)S(1)}, u32[]{:S(2)}, u32[]{:S(2)}) collective-permute-start(bf16[2,64,320]{2,1,0:T(8,128)(2,1)S(1)} %get-tuple-element.46), channel_id=1, source_target_pairs={{0,2},{1,3},{2,0},{3,1},{4,6},{5,7},{6,4},{7,5},{8,10},{9,11},{10,... | collective-permute-start | bytes 245768 | tf_op jit(solution)/shard_map/ppermute | solution.py:26

commit v7 on v6

--- a/solution.py
+++ b/solution.py
@@ -34,8 +34,12 @@
     return permute(value, lambda h, y, c, l, x: (h, y + d, c, l, x))
 
 
-def to_z(value, d):
-    return permute(value, lambda h, y, c, l, x: (h + d, y, c, l, x))
+def to_near_h(value):
+    return permute(value, lambda h, y, c, l, x: (near(h), y, c, l, x))
+
+
+def to_far_h(value):
+    return permute(value, lambda h, y, c, l, x: (far(h), y, c, l, x))
 
 
 def near(x):
@@ -106,19 +110,46 @@
     both[16:, :] = z2[:16, :]
 
 
-def project_kernel(cuts, first, count, *refs):
-    tiles, (w_ref, f_ref, out) = refs[:-3], refs[-3:]
+def load_kernel(first, w_hbm, f_ref, out, sems):
+    copies = []
+    for c in range(out.shape[0]):
+        for i in range(4):
+            at = pl.ds(i * 80, 80)
+            source, target = w_hbm.at[first + c, at, :], out.at[c, at, :]
+            copies.append((c, at, pltpu.make_async_copy(source, target, sems.at[c * 4 + i])))
+    for _, _, copy in copies:
+        copy.start()
+    for c, at, copy in copies:
+        copy.wait()
+        out[c, at, :] = out[c, at, :] * f_ref[first + c]
+
+
+def load(w_t, factor, first, count, after=()):
+    def run(*refs):
+        load_kernel(first, *refs[:2], *refs[-2:])
+
+    return pl.pallas_call(
+        run,
+        out_shape=like((count, *w_t.shape[1:])),
+        in_specs=[pl.BlockSpec(memory_space=pl.ANY), VMEM] + [VMEM] * len(after),
+        out_specs=VMEM,
+        scratch_shapes=[pltpu.SemaphoreType.DMA((count * 4,))],
+        compiler_params=pltpu.CompilerParams(vmem_limit_bytes=44 * 1024 * 1024),
+        cost_estimate=SMALL,
+    )(w_t, factor, *after)
+
+
+def project_kernel(cuts, *refs):
+    tiles, (w_ref, out) = refs[:-2], refs[-2:]
     tile = jnp.concatenate([tiles[i][lo:hi, :] for i, lo, hi in cuts], axis=0)
-    for c in range(count):
-        weff = w_ref[first + c] * f_ref[first + c]
-        part = lax.dot_general(weff, tile, BY_ROW, preferred_element_type=F32)
+    for c in range(w_ref.shape[0]):
+        part = lax.dot_general(w_ref[c], tile, BY_ROW, preferred_element_type=F32)
         out[c * 320 : (c + 1) * 320, :] = part.astype(BF16)
 
 
-def project(tiles, cuts, w_t, factor, first, count, after=()):
-    shape = (count * w_t.shape[1], sum(hi - lo for _, lo, hi in cuts))
-    kernel = functools.partial(project_kernel, cuts, first, count)
-    return call(kernel, like(shape), *tiles, w_t, factor, after=after)
+def project(tiles, cuts, weff, after=()):
+    shape = (weff.shape[0] * weff.shape[1], sum(hi - lo for _, lo, hi in cuts))
+    return call(functools.partial(project_kernel, cuts), like(shape), *tiles, weff, after=after)
 
 
 def grads_kernel(which, my, kv1, kv2, weight, moved, gate_t, up_t, down_t, out):
@@ -147,14 +178,23 @@
         out[...] = (own[at, :] + got[at, :].astype(F32)).astype(out.dtype)
 
 
-def sum_kernel(mine, a, b, c, total, rounded):
+def sum_kernel(mine, a, b, c, total, upper, lower):
     result = mine[...] + a[...].astype(F32) + b[...].astype(F32) + c[...].astype(F32)
     total[...] = result
-    rounded[...] = result.astype(BF16)
-
-
-def renorm_kernel(my, mine, a, b, c, gate_t, up_t, down_t, out):
-    total = mine[...] + a[...].astype(F32) + b[...].astype(F32) + c[...].astype(F32)
+    upper[...] = result[:40].astype(BF16)
+    lower[...] = result[40:].astype(BF16)
+
+
+def pair_kernel(mine, a, b, total, upper, lower):
+    total[:40, :] = mine[:40, :] + a[...].astype(F32)
+    total[40:, :] = mine[40:, :] + b[...].astype(F32)
+    upper[...] = total[:40, :].astype(BF16)
+    lower[...] = total[40:, :].astype(BF16)
+
+
+def renorm_kernel(my, mine, a, b, gate_t, up_t, down_t, out):
+    got = jnp.concatenate([a[...].astype(F32), b[...].astype(F32)], axis=0)
+    total = mine[...] + got
     mine_rows = pl.ds(pl.multiple_of(my[BLOCK], 16), 80)
     for i, old in enumerate((gate_t, up_t, down_t)):
         at = slice(i * 320, (i + 1) * 320)
@@ -272,9 +312,10 @@
     )
     moved = permute(sent, lambda h, y, c, l, x: (h - 1 if l else h + 1, y, c, l, x))
     old_t = [w[0].T for w in (fast_gate, fast_up, fast_down)]
-    plane, others = gather(tokens, (factor, weight, *old_t))
-    kv1 = project(plane, PLANE, w_t, factor, 1, 2, after=others[2:6])
-    kv2 = project(others, OTHERS, w_t, factor, 1, 2, after=(kv1,))
+    weff = load(w_t, factor, 1, 2, after=(weight, *old_t))
+    plane, others = gather(tokens, (weff,))
+    kv1 = project(plane, PLANE, weff, after=others[2:6])
+    kv2 = project(others, OTHERS, weff, after=(kv1,))
 
     grads = (my, kv1, kv2, weight, moved, *old_t)
     sent = call(
@@ -292,21 +333,16 @@
         halves_kernel, [like((80, 960))] * 3 + [like((80, 960), F32)], my, own, got, scalars=1
     )
     got = to_y(to2, 2), to_y(to1, 1), to_y(to3, 3)
-    mine, small = call(sum_kernel, [like((80, 960), F32), like((80, 960))], mine, *got)
-
-    got = to_z(small, 2), to_z(small, 1), to_z(small, 3)
+    weff_q = load(w_t, factor, 0, 1, after=(to1,))
+    parts = [like((80, 960), F32), like((40, 960)), like((40, 960))]
+    mine, upper, lower = call(sum_kernel, parts, mine, *got, after=(weff_q,))
+
+    got = to_near_h(upper), to_far_h(lower)
     cuts = PLANE + [(len(plane) + i, lo, hi) for i, lo, hi in OTHERS]
-    query = project(plane + others, cuts, w_t, factor, 0, 1, after=(small,))
-    block = call(
-        renorm_kernel,
-        like((80, 960)),
-        my,
-        mine,
-        *got,
-        *old_t,
-        scalars=1,
-        after=(query,),
-    )
+    query = project(plane + others, cuts, weff_q, after=(upper,))
+    mine, upper, lower = call(pair_kernel, parts, mine, *got, after=(query,))
+    got = to_far_h(upper), to_near_h(lower)
+    block = call(renorm_kernel, like((80, 960)), my, mine, *got, *old_t, scalars=1)
     column = jnp.concatenate([block, to_y(block, 2), to_y(block, 1), to_y(block, 3)], axis=0)
     other = to_core(column)
 

time: 121 us -> 113 us (0.934)
  local copies, waits for them, and re-layouts: 10.9 us -> 5.21 us
  Pallas kernels: 15.1 us -> 20.2 us
  starting transfers between devices: 59 us -> 54.7 us
  waiting for transfers between devices: 34.3 us -> 30.5 us
    unnamed x19 -> x15, local copies, waits for them, and re-layouts: 7.96 us -> 2.31 us
    pallas_call x0 -> x2, Pallas kernels: none -> 5 us  [load(): pl.pallas_call(run, out_shape=like((count, *w_t.shape[1:])), in_specs=[pl...]
    ppermute x29 -> x30, starting transfers between devices: 59 us -> 54.7 us  [permute(): return lax.ppermute(value, AXES, pairs)]
    ppermute x29 -> x30, waiting for transfers between devices: 34.3 us -> 30.5 us  [permute(): return lax.ppermute(value, AXES, pairs)]
    pallas_call x14 -> x15, Pallas kernels: 15.1 us -> 15.1 us  [call(): pl.pallas_call(run, out_shape=out_shape, in_specs=[SMEM] * scalars + [VME...]
  transfers between devices with their start and end apart: 29 -> 30, of which waited for: 16 -> 16; matrix products, arithmetic and copies ran while one was open for 4% -> 4% of each run, Pallas kernels for 8% -> 13%
where the time goes in v7:
time: 113 us; the launch traced here: 112 us
  starting transfers between devices  54.7 us (48%)
  waiting for transfers between devices  30.5 us (27%)
  Pallas kernels  20.2 us (18%)
  local copies, waits for them, and re-layouts  5.21 us (5%)
    ppermute x30, starting transfers between devices, permute(): return lax.ppermute(value, AXES, pairs)  54.7 us
    ppermute x30, waiting for transfers between devices, permute(): return lax.ppermute(value, AXES, pairs)  30.5 us
    pallas_call x15, Pallas kernels, call(): pl.pallas_call(run, out_shape=out_shape, in_specs=[SMEM] * scalars + [VME...  15.1 us
    pallas_call x2, Pallas kernels, load(): pl.pallas_call(run, out_shape=like((count, *w_t.shape[1:])), in_specs=[pl...  5 us
    unnamed x15, local copies, waits for them, and re-layouts  2.31 us
  transfers between devices with their start and end apart: 30, of which 16 were waited for; matrix products, arithmetic and copies ran while one was open for 4% of the time, Pallas kernels for 13%

profile of v7, /device:TPU:2, one launch (start us, length us, event | category | flops | bytes accessed | tf_op | source)
XLA Modules:
  0.0 112.2 jit_solution(15802125165463314512)
XLA Ops:
  0.0 0.8 dynamic-slice_bitcast_fusion.refs_0_
  0.8 1.5 %collective-permute-start.1 = (bf16[64,5120]{1,0:T(8,128)(2,1)}, bf16[64,5120]{1,0:T(8,128)(2,1)S(1)}, u32[]{:S(2)}, u32[]{:S(2)}) collective-permute-start(bf16[64,5120]{1,0:T(8,128)(2,1)} %refs_0_.1), channel_id=1, source_target_pairs={{0,3},{1,2},{2,1},{3,0},{4,7},{5,6},{6,5},{7,4},{8,11},{9,10},{10,... | collective-permute-start | bytes 1966088 | tf_op jit(solution)/shard_map/ppermute | solution.py:26
  2.3 1.8 %collective-permute-start = (bf16[64,5120]{1,0:T(8,128)(2,1)}, bf16[64,5120]{1,0:T(8,128)(2,1)S(1)}, u32[]{:S(2)}, u32[]{:S(2)}) collective-permute-start(bf16[64,5120]{1,0:T(8,128)(2,1)} %refs_0_.1), channel_id=1, source_target_pairs={{0,1},{1,0},{2,3},{3,2},{4,5},{5,4},{6,7},{7,6},{8,9},{9,8},{10,11... | collective-permute-start | bytes 1966088 | tf_op jit(solution)/shard_map/ppermute | solution.py:26
  4.1 1.9 %fusion = (bf16[32,5120]{1,0:T(8,128)(2,1)}, bf16[32,5120]{1,0:T(8,128)(2,1)}) fusion(bf16[64,5120]{1,0:T(8,128)(2,1)} %refs_0_.1), kind=kLoop, calls=%fused_computation.4 | loop fusion | bytes 1310720 | tf_op jit(solution)/shard_map/slice | solution.py:230
  6.0 5.9 %collective-permute-start.3 = (bf16[32,5120]{1,0:T(8,128)(2,1)}, bf16[32,5120]{1,0:T(8,128)(2,1)S(1)}, u32[]{:S(2)}, u32[]{:S(2)}) collective-permute-start(bf16[32,5120]{1,0:T(8,128)(2,1)} %get-tuple-element.55), channel_id=1, source_target_pairs={{0,196},{1,197},{2,198},{3,199},{4,64},{5,65},{6,66},{7,67},{8,204... | collective-permute-start | bytes 983048 | tf_op jit(solution)/shard_map/ppermute | solution.py:26
  12.6 0.5 broadcast.3
  13.0 0.6 reduce.3
  13.7 0.6 shard_map.91
  14.3 0.1 broadcast_in_dim.3
  14.5 0.3 copy.13
  14.7 0.3 copy.14
  15.0 1.3 %copy.15 = bf16[1,320,640]{1,2,0:T(8,128)(2,1)S(1)} copy(bf16[1,320,640]{2,1,0:T(8,128)(2,1)} %param.16) | data formatting | bytes 819200 | tf_op args[7]
  16.3 3.0 %shard_map.92.refs_4_.refs_5_.refs_8_ = bf16[2,320,5120]{2,1,0:T(8,128)(2,1)S(1)} custom-call(bf16[3,320,5120]{2,1,0:T(8,128)(2,1)} %bitcast.28, bf16[3,1,5120]{2,1,0:T(2,128)(2,1)S(1)} %broadcast_in_dim_reshape.4.refs_1_, f32[1,384]{1,0:T(1,128)S(1)} %get-tuple-element.32.refs_2_.refs_3_, bf16[640,320]{1,0:T(8,128)(2,1)S(1)} %bitcast.16, ...), custom_call_target="tpu_custom_call" | custom-call | flops 1000 | bytes 1000 | tf_op jit(solution)/shard_map/pallas_call | solution.py:131
  19.3 1.4 %collective-permute-done.2.refs_2_.refs_0_.refs_5_ = bf16[32,5120]{1,0:T(8,128)(2,1)S(1)} collective-permute-done((bf16[32,5120]{1,0:T(8,128)(2,1)}, bf16[32,5120]{1,0:T(8,128)(2,1)S(1)}, u32[]{:S(2)}, u32[]{:S(2)}) %collective-permute-start.2) | collective-permute-done | bytes 327712 | tf_op jit(solution)/shard_map/ppermute | solution.py:26
  20.7 0.1 shard_map.93
  20.8 0.1 collective-permute-start.4
  20.9 1.4 %collective-permute-start.5 = (bf16[32,5120]{1,0:T(8,128)(2,1)S(1)}, bf16[32,5120]{1,0:T(8,128)(2,1)S(1)}, u32[]{:S(2)}, u32[]{:S(2)}) collective-permute-start(bf16[32,5120]{1,0:T(8,128)(2,1)S(1)} %get-tuple-element.34), channel_id=1, source_target_pairs={{0,1},{1,0},{2,3},{3,2},{4,5},{5,4},{6,7},{7,6},{8,9},{9,8},{10,11... | collective-permute-start | bytes 983048 | tf_op jit(solution)/shard_map/ppermute | solution.py:26
  22.3 1.8 %collective-permute-start.8 = (bf16[32,5120]{1,0:T(8,128)(2,1)S(1)}, bf16[32,5120]{1,0:T(8,128)(2,1)S(1)}, u32[]{:S(2)}, u32[]{:S(2)}) collective-permute-start(bf16[32,5120]{1,0:T(8,128)(2,1)S(1)} %get-tuple-element.36), channel_id=1, source_target_pairs={{0,4},{1,5},{2,6},{3,7},{4,0},{5,1},{6,2},{7,3},{8,12},{9,13},{10,... | collective-permute-start | bytes 983048 | tf_op jit(solution)/shard_map/ppermute | solution.py:26
  24.1 4.9 %collective-permute-start.9 = (bf16[32,5120]{1,0:T(8,128)(2,1)S(1)}, bf16[32,5120]{1,0:T(8,128)(2,1)S(1)}, u32[]{:S(2)}, u32[]{:S(2)}) collective-permute-start(bf16[32,5120]{1,0:T(8,128)(2,1)S(1)} %get-tuple-element.37), channel_id=1, source_target_pairs={{0,196},{1,197},{2,198},{3,199},{4,64},{5,65},{6,66},{7,67},{8,204... | collective-permute-start | bytes 983048 | tf_op jit(solution)/shard_map/ppermute | solution.py:26
  29.1 1.1 %collective-permute-start.7 = (bf16[32,5120]{1,0:T(8,128)(2,1)S(1)}, bf16[32,5120]{1,0:T(8,128)(2,1)S(1)}, u32[]{:S(2)}, u32[]{:S(2)}) collective-permute-start(bf16[32,5120]{1,0:T(8,128)(2,1)S(1)} %get-tuple-element.35), channel_id=1, source_target_pairs={{0,3},{1,2},{2,1},{3,0},{4,7},{5,6},{6,5},{7,4},{8,11},{9,10},{10,... | collective-permute-start | bytes 983048 | tf_op jit(solution)/shard_map/ppermute | solution.py:26
  30.2 0.6 collective-permute-start.6
  30.8 3.4 %collective-permute-start.10 = (bf16[32,5120]{1,0:T(8,128)(2,1)S(1)}, bf16[32,5120]{1,0:T(8,128)(2,1)S(1)}, u32[]{:S(2)}, u32[]{:S(2)}) collective-permute-start(bf16[32,5120]{1,0:T(8,128)(2,1)S(1)} %collective-permute-done.4.refs_3_), channel_id=1, source_target_pairs={{0,4},{1,5},{2,6},{3,7},{4,0},{5,1},{6,2},{7,3},{8,12},{9,13},{10,... | collective-permute-start | bytes 983048 | tf_op jit(solution)/shard_map/ppermute | solution.py:26
  34.2 5.2 %collective-permute-start.11 = (bf16[32,5120]{1,0:T(8,128)(2,1)S(1)}, bf16[32,5120]{1,0:T(8,128)(2,1)S(1)}, u32[]{:S(2)}, u32[]{:S(2)}) collective-permute-start(bf16[32,5120]{1,0:T(8,128)(2,1)S(1)} %collective-permute-done.5.refs_4_), channel_id=1, source_target_pairs={{0,196},{1,197},{2,198},{3,199},{4,64},{5,65},{6,66},{7,67},{8,204... | collective-permute-start | bytes 983048 | tf_op jit(solution)/shard_map/ppermute | solution.py:26
  39.5 1.9 %shard_map.94.refs_9_.refs_1_ = bf16[640,256]{1,0:T(8,128)(2,1)S(1)} custom-call(bf16[64,5120]{1,0:T(8,128)(2,1)S(1)} %copy-done, bf16[64,5120]{1,0:T(8,128)(2,1)S(1)} %collective-permute-done.refs_0_.refs_1_, bf16[64,5120]{1,0:T(8,128)(2,1)S(1)} %collective-permute-done.1.refs_1_.refs_2_, bf16[32,5120]{1,0:T(8,128)(2,1)S(1)} %collective-permute-done.4.refs_3_, ...), custom_call_target="tpu_custom_call" | custom-call | flops 1000 | bytes 1000 | tf_op jit(solution)/shard_map/pallas_call | solution.py:91
  41.4 3.1 %collective-permute-done.11.refs_7_.refs_12_ = bf16[32,5120]{1,0:T(8,128)(2,1)S(1)} collective-permute-done((bf16[32,5120]{1,0:T(8,128)(2,1)S(1)}, bf16[32,5120]{1,0:T(8,128)(2,1)S(1)}, u32[]{:S(2)}, u32[]{:S(2)}) %collective-permute-start.11) | collective-permute-done | bytes 327712 | tf_op jit(solution)/shard_map/ppermute | solution.py:26
  44.5 1.9 %shard_map.95.refs_2_ = bf16[640,256]{1,0:T(8,128)(2,1)S(1)} custom-call(bf16[32,5120]{1,0:T(8,128)(2,1)S(1)} %collective-permute-done.2.refs_2_.refs_0_.refs_5_, bf16[32,5120]{1,0:T(8,128)(2,1)S(1)} %collective-permute-done.3.refs_3_.refs_1_.refs_6_, bf16[32,5120]{1,0:T(8,128)(2,1)S(1)} %collective-permute-done.6.refs_6_.refs_2_.refs_7_, ...), custom_call_target="tpu_custom_call" | custom-call | flops 1000 | bytes 1000 | tf_op jit(solution)/shard_map/pallas_call | solution.py:91
  46.4 1.9 %shard_map.96.refs_8_ = bf16[320,960]{1,0:T(8,128)(2,1)S(1)} custom-call(s32[32]{0:T(128)S(1)} %dynamic-slice_bitcast_fusion.refs_0_, bf16[640,256]{1,0:T(8,128)(2,1)S(1)} %shard_map.94.refs_9_.refs_1_, bf16[640,256]{1,0:T(8,128)(2,1)S(1)} %shard_map.95.refs_2_, f32[1,384]{1,0:T(1,128)S(1)} %get-tuple-element.32.refs_2_.refs_3_, ...), custom_call_target="tpu_custom_call" | custom-call | flops 1000 | bytes 1000 | tf_op jit(solution)/shard_map/pallas_call | solution.py:91
  48.3 0.1 collective-permute-start.13
  48.4 1.9 %shard_map.97.refs_1_ = f32[320,960]{1,0:T(8,128)S(1)} custom-call(s32[32]{0:T(128)S(1)} %dynamic-slice_bitcast_fusion.refs_0_, bf16[640,256]{1,0:T(8,128)(2,1)S(1)} %shard_map.94.refs_9_.refs_1_, bf16[640,256]{1,0:T(8,128)(2,1)S(1)} %shard_map.95.refs_2_, f32[1,384]{1,0:T(1,128)S(1)} %get-tuple-element.32.refs_2_.refs_3_, ...), custom_call_target="tpu_custom_call" | custom-call | flops 1000 | bytes 1000 | tf_op jit(solution)/shard_map/pallas_call | solution.py:91
  50.3 0.2 collective-permute-done.13.refs_2_
  50.5 0.7 shard_map.98
  51.2 3.3 %collective-permute-start.14 = (bf16[80,960]{1,0:T(8,128)(2,1)S(1)}, bf16[80,960]{1,0:T(8,128)(2,1)S(1)}, u32[]{:S(2)}, u32[]{:S(2)}) collective-permute-start(bf16[80,960]{1,0:T(8,128)(2,1)S(1)} %get-tuple-element.41), channel_id=1, source_target_pairs={{0,32},{1,33},{2,34},{3,35},{4,36},{5,37},{6,38},{7,39},{8,40},{9,... | collective-permute-start | bytes 460808 | tf_op jit(solution)/shard_map/ppermute | solution.py:26
  54.4 1.1 collective-permute-start.16
  55.5 1.0 collective-permute-start.15
  56.5 2.0 %shard_map.99.refs_4_.refs_13_ = bf16[1,320,5120]{2,1,0:T(8,128)(2,1)S(1)} custom-call(bf16[3,320,5120]{2,1,0:T(8,128)(2,1)} %bitcast.29, bf16[3,1,5120]{2,1,0:T(2,128)(2,1)S(1)} %broadcast_in_dim_reshape.4.refs_1_, bf16[80,960]{1,0:T(8,128)(2,1)S(1)} %get-tuple-element.39.refs_2_), custom_call_target="tpu_custom_call" | custom-call | flops 1000 | bytes 1000 | tf_op jit(solution)/shard_map/pallas_call | solution.py:131
  58.5 1.3 %collective-permute-done.14.refs_1_ = bf16[80,960]{1,0:T(8,128)(2,1)S(1)} collective-permute-done((bf16[80,960]{1,0:T(8,128)(2,1)S(1)}, bf16[80,960]{1,0:T(8,128)(2,1)S(1)}, u32[]{:S(2)}, u32[]{:S(2)}) %collective-permute-start.14) | collective-permute-done | bytes 153632 | tf_op jit(solution)/shard_map/ppermute | solution.py:26
  59.8 3.3 %collective-permute-done.16.refs_3_ = bf16[80,960]{1,0:T(8,128)(2,1)S(1)} collective-permute-done((bf16[80,960]{1,0:T(8,128)(2,1)S(1)}, bf16[80,960]{1,0:T(8,128)(2,1)S(1)}, u32[]{:S(2)}, u32[]{:S(2)}) %collective-permute-start.16) | collective-permute-done | bytes 153632 | tf_op jit(solution)/shard_map/ppermute | solution.py:26
  63.2 2.6 %collective-permute-start.18 = (bf16[40,960]{1,0:T(8,128)(2,1)S(1)}, bf16[40,960]{1,0:T(8,128)(2,1)S(1)}, u32[]{:S(2)}, u32[]{:S(2)}) collective-permute-start(bf16[40,960]{1,0:T(8,128)(2,1)S(1)} %get-tuple-element.45), channel_id=1, source_target_pairs={{0,192},{1,193},{2,194},{3,195},{4,196},{5,197},{6,198},{7,199},{8... | collective-permute-start | bytes 230408 | tf_op jit(solution)/shard_map/ppermute | solution.py:26
  65.8 2.7 %collective-permute-start.17 = (bf16[40,960]{1,0:T(8,128)(2,1)S(1)}, bf16[40,960]{1,0:T(8,128)(2,1)S(1)}, u32[]{:S(2)}, u32[]{:S(2)}) collective-permute-start(bf16[40,960]{1,0:T(8,128)(2,1)S(1)} %get-tuple-element.43.refs_14_), channel_id=1, source_target_pairs={{0,64},{1,65},{2,66},{3,67},{4,68},{5,69},{6,70},{7,71},{8,72},{9,... | collective-permute-start | bytes 230408 | tf_op jit(solution)/shard_map/ppermute | solution.py:26
  68.4 1.9 %shard_map.101.refs_3_.refs_0_ = bf16[320,512]{1,0:T(8,128)(2,1)S(1)} custom-call(bf16[64,5120]{1,0:T(8,128)(2,1)S(1)} %copy-done, bf16[64,5120]{1,0:T(8,128)(2,1)S(1)} %collective-permute-done.refs_0_.refs_1_, bf16[64,5120]{1,0:T(8,128)(2,1)S(1)} %collective-permute-done.1.refs_1_.refs_2_, bf16[32,5120]{1,0:T(8,128)(2,1)S(1)} %collective-permute-done.4.refs_3_, ...), custom_call_target="tpu_custom_call" | custom-call | flops 1000 | bytes 1000 | tf_op jit(solution)/shard_map/pallas_call | solution.py:91
  70.3 0.8 collective-permute-done.18.refs_2_
  71.1 1.7 %collective-permute-done.17.refs_1_ = bf16[40,960]{1,0:T(8,128)(2,1)S(1)} collective-permute-done((bf16[40,960]{1,0:T(8,128)(2,1)S(1)}, bf16[40,960]{1,0:T(8,128)(2,1)S(1)}, u32[]{:S(2)}, u32[]{:S(2)}) %collective-permute-start.17) | collective-permute-done | bytes 76832 | tf_op jit(solution)/shard_map/ppermute | solution.py:26
  72.9 0.9 collective-permute-start.19
  73.8 2.4 %collective-permute-start.20 = (bf16[40,960]{1,0:T(8,128)(2,1)S(1)}, bf16[40,960]{1,0:T(8,128)(2,1)S(1)}, u32[]{:S(2)}, u32[]{:S(2)}) collective-permute-start(bf16[40,960]{1,0:T(8,128)(2,1)S(1)} %get-tuple-element.48), channel_id=1, source_target_pairs={{0,64},{1,65},{2,66},{3,67},{4,68},{5,69},{6,70},{7,71},{8,72},{9,... | collective-permute-start | bytes 230408 | tf_op jit(solution)/shard_map/ppermute | solution.py:26
  76.2 3.7 %collective-permute-done.19.refs_2_ = bf16[40,960]{1,0:T(8,128)(2,1)S(1)} collective-permute-done((bf16[40,960]{1,0:T(8,128)(2,1)S(1)}, bf16[40,960]{1,0:T(8,128)(2,1)S(1)}, u32[]{:S(2)}, u32[]{:S(2)}) %collective-permute-start.19) | collective-permute-done | bytes 76832 | tf_op jit(solution)/shard_map/ppermute | solution.py:26
  80.0 0.9 shard_map.103
  80.8 3.2 %collective-permute-start.23 = (bf16[80,960]{1,0:T(8,128)(2,1)S(1)}, bf16[80,960]{1,0:T(8,128)(2,1)S(1)}, u32[]{:S(2)}, u32[]{:S(2)}) collective-permute-start(bf16[80,960]{1,0:T(8,128)(2,1)S(1)} %shard_map.103), channel_id=1, source_target_pairs={{0,48},{1,49},{2,50},{3,51},{4,52},{5,53},{6,54},{7,55},{8,56},{9,... | collective-permute-start | bytes 460808 | tf_op jit(solution)/shard_map/ppermute | solution.py:26
  84.0 2.2 %collective-permute-start.21 = (bf16[80,960]{1,0:T(8,128)(2,1)S(1)}, bf16[80,960]{1,0:T(8,128)(2,1)S(1)}, u32[]{:S(2)}, u32[]{:S(2)}) collective-permute-start(bf16[80,960]{1,0:T(8,128)(2,1)S(1)} %shard_map.103), channel_id=1, source_target_pairs={{0,32},{1,33},{2,34},{3,35},{4,36},{5,37},{6,38},{7,39},{8,40},{9,... | collective-permute-start | bytes 460808 | tf_op jit(solution)/shard_map/ppermute | solution.py:26
  86.2 2.3 %collective-permute-done.23 = bf16[80,960]{1,0:T(8,128)(2,1)S(1)} collective-permute-done((bf16[80,960]{1,0:T(8,128)(2,1)S(1)}, bf16[80,960]{1,0:T(8,128)(2,1)S(1)}, u32[]{:S(2)}, u32[]{:S(2)}) %collective-permute-start.23) | collective-permute-done | bytes 153632 | tf_op jit(solution)/shard_map/ppermute | solution.py:26
  88.5 3.8 %collective-permute-done.22 = bf16[80,960]{1,0:T(8,128)(2,1)S(1)} collective-permute-done((bf16[80,960]{1,0:T(8,128)(2,1)S(1)}, bf16[80,960]{1,0:T(8,128)(2,1)S(1)}, u32[]{:S(2)}, u32[]{:S(2)}) %collective-permute-start.22) | collective-permute-done | bytes 153632 | tf_op jit(solution)/shard_map/ppermute | solution.py:26
  92.4 0.1 collective-permute-start.24
  92.5 2.1 %collective-permute-done.24.refs_2_ = bf16[320,960]{1,0:T(8,128)(2,1)S(1)} collective-permute-done((bf16[320,960]{1,0:T(8,128)(2,1)S(1)}, bf16[320,960]{1,0:T(8,128)(2,1)S(1)}, u32[]{:S(2)}, u32[]{:S(2)}) %collective-permute-start.24) | collective-permute-done | bytes 614432 | tf_op jit(solution)/shard_map/ppermute | solution.py:26
  94.6 0.9 shard_map.104
  95.5 3.4 %collective-permute-start.26 = (bf16[128,320]{1,0:T(8,128)(2,1)S(1)}, bf16[128,320]{1,0:T(8,128)(2,1)S(1)}, u32[]{:S(2)}, u32[]{:S(2)}) collective-permute-start(bf16[128,320]{1,0:T(8,128)(2,1)S(1)} %get-tuple-element.50), channel_id=1, source_target_pairs={{0,196},{1,197},{2,198},{3,199},{4,64},{5,65},{6,66},{7,67},{8,204... | collective-permute-start | bytes 245768 | tf_op jit(solution)/shard_map/ppermute | solution.py:26
  98.9 0.9 shard_map.105.refs_0_
  99.9 2.2 %collective-permute-done.26.refs_2_ = bf16[128,320]{1,0:T(8,128)(2,1)S(1)} collective-permute-done((bf16[128,320]{1,0:T(8,128)(2,1)S(1)}, bf16[128,320]{1,0:T(8,128)(2,1)S(1)}, u32[]{:S(2)}, u32[]{:S(2)}) %collective-permute-start.26) | collective-permute-done | bytes 81952 | tf_op jit(solution)/shard_map/ppermute | solution.py:26
  102.0 1.5 %collective-permute-done.25.refs_1_ = bf16[128,320]{1,0:T(8,128)(2,1)S(1)} collective-permute-done((bf16[128,320]{1,0:T(8,128)(2,1)S(1)}, bf16[128,320]{1,0:T(8,128)(2,1)S(1)}, u32[]{:S(2)}, u32[]{:S(2)}) %collective-permute-start.25) | collective-permute-done | bytes 81952 | tf_op jit(solution)/shard_map/ppermute | solution.py:26
  103.6 0.1 collective-permute-start.27
  103.7 1.0 collective-permute-start.28
  104.7 3.1 %collective-permute-start.29 = (bf16[2,64,320]{2,1,0:T(8,128)(2,1)S(1)}, bf16[2,64,320]{2,1,0:T(8,128)(2,1)S(1)}, u32[]{:S(2)}, u32[]{:S(2)}) collective-permute-start(bf16[2,64,320]{2,1,0:T(8,128)(2,1)S(1)} %get-tuple-element.54), channel_id=1, source_target_pairs={{0,2},{1,3},{2,0},{3,1},{4,6},{5,7},{6,4},{7,5},{8,10},{9,11},{10,... | collective-permute-start | bytes 245768 | tf_op jit(solution)/shard_map/ppermute | solution.py:26
  107.8 1.2 %collective-permute-done.27.refs_2_ = bf16[2,64,320]{2,1,0:T(8,128)(2,1)S(1)} collective-permute-done((bf16[2,64,320]{2,1,0:T(8,128)(2,1)S(1)}, bf16[2,64,320]{2,1,0:T(8,128)(2,1)S(1)}, u32[]{:S(2)}, u32[]{:S(2)}) %collective-permute-start.27) | collective-permute-done | bytes 81952 | tf_op jit(solution)/shard_map/ppermute | solution.py:26
  109.0 0.3 collective-permute-done.28.refs_3_
  109.3 1.5 %collective-permute-done.29.refs_4_ = bf16[2,64,320]{2,1,0:T(8,128)(2,1)S(1)} collective-permute-done((bf16[2,64,320]{2,1,0:T(8,128)(2,1)S(1)}, bf16[2,64,320]{2,1,0:T(8,128)(2,1)S(1)}, u32[]{:S(2)}, u32[]{:S(2)}) %collective-permute-start.29) | collective-permute-done | bytes 81952 | tf_op jit(solution)/shard_map/ppermute | solution.py:26
  110.8 1.4 %shard_map.107 = bf16[64,2560]{1,0:T(8,128)(2,1)} custom-call(s32[32]{0:T(128)S(1)} %dynamic-slice_bitcast_fusion.refs_0_, bf16[2,64,320]{2,1,0:T(8,128)(2,1)S(1)} %get-tuple-element.51.refs_1_, bf16[2,64,320]{2,1,0:T(8,128)(2,1)S(1)} %collective-permute-done.27.refs_2_, bf16[2,64,320]{2,1,0:T(8,128)(2,1)S(1)} %collective-permute-done.28.refs_3_, ...), custom_call_target="tpu_custom_call" | custom-call | flops 1000 | bytes 1000 | tf_op jit(solution)/shard_map/pallas_call | solution.py:91
  (36 shorter events, 0.4 us)
Async XLA Ops:
  0.0 13.0 %copy-start.3 = (s32[512,1]{0,1:T(1,128)S(1)}, s32[512,1]{0,1:T(1,128)}, u32[]{:S(2)}) copy-start(s32[512,1]{0,1:T(1,128)} %param.12) | copy-start | bytes 6148
  0.0 14.3 %copy-start.4 = (s32[3,40,1]{1,2,0:T(1,128)S(1)}, s32[3,40,1]{1,2,0:T(1,128)}, u32[]{:S(2)}) copy-start(s32[3,40,1]{1,2,0:T(1,128)} %param.11) | copy-start | bytes 1444
  0.0 14.5 %copy-start.1 = (bf16[1,320,640]{2,1,0:T(8,128)(2,1)S(1)}, bf16[1,320,640]{2,1,0:T(8,128)(2,1)}, u32[]{:S(2)}) copy-start(bf16[1,320,640]{2,1,0:T(8,128)(2,1)} %param.14) | copy-start | bytes 1228804
  0.0 14.7 %copy-start.2 = (bf16[1,320,640]{2,1,0:T(8,128)(2,1)S(1)}, bf16[1,320,640]{2,1,0:T(8,128)(2,1)}, u32[]{:S(2)}) copy-start(bf16[1,320,640]{2,1,0:T(8,128)(2,1)} %param.15) | copy-start | bytes 1228804
  0.8 19.9 %collective-permute-start.1 = (bf16[64,5120]{1,0:T(8,128)(2,1)}, bf16[64,5120]{1,0:T(8,128)(2,1)S(1)}, u32[]{:S(2)}, u32[]{:S(2)}) collective-permute-start(bf16[64,5120]{1,0:T(8,128)(2,1)} %refs_0_.1), channel_id=1, source_target_pairs={{0,3},{1,2},{2,1},{3,0},{4,7},{5,6},{6,5},{7,4},{8,11},{9,10},{10,... | collective-permute-start | bytes 1966088 | tf_op jit(solution)/shard_map/ppermute | solution.py:26
  2.3 18.4 %collective-permute-start = (bf16[64,5120]{1,0:T(8,128)(2,1)}, bf16[64,5120]{1,0:T(8,128)(2,1)S(1)}, u32[]{:S(2)}, u32[]{:S(2)}) collective-permute-start(bf16[64,5120]{1,0:T(8,128)(2,1)} %refs_0_.1), channel_id=1, source_target_pairs={{0,1},{1,0},{2,3},{3,2},{4,5},{5,4},{6,7},{7,6},{8,9},{9,8},{10,11... | collective-permute-start | bytes 1966088 | tf_op jit(solution)/shard_map/ppermute | solution.py:26
  6.0 13.3 %collective-permute-start.3 = (bf16[32,5120]{1,0:T(8,128)(2,1)}, bf16[32,5120]{1,0:T(8,128)(2,1)S(1)}, u32[]{:S(2)}, u32[]{:S(2)}) collective-permute-start(bf16[32,5120]{1,0:T(8,128)(2,1)} %get-tuple-element.55), channel_id=1, source_target_pairs={{0,196},{1,197},{2,198},{3,199},{4,64},{5,65},{6,66},{7,67},{8,204... | collective-permute-start | bytes 983048 | tf_op jit(solution)/shard_map/ppermute | solution.py:26
  11.9 8.8 %collective-permute-start.2 = (bf16[32,5120]{1,0:T(8,128)(2,1)}, bf16[32,5120]{1,0:T(8,128)(2,1)S(1)}, u32[]{:S(2)}, u32[]{:S(2)}) collective-permute-start(bf16[32,5120]{1,0:T(8,128)(2,1)} %get-tuple-element.56), channel_id=1, source_target_pairs={{0,4},{1,5},{2,6},{3,7},{4,0},{5,1},{6,2},{7,3},{8,12},{9,13},{10,... | collective-permute-start | bytes 983048 | tf_op jit(solution)/shard_map/ppermute | solution.py:26
  19.3 20.1 %copy-start = (bf16[64,5120]{1,0:T(8,128)(2,1)S(1)}, bf16[64,5120]{1,0:T(8,128)(2,1)}, u32[]{:S(2)}) copy-start(bf16[64,5120]{1,0:T(8,128)(2,1)} %refs_0_.1) | copy-start | bytes 1966084
  20.8 9.4 %collective-permute-start.4 = (bf16[32,5120]{1,0:T(8,128)(2,1)S(1)}, bf16[32,5120]{1,0:T(8,128)(2,1)S(1)}, u32[]{:S(2)}, u32[]{:S(2)}) collective-permute-start(bf16[32,5120]{1,0:T(8,128)(2,1)S(1)} %get-tuple-element.33), channel_id=1, source_target_pairs={{0,3},{1,2},{2,1},{3,0},{4,7},{5,6},{6,5},{7,4},{8,11},{9,10},{10,... | collective-permute-start | bytes 983048 | tf_op jit(solution)/shard_map/ppermute | solution.py:26
  20.9 9.9 %collective-permute-start.5 = (bf16[32,5120]{1,0:T(8,128)(2,1)S(1)}, bf16[32,5120]{1,0:T(8,128)(2,1)S(1)}, u32[]{:S(2)}, u32[]{:S(2)}) collective-permute-start(bf16[32,5120]{1,0:T(8,128)(2,1)S(1)} %get-tuple-element.34), channel_id=1, source_target_pairs={{0,1},{1,0},{2,3},{3,2},{4,5},{5,4},{6,7},{7,6},{8,9},{9,8},{10,11... | collective-permute-start | bytes 983048 | tf_op jit(solution)/shard_map/ppermute | solution.py:26
  22.3 11.9 %collective-permute-start.8 = (bf16[32,5120]{1,0:T(8,128)(2,1)S(1)}, bf16[32,5120]{1,0:T(8,128)(2,1)S(1)}, u32[]{:S(2)}, u32[]{:S(2)}) collective-permute-start(bf16[32,5120]{1,0:T(8,128)(2,1)S(1)} %get-tuple-element.36), channel_id=1, source_target_pairs={{0,4},{1,5},{2,6},{3,7},{4,0},{5,1},{6,2},{7,3},{8,12},{9,13},{10,... | collective-permute-start | bytes 983048 | tf_op jit(solution)/shard_map/ppermute | solution.py:26
  24.1 15.3 %collective-permute-start.9 = (bf16[32,5120]{1,0:T(8,128)(2,1)S(1)}, bf16[32,5120]{1,0:T(8,128)(2,1)S(1)}, u32[]{:S(2)}, u32[]{:S(2)}) collective-permute-start(bf16[32,5120]{1,0:T(8,128)(2,1)S(1)} %get-tuple-element.37), channel_id=1, source_target_pairs={{0,196},{1,197},{2,198},{3,199},{4,64},{5,65},{6,66},{7,67},{8,204... | collective-permute-start | bytes 983048 | tf_op jit(solution)/shard_map/ppermute | solution.py:26
  29.1 10.4 %collective-permute-start.7 = (bf16[32,5120]{1,0:T(8,128)(2,1)S(1)}, bf16[32,5120]{1,0:T(8,128)(2,1)S(1)}, u32[]{:S(2)}, u32[]{:S(2)}) collective-permute-start(bf16[32,5120]{1,0:T(8,128)(2,1)S(1)} %get-tuple-element.35), channel_id=1, source_target_pairs={{0,3},{1,2},{2,1},{3,0},{4,7},{5,6},{6,5},{7,4},{8,11},{9,10},{10,... | collective-permute-start | bytes 983048 | tf_op jit(solution)/shard_map/ppermute | solution.py:26
  30.2 9.2 %collective-permute-start.6 = (bf16[32,5120]{1,0:T(8,128)(2,1)S(1)}, bf16[32,5120]{1,0:T(8,128)(2,1)S(1)}, u32[]{:S(2)}, u32[]{:S(2)}) collective-permute-start(bf16[32,5120]{1,0:T(8,128)(2,1)S(1)} %get-tuple-element.35), channel_id=1, source_target_pairs={{0,1},{1,0},{2,3},{3,2},{4,5},{5,4},{6,7},{7,6},{8,9},{9,8},{10,11... | collective-permute-start | bytes 983048 | tf_op jit(solution)/shard_map/ppermute | solution.py:26
  30.8 10.5 %collective-permute-start.10 = (bf16[32,5120]{1,0:T(8,128)(2,1)S(1)}, bf16[32,5120]{1,0:T(8,128)(2,1)S(1)}, u32[]{:S(2)}, u32[]{:S(2)}) collective-permute-start(bf16[32,5120]{1,0:T(8,128)(2,1)S(1)} %collective-permute-done.4.refs_3_), channel_id=1, source_target_pairs={{0,4},{1,5},{2,6},{3,7},{4,0},{5,1},{6,2},{7,3},{8,12},{9,13},{10,... | collective-permute-start | bytes 983048 | tf_op jit(solution)/shard_map/ppermute | solution.py:26
  34.2 10.2 %collective-permute-start.11 = (bf16[32,5120]{1,0:T(8,128)(2,1)S(1)}, bf16[32,5120]{1,0:T(8,128)(2,1)S(1)}, u32[]{:S(2)}, u32[]{:S(2)}) collective-permute-start(bf16[32,5120]{1,0:T(8,128)(2,1)S(1)} %collective-permute-done.5.refs_4_), channel_id=1, source_target_pairs={{0,196},{1,197},{2,198},{3,199},{4,64},{5,65},{6,66},{7,67},{8,204... | collective-permute-start | bytes 983048 | tf_op jit(solution)/shard_map/ppermute | solution.py:26
  39.4 6.9 %collective-permute-start.12 = (f32[1,128]{1,0:T(1,128)S(1)}, f32[1,128]{1,0:T(1,128)S(1)}, u32[]{:S(2)}, u32[]{:S(2)}) collective-permute-start(f32[1,128]{1,0:T(1,128)S(1)} %get-tuple-element.38), channel_id=1, source_target_pairs={{0,64},{1,65},{2,66},{3,67},{4,196},{5,197},{6,198},{7,199},{8,72}... | collective-permute-start | bytes 1544 | tf_op jit(solution)/shard_map/ppermute | solution.py:26
  48.3 2.2 %collective-permute-start.13 = (bf16[320,960]{1,0:T(8,128)(2,1)S(1)}, bf16[320,960]{1,0:T(8,128)(2,1)S(1)}, u32[]{:S(2)}, u32[]{:S(2)}) collective-permute-start(bf16[320,960]{1,0:T(8,128)(2,1)S(1)} %shard_map.96.refs_8_), channel_id=1, source_target_pairs={{0,8},{1,9},{2,10},{3,11},{4,12},{5,13},{6,14},{7,15},{8,0},{9,1},... | collective-permute-start | bytes 1843208 | tf_op jit(solution)/shard_map/ppermute | solution.py:26
  51.2 8.6 %collective-permute-start.14 = (bf16[80,960]{1,0:T(8,128)(2,1)S(1)}, bf16[80,960]{1,0:T(8,128)(2,1)S(1)}, u32[]{:S(2)}, u32[]{:S(2)}) collective-permute-start(bf16[80,960]{1,0:T(8,128)(2,1)S(1)} %get-tuple-element.41), channel_id=1, source_target_pairs={{0,32},{1,33},{2,34},{3,35},{4,36},{5,37},{6,38},{7,39},{8,40},{9,... | collective-permute-start | bytes 460808 | tf_op jit(solution)/shard_map/ppermute | solution.py:26
  54.4 8.7 %collective-permute-start.16 = (bf16[80,960]{1,0:T(8,128)(2,1)S(1)}, bf16[80,960]{1,0:T(8,128)(2,1)S(1)}, u32[]{:S(2)}, u32[]{:S(2)}) collective-permute-start(bf16[80,960]{1,0:T(8,128)(2,1)S(1)} %get-tuple-element.42), channel_id=1, source_target_pairs={{0,48},{1,49},{2,50},{3,51},{4,52},{5,53},{6,54},{7,55},{8,56},{9,... | collective-permute-start | bytes 460808 | tf_op jit(solution)/shard_map/ppermute | solution.py:26
  55.5 7.6 %collective-permute-start.15 = (bf16[80,960]{1,0:T(8,128)(2,1)S(1)}, bf16[80,960]{1,0:T(8,128)(2,1)S(1)}, u32[]{:S(2)}, u32[]{:S(2)}) collective-permute-start(bf16[80,960]{1,0:T(8,128)(2,1)S(1)} %get-tuple-element.39.refs_2_), channel_id=1, source_target_pairs={{0,16},{1,17},{2,18},{3,19},{4,20},{5,21},{6,22},{7,23},{8,24},{9,... | collective-permute-start | bytes 460808 | tf_op jit(solution)/shard_map/ppermute | solution.py:26
  63.2 8.0 %collective-permute-start.18 = (bf16[40,960]{1,0:T(8,128)(2,1)S(1)}, bf16[40,960]{1,0:T(8,128)(2,1)S(1)}, u32[]{:S(2)}, u32[]{:S(2)}) collective-permute-start(bf16[40,960]{1,0:T(8,128)(2,1)S(1)} %get-tuple-element.45), channel_id=1, source_target_pairs={{0,192},{1,193},{2,194},{3,195},{4,196},{5,197},{6,198},{7,199},{8... | collective-permute-start | bytes 230408 | tf_op jit(solution)/shard_map/ppermute | solution.py:26
  65.8 7.1 %collective-permute-start.17 = (bf16[40,960]{1,0:T(8,128)(2,1)S(1)}, bf16[40,960]{1,0:T(8,128)(2,1)S(1)}, u32[]{:S(2)}, u32[]{:S(2)}) collective-permute-start(bf16[40,960]{1,0:T(8,128)(2,1)S(1)} %get-tuple-element.43.refs_14_), channel_id=1, source_target_pairs={{0,64},{1,65},{2,66},{3,67},{4,68},{5,69},{6,70},{7,71},{8,72},{9,... | collective-permute-start | bytes 230408 | tf_op jit(solution)/shard_map/ppermute | solution.py:26
  72.9 7.1 %collective-permute-start.19 = (bf16[40,960]{1,0:T(8,128)(2,1)S(1)}, bf16[40,960]{1,0:T(8,128)(2,1)S(1)}, u32[]{:S(2)}, u32[]{:S(2)}) collective-permute-start(bf16[40,960]{1,0:T(8,128)(2,1)S(1)} %get-tuple-element.47), channel_id=1, source_target_pairs={{0,192},{1,193},{2,194},{3,195},{4,196},{5,197},{6,198},{7,199},{8... | collective-permute-start | bytes 230408 | tf_op jit(solution)/shard_map/ppermute | solution.py:26
  73.8 6.1 %collective-permute-start.20 = (bf16[40,960]{1,0:T(8,128)(2,1)S(1)}, bf16[40,960]{1,0:T(8,128)(2,1)S(1)}, u32[]{:S(2)}, u32[]{:S(2)}) collective-permute-start(bf16[40,960]{1,0:T(8,128)(2,1)S(1)} %get-tuple-element.48), channel_id=1, source_target_pairs={{0,64},{1,65},{2,66},{3,67},{4,68},{5,69},{6,70},{7,71},{8,72},{9,... | collective-permute-start | bytes 230408 | tf_op jit(solution)/shard_map/ppermute | solution.py:26
  80.8 7.7 %collective-permute-start.23 = (bf16[80,960]{1,0:T(8,128)(2,1)S(1)}, bf16[80,960]{1,0:T(8,128)(2,1)S(1)}, u32[]{:S(2)}, u32[]{:S(2)}) collective-permute-start(bf16[80,960]{1,0:T(8,128)(2,1)S(1)} %shard_map.103), channel_id=1, source_target_pairs={{0,48},{1,49},{2,50},{3,51},{4,52},{5,53},{6,54},{7,55},{8,56},{9,... | collective-permute-start | bytes 460808 | tf_op jit(solution)/shard_map/ppermute | solution.py:26
  84.0 8.4 %collective-permute-start.22 = (bf16[80,960]{1,0:T(8,128)(2,1)S(1)}, bf16[80,960]{1,0:T(8,128)(2,1)S(1)}, u32[]{:S(2)}, u32[]{:S(2)}) collective-permute-start(bf16[80,960]{1,0:T(8,128)(2,1)S(1)} %shard_map.103), channel_id=1, source_target_pairs={{0,16},{1,17},{2,18},{3,19},{4,20},{5,21},{6,22},{7,23},{8,24},{9,... | collective-permute-start | bytes 460808 | tf_op jit(solution)/shard_map/ppermute | solution.py:26
  84.0 8.4 %collective-permute-start.21 = (bf16[80,960]{1,0:T(8,128)(2,1)S(1)}, bf16[80,960]{1,0:T(8,128)(2,1)S(1)}, u32[]{:S(2)}, u32[]{:S(2)}) collective-permute-start(bf16[80,960]{1,0:T(8,128)(2,1)S(1)} %shard_map.103), channel_id=1, source_target_pairs={{0,32},{1,33},{2,34},{3,35},{4,36},{5,37},{6,38},{7,39},{8,40},{9,... | collective-permute-start | bytes 460808 | tf_op jit(solution)/shard_map/ppermute | solution.py:26
  92.4 2.2 %collective-permute-start.24 = (bf16[320,960]{1,0:T(8,128)(2,1)S(1)}, bf16[320,960]{1,0:T(8,128)(2,1)S(1)}, u32[]{:S(2)}, u32[]{:S(2)}) collective-permute-start(bf16[320,960]{1,0:T(8,128)(2,1)S(1)} %pad_maximum_fusion.refs_1_), channel_id=1, source_target_pairs={{0,8},{1,9},{2,10},{3,11},{4,12},{5,13},{6,14},{7,15},{8,0},{9,1},... | collective-permute-start | bytes 1843208 | tf_op jit(solution)/shard_map/ppermute | solution.py:26
  95.5 6.5 %collective-permute-start.26 = (bf16[128,320]{1,0:T(8,128)(2,1)S(1)}, bf16[128,320]{1,0:T(8,128)(2,1)S(1)}, u32[]{:S(2)}, u32[]{:S(2)}) collective-permute-start(bf16[128,320]{1,0:T(8,128)(2,1)S(1)} %get-tuple-element.50), channel_id=1, source_target_pairs={{0,196},{1,197},{2,198},{3,199},{4,64},{5,65},{6,66},{7,67},{8,204... | collective-permute-start | bytes 245768 | tf_op jit(solution)/shard_map/ppermute | solution.py:26
  98.9 4.6 %collective-permute-start.25 = (bf16[128,320]{1,0:T(8,128)(2,1)S(1)}, bf16[128,320]{1,0:T(8,128)(2,1)S(1)}, u32[]{:S(2)}, u32[]{:S(2)}) collective-permute-start(bf16[128,320]{1,0:T(8,128)(2,1)S(1)} %get-tuple-element.49.refs_3_), channel_id=1, source_target_pairs={{0,4},{1,5},{2,6},{3,7},{4,0},{5,1},{6,2},{7,3},{8,12},{9,13},{10,... | collective-permute-start | bytes 245768 | tf_op jit(solution)/shard_map/ppermute | solution.py:26
  103.6 5.4 %collective-permute-start.27 = (bf16[2,64,320]{2,1,0:T(8,128)(2,1)S(1)}, bf16[2,64,320]{2,1,0:T(8,128)(2,1)S(1)}, u32[]{:S(2)}, u32[]{:S(2)}) collective-permute-start(bf16[2,64,320]{2,1,0:T(8,128)(2,1)S(1)} %get-tuple-element.52), channel_id=1, source_target_pairs={{0,1},{1,0},{2,3},{3,2},{4,5},{5,4},{6,7},{7,6},{8,9},{9,8},{10,11... | collective-permute-start | bytes 245768 | tf_op jit(solution)/shard_map/ppermute | solution.py:26
  103.7 5.6 %collective-permute-start.28 = (bf16[2,64,320]{2,1,0:T(8,128)(2,1)S(1)}, bf16[2,64,320]{2,1,0:T(8,128)(2,1)S(1)}, u32[]{:S(2)}, u32[]{:S(2)}) collective-permute-start(bf16[2,64,320]{2,1,0:T(8,128)(2,1)S(1)} %get-tuple-element.53), channel_id=1, source_target_pairs={{0,3},{1,2},{2,1},{3,0},{4,7},{5,6},{6,5},{7,4},{8,11},{9,10},{10,... | collective-permute-start | bytes 245768 | tf_op jit(solution)/shard_map/ppermute | solution.py:26
  104.7 6.1 %collective-permute-start.29 = (bf16[2,64,320]{2,1,0:T(8,128)(2,1)S(1)}, bf16[2,64,320]{2,1,0:T(8,128)(2,1)S(1)}, u32[]{:S(2)}, u32[]{:S(2)}) collective-permute-start(bf16[2,64,320]{2,1,0:T(8,128)(2,1)S(1)} %get-tuple-element.54), channel_id=1, source_target_pairs={{0,2},{1,3},{2,0},{3,1},{4,6},{5,7},{6,4},{7,5},{8,10},{9,11},{10,... | collective-permute-start | bytes 245768 | tf_op jit(solution)/shard_map/ppermute | solution.py:26

commit v8 on v7

--- a/solution.py
+++ b/solution.py
@@ -205,8 +205,9 @@
         out[:, at] = (fresh * (old_norm / jnp.sqrt(new_sq + 1e-06))).astype(BF16)
 
 
-def respond_kernel(start, query_ref, column, other, *outs):
-    renorm = jnp.concatenate([column[...], other[...]], axis=0)
+def respond_kernel(start, query_ref, *refs):
+    blocks, outs = refs[:8], refs[8:]
+    renorm = jnp.concatenate([block[...] for block in blocks], axis=0)
     query = query_ref[:, start : start + 256]
     gate = jnp.dot(renorm[:, :320], query, preferred_element_type=F32)
     upper = jnp.dot(renorm[:, 320:640], query, preferred_element_type=F32)
@@ -216,8 +217,10 @@
     answer = scaled.astype(BF16)
     at = 0
     for out in outs:
-        out[...] = answer[at : at + out.shape[0]]
-        at += out.shape[0]
+        n = out.shape[0]
+        out[:, :320] = answer[at : at + n]
+        out[:, 320:] = answer[at + n : at + 2 * n]
+        at += 2 * n
 
 
 PLANE = [(0, 0, 64), (1, 0, 64), (2, 0, 64), (3, 0, 32), (4, 0, 32)]
@@ -265,31 +268,38 @@
         sent[:, i * 32 : (i + 1) * 32] = other[:, 32:]
 
 
-def pieces_kernel(plane, from_near, from_far, *outs):
+def pieces_kernel(from_near, from_far, *outs):
     for i, out in enumerate(outs):
-        out[0] = plane[i * 64 : (i + 1) * 64, :]
-        out[1, :32] = from_near[i * 32 : (i + 1) * 32, :]
-        out[1, 32:] = from_far[i * 32 : (i + 1) * 32, :]
-
-
-def place_kernel(my, a, b, c, d, out, slots):
-    for i, piece in enumerate((a, b, c, d)):
-        slots[2 * i : 2 * i + 2] = piece[...]
+        at = slice(i % 2 * 32, i % 2 * 32 + 32), slice(i // 2 * 320, i // 2 * 320 + 320)
+        out[:, :320] = from_near[at]
+        out[:, 320:] = from_far[at]
+
+
+def place_kernel(my, *refs):
+    pieces, out, slots = refs[:8], refs[8], refs[9]
+    for i, piece in enumerate(pieces):
+        slots[i, :32] = piece[:, :320]
+        slots[i, 32:] = piece[:, 320:]
     for head in range(8):
         out[:, head * 320 : (head + 1) * 320] = slots[my[SLOT + head]]
 
 
+def to_plane(pieces):
+    opposite, near_piece = to_opposite_x(pieces[3]), to_near_x(pieces[1])
+    return pieces[0], near_piece, to_far_x(pieces[2]), opposite
+
+
 def send_back(my, plane, for_near, for_far):
-    pieces = call(
-        pieces_kernel, [like((2, 64, 320))] * 4, plane, to_near_z(for_near), to_far_z(for_far)
-    )
-    opposite = to_opposite_x(pieces[3])
-    pieces = pieces[0], to_near_x(pieces[1]), to_far_x(pieces[2]), opposite
+    from_near, from_far = to_near_z(for_near), to_far_z(for_far)
+    own = to_plane(plane)
+    pieces = call(pieces_kernel, [like((32, 640))] * 4, from_near, from_far, after=own[1:])
+    other = to_plane(pieces)
+    slots = [piece for pair in zip(own, other) for piece in pair]
     return call(
         place_kernel,
         like((64, 2560)),
         my,
-        *pieces,
+        *slots,
         scalars=1,
         scratch=[pltpu.VMEM((8, 64, 320), BF16)],
     )
@@ -343,21 +353,20 @@
     mine, upper, lower = call(pair_kernel, parts, mine, *got, after=(query,))
     got = to_far_h(upper), to_near_h(lower)
     block = call(renorm_kernel, like((80, 960)), my, mine, *got, *old_t, scalars=1)
-    column = jnp.concatenate([block, to_y(block, 2), to_y(block, 1), to_y(block, 3)], axis=0)
-    other = to_core(column)
+    column = [block, to_y(block, 1), to_y(block, 3), to_y(block, 2)]
+    blocks = column + [to_core(b) for b in column]
 
     for_near, for_far = call(
-        functools.partial(respond_kernel, 256), [like((128, 320))] * 2, query, column, other
-    )
-    (answers,) = call(
+        functools.partial(respond_kernel, 256), [like((64, 640))] * 2, query, *blocks
+    )
+    plane = call(
         functools.partial(respond_kernel, 0),
-        [like((256, 320))],
+        [like((32, 640))] * 4,
         query,
-        column,
-        other,
+        *blocks,
         after=(for_near,),
     )
-    return send_back(my, answers, for_near, for_far)
+    return send_back(my, plane, for_near, for_far)
 
 
 def solution(mesh):

time: 113 us -> 115 us (1.018)
  starting transfers between devices: 54.7 us -> 51.5 us
  local copies, waits for them, and re-layouts: 5.21 us -> 7.22 us
  waiting for transfers between devices: 30.5 us -> 32.4 us
  other arithmetic: 0.64 us -> 2.08 us
    ppermute x30 -> x36, starting transfers between devices: 54.7 us -> 51.5 us  [permute(): return lax.ppermute(value, AXES, pairs)]
    unnamed x15 -> x7, local copies, waits for them, and re-layouts: 2.31 us -> 4.39 us
    ppermute x30 -> x36, waiting for transfers between devices: 30.5 us -> 32.4 us  [permute(): return lax.ppermute(value, AXES, pairs)]
  transfers between devices with their start and end apart: 30 -> 36, of which waited for: 16 -> 19; matrix products, arithmetic and copies ran while one was open for 4% -> 8% of each run, Pallas kernels for 13% -> 12%
where the time goes in v8:
time: 115 us
  starting transfers between devices  51.5 us (45%)
  waiting for transfers between devices  32.4 us (28%)
  Pallas kernels  20.4 us (18%)
  local copies, waits for them, and re-layouts  7.22 us (6%)
  other arithmetic  2.08 us (2%)
    ppermute x36, starting transfers between devices, permute(): return lax.ppermute(value, AXES, pairs)  51.5 us
    ppermute x36, waiting for transfers between devices, permute(): return lax.ppermute(value, AXES, pairs)  32.4 us
    pallas_call x15, Pallas kernels, call(): pl.pallas_call(run, out_shape=out_shape, in_specs=[SMEM] * scalars + [VME...  15.4 us
    pallas_call x2, Pallas kernels, load(): pl.pallas_call(run, out_shape=like((count, *w_t.shape[1:])), in_specs=[pl...  5 us
    unnamed x7, local copies, waits for them, and re-layouts  4.39 us
  transfers between devices with their start and end apart: 36, of which 19 were waited for; matrix products, arithmetic and copies ran while one was open for 8% of the time, Pallas kernels for 12%

profile of v8, /device:TPU:2, one launch (start us, length us, event | category | flops | bytes accessed | tf_op | source)
XLA Modules:
  0.0 114.5 jit_solution(2582196173111698221)
XLA Ops:
  0.0 0.7 dynamic-slice_bitcast_fusion.refs_0_
  0.7 1.5 %collective-permute-start.1 = (bf16[64,5120]{1,0:T(8,128)(2,1)}, bf16[64,5120]{1,0:T(8,128)(2,1)S(1)}, u32[]{:S(2)}, u32[]{:S(2)}) collective-permute-start(bf16[64,5120]{1,0:T(8,128)(2,1)} %refs_0_.1), channel_id=1, source_target_pairs={{0,3},{1,2},{2,1},{3,0},{4,7},{5,6},{6,5},{7,4},{8,11},{9,10},{10,... | collective-permute-start | bytes 1966088 | tf_op jit(solution)/shard_map/ppermute | solution.py:26
  2.2 1.8 %collective-permute-start = (bf16[64,5120]{1,0:T(8,128)(2,1)}, bf16[64,5120]{1,0:T(8,128)(2,1)S(1)}, u32[]{:S(2)}, u32[]{:S(2)}) collective-permute-start(bf16[64,5120]{1,0:T(8,128)(2,1)} %refs_0_.1), channel_id=1, source_target_pairs={{0,1},{1,0},{2,3},{3,2},{4,5},{5,4},{6,7},{7,6},{8,9},{9,8},{10,11... | collective-permute-start | bytes 1966088 | tf_op jit(solution)/shard_map/ppermute | solution.py:26
  4.0 2.0 %fusion = (bf16[32,5120]{1,0:T(8,128)(2,1)}, bf16[32,5120]{1,0:T(8,128)(2,1)}) fusion(bf16[64,5120]{1,0:T(8,128)(2,1)} %refs_0_.1), kind=kLoop, calls=%fused_computation.3 | loop fusion | bytes 1310720 | tf_op jit(solution)/shard_map/slice | solution.py:233
  5.9 5.9 %collective-permute-start.3 = (bf16[32,5120]{1,0:T(8,128)(2,1)}, bf16[32,5120]{1,0:T(8,128)(2,1)S(1)}, u32[]{:S(2)}, u32[]{:S(2)}) collective-permute-start(bf16[32,5120]{1,0:T(8,128)(2,1)} %get-tuple-element.63), channel_id=1, source_target_pairs={{0,196},{1,197},{2,198},{3,199},{4,64},{5,65},{6,66},{7,67},{8,204... | collective-permute-start | bytes 983048 | tf_op jit(solution)/shard_map/ppermute | solution.py:26
  12.5 0.6 broadcast.3
  13.0 1.4 %reduce.3 = s32[512]{0:T(512)S(1)} reduce(s32[512,1]{0,1:T(1,128)} %param.12, s32[]{:T(128)} %broadcast.3), dimensions={1}, to_apply=%param.12.reduce_sub_computation.3 | reduce | bytes 4100 | tf_op args[3]
  14.5 0.6 shard_map.91
  15.1 0.7 exponential_convert_fusion
  15.9 1.3 %copy.13 = bf16[1,320,640]{1,2,0:T(8,128)(2,1)S(1)} copy(bf16[1,320,640]{2,1,0:T(8,128)(2,1)} %param.14) | data formatting | bytes 819200 | tf_op args[5]
  17.2 1.3 %copy.14 = bf16[1,320,640]{1,2,0:T(8,128)(2,1)S(1)} copy(bf16[1,320,640]{2,1,0:T(8,128)(2,1)} %param.15) | data formatting | bytes 819200 | tf_op args[6]
  18.5 1.3 %copy.15 = bf16[1,320,640]{1,2,0:T(8,128)(2,1)S(1)} copy(bf16[1,320,640]{2,1,0:T(8,128)(2,1)} %param.16) | data formatting | bytes 819200 | tf_op args[7]
  19.8 3.0 %shard_map.92.refs_4_.refs_5_.refs_8_ = bf16[2,320,5120]{2,1,0:T(8,128)(2,1)S(1)} custom-call(bf16[3,320,5120]{2,1,0:T(8,128)(2,1)} %bitcast.28, bf16[3,1,5120]{2,1,0:T(2,128)(2,1)S(1)} %broadcast_in_dim_reshape.4.refs_1_, f32[1,384]{1,0:T(1,128)S(1)} %get-tuple-element.36.refs_2_.refs_3_, bf16[640,320]{1,0:T(8,128)(2,1)S(1)} %bitcast.16, ...), custom_call_target="tpu_custom_call" | custom-call | flops 1000 | bytes 1000 | tf_op jit(solution)/shard_map/pallas_call | solution.py:131
  23.0 1.4 %collective-permute-start.5 = (bf16[32,5120]{1,0:T(8,128)(2,1)S(1)}, bf16[32,5120]{1,0:T(8,128)(2,1)S(1)}, u32[]{:S(2)}, u32[]{:S(2)}) collective-permute-start(bf16[32,5120]{1,0:T(8,128)(2,1)S(1)} %get-tuple-element.38), channel_id=1, source_target_pairs={{0,1},{1,0},{2,3},{3,2},{4,5},{5,4},{6,7},{7,6},{8,9},{9,8},{10,11... | collective-permute-start | bytes 983048 | tf_op jit(solution)/shard_map/ppermute | solution.py:26
  24.4 2.0 %collective-permute-start.8 = (bf16[32,5120]{1,0:T(8,128)(2,1)S(1)}, bf16[32,5120]{1,0:T(8,128)(2,1)S(1)}, u32[]{:S(2)}, u32[]{:S(2)}) collective-permute-start(bf16[32,5120]{1,0:T(8,128)(2,1)S(1)} %get-tuple-element.40), channel_id=1, source_target_pairs={{0,4},{1,5},{2,6},{3,7},{4,0},{5,1},{6,2},{7,3},{8,12},{9,13},{10,... | collective-permute-start | bytes 983048 | tf_op jit(solution)/shard_map/ppermute | solution.py:26
  26.4 2.5 %collective-permute-start.9 = (bf16[32,5120]{1,0:T(8,128)(2,1)S(1)}, bf16[32,5120]{1,0:T(8,128)(2,1)S(1)}, u32[]{:S(2)}, u32[]{:S(2)}) collective-permute-start(bf16[32,5120]{1,0:T(8,128)(2,1)S(1)} %get-tuple-element.41), channel_id=1, source_target_pairs={{0,196},{1,197},{2,198},{3,199},{4,64},{5,65},{6,66},{7,67},{8,204... | collective-permute-start | bytes 983048 | tf_op jit(solution)/shard_map/ppermute | solution.py:26
  28.9 1.1 collective-permute-start.7
  30.1 3.6 %collective-permute-done.4.refs_3_ = bf16[32,5120]{1,0:T(8,128)(2,1)S(1)} collective-permute-done((bf16[32,5120]{1,0:T(8,128)(2,1)S(1)}, bf16[32,5120]{1,0:T(8,128)(2,1)S(1)}, u32[]{:S(2)}, u32[]{:S(2)}) %collective-permute-start.4) | collective-permute-done | bytes 327712 | tf_op jit(solution)/shard_map/ppermute | solution.py:26
  33.7 1.4 %collective-permute-start.6 = (bf16[32,5120]{1,0:T(8,128)(2,1)S(1)}, bf16[32,5120]{1,0:T(8,128)(2,1)S(1)}, u32[]{:S(2)}, u32[]{:S(2)}) collective-permute-start(bf16[32,5120]{1,0:T(8,128)(2,1)S(1)} %get-tuple-element.39), channel_id=1, source_target_pairs={{0,1},{1,0},{2,3},{3,2},{4,5},{5,4},{6,7},{7,6},{8,9},{9,8},{10,11... | collective-permute-start | bytes 983048 | tf_op jit(solution)/shard_map/ppermute | solution.py:26
  35.1 2.0 %collective-permute-start.10 = (bf16[32,5120]{1,0:T(8,128)(2,1)S(1)}, bf16[32,5120]{1,0:T(8,128)(2,1)S(1)}, u32[]{:S(2)}, u32[]{:S(2)}) collective-permute-start(bf16[32,5120]{1,0:T(8,128)(2,1)S(1)} %collective-permute-done.4.refs_3_), channel_id=1, source_target_pairs={{0,4},{1,5},{2,6},{3,7},{4,0},{5,1},{6,2},{7,3},{8,12},{9,13},{10,... | collective-permute-start | bytes 983048 | tf_op jit(solution)/shard_map/ppermute | solution.py:26
  37.1 2.2 %collective-permute-start.11 = (bf16[32,5120]{1,0:T(8,128)(2,1)S(1)}, bf16[32,5120]{1,0:T(8,128)(2,1)S(1)}, u32[]{:S(2)}, u32[]{:S(2)}) collective-permute-start(bf16[32,5120]{1,0:T(8,128)(2,1)S(1)} %collective-permute-done.5.refs_4_), channel_id=1, source_target_pairs={{0,196},{1,197},{2,198},{3,199},{4,64},{5,65},{6,66},{7,67},{8,204... | collective-permute-start | bytes 983048 | tf_op jit(solution)/shard_map/ppermute | solution.py:26
  39.3 1.4 %collective-permute-done.6.refs_6_.refs_2_.refs_7_ = bf16[32,5120]{1,0:T(8,128)(2,1)S(1)} collective-permute-done((bf16[32,5120]{1,0:T(8,128)(2,1)S(1)}, bf16[32,5120]{1,0:T(8,128)(2,1)S(1)}, u32[]{:S(2)}, u32[]{:S(2)}) %collective-permute-start.6) | collective-permute-done | bytes 327712 | tf_op jit(solution)/shard_map/ppermute | solution.py:26
  40.8 1.9 %shard_map.94.refs_9_.refs_1_ = bf16[640,256]{1,0:T(8,128)(2,1)S(1)} custom-call(bf16[64,5120]{1,0:T(8,128)(2,1)S(1)} %copy-done, bf16[64,5120]{1,0:T(8,128)(2,1)S(1)} %collective-permute-done.refs_0_.refs_1_, bf16[64,5120]{1,0:T(8,128)(2,1)S(1)} %collective-permute-done.1.refs_1_.refs_2_, bf16[32,5120]{1,0:T(8,128)(2,1)S(1)} %collective-permute-done.4.refs_3_, ...), custom_call_target="tpu_custom_call" | custom-call | flops 1000 | bytes 1000 | tf_op jit(solution)/shard_map/pallas_call | solution.py:91
  42.7 2.8 %collective-permute-done.11.refs_7_.refs_12_ = bf16[32,5120]{1,0:T(8,128)(2,1)S(1)} collective-permute-done((bf16[32,5120]{1,0:T(8,128)(2,1)S(1)}, bf16[32,5120]{1,0:T(8,128)(2,1)S(1)}, u32[]{:S(2)}, u32[]{:S(2)}) %collective-permute-start.11) | collective-permute-done | bytes 327712 | tf_op jit(solution)/shard_map/ppermute | solution.py:26
  45.4 1.9 %shard_map.95.refs_2_ = bf16[640,256]{1,0:T(8,128)(2,1)S(1)} custom-call(bf16[32,5120]{1,0:T(8,128)(2,1)S(1)} %collective-permute-done.2.refs_2_.refs_0_.refs_5_, bf16[32,5120]{1,0:T(8,128)(2,1)S(1)} %collective-permute-done.3.refs_3_.refs_1_.refs_6_, bf16[32,5120]{1,0:T(8,128)(2,1)S(1)} %collective-permute-done.6.refs_6_.refs_2_.refs_7_, ...), custom_call_target="tpu_custom_call" | custom-call | flops 1000 | bytes 1000 | tf_op jit(solution)/shard_map/pallas_call | solution.py:91
  47.3 1.9 %shard_map.96.refs_8_ = bf16[320,960]{1,0:T(8,128)(2,1)S(1)} custom-call(s32[32]{0:T(128)S(1)} %dynamic-slice_bitcast_fusion.refs_0_, bf16[640,256]{1,0:T(8,128)(2,1)S(1)} %shard_map.94.refs_9_.refs_1_, bf16[640,256]{1,0:T(8,128)(2,1)S(1)} %shard_map.95.refs_2_, f32[1,384]{1,0:T(1,128)S(1)} %get-tuple-element.36.refs_2_.refs_3_, ...), custom_call_target="tpu_custom_call" | custom-call | flops 1000 | bytes 1000 | tf_op jit(solution)/shard_map/pallas_call | solution.py:91
  49.4 1.9 %shard_map.97.refs_1_ = f32[320,960]{1,0:T(8,128)S(1)} custom-call(s32[32]{0:T(128)S(1)} %dynamic-slice_bitcast_fusion.refs_0_, bf16[640,256]{1,0:T(8,128)(2,1)S(1)} %shard_map.94.refs_9_.refs_1_, bf16[640,256]{1,0:T(8,128)(2,1)S(1)} %shard_map.95.refs_2_, f32[1,384]{1,0:T(1,128)S(1)} %get-tuple-element.36.refs_2_.refs_3_, ...), custom_call_target="tpu_custom_call" | custom-call | flops 1000 | bytes 1000 | tf_op jit(solution)/shard_map/pallas_call | solution.py:91
  51.5 0.7 shard_map.98
  52.1 3.3 %collective-permute-start.14 = (bf16[80,960]{1,0:T(8,128)(2,1)S(1)}, bf16[80,960]{1,0:T(8,128)(2,1)S(1)}, u32[]{:S(2)}, u32[]{:S(2)}) collective-permute-start(bf16[80,960]{1,0:T(8,128)(2,1)S(1)} %get-tuple-element.45), channel_id=1, source_target_pairs={{0,32},{1,33},{2,34},{3,35},{4,36},{5,37},{6,38},{7,39},{8,40},{9,... | collective-permute-start | bytes 460808 | tf_op jit(solution)/shard_map/ppermute | solution.py:26
  55.4 1.1 collective-permute-start.16
  56.5 1.0 collective-permute-start.15
  57.4 2.0 %shard_map.99.refs_4_.refs_13_ = bf16[1,320,5120]{2,1,0:T(8,128)(2,1)S(1)} custom-call(bf16[3,320,5120]{2,1,0:T(8,128)(2,1)} %bitcast.29, bf16[3,1,5120]{2,1,0:T(2,128)(2,1)S(1)} %broadcast_in_dim_reshape.4.refs_1_, bf16[80,960]{1,0:T(8,128)(2,1)S(1)} %get-tuple-element.43.refs_2_), custom_call_target="tpu_custom_call" | custom-call | flops 1000 | bytes 1000 | tf_op jit(solution)/shard_map/pallas_call | solution.py:131
  59.4 1.3 %collective-permute-done.14.refs_1_ = bf16[80,960]{1,0:T(8,128)(2,1)S(1)} collective-permute-done((bf16[80,960]{1,0:T(8,128)(2,1)S(1)}, bf16[80,960]{1,0:T(8,128)(2,1)S(1)}, u32[]{:S(2)}, u32[]{:S(2)}) %collective-permute-start.14) | collective-permute-done | bytes 153632 | tf_op jit(solution)/shard_map/ppermute | solution.py:26
  60.7 3.3 %collective-permute-done.16.refs_3_ = bf16[80,960]{1,0:T(8,128)(2,1)S(1)} collective-permute-done((bf16[80,960]{1,0:T(8,128)(2,1)S(1)}, bf16[80,960]{1,0:T(8,128)(2,1)S(1)}, u32[]{:S(2)}, u32[]{:S(2)}) %collective-permute-start.16) | collective-permute-done | bytes 153632 | tf_op jit(solution)/shard_map/ppermute | solution.py:26
  64.1 1.5 %collective-permute-start.18 = (bf16[40,960]{1,0:T(8,128)(2,1)S(1)}, bf16[40,960]{1,0:T(8,128)(2,1)S(1)}, u32[]{:S(2)}, u32[]{:S(2)}) collective-permute-start(bf16[40,960]{1,0:T(8,128)(2,1)S(1)} %get-tuple-element.49), channel_id=1, source_target_pairs={{0,192},{1,193},{2,194},{3,195},{4,196},{5,197},{6,198},{7,199},{8... | collective-permute-start | bytes 230408 | tf_op jit(solution)/shard_map/ppermute | solution.py:26
  65.6 2.7 %collective-permute-start.17 = (bf16[40,960]{1,0:T(8,128)(2,1)S(1)}, bf16[40,960]{1,0:T(8,128)(2,1)S(1)}, u32[]{:S(2)}, u32[]{:S(2)}) collective-permute-start(bf16[40,960]{1,0:T(8,128)(2,1)S(1)} %get-tuple-element.47.refs_14_), channel_id=1, source_target_pairs={{0,64},{1,65},{2,66},{3,67},{4,68},{5,69},{6,70},{7,71},{8,72},{9,... | collective-permute-start | bytes 230408 | tf_op jit(solution)/shard_map/ppermute | solution.py:26
  68.3 1.9 %shard_map.101.refs_3_.refs_0_ = bf16[320,512]{1,0:T(8,128)(2,1)S(1)} custom-call(bf16[64,5120]{1,0:T(8,128)(2,1)S(1)} %copy-done, bf16[64,5120]{1,0:T(8,128)(2,1)S(1)} %collective-permute-done.refs_0_.refs_1_, bf16[64,5120]{1,0:T(8,128)(2,1)S(1)} %collective-permute-done.1.refs_1_.refs_2_, bf16[32,5120]{1,0:T(8,128)(2,1)S(1)} %collective-permute-done.4.refs_3_, ...), custom_call_target="tpu_custom_call" | custom-call | flops 1000 | bytes 1000 | tf_op jit(solution)/shard_map/pallas_call | solution.py:91
  70.2 1.3 %collective-permute-done.18.refs_2_ = bf16[40,960]{1,0:T(8,128)(2,1)S(1)} collective-permute-done((bf16[40,960]{1,0:T(8,128)(2,1)S(1)}, bf16[40,960]{1,0:T(8,128)(2,1)S(1)}, u32[]{:S(2)}, u32[]{:S(2)}) %collective-permute-start.18) | collective-permute-done | bytes 76832 | tf_op jit(solution)/shard_map/ppermute | solution.py:26
  71.5 0.3 collective-permute-done.17.refs_1_
  71.9 2.3 %collective-permute-start.19 = (bf16[40,960]{1,0:T(8,128)(2,1)S(1)}, bf16[40,960]{1,0:T(8,128)(2,1)S(1)}, u32[]{:S(2)}, u32[]{:S(2)}) collective-permute-start(bf16[40,960]{1,0:T(8,128)(2,1)S(1)} %get-tuple-element.51), channel_id=1, source_target_pairs={{0,192},{1,193},{2,194},{3,195},{4,196},{5,197},{6,198},{7,199},{8... | collective-permute-start | bytes 230408 | tf_op jit(solution)/shard_map/ppermute | solution.py:26
  74.2 1.2 %collective-permute-start.20 = (bf16[40,960]{1,0:T(8,128)(2,1)S(1)}, bf16[40,960]{1,0:T(8,128)(2,1)S(1)}, u32[]{:S(2)}, u32[]{:S(2)}) collective-permute-start(bf16[40,960]{1,0:T(8,128)(2,1)S(1)} %get-tuple-element.52), channel_id=1, source_target_pairs={{0,64},{1,65},{2,66},{3,67},{4,68},{5,69},{6,70},{7,71},{8,72},{9,... | collective-permute-start | bytes 230408 | tf_op jit(solution)/shard_map/ppermute | solution.py:26
  75.4 3.4 %collective-permute-done.19.refs_2_ = bf16[40,960]{1,0:T(8,128)(2,1)S(1)} collective-permute-done((bf16[40,960]{1,0:T(8,128)(2,1)S(1)}, bf16[40,960]{1,0:T(8,128)(2,1)S(1)}, u32[]{:S(2)}, u32[]{:S(2)}) %collective-permute-start.19) | collective-permute-done | bytes 76832 | tf_op jit(solution)/shard_map/ppermute | solution.py:26
  78.8 1.6 %collective-permute-done.20.refs_3_ = bf16[40,960]{1,0:T(8,128)(2,1)S(1)} collective-permute-done((bf16[40,960]{1,0:T(8,128)(2,1)S(1)}, bf16[40,960]{1,0:T(8,128)(2,1)S(1)}, u32[]{:S(2)}, u32[]{:S(2)}) %collective-permute-start.20) | collective-permute-done | bytes 76832 | tf_op jit(solution)/shard_map/ppermute | solution.py:26
  80.4 0.9 shard_map.103.refs_1_
  81.3 3.4 %collective-permute-start.23 = (bf16[80,960]{1,0:T(8,128)(2,1)S(1)}, bf16[80,960]{1,0:T(8,128)(2,1)S(1)}, u32[]{:S(2)}, u32[]{:S(2)}) collective-permute-start(bf16[80,960]{1,0:T(8,128)(2,1)S(1)} %shard_map.103.refs_1_), channel_id=1, source_target_pairs={{0,32},{1,33},{2,34},{3,35},{4,36},{5,37},{6,38},{7,39},{8,40},{9,... | collective-permute-start | bytes 460808 | tf_op jit(solution)/shard_map/ppermute | solution.py:26
  84.7 2.0 %collective-permute-start.21 = (bf16[80,960]{1,0:T(8,128)(2,1)S(1)}, bf16[80,960]{1,0:T(8,128)(2,1)S(1)}, u32[]{:S(2)}, u32[]{:S(2)}) collective-permute-start(bf16[80,960]{1,0:T(8,128)(2,1)S(1)} %shard_map.103.refs_1_), channel_id=1, source_target_pairs={{0,16},{1,17},{2,18},{3,19},{4,20},{5,21},{6,22},{7,23},{8,24},{9,... | collective-permute-start | bytes 460808 | tf_op jit(solution)/shard_map/ppermute | solution.py:26
  86.7 3.1 %collective-permute-done.23.refs_4_ = bf16[80,960]{1,0:T(8,128)(2,1)S(1)} collective-permute-done((bf16[80,960]{1,0:T(8,128)(2,1)S(1)}, bf16[80,960]{1,0:T(8,128)(2,1)S(1)}, u32[]{:S(2)}, u32[]{:S(2)}) %collective-permute-start.23) | collective-permute-done | bytes 153632 | tf_op jit(solution)/shard_map/ppermute | solution.py:26
  89.8 1.7 %collective-permute-done.22.refs_3_ = bf16[80,960]{1,0:T(8,128)(2,1)S(1)} collective-permute-done((bf16[80,960]{1,0:T(8,128)(2,1)S(1)}, bf16[80,960]{1,0:T(8,128)(2,1)S(1)}, u32[]{:S(2)}, u32[]{:S(2)}) %collective-permute-start.22) | collective-permute-done | bytes 153632 | tf_op jit(solution)/shard_map/ppermute | solution.py:26
  92.0 0.9 collective-permute-done.26.refs_7_
  93.2 1.0 shard_map.104
  94.2 1.4 %collective-permute-start.29 = (bf16[64,640]{1,0:T(8,128)(2,1)S(1)}, bf16[64,640]{1,0:T(8,128)(2,1)S(1)}, u32[]{:S(2)}, u32[]{:S(2)}) collective-permute-start(bf16[64,640]{1,0:T(8,128)(2,1)S(1)} %get-tuple-element.55), channel_id=1, source_target_pairs={{0,196},{1,197},{2,198},{3,199},{4,64},{5,65},{6,66},{7,67},{8,204... | collective-permute-start | bytes 245768 | tf_op jit(solution)/shard_map/ppermute | solution.py:26
  95.5 0.5 collective-permute-start.28
  96.1 1.0 shard_map.105
  97.1 0.7 collective-permute-start.30
  97.8 1.0 collective-permute-start.31
  98.8 2.5 %collective-permute-start.32 = (bf16[32,640]{1,0:T(8,128)(2,1)S(1)}, bf16[32,640]{1,0:T(8,128)(2,1)S(1)}, u32[]{:S(2)}, u32[]{:S(2)}) collective-permute-start(bf16[32,640]{1,0:T(8,128)(2,1)S(1)} %get-tuple-element.58), channel_id=1, source_target_pairs={{0,2},{1,3},{2,0},{3,1},{4,6},{5,7},{6,4},{7,5},{8,10},{9,11},{10,... | collective-permute-start | bytes 122888 | tf_op jit(solution)/shard_map/ppermute | solution.py:26
  101.2 0.5 collective-permute-done.31.refs_3_.refs_5_
  101.8 2.5 %collective-permute-done.32.refs_4_.refs_7_ = bf16[32,640]{1,0:T(8,128)(2,1)S(1)} collective-permute-done((bf16[32,640]{1,0:T(8,128)(2,1)S(1)}, bf16[32,640]{1,0:T(8,128)(2,1)S(1)}, u32[]{:S(2)}, u32[]{:S(2)}) %collective-permute-start.32) | collective-permute-done | bytes 40992 | tf_op jit(solution)/shard_map/ppermute | solution.py:26
  104.4 2.6 %collective-permute-start.33 = (bf16[32,640]{1,0:T(8,128)(2,1)S(1)}, bf16[32,640]{1,0:T(8,128)(2,1)S(1)}, u32[]{:S(2)}, u32[]{:S(2)}) collective-permute-start(bf16[32,640]{1,0:T(8,128)(2,1)S(1)} %get-tuple-element.60), channel_id=1, source_target_pairs={{0,1},{1,0},{2,3},{3,2},{4,5},{5,4},{6,7},{7,6},{8,9},{9,8},{10,11... | collective-permute-start | bytes 122888 | tf_op jit(solution)/shard_map/ppermute | solution.py:26
  107.0 0.5 collective-permute-start.34
  107.5 1.7 %collective-permute-start.35 = (bf16[32,640]{1,0:T(8,128)(2,1)S(1)}, bf16[32,640]{1,0:T(8,128)(2,1)S(1)}, u32[]{:S(2)}, u32[]{:S(2)}) collective-permute-start(bf16[32,640]{1,0:T(8,128)(2,1)S(1)} %get-tuple-element.62), channel_id=1, source_target_pairs={{0,2},{1,3},{2,0},{3,1},{4,6},{5,7},{6,4},{7,5},{8,10},{9,11},{10,... | collective-permute-start | bytes 122888 | tf_op jit(solution)/shard_map/ppermute | solution.py:26
  109.2 1.8 %collective-permute-done.34.refs_6_ = bf16[32,640]{1,0:T(8,128)(2,1)S(1)} collective-permute-done((bf16[32,640]{1,0:T(8,128)(2,1)S(1)}, bf16[32,640]{1,0:T(8,128)(2,1)S(1)}, u32[]{:S(2)}, u32[]{:S(2)}) %collective-permute-start.34) | collective-permute-done | bytes 40992 | tf_op jit(solution)/shard_map/ppermute | solution.py:26
  111.0 2.0 %collective-permute-done.35.refs_8_ = bf16[32,640]{1,0:T(8,128)(2,1)S(1)} collective-permute-done((bf16[32,640]{1,0:T(8,128)(2,1)S(1)}, bf16[32,640]{1,0:T(8,128)(2,1)S(1)}, u32[]{:S(2)}, u32[]{:S(2)}) %collective-permute-start.35) | collective-permute-done | bytes 40992 | tf_op jit(solution)/shard_map/ppermute | solution.py:26
  113.0 1.5 %shard_map.107 = bf16[64,2560]{1,0:T(8,128)(2,1)} custom-call(s32[32]{0:T(128)S(1)} %dynamic-slice_bitcast_fusion.refs_0_, bf16[32,640]{1,0:T(8,128)(2,1)S(1)} %get-tuple-element.54.refs_1_, bf16[32,640]{1,0:T(8,128)(2,1)S(1)} %get-tuple-element.59.refs_2_, bf16[32,640]{1,0:T(8,128)(2,1)S(1)} %collective-permute-done.30.refs_2_.refs_3_, ...), custom_call_target="tpu_custom_call" | custom-call | flops 1000 | bytes 1000 | tf_op jit(solution)/shard_map/pallas_call | solution.py:91
  (39 shorter events, 1.8 us)
Async XLA Ops:
  0.7 22.1 %collective-permute-start.1 = (bf16[64,5120]{1,0:T(8,128)(2,1)}, bf16[64,5120]{1,0:T(8,128)(2,1)S(1)}, u32[]{:S(2)}, u32[]{:S(2)}) collective-permute-start(bf16[64,5120]{1,0:T(8,128)(2,1)} %refs_0_.1), channel_id=1, source_target_pairs={{0,3},{1,2},{2,1},{3,0},{4,7},{5,6},{6,5},{7,4},{8,11},{9,10},{10,... | collective-permute-start | bytes 1966088 | tf_op jit(solution)/shard_map/ppermute | solution.py:26
  2.2 20.6 %collective-permute-start = (bf16[64,5120]{1,0:T(8,128)(2,1)}, bf16[64,5120]{1,0:T(8,128)(2,1)S(1)}, u32[]{:S(2)}, u32[]{:S(2)}) collective-permute-start(bf16[64,5120]{1,0:T(8,128)(2,1)} %refs_0_.1), channel_id=1, source_target_pairs={{0,1},{1,0},{2,3},{3,2},{4,5},{5,4},{6,7},{7,6},{8,9},{9,8},{10,11... | collective-permute-start | bytes 1966088 | tf_op jit(solution)/shard_map/ppermute | solution.py:26
  5.9 16.8 %collective-permute-start.3 = (bf16[32,5120]{1,0:T(8,128)(2,1)}, bf16[32,5120]{1,0:T(8,128)(2,1)S(1)}, u32[]{:S(2)}, u32[]{:S(2)}) collective-permute-start(bf16[32,5120]{1,0:T(8,128)(2,1)} %get-tuple-element.63), channel_id=1, source_target_pairs={{0,196},{1,197},{2,198},{3,199},{4,64},{5,65},{6,66},{7,67},{8,204... | collective-permute-start | bytes 983048 | tf_op jit(solution)/shard_map/ppermute | solution.py:26
  11.8 11.0 %collective-permute-start.2 = (bf16[32,5120]{1,0:T(8,128)(2,1)}, bf16[32,5120]{1,0:T(8,128)(2,1)S(1)}, u32[]{:S(2)}, u32[]{:S(2)}) collective-permute-start(bf16[32,5120]{1,0:T(8,128)(2,1)} %get-tuple-element.64), channel_id=1, source_target_pairs={{0,4},{1,5},{2,6},{3,7},{4,0},{5,1},{6,2},{7,3},{8,12},{9,13},{10,... | collective-permute-start | bytes 983048 | tf_op jit(solution)/shard_map/ppermute | solution.py:26
  22.8 18.0 %copy-start = (bf16[64,5120]{1,0:T(8,128)(2,1)S(1)}, bf16[64,5120]{1,0:T(8,128)(2,1)}, u32[]{:S(2)}) copy-start(bf16[64,5120]{1,0:T(8,128)(2,1)} %refs_0_.1) | copy-start | bytes 1966084
  22.9 10.7 %collective-permute-start.4 = (bf16[32,5120]{1,0:T(8,128)(2,1)S(1)}, bf16[32,5120]{1,0:T(8,128)(2,1)S(1)}, u32[]{:S(2)}, u32[]{:S(2)}) collective-permute-start(bf16[32,5120]{1,0:T(8,128)(2,1)S(1)} %get-tuple-element.37), channel_id=1, source_target_pairs={{0,3},{1,2},{2,1},{3,0},{4,7},{5,6},{6,5},{7,4},{8,11},{9,10},{10,... | collective-permute-start | bytes 983048 | tf_op jit(solution)/shard_map/ppermute | solution.py:26
  23.0 12.1 %collective-permute-start.5 = (bf16[32,5120]{1,0:T(8,128)(2,1)S(1)}, bf16[32,5120]{1,0:T(8,128)(2,1)S(1)}, u32[]{:S(2)}, u32[]{:S(2)}) collective-permute-start(bf16[32,5120]{1,0:T(8,128)(2,1)S(1)} %get-tuple-element.38), channel_id=1, source_target_pairs={{0,1},{1,0},{2,3},{3,2},{4,5},{5,4},{6,7},{7,6},{8,9},{9,8},{10,11... | collective-permute-start | bytes 983048 | tf_op jit(solution)/shard_map/ppermute | solution.py:26
  24.4 12.7 %collective-permute-start.8 = (bf16[32,5120]{1,0:T(8,128)(2,1)S(1)}, bf16[32,5120]{1,0:T(8,128)(2,1)S(1)}, u32[]{:S(2)}, u32[]{:S(2)}) collective-permute-start(bf16[32,5120]{1,0:T(8,128)(2,1)S(1)} %get-tuple-element.40), channel_id=1, source_target_pairs={{0,4},{1,5},{2,6},{3,7},{4,0},{5,1},{6,2},{7,3},{8,12},{9,13},{10,... | collective-permute-start | bytes 983048 | tf_op jit(solution)/shard_map/ppermute | solution.py:26
  26.4 12.9 %collective-permute-start.9 = (bf16[32,5120]{1,0:T(8,128)(2,1)S(1)}, bf16[32,5120]{1,0:T(8,128)(2,1)S(1)}, u32[]{:S(2)}, u32[]{:S(2)}) collective-permute-start(bf16[32,5120]{1,0:T(8,128)(2,1)S(1)} %get-tuple-element.41), channel_id=1, source_target_pairs={{0,196},{1,197},{2,198},{3,199},{4,64},{5,65},{6,66},{7,67},{8,204... | collective-permute-start | bytes 983048 | tf_op jit(solution)/shard_map/ppermute | solution.py:26
  28.9 10.4 %collective-permute-start.7 = (bf16[32,5120]{1,0:T(8,128)(2,1)S(1)}, bf16[32,5120]{1,0:T(8,128)(2,1)S(1)}, u32[]{:S(2)}, u32[]{:S(2)}) collective-permute-start(bf16[32,5120]{1,0:T(8,128)(2,1)S(1)} %get-tuple-element.39), channel_id=1, source_target_pairs={{0,3},{1,2},{2,1},{3,0},{4,7},{5,6},{6,5},{7,4},{8,11},{9,10},{10,... | collective-permute-start | bytes 983048 | tf_op jit(solution)/shard_map/ppermute | solution.py:26
  33.7 7.1 %collective-permute-start.6 = (bf16[32,5120]{1,0:T(8,128)(2,1)S(1)}, bf16[32,5120]{1,0:T(8,128)(2,1)S(1)}, u32[]{:S(2)}, u32[]{:S(2)}) collective-permute-start(bf16[32,5120]{1,0:T(8,128)(2,1)S(1)} %get-tuple-element.39), channel_id=1, source_target_pairs={{0,1},{1,0},{2,3},{3,2},{4,5},{5,4},{6,7},{7,6},{8,9},{9,8},{10,11... | collective-permute-start | bytes 983048 | tf_op jit(solution)/shard_map/ppermute | solution.py:26
  35.1 7.5 %collective-permute-start.10 = (bf16[32,5120]{1,0:T(8,128)(2,1)S(1)}, bf16[32,5120]{1,0:T(8,128)(2,1)S(1)}, u32[]{:S(2)}, u32[]{:S(2)}) collective-permute-start(bf16[32,5120]{1,0:T(8,128)(2,1)S(1)} %collective-permute-done.4.refs_3_), channel_id=1, source_target_pairs={{0,4},{1,5},{2,6},{3,7},{4,0},{5,1},{6,2},{7,3},{8,12},{9,13},{10,... | collective-permute-start | bytes 983048 | tf_op jit(solution)/shard_map/ppermute | solution.py:26
  37.1 8.3 %collective-permute-start.11 = (bf16[32,5120]{1,0:T(8,128)(2,1)S(1)}, bf16[32,5120]{1,0:T(8,128)(2,1)S(1)}, u32[]{:S(2)}, u32[]{:S(2)}) collective-permute-start(bf16[32,5120]{1,0:T(8,128)(2,1)S(1)} %collective-permute-done.5.refs_4_), channel_id=1, source_target_pairs={{0,196},{1,197},{2,198},{3,199},{4,64},{5,65},{6,66},{7,67},{8,204... | collective-permute-start | bytes 983048 | tf_op jit(solution)/shard_map/ppermute | solution.py:26
  39.3 8.0 %collective-permute-start.12 = (f32[1,128]{1,0:T(1,128)S(1)}, f32[1,128]{1,0:T(1,128)S(1)}, u32[]{:S(2)}, u32[]{:S(2)}) collective-permute-start(f32[1,128]{1,0:T(1,128)S(1)} %get-tuple-element.42), channel_id=1, source_target_pairs={{0,64},{1,65},{2,66},{3,67},{4,196},{5,197},{6,198},{7,199},{8,72}... | collective-permute-start | bytes 1544 | tf_op jit(solution)/shard_map/ppermute | solution.py:26
  49.3 2.2 %collective-permute-start.13 = (bf16[320,960]{1,0:T(8,128)(2,1)S(1)}, bf16[320,960]{1,0:T(8,128)(2,1)S(1)}, u32[]{:S(2)}, u32[]{:S(2)}) collective-permute-start(bf16[320,960]{1,0:T(8,128)(2,1)S(1)} %shard_map.96.refs_8_), channel_id=1, source_target_pairs={{0,8},{1,9},{2,10},{3,11},{4,12},{5,13},{6,14},{7,15},{8,0},{9,1},... | collective-permute-start | bytes 1843208 | tf_op jit(solution)/shard_map/ppermute | solution.py:26
  52.1 8.6 %collective-permute-start.14 = (bf16[80,960]{1,0:T(8,128)(2,1)S(1)}, bf16[80,960]{1,0:T(8,128)(2,1)S(1)}, u32[]{:S(2)}, u32[]{:S(2)}) collective-permute-start(bf16[80,960]{1,0:T(8,128)(2,1)S(1)} %get-tuple-element.45), channel_id=1, source_target_pairs={{0,32},{1,33},{2,34},{3,35},{4,36},{5,37},{6,38},{7,39},{8,40},{9,... | collective-permute-start | bytes 460808 | tf_op jit(solution)/shard_map/ppermute | solution.py:26
  55.4 8.7 %collective-permute-start.16 = (bf16[80,960]{1,0:T(8,128)(2,1)S(1)}, bf16[80,960]{1,0:T(8,128)(2,1)S(1)}, u32[]{:S(2)}, u32[]{:S(2)}) collective-permute-start(bf16[80,960]{1,0:T(8,128)(2,1)S(1)} %get-tuple-element.46), channel_id=1, source_target_pairs={{0,48},{1,49},{2,50},{3,51},{4,52},{5,53},{6,54},{7,55},{8,56},{9,... | collective-permute-start | bytes 460808 | tf_op jit(solution)/shard_map/ppermute | solution.py:26
  56.5 7.6 %collective-permute-start.15 = (bf16[80,960]{1,0:T(8,128)(2,1)S(1)}, bf16[80,960]{1,0:T(8,128)(2,1)S(1)}, u32[]{:S(2)}, u32[]{:S(2)}) collective-permute-start(bf16[80,960]{1,0:T(8,128)(2,1)S(1)} %get-tuple-element.43.refs_2_), channel_id=1, source_target_pairs={{0,16},{1,17},{2,18},{3,19},{4,20},{5,21},{6,22},{7,23},{8,24},{9,... | collective-permute-start | bytes 460808 | tf_op jit(solution)/shard_map/ppermute | solution.py:26
  64.1 7.3 %collective-permute-start.18 = (bf16[40,960]{1,0:T(8,128)(2,1)S(1)}, bf16[40,960]{1,0:T(8,128)(2,1)S(1)}, u32[]{:S(2)}, u32[]{:S(2)}) collective-permute-start(bf16[40,960]{1,0:T(8,128)(2,1)S(1)} %get-tuple-element.49), channel_id=1, source_target_pairs={{0,192},{1,193},{2,194},{3,195},{4,196},{5,197},{6,198},{7,199},{8... | collective-permute-start | bytes 230408 | tf_op jit(solution)/shard_map/ppermute | solution.py:26
  65.6 6.2 %collective-permute-start.17 = (bf16[40,960]{1,0:T(8,128)(2,1)S(1)}, bf16[40,960]{1,0:T(8,128)(2,1)S(1)}, u32[]{:S(2)}, u32[]{:S(2)}) collective-permute-start(bf16[40,960]{1,0:T(8,128)(2,1)S(1)} %get-tuple-element.47.refs_14_), channel_id=1, source_target_pairs={{0,64},{1,65},{2,66},{3,67},{4,68},{5,69},{6,70},{7,71},{8,72},{9,... | collective-permute-start | bytes 230408 | tf_op jit(solution)/shard_map/ppermute | solution.py:26
  71.9 6.9 %collective-permute-start.19 = (bf16[40,960]{1,0:T(8,128)(2,1)S(1)}, bf16[40,960]{1,0:T(8,128)(2,1)S(1)}, u32[]{:S(2)}, u32[]{:S(2)}) collective-permute-start(bf16[40,960]{1,0:T(8,128)(2,1)S(1)} %get-tuple-element.51), channel_id=1, source_target_pairs={{0,192},{1,193},{2,194},{3,195},{4,196},{5,197},{6,198},{7,199},{8... | collective-permute-start | bytes 230408 | tf_op jit(solution)/shard_map/ppermute | solution.py:26
  74.2 6.2 %collective-permute-start.20 = (bf16[40,960]{1,0:T(8,128)(2,1)S(1)}, bf16[40,960]{1,0:T(8,128)(2,1)S(1)}, u32[]{:S(2)}, u32[]{:S(2)}) collective-permute-start(bf16[40,960]{1,0:T(8,128)(2,1)S(1)} %get-tuple-element.52), channel_id=1, source_target_pairs={{0,64},{1,65},{2,66},{3,67},{4,68},{5,69},{6,70},{7,71},{8,72},{9,... | collective-permute-start | bytes 230408 | tf_op jit(solution)/shard_map/ppermute | solution.py:26
  81.3 8.5 %collective-permute-start.23 = (bf16[80,960]{1,0:T(8,128)(2,1)S(1)}, bf16[80,960]{1,0:T(8,128)(2,1)S(1)}, u32[]{:S(2)}, u32[]{:S(2)}) collective-permute-start(bf16[80,960]{1,0:T(8,128)(2,1)S(1)} %shard_map.103.refs_1_), channel_id=1, source_target_pairs={{0,32},{1,33},{2,34},{3,35},{4,36},{5,37},{6,38},{7,39},{8,40},{9,... | collective-permute-start | bytes 460808 | tf_op jit(solution)/shard_map/ppermute | solution.py:26
  84.7 6.8 %collective-permute-start.22 = (bf16[80,960]{1,0:T(8,128)(2,1)S(1)}, bf16[80,960]{1,0:T(8,128)(2,1)S(1)}, u32[]{:S(2)}, u32[]{:S(2)}) collective-permute-start(bf16[80,960]{1,0:T(8,128)(2,1)S(1)} %shard_map.103.refs_1_), channel_id=1, source_target_pairs={{0,48},{1,49},{2,50},{3,51},{4,52},{5,53},{6,54},{7,55},{8,56},{9,... | collective-permute-start | bytes 460808 | tf_op jit(solution)/shard_map/ppermute | solution.py:26
  84.7 7.1 %collective-permute-start.21 = (bf16[80,960]{1,0:T(8,128)(2,1)S(1)}, bf16[80,960]{1,0:T(8,128)(2,1)S(1)}, u32[]{:S(2)}, u32[]{:S(2)}) collective-permute-start(bf16[80,960]{1,0:T(8,128)(2,1)S(1)} %shard_map.103.refs_1_), channel_id=1, source_target_pairs={{0,16},{1,17},{2,18},{3,19},{4,20},{5,21},{6,22},{7,23},{8,24},{9,... | collective-permute-start | bytes 460808 | tf_op jit(solution)/shard_map/ppermute | solution.py:26
  86.7 5.3 %collective-permute-start.24 = (bf16[80,960]{1,0:T(8,128)(2,1)S(1)}, bf16[80,960]{1,0:T(8,128)(2,1)S(1)}, u32[]{:S(2)}, u32[]{:S(2)}) collective-permute-start(bf16[80,960]{1,0:T(8,128)(2,1)S(1)} %shard_map.103.refs_1_), channel_id=1, source_target_pairs={{0,8},{1,9},{2,10},{3,11},{4,12},{5,13},{6,14},{7,15},{8,0},{9,1},... | collective-permute-start | bytes 460808 | tf_op jit(solution)/shard_map/ppermute | solution.py:26
  89.8 2.2 %collective-permute-start.27 = (bf16[80,960]{1,0:T(8,128)(2,1)S(1)}, bf16[80,960]{1,0:T(8,128)(2,1)S(1)}, u32[]{:S(2)}, u32[]{:S(2)}) collective-permute-start(bf16[80,960]{1,0:T(8,128)(2,1)S(1)} %collective-permute-done.23.refs_4_), channel_id=1, source_target_pairs={{0,8},{1,9},{2,10},{3,11},{4,12},{5,13},{6,14},{7,15},{8,0},{9,1},... | collective-permute-start | bytes 460808 | tf_op jit(solution)/shard_map/ppermute | solution.py:26
  91.5 1.4 %collective-permute-start.26 = (bf16[80,960]{1,0:T(8,128)(2,1)S(1)}, bf16[80,960]{1,0:T(8,128)(2,1)S(1)}, u32[]{:S(2)}, u32[]{:S(2)}) collective-permute-start(bf16[80,960]{1,0:T(8,128)(2,1)S(1)} %collective-permute-done.22.refs_3_), channel_id=1, source_target_pairs={{0,8},{1,9},{2,10},{3,11},{4,12},{5,13},{6,14},{7,15},{8,0},{9,1},... | collective-permute-start | bytes 460808 | tf_op jit(solution)/shard_map/ppermute | solution.py:26
  91.8 1.4 %collective-permute-start.25 = (bf16[80,960]{1,0:T(8,128)(2,1)S(1)}, bf16[80,960]{1,0:T(8,128)(2,1)S(1)}, u32[]{:S(2)}, u32[]{:S(2)}) collective-permute-start(bf16[80,960]{1,0:T(8,128)(2,1)S(1)} %collective-permute-done.21.refs_2_), channel_id=1, source_target_pairs={{0,8},{1,9},{2,10},{3,11},{4,12},{5,13},{6,14},{7,15},{8,0},{9,1},... | collective-permute-start | bytes 460808 | tf_op jit(solution)/shard_map/ppermute | solution.py:26
  94.2 10.1 %collective-permute-start.29 = (bf16[64,640]{1,0:T(8,128)(2,1)S(1)}, bf16[64,640]{1,0:T(8,128)(2,1)S(1)}, u32[]{:S(2)}, u32[]{:S(2)}) collective-permute-start(bf16[64,640]{1,0:T(8,128)(2,1)S(1)} %get-tuple-element.55), channel_id=1, source_target_pairs={{0,196},{1,197},{2,198},{3,199},{4,64},{5,65},{6,66},{7,67},{8,204... | collective-permute-start | bytes 245768 | tf_op jit(solution)/shard_map/ppermute | solution.py:26
  95.5 8.7 %collective-permute-start.28 = (bf16[64,640]{1,0:T(8,128)(2,1)S(1)}, bf16[64,640]{1,0:T(8,128)(2,1)S(1)}, u32[]{:S(2)}, u32[]{:S(2)}) collective-permute-start(bf16[64,640]{1,0:T(8,128)(2,1)S(1)} %get-tuple-element.53.refs_9_), channel_id=1, source_target_pairs={{0,4},{1,5},{2,6},{3,7},{4,0},{5,1},{6,2},{7,3},{8,12},{9,13},{10,... | collective-permute-start | bytes 245768 | tf_op jit(solution)/shard_map/ppermute | solution.py:26
  97.1 4.2 %collective-permute-start.30 = (bf16[32,640]{1,0:T(8,128)(2,1)S(1)}, bf16[32,640]{1,0:T(8,128)(2,1)S(1)}, u32[]{:S(2)}, u32[]{:S(2)}) collective-permute-start(bf16[32,640]{1,0:T(8,128)(2,1)S(1)} %get-tuple-element.56), channel_id=1, source_target_pairs={{0,1},{1,0},{2,3},{3,2},{4,5},{5,4},{6,7},{7,6},{8,9},{9,8},{10,11... | collective-permute-start | bytes 122888 | tf_op jit(solution)/shard_map/ppermute | solution.py:26
  97.8 4.0 %collective-permute-start.31 = (bf16[32,640]{1,0:T(8,128)(2,1)S(1)}, bf16[32,640]{1,0:T(8,128)(2,1)S(1)}, u32[]{:S(2)}, u32[]{:S(2)}) collective-permute-start(bf16[32,640]{1,0:T(8,128)(2,1)S(1)} %get-tuple-element.57), channel_id=1, source_target_pairs={{0,3},{1,2},{2,1},{3,0},{4,7},{5,6},{6,5},{7,4},{8,11},{9,10},{10,... | collective-permute-start | bytes 122888 | tf_op jit(solution)/shard_map/ppermute | solution.py:26
  98.8 5.5 %collective-permute-start.32 = (bf16[32,640]{1,0:T(8,128)(2,1)S(1)}, bf16[32,640]{1,0:T(8,128)(2,1)S(1)}, u32[]{:S(2)}, u32[]{:S(2)}) collective-permute-start(bf16[32,640]{1,0:T(8,128)(2,1)S(1)} %get-tuple-element.58), channel_id=1, source_target_pairs={{0,2},{1,3},{2,0},{3,1},{4,6},{5,7},{6,4},{7,5},{8,10},{9,11},{10,... | collective-permute-start | bytes 122888 | tf_op jit(solution)/shard_map/ppermute | solution.py:26
  104.4 4.8 %collective-permute-start.33 = (bf16[32,640]{1,0:T(8,128)(2,1)S(1)}, bf16[32,640]{1,0:T(8,128)(2,1)S(1)}, u32[]{:S(2)}, u32[]{:S(2)}) collective-permute-start(bf16[32,640]{1,0:T(8,128)(2,1)S(1)} %get-tuple-element.60), channel_id=1, source_target_pairs={{0,1},{1,0},{2,3},{3,2},{4,5},{5,4},{6,7},{7,6},{8,9},{9,8},{10,11... | collective-permute-start | bytes 122888 | tf_op jit(solution)/shard_map/ppermute | solution.py:26
  107.0 4.0 %collective-permute-start.34 = (bf16[32,640]{1,0:T(8,128)(2,1)S(1)}, bf16[32,640]{1,0:T(8,128)(2,1)S(1)}, u32[]{:S(2)}, u32[]{:S(2)}) collective-permute-start(bf16[32,640]{1,0:T(8,128)(2,1)S(1)} %get-tuple-element.61), channel_id=1, source_target_pairs={{0,3},{1,2},{2,1},{3,0},{4,7},{5,6},{6,5},{7,4},{8,11},{9,10},{10,... | collective-permute-start | bytes 122888 | tf_op jit(solution)/shard_map/ppermute | solution.py:26
  107.5 5.5 %collective-permute-start.35 = (bf16[32,640]{1,0:T(8,128)(2,1)S(1)}, bf16[32,640]{1,0:T(8,128)(2,1)S(1)}, u32[]{:S(2)}, u32[]{:S(2)}) collective-permute-start(bf16[32,640]{1,0:T(8,128)(2,1)S(1)} %get-tuple-element.62), channel_id=1, source_target_pairs={{0,2},{1,3},{2,0},{3,1},{4,6},{5,7},{6,4},{7,5},{8,10},{9,11},{10,... | collective-permute-start | bytes 122888 | tf_op jit(solution)/shard_map/ppermute | solution.py:26

commit v9 on v8

--- a/solution.py
+++ b/solution.py
@@ -99,13 +99,16 @@
     )(*args, *after)
 
 
-def split_kernel(near_tile, far_tile, z1, z2, near_first, far_second, first, second, both):
-    near_first[...] = near_tile[:32, :]
-    far_second[...] = far_tile[32:, :]
-    first[:16, :] = near_tile[16:32, :]
-    first[16:, :] = far_tile[16:32, :]
-    second[:16, :] = near_tile[48:, :]
-    second[16:, :] = far_tile[48:, :]
+def halve_kernel(tile, first, second):
+    first[...] = tile[:32, :]
+    second[...] = tile[32:, :]
+
+
+def split_kernel(near_a, near_b, far_a, far_b, z1, z2, first, second, both):
+    first[:16, :] = near_a[16:, :]
+    first[16:, :] = far_a[16:, :]
+    second[:16, :] = near_b[16:, :]
+    second[16:, :] = far_b[16:, :]
     both[:16, :] = z1[:16, :]
     both[16:, :] = z2[:16, :]
 
@@ -223,23 +226,26 @@
         at += 2 * n
 
 
-PLANE = [(0, 0, 64), (1, 0, 64), (2, 0, 64), (3, 0, 32), (4, 0, 32)]
+PLANE = [(0, 0, 64)] + [(i, 0, 32) for i in range(1, 7)]
 OTHERS = [(0, 0, 32), (2, 0, 16), (4, 0, 16), (3, 0, 16), (4, 16, 32), (6, 0, 32)]
 OTHERS += [(1, 0, 32), (2, 16, 32), (5, 0, 16), (3, 16, 32), (5, 16, 32), (7, 0, 32)]
 
 
 def gather(tokens, work):
-    near_tile, far_tile = to_near_x(tokens), to_far_x(tokens)
-    z1, z2 = to_near_z(tokens[:32]), to_far_z(tokens[32:])
-    near_first, far_second, first, second, both = call(
-        split_kernel, [like((32, 5120))] * 5, near_tile, far_tile, z1, z2, after=work
-    )
-    opposite_first, opposite_second = to_far_x(near_first), to_near_x(far_second)
+    half = [like((32, 5120))]
+    a, b = call(halve_kernel, half * 2, tokens)
+    near_a, far_b = to_near_x(a), to_far_x(b)
+    z1, z2 = to_near_z(a), to_far_z(b)
+    near_b, far_a = to_near_x(b), to_far_x(a)
+    opposite_first, opposite_second = to_far_x(near_a), to_near_x(far_b)
+    first, second, both = call(
+        split_kernel, half * 3, near_a, near_b, far_a, far_b, z1, z2, after=work
+    )
     z3, z4 = to_near_z(first), to_far_z(second)
     near_both, far_both = to_near_x(both), to_far_x(both)
     z5, z6 = to_near_z(opposite_first), to_far_z(opposite_second)
     return (
-        [tokens, near_tile, far_tile, opposite_first, opposite_second],
+        [tokens, near_a, near_b, far_a, far_b, opposite_first, opposite_second],
         [z1, z2, near_both, far_both, z3, z4, z5, z6],
     )
 
@@ -268,38 +274,34 @@
         sent[:, i * 32 : (i + 1) * 32] = other[:, 32:]
 
 
-def pieces_kernel(from_near, from_far, *outs):
+def pieces_kernel(plane, from_near, from_far, *outs):
     for i, out in enumerate(outs):
-        at = slice(i % 2 * 32, i % 2 * 32 + 32), slice(i // 2 * 320, i // 2 * 320 + 320)
-        out[:, :320] = from_near[at]
-        out[:, 320:] = from_far[at]
-
-
-def place_kernel(my, *refs):
-    pieces, out, slots = refs[:8], refs[8], refs[9]
-    for i, piece in enumerate(pieces):
-        slots[i, :32] = piece[:, :320]
-        slots[i, 32:] = piece[:, 320:]
+        run = slice(i // 2 * 320, i // 2 * 320 + 320)
+        half = slice(i % 2 * 32, i % 2 * 32 + 32)
+        out[:, :320] = plane[i % 2 * 64 : i % 2 * 64 + 64, run]
+        out[:32, 320:] = from_near[half, run]
+        out[32:, 320:] = from_far[half, run]
+
+
+def place_kernel(my, a, b, c, d, out, slots):
+    for i, piece in enumerate((a, b, c, d)):
+        slots[2 * i] = piece[:, :320]
+        slots[2 * i + 1] = piece[:, 320:]
     for head in range(8):
         out[:, head * 320 : (head + 1) * 320] = slots[my[SLOT + head]]
 
 
-def to_plane(pieces):
-    opposite, near_piece = to_opposite_x(pieces[3]), to_near_x(pieces[1])
-    return pieces[0], near_piece, to_far_x(pieces[2]), opposite
-
-
 def send_back(my, plane, for_near, for_far):
-    from_near, from_far = to_near_z(for_near), to_far_z(for_far)
-    own = to_plane(plane)
-    pieces = call(pieces_kernel, [like((32, 640))] * 4, from_near, from_far, after=own[1:])
-    other = to_plane(pieces)
-    slots = [piece for pair in zip(own, other) for piece in pair]
+    pieces = call(
+        pieces_kernel, [like((64, 640))] * 4, plane, to_near_z(for_near), to_far_z(for_far)
+    )
+    opposite = to_opposite_x(pieces[3])
+    pieces = pieces[0], to_near_x(pieces[1]), to_far_x(pieces[2]), opposite
     return call(
         place_kernel,
         like((64, 2560)),
         my,
-        *slots,
+        *pieces,
         scalars=1,
         scratch=[pltpu.VMEM((8, 64, 320), BF16)],
     )
@@ -359,9 +361,9 @@
     for_near, for_far = call(
         functools.partial(respond_kernel, 256), [like((64, 640))] * 2, query, *blocks
     )
-    plane = call(
+    (plane,) = call(
         functools.partial(respond_kernel, 0),
-        [like((32, 640))] * 4,
+        [like((128, 640))],
         query,
         *blocks,
         after=(for_near,),

time: 115 us -> 117 us (1.017); the launches traced: 115 us -> 115 us
  starting transfers between devices: 51.5 us -> 55.2 us
  waiting for transfers between devices: 32.4 us -> 29.1 us
    ppermute x36 -> x35, starting transfers between devices: 51.5 us -> 55.2 us  [permute(): return lax.ppermute(value, AXES, pairs)]
    ppermute x36 -> x35, waiting for transfers between devices: 32.4 us -> 29.1 us  [permute(): return lax.ppermute(value, AXES, pairs)]
    slice x1 -> x0, local copies, waits for them, and re-layouts: 1.96 us -> none  [gather(): z1, z2 = (to_near_z(tokens[:32]), to_far_z(tokens[32:]))]
    unnamed x7 -> x9, local copies, waits for them, and re-layouts: 4.39 us -> 5.47 us
    pallas_call x15 -> x16, Pallas kernels: 15.4 us -> 16.3 us  [call(): pl.pallas_call(run, out_shape=out_shape, in_specs=[SMEM] * scalars + [VME...]
  transfers between devices with their start and end apart: 36 -> 35, of which waited for: 19 -> 16; matrix products, arithmetic and copies ran while one was open for 8% -> 6% of each run, Pallas kernels for 12% -> 12%
where the time goes in v9:
time: 117 us; the launch traced here: 115 us
  starting transfers between devices  55.2 us (47%)
  waiting for transfers between devices  29.1 us (25%)
  Pallas kernels  21.4 us (18%)
  local copies, waits for them, and re-layouts  6.35 us (5%)
  other arithmetic  2.08 us (2%)
    ppermute x35, starting transfers between devices, permute(): return lax.ppermute(value, AXES, pairs)  55.2 us
    ppermute x35, waiting for transfers between devices, permute(): return lax.ppermute(value, AXES, pairs)  29.1 us
    pallas_call x16, Pallas kernels, call(): pl.pallas_call(run, out_shape=out_shape, in_specs=[SMEM] * scalars + [VME...  16.3 us
    unnamed x9, local copies, waits for them, and re-layouts  5.47 us
    pallas_call x2, Pallas kernels, load(): pl.pallas_call(run, out_shape=like((count, *w_t.shape[1:])), in_specs=[pl...  5 us
  transfers between devices with their start and end apart: 35, of which 16 were waited for; matrix products, arithmetic and copies ran while one was open for 6% of the time, Pallas kernels for 12%

profile of v9, /device:TPU:2, one launch (start us, length us, event | category | flops | bytes accessed | tf_op | source)
XLA Modules:
  0.0 115.0 jit_solution(10887962757630386990)
XLA Ops:
  0.0 0.7 dynamic-slice_bitcast_fusion.refs_0_
  0.7 1.1 copy-done
  1.8 0.9 shard_map.91
  2.7 1.9 %collective-permute-start.6 = (bf16[32,5120]{1,0:T(8,128)(2,1)}, bf16[32,5120]{1,0:T(8,128)(2,1)S(1)}, u32[]{:S(2)}, u32[]{:S(2)}) collective-permute-start(bf16[32,5120]{1,0:T(8,128)(2,1)} %get-tuple-element.32), channel_id=1, source_target_pairs={{0,4},{1,5},{2,6},{3,7},{4,0},{5,1},{6,2},{7,3},{8,12},{9,13},{10,... | collective-permute-start | bytes 983048 | tf_op jit(solution)/shard_map/ppermute | solution.py:26
  4.6 0.5 collective-permute-start
  5.1 2.2 %collective-permute-start.3 = (bf16[32,5120]{1,0:T(8,128)(2,1)}, bf16[32,5120]{1,0:T(8,128)(2,1)S(1)}, u32[]{:S(2)}, u32[]{:S(2)}) collective-permute-start(bf16[32,5120]{1,0:T(8,128)(2,1)} %get-tuple-element.33), channel_id=1, source_target_pairs={{0,3},{1,2},{2,1},{3,0},{4,7},{5,6},{6,5},{7,4},{8,11},{9,10},{10,... | collective-permute-start | bytes 983048 | tf_op jit(solution)/shard_map/ppermute | solution.py:26
  7.3 4.9 %collective-permute-start.7 = (bf16[32,5120]{1,0:T(8,128)(2,1)}, bf16[32,5120]{1,0:T(8,128)(2,1)S(1)}, u32[]{:S(2)}, u32[]{:S(2)}) collective-permute-start(bf16[32,5120]{1,0:T(8,128)(2,1)} %get-tuple-element.33), channel_id=1, source_target_pairs={{0,196},{1,197},{2,198},{3,199},{4,64},{5,65},{6,66},{7,67},{8,204... | collective-permute-start | bytes 983048 | tf_op jit(solution)/shard_map/ppermute | solution.py:26
  12.3 0.2 collective-permute-done.6.refs_4_.refs_0_.refs_7_
  12.5 2.3 %collective-permute-start.1 = (bf16[32,5120]{1,0:T(8,128)(2,1)}, bf16[32,5120]{1,0:T(8,128)(2,1)S(1)}, u32[]{:S(2)}, u32[]{:S(2)}) collective-permute-start(bf16[32,5120]{1,0:T(8,128)(2,1)} %get-tuple-element.33), channel_id=1, source_target_pairs={{0,1},{1,0},{2,3},{3,2},{4,5},{5,4},{6,7},{7,6},{8,9},{9,8},{10,11... | collective-permute-start | bytes 983048 | tf_op jit(solution)/shard_map/ppermute | solution.py:26
  15.5 0.6 broadcast.3
  16.0 1.4 %reduce.3 = s32[512]{0:T(512)S(1)} reduce(s32[512,1]{0,1:T(1,128)} %param.12, s32[]{:T(128)} %broadcast.3), dimensions={1}, to_apply=%param.12.reduce_sub_computation.3 | reduce | bytes 4100 | tf_op args[3]
  17.5 0.6 shard_map.92
  18.1 0.7 exponential_convert_fusion
  18.9 1.3 %copy.13 = bf16[1,320,640]{1,2,0:T(8,128)(2,1)S(1)} copy(bf16[1,320,640]{2,1,0:T(8,128)(2,1)} %param.14) | data formatting | bytes 819200 | tf_op args[5]
  20.2 1.3 %copy.14 = bf16[1,320,640]{1,2,0:T(8,128)(2,1)S(1)} copy(bf16[1,320,640]{2,1,0:T(8,128)(2,1)} %param.15) | data formatting | bytes 819200 | tf_op args[6]
  21.5 1.3 %copy.15 = bf16[1,320,640]{1,2,0:T(8,128)(2,1)S(1)} copy(bf16[1,320,640]{2,1,0:T(8,128)(2,1)} %param.16) | data formatting | bytes 819200 | tf_op args[7]
  22.8 3.0 %shard_map.93.refs_6_.refs_7_.refs_8_ = bf16[2,320,5120]{2,1,0:T(8,128)(2,1)S(1)} custom-call(bf16[3,320,5120]{2,1,0:T(8,128)(2,1)} %bitcast.28, bf16[3,1,5120]{2,1,0:T(2,128)(2,1)S(1)} %broadcast_in_dim_reshape.4.refs_1_, f32[1,384]{1,0:T(1,128)S(1)} %get-tuple-element.34.refs_2_.refs_3_, bf16[640,320]{1,0:T(8,128)(2,1)S(1)} %bitcast.16, ...), custom_call_target="tpu_custom_call" | custom-call | flops 1000 | bytes 1000 | tf_op jit(solution)/shard_map/pallas_call | solution.py:134
  25.8 1.6 %collective-permute-start.4 = (bf16[32,5120]{1,0:T(8,128)(2,1)S(1)}, bf16[32,5120]{1,0:T(8,128)(2,1)S(1)}, u32[]{:S(2)}, u32[]{:S(2)}) collective-permute-start(bf16[32,5120]{1,0:T(8,128)(2,1)S(1)} %collective-permute-done.refs_0_.refs_1_), channel_id=1, source_target_pairs={{0,3},{1,2},{2,1},{3,0},{4,7},{5,6},{6,5},{7,4},{8,11},{9,10},{10,... | collective-permute-start | bytes 983048 | tf_op jit(solution)/shard_map/ppermute | solution.py:26
  27.4 0.6 collective-permute-start.5
  28.1 1.6 %collective-permute-start.10 = (bf16[32,5120]{1,0:T(8,128)(2,1)S(1)}, bf16[32,5120]{1,0:T(8,128)(2,1)S(1)}, u32[]{:S(2)}, u32[]{:S(2)}) collective-permute-start(bf16[32,5120]{1,0:T(8,128)(2,1)S(1)} %get-tuple-element.36), channel_id=1, source_target_pairs={{0,4},{1,5},{2,6},{3,7},{4,0},{5,1},{6,2},{7,3},{8,12},{9,13},{10,... | collective-permute-start | bytes 983048 | tf_op jit(solution)/shard_map/ppermute | solution.py:26
  29.6 4.9 %collective-permute-start.11 = (bf16[32,5120]{1,0:T(8,128)(2,1)S(1)}, bf16[32,5120]{1,0:T(8,128)(2,1)S(1)}, u32[]{:S(2)}, u32[]{:S(2)}) collective-permute-start(bf16[32,5120]{1,0:T(8,128)(2,1)S(1)} %get-tuple-element.37), channel_id=1, source_target_pairs={{0,196},{1,197},{2,198},{3,199},{4,64},{5,65},{6,66},{7,67},{8,204... | collective-permute-start | bytes 983048 | tf_op jit(solution)/shard_map/ppermute | solution.py:26
  34.6 0.5 collective-permute-start.9
  35.1 0.8 collective-permute-start.8
  35.9 2.4 %collective-permute-start.12 = (bf16[32,5120]{1,0:T(8,128)(2,1)S(1)}, bf16[32,5120]{1,0:T(8,128)(2,1)S(1)}, u32[]{:S(2)}, u32[]{:S(2)}) collective-permute-start(bf16[32,5120]{1,0:T(8,128)(2,1)S(1)} %collective-permute-done.4.refs_5_), channel_id=1, source_target_pairs={{0,4},{1,5},{2,6},{3,7},{4,0},{5,1},{6,2},{7,3},{8,12},{9,13},{10,... | collective-permute-start | bytes 983048 | tf_op jit(solution)/shard_map/ppermute | solution.py:26
  38.2 5.9 %collective-permute-start.13 = (bf16[32,5120]{1,0:T(8,128)(2,1)S(1)}, bf16[32,5120]{1,0:T(8,128)(2,1)S(1)}, u32[]{:S(2)}, u32[]{:S(2)}) collective-permute-start(bf16[32,5120]{1,0:T(8,128)(2,1)S(1)} %collective-permute-done.5.refs_6_), channel_id=1, source_target_pairs={{0,196},{1,197},{2,198},{3,199},{4,64},{5,65},{6,66},{7,67},{8,204... | collective-permute-start | bytes 983048 | tf_op jit(solution)/shard_map/ppermute | solution.py:26
  44.2 1.9 %shard_map.95.refs_9_.refs_1_ = bf16[640,256]{1,0:T(8,128)(2,1)S(1)} custom-call(bf16[64,5120]{1,0:T(8,128)(2,1)S(1)} %copy-done.1, bf16[32,5120]{1,0:T(8,128)(2,1)S(1)} %collective-permute-done.refs_0_.refs_1_, bf16[32,5120]{1,0:T(8,128)(2,1)S(1)} %collective-permute-done.1.refs_1_.refs_2_, bf16[32,5120]{1,0:T(8,128)(2,1)S(1)} %collective-permute-done.2.refs_2_.refs_3_, ...), custom_call_target="tpu_custom_call" | custom-call | flops 1000 | bytes 1000 | tf_op jit(solution)/shard_map/pallas_call | solution.py:91
  46.1 3.1 %collective-permute-done.13.refs_7_.refs_14_ = bf16[32,5120]{1,0:T(8,128)(2,1)S(1)} collective-permute-done((bf16[32,5120]{1,0:T(8,128)(2,1)S(1)}, bf16[32,5120]{1,0:T(8,128)(2,1)S(1)}, u32[]{:S(2)}, u32[]{:S(2)}) %collective-permute-start.13) | collective-permute-done | bytes 327712 | tf_op jit(solution)/shard_map/ppermute | solution.py:26
  49.2 1.9 %shard_map.96.refs_2_ = bf16[640,256]{1,0:T(8,128)(2,1)S(1)} custom-call(bf16[32,5120]{1,0:T(8,128)(2,1)S(1)} %collective-permute-done.6.refs_4_.refs_0_.refs_7_, bf16[32,5120]{1,0:T(8,128)(2,1)S(1)} %collective-permute-done.7.refs_5_.refs_1_.refs_8_, bf16[32,5120]{1,0:T(8,128)(2,1)S(1)} %collective-permute-done.8.refs_8_.refs_2_.refs_9_, ...), custom_call_target="tpu_custom_call" | custom-call | flops 1000 | bytes 1000 | tf_op jit(solution)/shard_map/pallas_call | solution.py:91
  51.1 1.9 %shard_map.97.refs_8_ = bf16[320,960]{1,0:T(8,128)(2,1)S(1)} custom-call(s32[32]{0:T(128)S(1)} %dynamic-slice_bitcast_fusion.refs_0_, bf16[640,256]{1,0:T(8,128)(2,1)S(1)} %shard_map.95.refs_9_.refs_1_, bf16[640,256]{1,0:T(8,128)(2,1)S(1)} %shard_map.96.refs_2_, f32[1,384]{1,0:T(1,128)S(1)} %get-tuple-element.34.refs_2_.refs_3_, ...), custom_call_target="tpu_custom_call" | custom-call | flops 1000 | bytes 1000 | tf_op jit(solution)/shard_map/pallas_call | solution.py:91
  53.2 1.9 %shard_map.98.refs_1_ = f32[320,960]{1,0:T(8,128)S(1)} custom-call(s32[32]{0:T(128)S(1)} %dynamic-slice_bitcast_fusion.refs_0_, bf16[640,256]{1,0:T(8,128)(2,1)S(1)} %shard_map.95.refs_9_.refs_1_, bf16[640,256]{1,0:T(8,128)(2,1)S(1)} %shard_map.96.refs_2_, f32[1,384]{1,0:T(1,128)S(1)} %get-tuple-element.34.refs_2_.refs_3_, ...), custom_call_target="tpu_custom_call" | custom-call | flops 1000 | bytes 1000 | tf_op jit(solution)/shard_map/pallas_call | solution.py:91
  55.2 0.7 shard_map.99
  55.9 3.3 %collective-permute-start.16 = (bf16[80,960]{1,0:T(8,128)(2,1)S(1)}, bf16[80,960]{1,0:T(8,128)(2,1)S(1)}, u32[]{:S(2)}, u32[]{:S(2)}) collective-permute-start(bf16[80,960]{1,0:T(8,128)(2,1)S(1)} %get-tuple-element.41), channel_id=1, source_target_pairs={{0,32},{1,33},{2,34},{3,35},{4,36},{5,37},{6,38},{7,39},{8,40},{9,... | collective-permute-start | bytes 460808 | tf_op jit(solution)/shard_map/ppermute | solution.py:26
  59.2 1.1 collective-permute-start.18
  60.2 1.0 collective-permute-start.17
  61.2 2.0 %shard_map.100.refs_4_.refs_15_ = bf16[1,320,5120]{2,1,0:T(8,128)(2,1)S(1)} custom-call(bf16[3,320,5120]{2,1,0:T(8,128)(2,1)} %bitcast.29, bf16[3,1,5120]{2,1,0:T(2,128)(2,1)S(1)} %broadcast_in_dim_reshape.4.refs_1_, bf16[80,960]{1,0:T(8,128)(2,1)S(1)} %get-tuple-element.39.refs_2_), custom_call_target="tpu_custom_call" | custom-call | flops 1000 | bytes 1000 | tf_op jit(solution)/shard_map/pallas_call | solution.py:134
  63.2 1.3 %collective-permute-done.16.refs_1_ = bf16[80,960]{1,0:T(8,128)(2,1)S(1)} collective-permute-done((bf16[80,960]{1,0:T(8,128)(2,1)S(1)}, bf16[80,960]{1,0:T(8,128)(2,1)S(1)}, u32[]{:S(2)}, u32[]{:S(2)}) %collective-permute-start.16) | collective-permute-done | bytes 153632 | tf_op jit(solution)/shard_map/ppermute | solution.py:26
  64.5 3.3 %collective-permute-done.18.refs_3_ = bf16[80,960]{1,0:T(8,128)(2,1)S(1)} collective-permute-done((bf16[80,960]{1,0:T(8,128)(2,1)S(1)}, bf16[80,960]{1,0:T(8,128)(2,1)S(1)}, u32[]{:S(2)}, u32[]{:S(2)}) %collective-permute-start.18) | collective-permute-done | bytes 153632 | tf_op jit(solution)/shard_map/ppermute | solution.py:26
  67.9 2.6 %collective-permute-start.20 = (bf16[40,960]{1,0:T(8,128)(2,1)S(1)}, bf16[40,960]{1,0:T(8,128)(2,1)S(1)}, u32[]{:S(2)}, u32[]{:S(2)}) collective-permute-start(bf16[40,960]{1,0:T(8,128)(2,1)S(1)} %get-tuple-element.45), channel_id=1, source_target_pairs={{0,192},{1,193},{2,194},{3,195},{4,196},{5,197},{6,198},{7,199},{8... | collective-permute-start | bytes 230408 | tf_op jit(solution)/shard_map/ppermute | solution.py:26
  70.5 2.7 %collective-permute-start.19 = (bf16[40,960]{1,0:T(8,128)(2,1)S(1)}, bf16[40,960]{1,0:T(8,128)(2,1)S(1)}, u32[]{:S(2)}, u32[]{:S(2)}) collective-permute-start(bf16[40,960]{1,0:T(8,128)(2,1)S(1)} %get-tuple-element.43.refs_16_), channel_id=1, source_target_pairs={{0,64},{1,65},{2,66},{3,67},{4,68},{5,69},{6,70},{7,71},{8,72},{9,... | collective-permute-start | bytes 230408 | tf_op jit(solution)/shard_map/ppermute | solution.py:26
  73.2 1.9 %shard_map.102.refs_3_.refs_0_ = bf16[320,512]{1,0:T(8,128)(2,1)S(1)} custom-call(bf16[64,5120]{1,0:T(8,128)(2,1)S(1)} %copy-done.1, bf16[32,5120]{1,0:T(8,128)(2,1)S(1)} %collective-permute-done.refs_0_.refs_1_, bf16[32,5120]{1,0:T(8,128)(2,1)S(1)} %collective-permute-done.1.refs_1_.refs_2_, bf16[32,5120]{1,0:T(8,128)(2,1)S(1)} %collective-permute-done.2.refs_2_.refs_3_, ...), custom_call_target="tpu_custom_call" | custom-call | flops 1000 | bytes 1000 | tf_op jit(solution)/shard_map/pallas_call | solution.py:91
  75.1 0.8 collective-permute-done.20.refs_2_
  75.9 1.7 %collective-permute-done.19.refs_1_ = bf16[40,960]{1,0:T(8,128)(2,1)S(1)} collective-permute-done((bf16[40,960]{1,0:T(8,128)(2,1)S(1)}, bf16[40,960]{1,0:T(8,128)(2,1)S(1)}, u32[]{:S(2)}, u32[]{:S(2)}) %collective-permute-start.19) | collective-permute-done | bytes 76832 | tf_op jit(solution)/shard_map/ppermute | solution.py:26
  77.6 0.9 collective-permute-start.21
  78.6 2.4 %collective-permute-start.22 = (bf16[40,960]{1,0:T(8,128)(2,1)S(1)}, bf16[40,960]{1,0:T(8,128)(2,1)S(1)}, u32[]{:S(2)}, u32[]{:S(2)}) collective-permute-start(bf16[40,960]{1,0:T(8,128)(2,1)S(1)} %get-tuple-element.48), channel_id=1, source_target_pairs={{0,64},{1,65},{2,66},{3,67},{4,68},{5,69},{6,70},{7,71},{8,72},{9,... | collective-permute-start | bytes 230408 | tf_op jit(solution)/shard_map/ppermute | solution.py:26
  81.0 4.9 %collective-permute-done.21.refs_2_ = bf16[40,960]{1,0:T(8,128)(2,1)S(1)} collective-permute-done((bf16[40,960]{1,0:T(8,128)(2,1)S(1)}, bf16[40,960]{1,0:T(8,128)(2,1)S(1)}, u32[]{:S(2)}, u32[]{:S(2)}) %collective-permute-start.21) | collective-permute-done | bytes 76832 | tf_op jit(solution)/shard_map/ppermute | solution.py:26
  85.9 0.9 shard_map.104.refs_1_
  86.8 2.1 %collective-permute-start.25 = (bf16[80,960]{1,0:T(8,128)(2,1)S(1)}, bf16[80,960]{1,0:T(8,128)(2,1)S(1)}, u32[]{:S(2)}, u32[]{:S(2)}) collective-permute-start(bf16[80,960]{1,0:T(8,128)(2,1)S(1)} %shard_map.104.refs_1_), channel_id=1, source_target_pairs={{0,32},{1,33},{2,34},{3,35},{4,36},{5,37},{6,38},{7,39},{8,40},{9,... | collective-permute-start | bytes 460808 | tf_op jit(solution)/shard_map/ppermute | solution.py:26
  88.9 1.1 collective-permute-start.24
  90.0 0.9 collective-permute-start.23
  90.9 2.9 %collective-permute-done.25.refs_4_ = bf16[80,960]{1,0:T(8,128)(2,1)S(1)} collective-permute-done((bf16[80,960]{1,0:T(8,128)(2,1)S(1)}, bf16[80,960]{1,0:T(8,128)(2,1)S(1)}, u32[]{:S(2)}, u32[]{:S(2)}) %collective-permute-start.25) | collective-permute-done | bytes 153632 | tf_op jit(solution)/shard_map/ppermute | solution.py:26
  93.8 1.2 %collective-permute-done.24.refs_3_ = bf16[80,960]{1,0:T(8,128)(2,1)S(1)} collective-permute-done((bf16[80,960]{1,0:T(8,128)(2,1)S(1)}, bf16[80,960]{1,0:T(8,128)(2,1)S(1)}, u32[]{:S(2)}, u32[]{:S(2)}) %collective-permute-start.24) | collective-permute-done | bytes 153632 | tf_op jit(solution)/shard_map/ppermute | solution.py:26
  95.0 1.6 %collective-permute-done.23.refs_2_ = bf16[80,960]{1,0:T(8,128)(2,1)S(1)} collective-permute-done((bf16[80,960]{1,0:T(8,128)(2,1)S(1)}, bf16[80,960]{1,0:T(8,128)(2,1)S(1)}, u32[]{:S(2)}, u32[]{:S(2)}) %collective-permute-start.23) | collective-permute-done | bytes 153632 | tf_op jit(solution)/shard_map/ppermute | solution.py:26
  96.6 1.4 %collective-permute-done.27.refs_6_ = bf16[80,960]{1,0:T(8,128)(2,1)S(1)} collective-permute-done((bf16[80,960]{1,0:T(8,128)(2,1)S(1)}, bf16[80,960]{1,0:T(8,128)(2,1)S(1)}, u32[]{:S(2)}, u32[]{:S(2)}) %collective-permute-start.27) | collective-permute-done | bytes 153632 | tf_op jit(solution)/shard_map/ppermute | solution.py:26
  98.0 1.0 shard_map.105
  98.9 2.1 %collective-permute-start.31 = (bf16[64,640]{1,0:T(8,128)(2,1)S(1)}, bf16[64,640]{1,0:T(8,128)(2,1)S(1)}, u32[]{:S(2)}, u32[]{:S(2)}) collective-permute-start(bf16[64,640]{1,0:T(8,128)(2,1)S(1)} %get-tuple-element.50), channel_id=1, source_target_pairs={{0,196},{1,197},{2,198},{3,199},{4,64},{5,65},{6,66},{7,67},{8,204... | collective-permute-start | bytes 245768 | tf_op jit(solution)/shard_map/ppermute | solution.py:26
  101.1 0.6 collective-permute-start.30
  101.7 1.0 shard_map.106.refs_0_
  102.7 2.1 %collective-permute-done.31.refs_2_ = bf16[64,640]{1,0:T(8,128)(2,1)S(1)} collective-permute-done((bf16[64,640]{1,0:T(8,128)(2,1)S(1)}, bf16[64,640]{1,0:T(8,128)(2,1)S(1)}, u32[]{:S(2)}, u32[]{:S(2)}) %collective-permute-start.31) | collective-permute-done | bytes 81952 | tf_op jit(solution)/shard_map/ppermute | solution.py:26
  104.7 0.8 collective-permute-done.30.refs_1_
  105.8 1.8 %collective-permute-start.33 = (bf16[64,640]{1,0:T(8,128)(2,1)S(1)}, bf16[64,640]{1,0:T(8,128)(2,1)S(1)}, u32[]{:S(2)}, u32[]{:S(2)}) collective-permute-start(bf16[64,640]{1,0:T(8,128)(2,1)S(1)} %get-tuple-element.53), channel_id=1, source_target_pairs={{0,3},{1,2},{2,1},{3,0},{4,7},{5,6},{6,5},{7,4},{8,11},{9,10},{10,... | collective-permute-start | bytes 245768 | tf_op jit(solution)/shard_map/ppermute | solution.py:26
  107.5 2.3 %collective-permute-start.34 = (bf16[64,640]{1,0:T(8,128)(2,1)S(1)}, bf16[64,640]{1,0:T(8,128)(2,1)S(1)}, u32[]{:S(2)}, u32[]{:S(2)}) collective-permute-start(bf16[64,640]{1,0:T(8,128)(2,1)S(1)} %get-tuple-element.54), channel_id=1, source_target_pairs={{0,2},{1,3},{2,0},{3,1},{4,6},{5,7},{6,4},{7,5},{8,10},{9,11},{10,... | collective-permute-start | bytes 245768 | tf_op jit(solution)/shard_map/ppermute | solution.py:26
  109.8 1.2 %collective-permute-done.32.refs_2_ = bf16[64,640]{1,0:T(8,128)(2,1)S(1)} collective-permute-done((bf16[64,640]{1,0:T(8,128)(2,1)S(1)}, bf16[64,640]{1,0:T(8,128)(2,1)S(1)}, u32[]{:S(2)}, u32[]{:S(2)}) %collective-permute-start.32) | collective-permute-done | bytes 81952 | tf_op jit(solution)/shard_map/ppermute | solution.py:26
  111.0 2.5 %collective-permute-done.34.refs_4_ = bf16[64,640]{1,0:T(8,128)(2,1)S(1)} collective-permute-done((bf16[64,640]{1,0:T(8,128)(2,1)S(1)}, bf16[64,640]{1,0:T(8,128)(2,1)S(1)}, u32[]{:S(2)}, u32[]{:S(2)}) %collective-permute-start.34) | collective-permute-done | bytes 81952 | tf_op jit(solution)/shard_map/ppermute | solution.py:26
  113.5 1.5 %shard_map.108 = bf16[64,2560]{1,0:T(8,128)(2,1)} custom-call(s32[32]{0:T(128)S(1)} %dynamic-slice_bitcast_fusion.refs_0_, bf16[64,640]{1,0:T(8,128)(2,1)S(1)} %get-tuple-element.51.refs_1_, bf16[64,640]{1,0:T(8,128)(2,1)S(1)} %collective-permute-done.32.refs_2_, bf16[64,640]{1,0:T(8,128)(2,1)S(1)} %collective-permute-done.33.refs_3_, ...), custom_call_target="tpu_custom_call" | custom-call | flops 1000 | bytes 1000 | tf_op jit(solution)/shard_map/pallas_call | solution.py:91
  (39 shorter events, 1.0 us)
Async XLA Ops:
  0.7 1.1 copy-start
  2.7 9.8 %collective-permute-start.6 = (bf16[32,5120]{1,0:T(8,128)(2,1)}, bf16[32,5120]{1,0:T(8,128)(2,1)S(1)}, u32[]{:S(2)}, u32[]{:S(2)}) collective-permute-start(bf16[32,5120]{1,0:T(8,128)(2,1)} %get-tuple-element.32), channel_id=1, source_target_pairs={{0,4},{1,5},{2,6},{3,7},{4,0},{5,1},{6,2},{7,3},{8,12},{9,13},{10,... | collective-permute-start | bytes 983048 | tf_op jit(solution)/shard_map/ppermute | solution.py:26
  4.6 21.2 %collective-permute-start = (bf16[32,5120]{1,0:T(8,128)(2,1)}, bf16[32,5120]{1,0:T(8,128)(2,1)S(1)}, u32[]{:S(2)}, u32[]{:S(2)}) collective-permute-start(bf16[32,5120]{1,0:T(8,128)(2,1)} %get-tuple-element.32), channel_id=1, source_target_pairs={{0,1},{1,0},{2,3},{3,2},{4,5},{5,4},{6,7},{7,6},{8,9},{9,8},{10,11... | collective-permute-start | bytes 983048 | tf_op jit(solution)/shard_map/ppermute | solution.py:26
  5.1 22.2 %collective-permute-start.3 = (bf16[32,5120]{1,0:T(8,128)(2,1)}, bf16[32,5120]{1,0:T(8,128)(2,1)S(1)}, u32[]{:S(2)}, u32[]{:S(2)}) collective-permute-start(bf16[32,5120]{1,0:T(8,128)(2,1)} %get-tuple-element.33), channel_id=1, source_target_pairs={{0,3},{1,2},{2,1},{3,0},{4,7},{5,6},{6,5},{7,4},{8,11},{9,10},{10,... | collective-permute-start | bytes 983048 | tf_op jit(solution)/shard_map/ppermute | solution.py:26
  7.3 20.7 %collective-permute-start.2 = (bf16[32,5120]{1,0:T(8,128)(2,1)}, bf16[32,5120]{1,0:T(8,128)(2,1)S(1)}, u32[]{:S(2)}, u32[]{:S(2)}) collective-permute-start(bf16[32,5120]{1,0:T(8,128)(2,1)} %get-tuple-element.32), channel_id=1, source_target_pairs={{0,3},{1,2},{2,1},{3,0},{4,7},{5,6},{6,5},{7,4},{8,11},{9,10},{10,... | collective-permute-start | bytes 983048 | tf_op jit(solution)/shard_map/ppermute | solution.py:26
  7.3 20.7 %collective-permute-start.7 = (bf16[32,5120]{1,0:T(8,128)(2,1)}, bf16[32,5120]{1,0:T(8,128)(2,1)S(1)}, u32[]{:S(2)}, u32[]{:S(2)}) collective-permute-start(bf16[32,5120]{1,0:T(8,128)(2,1)} %get-tuple-element.33), channel_id=1, source_target_pairs={{0,196},{1,197},{2,198},{3,199},{4,64},{5,65},{6,66},{7,67},{8,204... | collective-permute-start | bytes 983048 | tf_op jit(solution)/shard_map/ppermute | solution.py:26
  12.5 15.5 %collective-permute-start.1 = (bf16[32,5120]{1,0:T(8,128)(2,1)}, bf16[32,5120]{1,0:T(8,128)(2,1)S(1)}, u32[]{:S(2)}, u32[]{:S(2)}) collective-permute-start(bf16[32,5120]{1,0:T(8,128)(2,1)} %get-tuple-element.33), channel_id=1, source_target_pairs={{0,1},{1,0},{2,3},{3,2},{4,5},{5,4},{6,7},{7,6},{8,9},{9,8},{10,11... | collective-permute-start | bytes 983048 | tf_op jit(solution)/shard_map/ppermute | solution.py:26
  25.8 18.4 %copy-start.1 = (bf16[64,5120]{1,0:T(8,128)(2,1)S(1)}, bf16[64,5120]{1,0:T(8,128)(2,1)}, u32[]{:S(2)}) copy-start(bf16[64,5120]{1,0:T(8,128)(2,1)} %refs_0_.2) | copy-start | bytes 1966084
  25.8 9.3 %collective-permute-start.4 = (bf16[32,5120]{1,0:T(8,128)(2,1)S(1)}, bf16[32,5120]{1,0:T(8,128)(2,1)S(1)}, u32[]{:S(2)}, u32[]{:S(2)}) collective-permute-start(bf16[32,5120]{1,0:T(8,128)(2,1)S(1)} %collective-permute-done.refs_0_.refs_1_), channel_id=1, source_target_pairs={{0,3},{1,2},{2,1},{3,0},{4,7},{5,6},{6,5},{7,4},{8,11},{9,10},{10,... | collective-permute-start | bytes 983048 | tf_op jit(solution)/shard_map/ppermute | solution.py:26
  27.4 8.5 %collective-permute-start.5 = (bf16[32,5120]{1,0:T(8,128)(2,1)S(1)}, bf16[32,5120]{1,0:T(8,128)(2,1)S(1)}, u32[]{:S(2)}, u32[]{:S(2)}) collective-permute-start(bf16[32,5120]{1,0:T(8,128)(2,1)S(1)} %collective-permute-done.3.refs_3_.refs_4_), channel_id=1, source_target_pairs={{0,1},{1,0},{2,3},{3,2},{4,5},{5,4},{6,7},{7,6},{8,9},{9,8},{10,11... | collective-permute-start | bytes 983048 | tf_op jit(solution)/shard_map/ppermute | solution.py:26
  28.1 10.2 %collective-permute-start.10 = (bf16[32,5120]{1,0:T(8,128)(2,1)S(1)}, bf16[32,5120]{1,0:T(8,128)(2,1)S(1)}, u32[]{:S(2)}, u32[]{:S(2)}) collective-permute-start(bf16[32,5120]{1,0:T(8,128)(2,1)S(1)} %get-tuple-element.36), channel_id=1, source_target_pairs={{0,4},{1,5},{2,6},{3,7},{4,0},{5,1},{6,2},{7,3},{8,12},{9,13},{10,... | collective-permute-start | bytes 983048 | tf_op jit(solution)/shard_map/ppermute | solution.py:26
  29.6 14.5 %collective-permute-start.11 = (bf16[32,5120]{1,0:T(8,128)(2,1)S(1)}, bf16[32,5120]{1,0:T(8,128)(2,1)S(1)}, u32[]{:S(2)}, u32[]{:S(2)}) collective-permute-start(bf16[32,5120]{1,0:T(8,128)(2,1)S(1)} %get-tuple-element.37), channel_id=1, source_target_pairs={{0,196},{1,197},{2,198},{3,199},{4,64},{5,65},{6,66},{7,67},{8,204... | collective-permute-start | bytes 983048 | tf_op jit(solution)/shard_map/ppermute | solution.py:26
  34.6 9.6 %collective-permute-start.9 = (bf16[32,5120]{1,0:T(8,128)(2,1)S(1)}, bf16[32,5120]{1,0:T(8,128)(2,1)S(1)}, u32[]{:S(2)}, u32[]{:S(2)}) collective-permute-start(bf16[32,5120]{1,0:T(8,128)(2,1)S(1)} %get-tuple-element.35), channel_id=1, source_target_pairs={{0,3},{1,2},{2,1},{3,0},{4,7},{5,6},{6,5},{7,4},{8,11},{9,10},{10,... | collective-permute-start | bytes 983048 | tf_op jit(solution)/shard_map/ppermute | solution.py:26
  35.1 9.1 %collective-permute-start.8 = (bf16[32,5120]{1,0:T(8,128)(2,1)S(1)}, bf16[32,5120]{1,0:T(8,128)(2,1)S(1)}, u32[]{:S(2)}, u32[]{:S(2)}) collective-permute-start(bf16[32,5120]{1,0:T(8,128)(2,1)S(1)} %get-tuple-element.35), channel_id=1, source_target_pairs={{0,1},{1,0},{2,3},{3,2},{4,5},{5,4},{6,7},{7,6},{8,9},{9,8},{10,11... | collective-permute-start | bytes 983048 | tf_op jit(solution)/shard_map/ppermute | solution.py:26
  35.9 10.2 %collective-permute-start.12 = (bf16[32,5120]{1,0:T(8,128)(2,1)S(1)}, bf16[32,5120]{1,0:T(8,128)(2,1)S(1)}, u32[]{:S(2)}, u32[]{:S(2)}) collective-permute-start(bf16[32,5120]{1,0:T(8,128)(2,1)S(1)} %collective-permute-done.4.refs_5_), channel_id=1, source_target_pairs={{0,4},{1,5},{2,6},{3,7},{4,0},{5,1},{6,2},{7,3},{8,12},{9,13},{10,... | collective-permute-start | bytes 983048 | tf_op jit(solution)/shard_map/ppermute | solution.py:26
  38.2 11.0 %collective-permute-start.13 = (bf16[32,5120]{1,0:T(8,128)(2,1)S(1)}, bf16[32,5120]{1,0:T(8,128)(2,1)S(1)}, u32[]{:S(2)}, u32[]{:S(2)}) collective-permute-start(bf16[32,5120]{1,0:T(8,128)(2,1)S(1)} %collective-permute-done.5.refs_6_), channel_id=1, source_target_pairs={{0,196},{1,197},{2,198},{3,199},{4,64},{5,65},{6,66},{7,67},{8,204... | collective-permute-start | bytes 983048 | tf_op jit(solution)/shard_map/ppermute | solution.py:26
  44.2 6.9 %collective-permute-start.14 = (f32[1,128]{1,0:T(1,128)S(1)}, f32[1,128]{1,0:T(1,128)S(1)}, u32[]{:S(2)}, u32[]{:S(2)}) collective-permute-start(f32[1,128]{1,0:T(1,128)S(1)} %get-tuple-element.38), channel_id=1, source_target_pairs={{0,64},{1,65},{2,66},{3,67},{4,196},{5,197},{6,198},{7,199},{8,72}... | collective-permute-start | bytes 1544 | tf_op jit(solution)/shard_map/ppermute | solution.py:26
  53.1 2.2 %collective-permute-start.15 = (bf16[320,960]{1,0:T(8,128)(2,1)S(1)}, bf16[320,960]{1,0:T(8,128)(2,1)S(1)}, u32[]{:S(2)}, u32[]{:S(2)}) collective-permute-start(bf16[320,960]{1,0:T(8,128)(2,1)S(1)} %shard_map.97.refs_8_), channel_id=1, source_target_pairs={{0,8},{1,9},{2,10},{3,11},{4,12},{5,13},{6,14},{7,15},{8,0},{9,1},... | collective-permute-start | bytes 1843208 | tf_op jit(solution)/shard_map/ppermute | solution.py:26
  55.9 8.6 %collective-permute-start.16 = (bf16[80,960]{1,0:T(8,128)(2,1)S(1)}, bf16[80,960]{1,0:T(8,128)(2,1)S(1)}, u32[]{:S(2)}, u32[]{:S(2)}) collective-permute-start(bf16[80,960]{1,0:T(8,128)(2,1)S(1)} %get-tuple-element.41), channel_id=1, source_target_pairs={{0,32},{1,33},{2,34},{3,35},{4,36},{5,37},{6,38},{7,39},{8,40},{9,... | collective-permute-start | bytes 460808 | tf_op jit(solution)/shard_map/ppermute | solution.py:26
  59.2 8.7 %collective-permute-start.18 = (bf16[80,960]{1,0:T(8,128)(2,1)S(1)}, bf16[80,960]{1,0:T(8,128)(2,1)S(1)}, u32[]{:S(2)}, u32[]{:S(2)}) collective-permute-start(bf16[80,960]{1,0:T(8,128)(2,1)S(1)} %get-tuple-element.42), channel_id=1, source_target_pairs={{0,48},{1,49},{2,50},{3,51},{4,52},{5,53},{6,54},{7,55},{8,56},{9,... | collective-permute-start | bytes 460808 | tf_op jit(solution)/shard_map/ppermute | solution.py:26
  60.2 7.6 %collective-permute-start.17 = (bf16[80,960]{1,0:T(8,128)(2,1)S(1)}, bf16[80,960]{1,0:T(8,128)(2,1)S(1)}, u32[]{:S(2)}, u32[]{:S(2)}) collective-permute-start(bf16[80,960]{1,0:T(8,128)(2,1)S(1)} %get-tuple-element.39.refs_2_), channel_id=1, source_target_pairs={{0,16},{1,17},{2,18},{3,19},{4,20},{5,21},{6,22},{7,23},{8,24},{9,... | collective-permute-start | bytes 460808 | tf_op jit(solution)/shard_map/ppermute | solution.py:26
  67.9 8.0 %collective-permute-start.20 = (bf16[40,960]{1,0:T(8,128)(2,1)S(1)}, bf16[40,960]{1,0:T(8,128)(2,1)S(1)}, u32[]{:S(2)}, u32[]{:S(2)}) collective-permute-start(bf16[40,960]{1,0:T(8,128)(2,1)S(1)} %get-tuple-element.45), channel_id=1, source_target_pairs={{0,192},{1,193},{2,194},{3,195},{4,196},{5,197},{6,198},{7,199},{8... | collective-permute-start | bytes 230408 | tf_op jit(solution)/shard_map/ppermute | solution.py:26
  70.5 7.1 %collective-permute-start.19 = (bf16[40,960]{1,0:T(8,128)(2,1)S(1)}, bf16[40,960]{1,0:T(8,128)(2,1)S(1)}, u32[]{:S(2)}, u32[]{:S(2)}) collective-permute-start(bf16[40,960]{1,0:T(8,128)(2,1)S(1)} %get-tuple-element.43.refs_16_), channel_id=1, source_target_pairs={{0,64},{1,65},{2,66},{3,67},{4,68},{5,69},{6,70},{7,71},{8,72},{9,... | collective-permute-start | bytes 230408 | tf_op jit(solution)/shard_map/ppermute | solution.py:26
  77.6 8.3 %collective-permute-start.21 = (bf16[40,960]{1,0:T(8,128)(2,1)S(1)}, bf16[40,960]{1,0:T(8,128)(2,1)S(1)}, u32[]{:S(2)}, u32[]{:S(2)}) collective-permute-start(bf16[40,960]{1,0:T(8,128)(2,1)S(1)} %get-tuple-element.47), channel_id=1, source_target_pairs={{0,192},{1,193},{2,194},{3,195},{4,196},{5,197},{6,198},{7,199},{8... | collective-permute-start | bytes 230408 | tf_op jit(solution)/shard_map/ppermute | solution.py:26
  78.6 7.3 %collective-permute-start.22 = (bf16[40,960]{1,0:T(8,128)(2,1)S(1)}, bf16[40,960]{1,0:T(8,128)(2,1)S(1)}, u32[]{:S(2)}, u32[]{:S(2)}) collective-permute-start(bf16[40,960]{1,0:T(8,128)(2,1)S(1)} %get-tuple-element.48), channel_id=1, source_target_pairs={{0,64},{1,65},{2,66},{3,67},{4,68},{5,69},{6,70},{7,71},{8,72},{9,... | collective-permute-start | bytes 230408 | tf_op jit(solution)/shard_map/ppermute | solution.py:26
  86.8 7.0 %collective-permute-start.25 = (bf16[80,960]{1,0:T(8,128)(2,1)S(1)}, bf16[80,960]{1,0:T(8,128)(2,1)S(1)}, u32[]{:S(2)}, u32[]{:S(2)}) collective-permute-start(bf16[80,960]{1,0:T(8,128)(2,1)S(1)} %shard_map.104.refs_1_), channel_id=1, source_target_pairs={{0,32},{1,33},{2,34},{3,35},{4,36},{5,37},{6,38},{7,39},{8,40},{9,... | collective-permute-start | bytes 460808 | tf_op jit(solution)/shard_map/ppermute | solution.py:26
  88.9 6.1 %collective-permute-start.24 = (bf16[80,960]{1,0:T(8,128)(2,1)S(1)}, bf16[80,960]{1,0:T(8,128)(2,1)S(1)}, u32[]{:S(2)}, u32[]{:S(2)}) collective-permute-start(bf16[80,960]{1,0:T(8,128)(2,1)S(1)} %shard_map.104.refs_1_), channel_id=1, source_target_pairs={{0,48},{1,49},{2,50},{3,51},{4,52},{5,53},{6,54},{7,55},{8,56},{9,... | collective-permute-start | bytes 460808 | tf_op jit(solution)/shard_map/ppermute | solution.py:26
  90.0 6.5 %collective-permute-start.23 = (bf16[80,960]{1,0:T(8,128)(2,1)S(1)}, bf16[80,960]{1,0:T(8,128)(2,1)S(1)}, u32[]{:S(2)}, u32[]{:S(2)}) collective-permute-start(bf16[80,960]{1,0:T(8,128)(2,1)S(1)} %shard_map.104.refs_1_), channel_id=1, source_target_pairs={{0,16},{1,17},{2,18},{3,19},{4,20},{5,21},{6,22},{7,23},{8,24},{9,... | collective-permute-start | bytes 460808 | tf_op jit(solution)/shard_map/ppermute | solution.py:26
  90.9 5.7 %collective-permute-start.26 = (bf16[80,960]{1,0:T(8,128)(2,1)S(1)}, bf16[80,960]{1,0:T(8,128)(2,1)S(1)}, u32[]{:S(2)}, u32[]{:S(2)}) collective-permute-start(bf16[80,960]{1,0:T(8,128)(2,1)S(1)} %shard_map.104.refs_1_), channel_id=1, source_target_pairs={{0,8},{1,9},{2,10},{3,11},{4,12},{5,13},{6,14},{7,15},{8,0},{9,1},... | collective-permute-start | bytes 460808 | tf_op jit(solution)/shard_map/ppermute | solution.py:26
  93.8 2.8 %collective-permute-start.29 = (bf16[80,960]{1,0:T(8,128)(2,1)S(1)}, bf16[80,960]{1,0:T(8,128)(2,1)S(1)}, u32[]{:S(2)}, u32[]{:S(2)}) collective-permute-start(bf16[80,960]{1,0:T(8,128)(2,1)S(1)} %collective-permute-done.25.refs_4_), channel_id=1, source_target_pairs={{0,8},{1,9},{2,10},{3,11},{4,12},{5,13},{6,14},{7,15},{8,0},{9,1},... | collective-permute-start | bytes 460808 | tf_op jit(solution)/shard_map/ppermute | solution.py:26
  95.0 1.6 %collective-permute-start.28 = (bf16[80,960]{1,0:T(8,128)(2,1)S(1)}, bf16[80,960]{1,0:T(8,128)(2,1)S(1)}, u32[]{:S(2)}, u32[]{:S(2)}) collective-permute-start(bf16[80,960]{1,0:T(8,128)(2,1)S(1)} %collective-permute-done.24.refs_3_), channel_id=1, source_target_pairs={{0,8},{1,9},{2,10},{3,11},{4,12},{5,13},{6,14},{7,15},{8,0},{9,1},... | collective-permute-start | bytes 460808 | tf_op jit(solution)/shard_map/ppermute | solution.py:26
  96.6 1.4 %collective-permute-start.27 = (bf16[80,960]{1,0:T(8,128)(2,1)S(1)}, bf16[80,960]{1,0:T(8,128)(2,1)S(1)}, u32[]{:S(2)}, u32[]{:S(2)}) collective-permute-start(bf16[80,960]{1,0:T(8,128)(2,1)S(1)} %collective-permute-done.23.refs_2_), channel_id=1, source_target_pairs={{0,8},{1,9},{2,10},{3,11},{4,12},{5,13},{6,14},{7,15},{8,0},{9,1},... | collective-permute-start | bytes 460808 | tf_op jit(solution)/shard_map/ppermute | solution.py:26
  98.9 5.8 %collective-permute-start.31 = (bf16[64,640]{1,0:T(8,128)(2,1)S(1)}, bf16[64,640]{1,0:T(8,128)(2,1)S(1)}, u32[]{:S(2)}, u32[]{:S(2)}) collective-permute-start(bf16[64,640]{1,0:T(8,128)(2,1)S(1)} %get-tuple-element.50), channel_id=1, source_target_pairs={{0,196},{1,197},{2,198},{3,199},{4,64},{5,65},{6,66},{7,67},{8,204... | collective-permute-start | bytes 245768 | tf_op jit(solution)/shard_map/ppermute | solution.py:26
  101.1 4.4 %collective-permute-start.30 = (bf16[64,640]{1,0:T(8,128)(2,1)S(1)}, bf16[64,640]{1,0:T(8,128)(2,1)S(1)}, u32[]{:S(2)}, u32[]{:S(2)}) collective-permute-start(bf16[64,640]{1,0:T(8,128)(2,1)S(1)} %get-tuple-element.49.refs_9_), channel_id=1, source_target_pairs={{0,4},{1,5},{2,6},{3,7},{4,0},{5,1},{6,2},{7,3},{8,12},{9,13},{10,... | collective-permute-start | bytes 245768 | tf_op jit(solution)/shard_map/ppermute | solution.py:26
  105.7 5.3 %collective-permute-start.32 = (bf16[64,640]{1,0:T(8,128)(2,1)S(1)}, bf16[64,640]{1,0:T(8,128)(2,1)S(1)}, u32[]{:S(2)}, u32[]{:S(2)}) collective-permute-start(bf16[64,640]{1,0:T(8,128)(2,1)S(1)} %get-tuple-element.52), channel_id=1, source_target_pairs={{0,1},{1,0},{2,3},{3,2},{4,5},{5,4},{6,7},{7,6},{8,9},{9,8},{10,11... | collective-permute-start | bytes 245768 | tf_op jit(solution)/shard_map/ppermute | solution.py:26
  105.8 5.2 %collective-permute-start.33 = (bf16[64,640]{1,0:T(8,128)(2,1)S(1)}, bf16[64,640]{1,0:T(8,128)(2,1)S(1)}, u32[]{:S(2)}, u32[]{:S(2)}) collective-permute-start(bf16[64,640]{1,0:T(8,128)(2,1)S(1)} %get-tuple-element.53), channel_id=1, source_target_pairs={{0,3},{1,2},{2,1},{3,0},{4,7},{5,6},{6,5},{7,4},{8,11},{9,10},{10,... | collective-permute-start | bytes 245768 | tf_op jit(solution)/shard_map/ppermute | solution.py:26
  107.5 5.9 %collective-permute-start.34 = (bf16[64,640]{1,0:T(8,128)(2,1)S(1)}, bf16[64,640]{1,0:T(8,128)(2,1)S(1)}, u32[]{:S(2)}, u32[]{:S(2)}) collective-permute-start(bf16[64,640]{1,0:T(8,128)(2,1)S(1)} %get-tuple-element.54), channel_id=1, source_target_pairs={{0,2},{1,3},{2,0},{3,1},{4,6},{5,7},{6,4},{7,5},{8,10},{9,11},{10,... | collective-permute-start | bytes 245768 | tf_op jit(solution)/shard_map/ppermute | solution.py:26

commit v10 on v9

--- a/solution.py
+++ b/solution.py
@@ -99,16 +99,13 @@
     )(*args, *after)
 
 
-def halve_kernel(tile, first, second):
-    first[...] = tile[:32, :]
-    second[...] = tile[32:, :]
-
-
-def split_kernel(near_a, near_b, far_a, far_b, z1, z2, first, second, both):
-    first[:16, :] = near_a[16:, :]
-    first[16:, :] = far_a[16:, :]
-    second[:16, :] = near_b[16:, :]
-    second[16:, :] = far_b[16:, :]
+def split_kernel(near_tile, far_tile, z1, z2, near_first, far_second, first, second, both):
+    near_first[...] = near_tile[:32, :]
+    far_second[...] = far_tile[32:, :]
+    first[:16, :] = near_tile[16:32, :]
+    first[16:, :] = far_tile[16:32, :]
+    second[:16, :] = near_tile[48:, :]
+    second[16:, :] = far_tile[48:, :]
     both[:16, :] = z1[:16, :]
     both[16:, :] = z2[:16, :]
 
@@ -226,26 +223,23 @@
         at += 2 * n
 
 
-PLANE = [(0, 0, 64)] + [(i, 0, 32) for i in range(1, 7)]
+PLANE = [(0, 0, 64), (1, 0, 64), (2, 0, 64), (3, 0, 32), (4, 0, 32)]
 OTHERS = [(0, 0, 32), (2, 0, 16), (4, 0, 16), (3, 0, 16), (4, 16, 32), (6, 0, 32)]
 OTHERS += [(1, 0, 32), (2, 16, 32), (5, 0, 16), (3, 16, 32), (5, 16, 32), (7, 0, 32)]
 
 
 def gather(tokens, work):
-    half = [like((32, 5120))]
-    a, b = call(halve_kernel, half * 2, tokens)
-    near_a, far_b = to_near_x(a), to_far_x(b)
-    z1, z2 = to_near_z(a), to_far_z(b)
-    near_b, far_a = to_near_x(b), to_far_x(a)
-    opposite_first, opposite_second = to_far_x(near_a), to_near_x(far_b)
-    first, second, both = call(
-        split_kernel, half * 3, near_a, near_b, far_a, far_b, z1, z2, after=work
-    )
+    near_tile, far_tile = to_near_x(tokens), to_far_x(tokens)
+    z1, z2 = to_near_z(tokens[:32]), to_far_z(tokens[32:])
+    near_first, far_second, first, second, both = call(
+        split_kernel, [like((32, 5120))] * 5, near_tile, far_tile, z1, z2, after=work
+    )
+    opposite_first, opposite_second = to_far_x(near_first), to_near_x(far_second)
     z3, z4 = to_near_z(first), to_far_z(second)
     near_both, far_both = to_near_x(both), to_far_x(both)
     z5, z6 = to_near_z(opposite_first), to_far_z(opposite_second)
     return (
-        [tokens, near_a, near_b, far_a, far_b, opposite_first, opposite_second],
+        [tokens, near_tile, far_tile, opposite_first, opposite_second],
         [z1, z2, near_both, far_both, z3, z4, z5, z6],
     )
 

time: 117 us -> 111 us (0.949)
  starting transfers between devices: 55.2 us -> 46.9 us
  waiting for transfers between devices: 29.1 us -> 31.8 us
    ppermute x35 -> x33, starting transfers between devices: 55.2 us -> 46.9 us  [permute(): return lax.ppermute(value, AXES, pairs)]
    ppermute x35 -> x33, waiting for transfers between devices: 29.1 us -> 31.8 us  [permute(): return lax.ppermute(value, AXES, pairs)]
    slice x0 -> x1, local copies, waits for them, and re-layouts: none -> 1.95 us  [gather(): z1, z2 = (to_near_z(tokens[:32]), to_far_z(tokens[32:]))]
    unnamed x9 -> x7, local copies, waits for them, and re-layouts: 5.47 us -> 4.37 us
    pallas_call x16 -> x15, Pallas kernels: 16.3 us -> 15.5 us  [call(): pl.pallas_call(run, out_shape=out_shape, in_specs=[SMEM] * scalars + [VME...]
  transfers between devices with their start and end apart: 35 -> 33, of which waited for: 16 -> 19; matrix products, arithmetic and copies ran while one was open for 6% -> 8% of each run, Pallas kernels for 12% -> 13%
where the time goes in v10:
time: 111 us; the launch traced here: 109 us
  starting transfers between devices  46.9 us (42%)
  waiting for transfers between devices  31.8 us (29%)
  Pallas kernels  20.5 us (18%)
  local copies, waits for them, and re-layouts  7.2 us (6%)
  other arithmetic  2.06 us (2%)
    ppermute x33, starting transfers between devices, permute(): return lax.ppermute(value, AXES, pairs)  46.9 us
    ppermute x33, waiting for transfers between devices, permute(): return lax.ppermute(value, AXES, pairs)  31.8 us
    pallas_call x15, Pallas kernels, call(): pl.pallas_call(run, out_shape=out_shape, in_specs=[SMEM] * scalars + [VME...  15.5 us
    pallas_call x2, Pallas kernels, load(): pl.pallas_call(run, out_shape=like((count, *w_t.shape[1:])), in_specs=[pl...  5 us
    unnamed x7, local copies, waits for them, and re-layouts  4.37 us
  transfers between devices with their start and end apart: 33, of which 19 were waited for; matrix products, arithmetic and copies ran while one was open for 8% of the time, Pallas kernels for 13%

profile of v10, /device:TPU:2, one launch (start us, length us, event | category | flops | bytes accessed | tf_op | source)
XLA Modules:
  0.0 109.3 jit_solution(16763399673717870692)
XLA Ops:
  0.0 0.7 dynamic-slice_bitcast_fusion.refs_0_
  0.7 1.5 %collective-permute-start.1 = (bf16[64,5120]{1,0:T(8,128)(2,1)}, bf16[64,5120]{1,0:T(8,128)(2,1)S(1)}, u32[]{:S(2)}, u32[]{:S(2)}) collective-permute-start(bf16[64,5120]{1,0:T(8,128)(2,1)} %refs_0_.1), channel_id=1, source_target_pairs={{0,3},{1,2},{2,1},{3,0},{4,7},{5,6},{6,5},{7,4},{8,11},{9,10},{10,... | collective-permute-start | bytes 1966088 | tf_op jit(solution)/shard_map/ppermute | solution.py:26
  2.2 1.8 %collective-permute-start = (bf16[64,5120]{1,0:T(8,128)(2,1)}, bf16[64,5120]{1,0:T(8,128)(2,1)S(1)}, u32[]{:S(2)}, u32[]{:S(2)}) collective-permute-start(bf16[64,5120]{1,0:T(8,128)(2,1)} %refs_0_.1), channel_id=1, source_target_pairs={{0,1},{1,0},{2,3},{3,2},{4,5},{5,4},{6,7},{7,6},{8,9},{9,8},{10,11... | collective-permute-start | bytes 1966088 | tf_op jit(solution)/shard_map/ppermute | solution.py:26
  4.0 1.9 %fusion = (bf16[32,5120]{1,0:T(8,128)(2,1)}, bf16[32,5120]{1,0:T(8,128)(2,1)}) fusion(bf16[64,5120]{1,0:T(8,128)(2,1)} %refs_0_.1), kind=kLoop, calls=%fused_computation.3 | loop fusion | bytes 1310720 | tf_op jit(solution)/shard_map/slice | solution.py:233
  5.9 5.9 %collective-permute-start.3 = (bf16[32,5120]{1,0:T(8,128)(2,1)}, bf16[32,5120]{1,0:T(8,128)(2,1)S(1)}, u32[]{:S(2)}, u32[]{:S(2)}) collective-permute-start(bf16[32,5120]{1,0:T(8,128)(2,1)} %get-tuple-element.55), channel_id=1, source_target_pairs={{0,196},{1,197},{2,198},{3,199},{4,64},{5,65},{6,66},{7,67},{8,204... | collective-permute-start | bytes 983048 | tf_op jit(solution)/shard_map/ppermute | solution.py:26
  12.4 0.6 broadcast.3
  13.0 1.4 %reduce.3 = s32[512]{0:T(512)S(1)} reduce(s32[512,1]{0,1:T(1,128)} %param.12, s32[]{:T(128)} %broadcast.3), dimensions={1}, to_apply=%param.12.reduce_sub_computation.3 | reduce | bytes 4100 | tf_op args[3]
  14.5 0.6 shard_map.91
  15.1 0.7 exponential_convert_fusion
  15.9 1.3 %copy.13 = bf16[1,320,640]{1,2,0:T(8,128)(2,1)S(1)} copy(bf16[1,320,640]{2,1,0:T(8,128)(2,1)} %param.14) | data formatting | bytes 819200 | tf_op args[5]
  17.2 1.3 %copy.14 = bf16[1,320,640]{1,2,0:T(8,128)(2,1)S(1)} copy(bf16[1,320,640]{2,1,0:T(8,128)(2,1)} %param.15) | data formatting | bytes 819200 | tf_op args[6]
  18.4 1.3 %copy.15 = bf16[1,320,640]{1,2,0:T(8,128)(2,1)S(1)} copy(bf16[1,320,640]{2,1,0:T(8,128)(2,1)} %param.16) | data formatting | bytes 819200 | tf_op args[7]
  19.7 3.0 %shard_map.92.refs_4_.refs_5_.refs_8_ = bf16[2,320,5120]{2,1,0:T(8,128)(2,1)S(1)} custom-call(bf16[3,320,5120]{2,1,0:T(8,128)(2,1)} %bitcast.28, bf16[3,1,5120]{2,1,0:T(2,128)(2,1)S(1)} %broadcast_in_dim_reshape.4.refs_1_, f32[1,384]{1,0:T(1,128)S(1)} %get-tuple-element.32.refs_2_.refs_3_, bf16[640,320]{1,0:T(8,128)(2,1)S(1)} %bitcast.16, ...), custom_call_target="tpu_custom_call" | custom-call | flops 1000 | bytes 1000 | tf_op jit(solution)/shard_map/pallas_call | solution.py:131
  23.0 1.4 %collective-permute-start.5 = (bf16[32,5120]{1,0:T(8,128)(2,1)S(1)}, bf16[32,5120]{1,0:T(8,128)(2,1)S(1)}, u32[]{:S(2)}, u32[]{:S(2)}) collective-permute-start(bf16[32,5120]{1,0:T(8,128)(2,1)S(1)} %get-tuple-element.34), channel_id=1, source_target_pairs={{0,1},{1,0},{2,3},{3,2},{4,5},{5,4},{6,7},{7,6},{8,9},{9,8},{10,11... | collective-permute-start | bytes 983048 | tf_op jit(solution)/shard_map/ppermute | solution.py:26
  24.4 2.0 %collective-permute-start.8 = (bf16[32,5120]{1,0:T(8,128)(2,1)S(1)}, bf16[32,5120]{1,0:T(8,128)(2,1)S(1)}, u32[]{:S(2)}, u32[]{:S(2)}) collective-permute-start(bf16[32,5120]{1,0:T(8,128)(2,1)S(1)} %get-tuple-element.36), channel_id=1, source_target_pairs={{0,4},{1,5},{2,6},{3,7},{4,0},{5,1},{6,2},{7,3},{8,12},{9,13},{10,... | collective-permute-start | bytes 983048 | tf_op jit(solution)/shard_map/ppermute | solution.py:26
  26.4 2.6 %collective-permute-start.9 = (bf16[32,5120]{1,0:T(8,128)(2,1)S(1)}, bf16[32,5120]{1,0:T(8,128)(2,1)S(1)}, u32[]{:S(2)}, u32[]{:S(2)}) collective-permute-start(bf16[32,5120]{1,0:T(8,128)(2,1)S(1)} %get-tuple-element.37), channel_id=1, source_target_pairs={{0,196},{1,197},{2,198},{3,199},{4,64},{5,65},{6,66},{7,67},{8,204... | collective-permute-start | bytes 983048 | tf_op jit(solution)/shard_map/ppermute | solution.py:26
  28.9 1.1 %collective-permute-start.7 = (bf16[32,5120]{1,0:T(8,128)(2,1)S(1)}, bf16[32,5120]{1,0:T(8,128)(2,1)S(1)}, u32[]{:S(2)}, u32[]{:S(2)}) collective-permute-start(bf16[32,5120]{1,0:T(8,128)(2,1)S(1)} %get-tuple-element.35), channel_id=1, source_target_pairs={{0,3},{1,2},{2,1},{3,0},{4,7},{5,6},{6,5},{7,4},{8,11},{9,10},{10,... | collective-permute-start | bytes 983048 | tf_op jit(solution)/shard_map/ppermute | solution.py:26
  30.1 3.6 %collective-permute-done.4.refs_3_ = bf16[32,5120]{1,0:T(8,128)(2,1)S(1)} collective-permute-done((bf16[32,5120]{1,0:T(8,128)(2,1)S(1)}, bf16[32,5120]{1,0:T(8,128)(2,1)S(1)}, u32[]{:S(2)}, u32[]{:S(2)}) %collective-permute-start.4) | collective-permute-done | bytes 327712 | tf_op jit(solution)/shard_map/ppermute | solution.py:26
  33.6 1.4 %collective-permute-start.6 = (bf16[32,5120]{1,0:T(8,128)(2,1)S(1)}, bf16[32,5120]{1,0:T(8,128)(2,1)S(1)}, u32[]{:S(2)}, u32[]{:S(2)}) collective-permute-start(bf16[32,5120]{1,0:T(8,128)(2,1)S(1)} %get-tuple-element.35), channel_id=1, source_target_pairs={{0,1},{1,0},{2,3},{3,2},{4,5},{5,4},{6,7},{7,6},{8,9},{9,8},{10,11... | collective-permute-start | bytes 983048 | tf_op jit(solution)/shard_map/ppermute | solution.py:26
  35.1 2.0 %collective-permute-start.10 = (bf16[32,5120]{1,0:T(8,128)(2,1)S(1)}, bf16[32,5120]{1,0:T(8,128)(2,1)S(1)}, u32[]{:S(2)}, u32[]{:S(2)}) collective-permute-start(bf16[32,5120]{1,0:T(8,128)(2,1)S(1)} %collective-permute-done.4.refs_3_), channel_id=1, source_target_pairs={{0,4},{1,5},{2,6},{3,7},{4,0},{5,1},{6,2},{7,3},{8,12},{9,13},{10,... | collective-permute-start | bytes 983048 | tf_op jit(solution)/shard_map/ppermute | solution.py:26
  37.1 2.2 %collective-permute-start.11 = (bf16[32,5120]{1,0:T(8,128)(2,1)S(1)}, bf16[32,5120]{1,0:T(8,128)(2,1)S(1)}, u32[]{:S(2)}, u32[]{:S(2)}) collective-permute-start(bf16[32,5120]{1,0:T(8,128)(2,1)S(1)} %collective-permute-done.5.refs_4_), channel_id=1, source_target_pairs={{0,196},{1,197},{2,198},{3,199},{4,64},{5,65},{6,66},{7,67},{8,204... | collective-permute-start | bytes 983048 | tf_op jit(solution)/shard_map/ppermute | solution.py:26
  39.3 1.4 %collective-permute-done.6.refs_6_.refs_2_.refs_7_ = bf16[32,5120]{1,0:T(8,128)(2,1)S(1)} collective-permute-done((bf16[32,5120]{1,0:T(8,128)(2,1)S(1)}, bf16[32,5120]{1,0:T(8,128)(2,1)S(1)}, u32[]{:S(2)}, u32[]{:S(2)}) %collective-permute-start.6) | collective-permute-done | bytes 327712 | tf_op jit(solution)/shard_map/ppermute | solution.py:26
  40.7 1.9 %shard_map.94.refs_9_.refs_1_ = bf16[640,256]{1,0:T(8,128)(2,1)S(1)} custom-call(bf16[64,5120]{1,0:T(8,128)(2,1)S(1)} %copy-done, bf16[64,5120]{1,0:T(8,128)(2,1)S(1)} %collective-permute-done.refs_0_.refs_1_, bf16[64,5120]{1,0:T(8,128)(2,1)S(1)} %collective-permute-done.1.refs_1_.refs_2_, bf16[32,5120]{1,0:T(8,128)(2,1)S(1)} %collective-permute-done.4.refs_3_, ...), custom_call_target="tpu_custom_call" | custom-call | flops 1000 | bytes 1000 | tf_op jit(solution)/shard_map/pallas_call | solution.py:91
  42.6 2.8 %collective-permute-done.11.refs_7_.refs_12_ = bf16[32,5120]{1,0:T(8,128)(2,1)S(1)} collective-permute-done((bf16[32,5120]{1,0:T(8,128)(2,1)S(1)}, bf16[32,5120]{1,0:T(8,128)(2,1)S(1)}, u32[]{:S(2)}, u32[]{:S(2)}) %collective-permute-start.11) | collective-permute-done | bytes 327712 | tf_op jit(solution)/shard_map/ppermute | solution.py:26
  45.4 1.9 %shard_map.95.refs_2_ = bf16[640,256]{1,0:T(8,128)(2,1)S(1)} custom-call(bf16[32,5120]{1,0:T(8,128)(2,1)S(1)} %collective-permute-done.2.refs_2_.refs_0_.refs_5_, bf16[32,5120]{1,0:T(8,128)(2,1)S(1)} %collective-permute-done.3.refs_3_.refs_1_.refs_6_, bf16[32,5120]{1,0:T(8,128)(2,1)S(1)} %collective-permute-done.6.refs_6_.refs_2_.refs_7_, ...), custom_call_target="tpu_custom_call" | custom-call | flops 1000 | bytes 1000 | tf_op jit(solution)/shard_map/pallas_call | solution.py:91
  47.3 1.9 %shard_map.96.refs_8_ = bf16[320,960]{1,0:T(8,128)(2,1)S(1)} custom-call(s32[32]{0:T(128)S(1)} %dynamic-slice_bitcast_fusion.refs_0_, bf16[640,256]{1,0:T(8,128)(2,1)S(1)} %shard_map.94.refs_9_.refs_1_, bf16[640,256]{1,0:T(8,128)(2,1)S(1)} %shard_map.95.refs_2_, f32[1,384]{1,0:T(1,128)S(1)} %get-tuple-element.32.refs_2_.refs_3_, ...), custom_call_target="tpu_custom_call" | custom-call | flops 1000 | bytes 1000 | tf_op jit(solution)/shard_map/pallas_call | solution.py:91
  49.3 1.9 %shard_map.97.refs_1_ = f32[320,960]{1,0:T(8,128)S(1)} custom-call(s32[32]{0:T(128)S(1)} %dynamic-slice_bitcast_fusion.refs_0_, bf16[640,256]{1,0:T(8,128)(2,1)S(1)} %shard_map.94.refs_9_.refs_1_, bf16[640,256]{1,0:T(8,128)(2,1)S(1)} %shard_map.95.refs_2_, f32[1,384]{1,0:T(1,128)S(1)} %get-tuple-element.32.refs_2_.refs_3_, ...), custom_call_target="tpu_custom_call" | custom-call | flops 1000 | bytes 1000 | tf_op jit(solution)/shard_map/pallas_call | solution.py:91
  51.4 0.7 shard_map.98
  52.1 3.3 %collective-permute-start.14 = (bf16[80,960]{1,0:T(8,128)(2,1)S(1)}, bf16[80,960]{1,0:T(8,128)(2,1)S(1)}, u32[]{:S(2)}, u32[]{:S(2)}) collective-permute-start(bf16[80,960]{1,0:T(8,128)(2,1)S(1)} %get-tuple-element.41), channel_id=1, source_target_pairs={{0,32},{1,33},{2,34},{3,35},{4,36},{5,37},{6,38},{7,39},{8,40},{9,... | collective-permute-start | bytes 460808 | tf_op jit(solution)/shard_map/ppermute | solution.py:26
  55.4 1.1 collective-permute-start.16
  56.4 1.0 collective-permute-start.15
  57.4 2.0 %shard_map.99.refs_4_.refs_13_ = bf16[1,320,5120]{2,1,0:T(8,128)(2,1)S(1)} custom-call(bf16[3,320,5120]{2,1,0:T(8,128)(2,1)} %bitcast.29, bf16[3,1,5120]{2,1,0:T(2,128)(2,1)S(1)} %broadcast_in_dim_reshape.4.refs_1_, bf16[80,960]{1,0:T(8,128)(2,1)S(1)} %get-tuple-element.39.refs_2_), custom_call_target="tpu_custom_call" | custom-call | flops 1000 | bytes 1000 | tf_op jit(solution)/shard_map/pallas_call | solution.py:131
  59.4 1.3 %collective-permute-done.14.refs_1_ = bf16[80,960]{1,0:T(8,128)(2,1)S(1)} collective-permute-done((bf16[80,960]{1,0:T(8,128)(2,1)S(1)}, bf16[80,960]{1,0:T(8,128)(2,1)S(1)}, u32[]{:S(2)}, u32[]{:S(2)}) %collective-permute-start.14) | collective-permute-done | bytes 153632 | tf_op jit(solution)/shard_map/ppermute | solution.py:26
  60.7 3.3 %collective-permute-done.16.refs_3_ = bf16[80,960]{1,0:T(8,128)(2,1)S(1)} collective-permute-done((bf16[80,960]{1,0:T(8,128)(2,1)S(1)}, bf16[80,960]{1,0:T(8,128)(2,1)S(1)}, u32[]{:S(2)}, u32[]{:S(2)}) %collective-permute-start.16) | collective-permute-done | bytes 153632 | tf_op jit(solution)/shard_map/ppermute | solution.py:26
  64.1 1.5 %collective-permute-start.18 = (bf16[40,960]{1,0:T(8,128)(2,1)S(1)}, bf16[40,960]{1,0:T(8,128)(2,1)S(1)}, u32[]{:S(2)}, u32[]{:S(2)}) collective-permute-start(bf16[40,960]{1,0:T(8,128)(2,1)S(1)} %get-tuple-element.45), channel_id=1, source_target_pairs={{0,192},{1,193},{2,194},{3,195},{4,196},{5,197},{6,198},{7,199},{8... | collective-permute-start | bytes 230408 | tf_op jit(solution)/shard_map/ppermute | solution.py:26
  65.6 2.7 %collective-permute-start.17 = (bf16[40,960]{1,0:T(8,128)(2,1)S(1)}, bf16[40,960]{1,0:T(8,128)(2,1)S(1)}, u32[]{:S(2)}, u32[]{:S(2)}) collective-permute-start(bf16[40,960]{1,0:T(8,128)(2,1)S(1)} %get-tuple-element.43.refs_14_), channel_id=1, source_target_pairs={{0,64},{1,65},{2,66},{3,67},{4,68},{5,69},{6,70},{7,71},{8,72},{9,... | collective-permute-start | bytes 230408 | tf_op jit(solution)/shard_map/ppermute | solution.py:26
  68.3 1.9 %shard_map.101.refs_3_.refs_0_ = bf16[320,512]{1,0:T(8,128)(2,1)S(1)} custom-call(bf16[64,5120]{1,0:T(8,128)(2,1)S(1)} %copy-done, bf16[64,5120]{1,0:T(8,128)(2,1)S(1)} %collective-permute-done.refs_0_.refs_1_, bf16[64,5120]{1,0:T(8,128)(2,1)S(1)} %collective-permute-done.1.refs_1_.refs_2_, bf16[32,5120]{1,0:T(8,128)(2,1)S(1)} %collective-permute-done.4.refs_3_, ...), custom_call_target="tpu_custom_call" | custom-call | flops 1000 | bytes 1000 | tf_op jit(solution)/shard_map/pallas_call | solution.py:91
  70.2 1.2 %collective-permute-done.18.refs_2_ = bf16[40,960]{1,0:T(8,128)(2,1)S(1)} collective-permute-done((bf16[40,960]{1,0:T(8,128)(2,1)S(1)}, bf16[40,960]{1,0:T(8,128)(2,1)S(1)}, u32[]{:S(2)}, u32[]{:S(2)}) %collective-permute-start.18) | collective-permute-done | bytes 76832 | tf_op jit(solution)/shard_map/ppermute | solution.py:26
  71.4 0.4 collective-permute-done.17.refs_1_
  71.9 2.3 %collective-permute-start.19 = (bf16[40,960]{1,0:T(8,128)(2,1)S(1)}, bf16[40,960]{1,0:T(8,128)(2,1)S(1)}, u32[]{:S(2)}, u32[]{:S(2)}) collective-permute-start(bf16[40,960]{1,0:T(8,128)(2,1)S(1)} %get-tuple-element.47), channel_id=1, source_target_pairs={{0,192},{1,193},{2,194},{3,195},{4,196},{5,197},{6,198},{7,199},{8... | collective-permute-start | bytes 230408 | tf_op jit(solution)/shard_map/ppermute | solution.py:26
  74.2 1.2 %collective-permute-start.20 = (bf16[40,960]{1,0:T(8,128)(2,1)S(1)}, bf16[40,960]{1,0:T(8,128)(2,1)S(1)}, u32[]{:S(2)}, u32[]{:S(2)}) collective-permute-start(bf16[40,960]{1,0:T(8,128)(2,1)S(1)} %get-tuple-element.48), channel_id=1, source_target_pairs={{0,64},{1,65},{2,66},{3,67},{4,68},{5,69},{6,70},{7,71},{8,72},{9,... | collective-permute-start | bytes 230408 | tf_op jit(solution)/shard_map/ppermute | solution.py:26
  75.4 3.6 %collective-permute-done.19.refs_2_ = bf16[40,960]{1,0:T(8,128)(2,1)S(1)} collective-permute-done((bf16[40,960]{1,0:T(8,128)(2,1)S(1)}, bf16[40,960]{1,0:T(8,128)(2,1)S(1)}, u32[]{:S(2)}, u32[]{:S(2)}) %collective-permute-start.19) | collective-permute-done | bytes 76832 | tf_op jit(solution)/shard_map/ppermute | solution.py:26
  78.9 1.5 %collective-permute-done.20.refs_3_ = bf16[40,960]{1,0:T(8,128)(2,1)S(1)} collective-permute-done((bf16[40,960]{1,0:T(8,128)(2,1)S(1)}, bf16[40,960]{1,0:T(8,128)(2,1)S(1)}, u32[]{:S(2)}, u32[]{:S(2)}) %collective-permute-start.20) | collective-permute-done | bytes 76832 | tf_op jit(solution)/shard_map/ppermute | solution.py:26
  80.4 0.9 shard_map.103.refs_1_
  81.3 3.5 %collective-permute-start.23 = (bf16[80,960]{1,0:T(8,128)(2,1)S(1)}, bf16[80,960]{1,0:T(8,128)(2,1)S(1)}, u32[]{:S(2)}, u32[]{:S(2)}) collective-permute-start(bf16[80,960]{1,0:T(8,128)(2,1)S(1)} %shard_map.103.refs_1_), channel_id=1, source_target_pairs={{0,32},{1,33},{2,34},{3,35},{4,36},{5,37},{6,38},{7,39},{8,40},{9,... | collective-permute-start | bytes 460808 | tf_op jit(solution)/shard_map/ppermute | solution.py:26
  84.8 2.0 %collective-permute-start.21 = (bf16[80,960]{1,0:T(8,128)(2,1)S(1)}, bf16[80,960]{1,0:T(8,128)(2,1)S(1)}, u32[]{:S(2)}, u32[]{:S(2)}) collective-permute-start(bf16[80,960]{1,0:T(8,128)(2,1)S(1)} %shard_map.103.refs_1_), channel_id=1, source_target_pairs={{0,16},{1,17},{2,18},{3,19},{4,20},{5,21},{6,22},{7,23},{8,24},{9,... | collective-permute-start | bytes 460808 | tf_op jit(solution)/shard_map/ppermute | solution.py:26
  86.8 3.1 %collective-permute-done.23.refs_4_ = bf16[80,960]{1,0:T(8,128)(2,1)S(1)} collective-permute-done((bf16[80,960]{1,0:T(8,128)(2,1)S(1)}, bf16[80,960]{1,0:T(8,128)(2,1)S(1)}, u32[]{:S(2)}, u32[]{:S(2)}) %collective-permute-start.23) | collective-permute-done | bytes 153632 | tf_op jit(solution)/shard_map/ppermute | solution.py:26
  89.9 1.7 %collective-permute-done.22.refs_3_ = bf16[80,960]{1,0:T(8,128)(2,1)S(1)} collective-permute-done((bf16[80,960]{1,0:T(8,128)(2,1)S(1)}, bf16[80,960]{1,0:T(8,128)(2,1)S(1)}, u32[]{:S(2)}, u32[]{:S(2)}) %collective-permute-start.22) | collective-permute-done | bytes 153632 | tf_op jit(solution)/shard_map/ppermute | solution.py:26
  91.6 0.3 collective-permute-done.21.refs_2_
  91.9 0.2 collective-permute-start.25
  92.1 0.9 collective-permute-done.26.refs_7_
  93.0 0.3 collective-permute-done.25.refs_6_
  93.3 1.0 shard_map.104
  94.2 1.4 %collective-permute-start.29 = (bf16[64,640]{1,0:T(8,128)(2,1)S(1)}, bf16[64,640]{1,0:T(8,128)(2,1)S(1)}, u32[]{:S(2)}, u32[]{:S(2)}) collective-permute-start(bf16[64,640]{1,0:T(8,128)(2,1)S(1)} %get-tuple-element.50), channel_id=1, source_target_pairs={{0,196},{1,197},{2,198},{3,199},{4,64},{5,65},{6,66},{7,67},{8,204... | collective-permute-start | bytes 245768 | tf_op jit(solution)/shard_map/ppermute | solution.py:26
  95.6 0.6 collective-permute-start.28
  96.2 1.0 shard_map.105.refs_0_
  97.2 3.0 %collective-permute-done.29.refs_2_ = bf16[64,640]{1,0:T(8,128)(2,1)S(1)} collective-permute-done((bf16[64,640]{1,0:T(8,128)(2,1)S(1)}, bf16[64,640]{1,0:T(8,128)(2,1)S(1)}, u32[]{:S(2)}, u32[]{:S(2)}) %collective-permute-start.29) | collective-permute-done | bytes 81952 | tf_op jit(solution)/shard_map/ppermute | solution.py:26
  100.3 1.1 collective-permute-start.30
  101.3 0.5 collective-permute-start.31
  101.8 2.6 %collective-permute-start.32 = (bf16[64,640]{1,0:T(8,128)(2,1)S(1)}, bf16[64,640]{1,0:T(8,128)(2,1)S(1)}, u32[]{:S(2)}, u32[]{:S(2)}) collective-permute-start(bf16[64,640]{1,0:T(8,128)(2,1)S(1)} %get-tuple-element.54), channel_id=1, source_target_pairs={{0,2},{1,3},{2,0},{3,1},{4,6},{5,7},{6,4},{7,5},{8,10},{9,11},{10,... | collective-permute-start | bytes 245768 | tf_op jit(solution)/shard_map/ppermute | solution.py:26
  104.4 0.4 collective-permute-done.30.refs_2_
  104.8 1.8 %collective-permute-done.31.refs_3_ = bf16[64,640]{1,0:T(8,128)(2,1)S(1)} collective-permute-done((bf16[64,640]{1,0:T(8,128)(2,1)S(1)}, bf16[64,640]{1,0:T(8,128)(2,1)S(1)}, u32[]{:S(2)}, u32[]{:S(2)}) %collective-permute-start.31) | collective-permute-done | bytes 81952 | tf_op jit(solution)/shard_map/ppermute | solution.py:26
  106.7 1.1 %collective-permute-done.32.refs_4_ = bf16[64,640]{1,0:T(8,128)(2,1)S(1)} collective-permute-done((bf16[64,640]{1,0:T(8,128)(2,1)S(1)}, bf16[64,640]{1,0:T(8,128)(2,1)S(1)}, u32[]{:S(2)}, u32[]{:S(2)}) %collective-permute-start.32) | collective-permute-done | bytes 81952 | tf_op jit(solution)/shard_map/ppermute | solution.py:26
  107.8 1.5 %shard_map.107 = bf16[64,2560]{1,0:T(8,128)(2,1)} custom-call(s32[32]{0:T(128)S(1)} %dynamic-slice_bitcast_fusion.refs_0_, bf16[64,640]{1,0:T(8,128)(2,1)S(1)} %get-tuple-element.51.refs_1_, bf16[64,640]{1,0:T(8,128)(2,1)S(1)} %collective-permute-done.30.refs_2_, bf16[64,640]{1,0:T(8,128)(2,1)S(1)} %collective-permute-done.31.refs_3_, ...), custom_call_target="tpu_custom_call" | custom-call | flops 1000 | bytes 1000 | tf_op jit(solution)/shard_map/pallas_call | solution.py:91
  (33 shorter events, 1.0 us)
Async XLA Ops:
  0.7 22.1 %collective-permute-start.1 = (bf16[64,5120]{1,0:T(8,128)(2,1)}, bf16[64,5120]{1,0:T(8,128)(2,1)S(1)}, u32[]{:S(2)}, u32[]{:S(2)}) collective-permute-start(bf16[64,5120]{1,0:T(8,128)(2,1)} %refs_0_.1), channel_id=1, source_target_pairs={{0,3},{1,2},{2,1},{3,0},{4,7},{5,6},{6,5},{7,4},{8,11},{9,10},{10,... | collective-permute-start | bytes 1966088 | tf_op jit(solution)/shard_map/ppermute | solution.py:26
  2.2 20.6 %collective-permute-start = (bf16[64,5120]{1,0:T(8,128)(2,1)}, bf16[64,5120]{1,0:T(8,128)(2,1)S(1)}, u32[]{:S(2)}, u32[]{:S(2)}) collective-permute-start(bf16[64,5120]{1,0:T(8,128)(2,1)} %refs_0_.1), channel_id=1, source_target_pairs={{0,1},{1,0},{2,3},{3,2},{4,5},{5,4},{6,7},{7,6},{8,9},{9,8},{10,11... | collective-permute-start | bytes 1966088 | tf_op jit(solution)/shard_map/ppermute | solution.py:26
  5.9 16.8 %collective-permute-start.3 = (bf16[32,5120]{1,0:T(8,128)(2,1)}, bf16[32,5120]{1,0:T(8,128)(2,1)S(1)}, u32[]{:S(2)}, u32[]{:S(2)}) collective-permute-start(bf16[32,5120]{1,0:T(8,128)(2,1)} %get-tuple-element.55), channel_id=1, source_target_pairs={{0,196},{1,197},{2,198},{3,199},{4,64},{5,65},{6,66},{7,67},{8,204... | collective-permute-start | bytes 983048 | tf_op jit(solution)/shard_map/ppermute | solution.py:26
  11.8 11.0 %collective-permute-start.2 = (bf16[32,5120]{1,0:T(8,128)(2,1)}, bf16[32,5120]{1,0:T(8,128)(2,1)S(1)}, u32[]{:S(2)}, u32[]{:S(2)}) collective-permute-start(bf16[32,5120]{1,0:T(8,128)(2,1)} %get-tuple-element.56), channel_id=1, source_target_pairs={{0,4},{1,5},{2,6},{3,7},{4,0},{5,1},{6,2},{7,3},{8,12},{9,13},{10,... | collective-permute-start | bytes 983048 | tf_op jit(solution)/shard_map/ppermute | solution.py:26
  22.7 18.0 %copy-start = (bf16[64,5120]{1,0:T(8,128)(2,1)S(1)}, bf16[64,5120]{1,0:T(8,128)(2,1)}, u32[]{:S(2)}) copy-start(bf16[64,5120]{1,0:T(8,128)(2,1)} %refs_0_.1) | copy-start | bytes 1966084
  22.9 10.7 %collective-permute-start.4 = (bf16[32,5120]{1,0:T(8,128)(2,1)S(1)}, bf16[32,5120]{1,0:T(8,128)(2,1)S(1)}, u32[]{:S(2)}, u32[]{:S(2)}) collective-permute-start(bf16[32,5120]{1,0:T(8,128)(2,1)S(1)} %get-tuple-element.33), channel_id=1, source_target_pairs={{0,3},{1,2},{2,1},{3,0},{4,7},{5,6},{6,5},{7,4},{8,11},{9,10},{10,... | collective-permute-start | bytes 983048 | tf_op jit(solution)/shard_map/ppermute | solution.py:26
  23.0 12.1 %collective-permute-start.5 = (bf16[32,5120]{1,0:T(8,128)(2,1)S(1)}, bf16[32,5120]{1,0:T(8,128)(2,1)S(1)}, u32[]{:S(2)}, u32[]{:S(2)}) collective-permute-start(bf16[32,5120]{1,0:T(8,128)(2,1)S(1)} %get-tuple-element.34), channel_id=1, source_target_pairs={{0,1},{1,0},{2,3},{3,2},{4,5},{5,4},{6,7},{7,6},{8,9},{9,8},{10,11... | collective-permute-start | bytes 983048 | tf_op jit(solution)/shard_map/ppermute | solution.py:26
  24.4 12.7 %collective-permute-start.8 = (bf16[32,5120]{1,0:T(8,128)(2,1)S(1)}, bf16[32,5120]{1,0:T(8,128)(2,1)S(1)}, u32[]{:S(2)}, u32[]{:S(2)}) collective-permute-start(bf16[32,5120]{1,0:T(8,128)(2,1)S(1)} %get-tuple-element.36), channel_id=1, source_target_pairs={{0,4},{1,5},{2,6},{3,7},{4,0},{5,1},{6,2},{7,3},{8,12},{9,13},{10,... | collective-permute-start | bytes 983048 | tf_op jit(solution)/shard_map/ppermute | solution.py:26
  26.4 12.9 %collective-permute-start.9 = (bf16[32,5120]{1,0:T(8,128)(2,1)S(1)}, bf16[32,5120]{1,0:T(8,128)(2,1)S(1)}, u32[]{:S(2)}, u32[]{:S(2)}) collective-permute-start(bf16[32,5120]{1,0:T(8,128)(2,1)S(1)} %get-tuple-element.37), channel_id=1, source_target_pairs={{0,196},{1,197},{2,198},{3,199},{4,64},{5,65},{6,66},{7,67},{8,204... | collective-permute-start | bytes 983048 | tf_op jit(solution)/shard_map/ppermute | solution.py:26
  28.9 10.4 %collective-permute-start.7 = (bf16[32,5120]{1,0:T(8,128)(2,1)S(1)}, bf16[32,5120]{1,0:T(8,128)(2,1)S(1)}, u32[]{:S(2)}, u32[]{:S(2)}) collective-permute-start(bf16[32,5120]{1,0:T(8,128)(2,1)S(1)} %get-tuple-element.35), channel_id=1, source_target_pairs={{0,3},{1,2},{2,1},{3,0},{4,7},{5,6},{6,5},{7,4},{8,11},{9,10},{10,... | collective-permute-start | bytes 983048 | tf_op jit(solution)/shard_map/ppermute | solution.py:26
  33.6 7.1 %collective-permute-start.6 = (bf16[32,5120]{1,0:T(8,128)(2,1)S(1)}, bf16[32,5120]{1,0:T(8,128)(2,1)S(1)}, u32[]{:S(2)}, u32[]{:S(2)}) collective-permute-start(bf16[32,5120]{1,0:T(8,128)(2,1)S(1)} %get-tuple-element.35), channel_id=1, source_target_pairs={{0,1},{1,0},{2,3},{3,2},{4,5},{5,4},{6,7},{7,6},{8,9},{9,8},{10,11... | collective-permute-start | bytes 983048 | tf_op jit(solution)/shard_map/ppermute | solution.py:26
  35.1 7.5 %collective-permute-start.10 = (bf16[32,5120]{1,0:T(8,128)(2,1)S(1)}, bf16[32,5120]{1,0:T(8,128)(2,1)S(1)}, u32[]{:S(2)}, u32[]{:S(2)}) collective-permute-start(bf16[32,5120]{1,0:T(8,128)(2,1)S(1)} %collective-permute-done.4.refs_3_), channel_id=1, source_target_pairs={{0,4},{1,5},{2,6},{3,7},{4,0},{5,1},{6,2},{7,3},{8,12},{9,13},{10,... | collective-permute-start | bytes 983048 | tf_op jit(solution)/shard_map/ppermute | solution.py:26
  37.1 8.3 %collective-permute-start.11 = (bf16[32,5120]{1,0:T(8,128)(2,1)S(1)}, bf16[32,5120]{1,0:T(8,128)(2,1)S(1)}, u32[]{:S(2)}, u32[]{:S(2)}) collective-permute-start(bf16[32,5120]{1,0:T(8,128)(2,1)S(1)} %collective-permute-done.5.refs_4_), channel_id=1, source_target_pairs={{0,196},{1,197},{2,198},{3,199},{4,64},{5,65},{6,66},{7,67},{8,204... | collective-permute-start | bytes 983048 | tf_op jit(solution)/shard_map/ppermute | solution.py:26
  39.3 8.0 %collective-permute-start.12 = (f32[1,128]{1,0:T(1,128)S(1)}, f32[1,128]{1,0:T(1,128)S(1)}, u32[]{:S(2)}, u32[]{:S(2)}) collective-permute-start(f32[1,128]{1,0:T(1,128)S(1)} %get-tuple-element.38), channel_id=1, source_target_pairs={{0,64},{1,65},{2,66},{3,67},{4,196},{5,197},{6,198},{7,199},{8,72}... | collective-permute-start | bytes 1544 | tf_op jit(solution)/shard_map/ppermute | solution.py:26
  49.2 2.2 %collective-permute-start.13 = (bf16[320,960]{1,0:T(8,128)(2,1)S(1)}, bf16[320,960]{1,0:T(8,128)(2,1)S(1)}, u32[]{:S(2)}, u32[]{:S(2)}) collective-permute-start(bf16[320,960]{1,0:T(8,128)(2,1)S(1)} %shard_map.96.refs_8_), channel_id=1, source_target_pairs={{0,8},{1,9},{2,10},{3,11},{4,12},{5,13},{6,14},{7,15},{8,0},{9,1},... | collective-permute-start | bytes 1843208 | tf_op jit(solution)/shard_map/ppermute | solution.py:26
  52.1 8.6 %collective-permute-start.14 = (bf16[80,960]{1,0:T(8,128)(2,1)S(1)}, bf16[80,960]{1,0:T(8,128)(2,1)S(1)}, u32[]{:S(2)}, u32[]{:S(2)}) collective-permute-start(bf16[80,960]{1,0:T(8,128)(2,1)S(1)} %get-tuple-element.41), channel_id=1, source_target_pairs={{0,32},{1,33},{2,34},{3,35},{4,36},{5,37},{6,38},{7,39},{8,40},{9,... | collective-permute-start | bytes 460808 | tf_op jit(solution)/shard_map/ppermute | solution.py:26
  55.4 8.7 %collective-permute-start.16 = (bf16[80,960]{1,0:T(8,128)(2,1)S(1)}, bf16[80,960]{1,0:T(8,128)(2,1)S(1)}, u32[]{:S(2)}, u32[]{:S(2)}) collective-permute-start(bf16[80,960]{1,0:T(8,128)(2,1)S(1)} %get-tuple-element.42), channel_id=1, source_target_pairs={{0,48},{1,49},{2,50},{3,51},{4,52},{5,53},{6,54},{7,55},{8,56},{9,... | collective-permute-start | bytes 460808 | tf_op jit(solution)/shard_map/ppermute | solution.py:26
  56.4 7.6 %collective-permute-start.15 = (bf16[80,960]{1,0:T(8,128)(2,1)S(1)}, bf16[80,960]{1,0:T(8,128)(2,1)S(1)}, u32[]{:S(2)}, u32[]{:S(2)}) collective-permute-start(bf16[80,960]{1,0:T(8,128)(2,1)S(1)} %get-tuple-element.39.refs_2_), channel_id=1, source_target_pairs={{0,16},{1,17},{2,18},{3,19},{4,20},{5,21},{6,22},{7,23},{8,24},{9,... | collective-permute-start | bytes 460808 | tf_op jit(solution)/shard_map/ppermute | solution.py:26
  64.1 7.3 %collective-permute-start.18 = (bf16[40,960]{1,0:T(8,128)(2,1)S(1)}, bf16[40,960]{1,0:T(8,128)(2,1)S(1)}, u32[]{:S(2)}, u32[]{:S(2)}) collective-permute-start(bf16[40,960]{1,0:T(8,128)(2,1)S(1)} %get-tuple-element.45), channel_id=1, source_target_pairs={{0,192},{1,193},{2,194},{3,195},{4,196},{5,197},{6,198},{7,199},{8... | collective-permute-start | bytes 230408 | tf_op jit(solution)/shard_map/ppermute | solution.py:26
  65.6 6.2 %collective-permute-start.17 = (bf16[40,960]{1,0:T(8,128)(2,1)S(1)}, bf16[40,960]{1,0:T(8,128)(2,1)S(1)}, u32[]{:S(2)}, u32[]{:S(2)}) collective-permute-start(bf16[40,960]{1,0:T(8,128)(2,1)S(1)} %get-tuple-element.43.refs_14_), channel_id=1, source_target_pairs={{0,64},{1,65},{2,66},{3,67},{4,68},{5,69},{6,70},{7,71},{8,72},{9,... | collective-permute-start | bytes 230408 | tf_op jit(solution)/shard_map/ppermute | solution.py:26
  71.9 7.1 %collective-permute-start.19 = (bf16[40,960]{1,0:T(8,128)(2,1)S(1)}, bf16[40,960]{1,0:T(8,128)(2,1)S(1)}, u32[]{:S(2)}, u32[]{:S(2)}) collective-permute-start(bf16[40,960]{1,0:T(8,128)(2,1)S(1)} %get-tuple-element.47), channel_id=1, source_target_pairs={{0,192},{1,193},{2,194},{3,195},{4,196},{5,197},{6,198},{7,199},{8... | collective-permute-start | bytes 230408 | tf_op jit(solution)/shard_map/ppermute | solution.py:26
  74.2 6.2 %collective-permute-start.20 = (bf16[40,960]{1,0:T(8,128)(2,1)S(1)}, bf16[40,960]{1,0:T(8,128)(2,1)S(1)}, u32[]{:S(2)}, u32[]{:S(2)}) collective-permute-start(bf16[40,960]{1,0:T(8,128)(2,1)S(1)} %get-tuple-element.48), channel_id=1, source_target_pairs={{0,64},{1,65},{2,66},{3,67},{4,68},{5,69},{6,70},{7,71},{8,72},{9,... | collective-permute-start | bytes 230408 | tf_op jit(solution)/shard_map/ppermute | solution.py:26
  81.3 8.6 %collective-permute-start.23 = (bf16[80,960]{1,0:T(8,128)(2,1)S(1)}, bf16[80,960]{1,0:T(8,128)(2,1)S(1)}, u32[]{:S(2)}, u32[]{:S(2)}) collective-permute-start(bf16[80,960]{1,0:T(8,128)(2,1)S(1)} %shard_map.103.refs_1_), channel_id=1, source_target_pairs={{0,32},{1,33},{2,34},{3,35},{4,36},{5,37},{6,38},{7,39},{8,40},{9,... | collective-permute-start | bytes 460808 | tf_op jit(solution)/shard_map/ppermute | solution.py:26
  84.8 6.8 %collective-permute-start.22 = (bf16[80,960]{1,0:T(8,128)(2,1)S(1)}, bf16[80,960]{1,0:T(8,128)(2,1)S(1)}, u32[]{:S(2)}, u32[]{:S(2)}) collective-permute-start(bf16[80,960]{1,0:T(8,128)(2,1)S(1)} %shard_map.103.refs_1_), channel_id=1, source_target_pairs={{0,48},{1,49},{2,50},{3,51},{4,52},{5,53},{6,54},{7,55},{8,56},{9,... | collective-permute-start | bytes 460808 | tf_op jit(solution)/shard_map/ppermute | solution.py:26
  84.8 7.1 %collective-permute-start.21 = (bf16[80,960]{1,0:T(8,128)(2,1)S(1)}, bf16[80,960]{1,0:T(8,128)(2,1)S(1)}, u32[]{:S(2)}, u32[]{:S(2)}) collective-permute-start(bf16[80,960]{1,0:T(8,128)(2,1)S(1)} %shard_map.103.refs_1_), channel_id=1, source_target_pairs={{0,16},{1,17},{2,18},{3,19},{4,20},{5,21},{6,22},{7,23},{8,24},{9,... | collective-permute-start | bytes 460808 | tf_op jit(solution)/shard_map/ppermute | solution.py:26
  86.8 5.3 %collective-permute-start.24 = (bf16[80,960]{1,0:T(8,128)(2,1)S(1)}, bf16[80,960]{1,0:T(8,128)(2,1)S(1)}, u32[]{:S(2)}, u32[]{:S(2)}) collective-permute-start(bf16[80,960]{1,0:T(8,128)(2,1)S(1)} %shard_map.103.refs_1_), channel_id=1, source_target_pairs={{0,8},{1,9},{2,10},{3,11},{4,12},{5,13},{6,14},{7,15},{8,0},{9,1},... | collective-permute-start | bytes 460808 | tf_op jit(solution)/shard_map/ppermute | solution.py:26
  89.9 2.2 %collective-permute-start.27 = (bf16[80,960]{1,0:T(8,128)(2,1)S(1)}, bf16[80,960]{1,0:T(8,128)(2,1)S(1)}, u32[]{:S(2)}, u32[]{:S(2)}) collective-permute-start(bf16[80,960]{1,0:T(8,128)(2,1)S(1)} %collective-permute-done.23.refs_4_), channel_id=1, source_target_pairs={{0,8},{1,9},{2,10},{3,11},{4,12},{5,13},{6,14},{7,15},{8,0},{9,1},... | collective-permute-start | bytes 460808 | tf_op jit(solution)/shard_map/ppermute | solution.py:26
  91.6 1.4 %collective-permute-start.26 = (bf16[80,960]{1,0:T(8,128)(2,1)S(1)}, bf16[80,960]{1,0:T(8,128)(2,1)S(1)}, u32[]{:S(2)}, u32[]{:S(2)}) collective-permute-start(bf16[80,960]{1,0:T(8,128)(2,1)S(1)} %collective-permute-done.22.refs_3_), channel_id=1, source_target_pairs={{0,8},{1,9},{2,10},{3,11},{4,12},{5,13},{6,14},{7,15},{8,0},{9,1},... | collective-permute-start | bytes 460808 | tf_op jit(solution)/shard_map/ppermute | solution.py:26
  91.9 1.4 %collective-permute-start.25 = (bf16[80,960]{1,0:T(8,128)(2,1)S(1)}, bf16[80,960]{1,0:T(8,128)(2,1)S(1)}, u32[]{:S(2)}, u32[]{:S(2)}) collective-permute-start(bf16[80,960]{1,0:T(8,128)(2,1)S(1)} %collective-permute-done.21.refs_2_), channel_id=1, source_target_pairs={{0,8},{1,9},{2,10},{3,11},{4,12},{5,13},{6,14},{7,15},{8,0},{9,1},... | collective-permute-start | bytes 460808 | tf_op jit(solution)/shard_map/ppermute | solution.py:26
  94.2 5.9 %collective-permute-start.29 = (bf16[64,640]{1,0:T(8,128)(2,1)S(1)}, bf16[64,640]{1,0:T(8,128)(2,1)S(1)}, u32[]{:S(2)}, u32[]{:S(2)}) collective-permute-start(bf16[64,640]{1,0:T(8,128)(2,1)S(1)} %get-tuple-element.50), channel_id=1, source_target_pairs={{0,196},{1,197},{2,198},{3,199},{4,64},{5,65},{6,66},{7,67},{8,204... | collective-permute-start | bytes 245768 | tf_op jit(solution)/shard_map/ppermute | solution.py:26
  95.6 4.5 %collective-permute-start.28 = (bf16[64,640]{1,0:T(8,128)(2,1)S(1)}, bf16[64,640]{1,0:T(8,128)(2,1)S(1)}, u32[]{:S(2)}, u32[]{:S(2)}) collective-permute-start(bf16[64,640]{1,0:T(8,128)(2,1)S(1)} %get-tuple-element.49.refs_9_), channel_id=1, source_target_pairs={{0,4},{1,5},{2,6},{3,7},{4,0},{5,1},{6,2},{7,3},{8,12},{9,13},{10,... | collective-permute-start | bytes 245768 | tf_op jit(solution)/shard_map/ppermute | solution.py:26
  100.3 4.6 %collective-permute-start.30 = (bf16[64,640]{1,0:T(8,128)(2,1)S(1)}, bf16[64,640]{1,0:T(8,128)(2,1)S(1)}, u32[]{:S(2)}, u32[]{:S(2)}) collective-permute-start(bf16[64,640]{1,0:T(8,128)(2,1)S(1)} %get-tuple-element.52), channel_id=1, source_target_pairs={{0,1},{1,0},{2,3},{3,2},{4,5},{5,4},{6,7},{7,6},{8,9},{9,8},{10,11... | collective-permute-start | bytes 245768 | tf_op jit(solution)/shard_map/ppermute | solution.py:26
  101.3 5.3 %collective-permute-start.31 = (bf16[64,640]{1,0:T(8,128)(2,1)S(1)}, bf16[64,640]{1,0:T(8,128)(2,1)S(1)}, u32[]{:S(2)}, u32[]{:S(2)}) collective-permute-start(bf16[64,640]{1,0:T(8,128)(2,1)S(1)} %get-tuple-element.53), channel_id=1, source_target_pairs={{0,3},{1,2},{2,1},{3,0},{4,7},{5,6},{6,5},{7,4},{8,11},{9,10},{10,... | collective-permute-start | bytes 245768 | tf_op jit(solution)/shard_map/ppermute | solution.py:26
  101.8 5.9 %collective-permute-start.32 = (bf16[64,640]{1,0:T(8,128)(2,1)S(1)}, bf16[64,640]{1,0:T(8,128)(2,1)S(1)}, u32[]{:S(2)}, u32[]{:S(2)}) collective-permute-start(bf16[64,640]{1,0:T(8,128)(2,1)S(1)} %get-tuple-element.54), channel_id=1, source_target_pairs={{0,2},{1,3},{2,0},{3,1},{4,6},{5,7},{6,4},{7,5},{8,10},{9,11},{10,... | collective-permute-start | bytes 245768 | tf_op jit(solution)/shard_map/ppermute | solution.py:26

commit v11 on v10

--- a/solution.py
+++ b/solution.py
@@ -228,9 +228,9 @@
 OTHERS += [(1, 0, 32), (2, 16, 32), (5, 0, 16), (3, 16, 32), (5, 16, 32), (7, 0, 32)]
 
 
-def gather(tokens, work):
+def gather(tokens, same_tokens, work):
     near_tile, far_tile = to_near_x(tokens), to_far_x(tokens)
-    z1, z2 = to_near_z(tokens[:32]), to_far_z(tokens[32:])
+    z1, z2 = to_near_z(same_tokens[:32]), to_far_z(same_tokens[32:])
     near_first, far_second, first, second, both = call(
         split_kernel, [like((32, 5120))] * 5, near_tile, far_tile, z1, z2, after=work
     )
@@ -304,7 +304,7 @@
 def body(tokens, w_qkv, scale_exp, gate_mask, rate, fast_gate, fast_up, fast_down):
     at = lax.axis_index("seq") * 8 + lax.axis_index("head")
     my = lax.dynamic_slice_in_dim(jnp.asarray(table()), at, 1, axis=0).reshape(32)
-    tokens, my = lax.optimization_barrier((tokens, my))
+    same_tokens, my = lax.optimization_barrier((tokens, my))
     factor = jnp.exp2(scale_exp.astype(F32)).astype(BF16)[:, :, 0]
     factor = jnp.repeat(factor, w_qkv.shape[1] // factor.shape[1], axis=1)[:, None, :]
     w_t = jnp.transpose(w_qkv, (0, 2, 1))
@@ -319,7 +319,7 @@
     moved = permute(sent, lambda h, y, c, l, x: (h - 1 if l else h + 1, y, c, l, x))
     old_t = [w[0].T for w in (fast_gate, fast_up, fast_down)]
     weff = load(w_t, factor, 1, 2, after=(weight, *old_t))
-    plane, others = gather(tokens, (weff,))
+    plane, others = gather(tokens, same_tokens, (weff,))
     kv1 = project(plane, PLANE, weff, after=others[2:6])
     kv2 = project(others, OTHERS, weff, after=(kv1,))
 

time: 111 us -> 110 us (level)
  starting transfers between devices: 46.9 us -> 44.5 us
  waiting for transfers between devices: 31.8 us -> 34.1 us
    ppermute x33, starting transfers between devices: 46.9 us -> 44.5 us  [permute(): return lax.ppermute(value, AXES, pairs)]
    ppermute x33, waiting for transfers between devices: 31.8 us -> 34.1 us  [permute(): return lax.ppermute(value, AXES, pairs)]
where the time goes in v11:
time: 110 us; the launch traced here: 109 us
  starting transfers between devices  44.5 us (40%)
  waiting for transfers between devices  34.1 us (31%)
  Pallas kernels  20.5 us (19%)
  local copies, waits for them, and re-layouts  7.2 us (7%)
  other arithmetic  2.06 us (2%)
    ppermute x33, starting transfers between devices, permute(): return lax.ppermute(value, AXES, pairs)  44.5 us
    ppermute x33, waiting for transfers between devices, permute(): return lax.ppermute(value, AXES, pairs)  34.1 us
    pallas_call x15, Pallas kernels, call(): pl.pallas_call(run, out_shape=out_shape, in_specs=[SMEM] * scalars + [VME...  15.5 us
    pallas_call x2, Pallas kernels, load(): pl.pallas_call(run, out_shape=like((count, *w_t.shape[1:])), in_specs=[pl...  5 us
    unnamed x7, local copies, waits for them, and re-layouts  4.37 us
  transfers between devices with their start and end apart: 33, of which 19 were waited for; matrix products, arithmetic and copies ran while one was open for 8% of the time, Pallas kernels for 13%

profile of v11, /device:TPU:2, one launch (start us, length us, event | category | flops | bytes accessed | tf_op | source)
XLA Modules:
  0.0 109.2 jit_solution(8941711152726644698)
XLA Ops:
  0.0 1.5 %collective-permute-start.1 = (bf16[64,5120]{1,0:T(8,128)(2,1)}, bf16[64,5120]{1,0:T(8,128)(2,1)S(1)}, u32[]{:S(2)}, u32[]{:S(2)}) collective-permute-start(bf16[64,5120]{1,0:T(8,128)(2,1)} %refs_0_.3), channel_id=1, source_target_pairs={{0,3},{1,2},{2,1},{3,0},{4,7},{5,6},{6,5},{7,4},{8,11},{9,10},{10,... | collective-permute-start | bytes 1966088 | tf_op jit(solution)/shard_map/ppermute | solution.py:26
  1.5 1.8 %collective-permute-start = (bf16[64,5120]{1,0:T(8,128)(2,1)}, bf16[64,5120]{1,0:T(8,128)(2,1)S(1)}, u32[]{:S(2)}, u32[]{:S(2)}) collective-permute-start(bf16[64,5120]{1,0:T(8,128)(2,1)} %refs_0_.3), channel_id=1, source_target_pairs={{0,1},{1,0},{2,3},{3,2},{4,5},{5,4},{6,7},{7,6},{8,9},{9,8},{10,11... | collective-permute-start | bytes 1966088 | tf_op jit(solution)/shard_map/ppermute | solution.py:26
  3.3 0.7 dynamic-slice_bitcast_fusion.refs_0_
  4.0 1.9 %fusion = (bf16[32,5120]{1,0:T(8,128)(2,1)}, bf16[32,5120]{1,0:T(8,128)(2,1)}) fusion(bf16[64,5120]{1,0:T(8,128)(2,1)} %refs_0_.3), kind=kLoop, calls=%fused_computation.3 | loop fusion | bytes 1310720 | tf_op jit(solution)/shard_map/slice | solution.py:233
  5.9 5.9 %collective-permute-start.3 = (bf16[32,5120]{1,0:T(8,128)(2,1)}, bf16[32,5120]{1,0:T(8,128)(2,1)S(1)}, u32[]{:S(2)}, u32[]{:S(2)}) collective-permute-start(bf16[32,5120]{1,0:T(8,128)(2,1)} %get-tuple-element.55), channel_id=1, source_target_pairs={{0,196},{1,197},{2,198},{3,199},{4,64},{5,65},{6,66},{7,67},{8,204... | collective-permute-start | bytes 983048 | tf_op jit(solution)/shard_map/ppermute | solution.py:26
  12.4 0.6 broadcast.3
  13.0 1.4 %reduce.3 = s32[512]{0:T(512)S(1)} reduce(s32[512,1]{0,1:T(1,128)} %param.12, s32[]{:T(128)} %broadcast.3), dimensions={1}, to_apply=%param.12.reduce_sub_computation.3 | reduce | bytes 4100 | tf_op args[3]
  14.5 0.6 shard_map.91
  15.1 0.7 exponential_convert_fusion
  15.9 1.3 %copy.13 = bf16[1,320,640]{1,2,0:T(8,128)(2,1)S(1)} copy(bf16[1,320,640]{2,1,0:T(8,128)(2,1)} %param.14) | data formatting | bytes 819200 | tf_op args[5]
  17.2 1.3 %copy.14 = bf16[1,320,640]{1,2,0:T(8,128)(2,1)S(1)} copy(bf16[1,320,640]{2,1,0:T(8,128)(2,1)} %param.15) | data formatting | bytes 819200 | tf_op args[6]
  18.4 1.3 %copy.15 = bf16[1,320,640]{1,2,0:T(8,128)(2,1)S(1)} copy(bf16[1,320,640]{2,1,0:T(8,128)(2,1)} %param.16) | data formatting | bytes 819200 | tf_op args[7]
  19.7 3.0 %shard_map.92.refs_4_.refs_5_.refs_8_ = bf16[2,320,5120]{2,1,0:T(8,128)(2,1)S(1)} custom-call(bf16[3,320,5120]{2,1,0:T(8,128)(2,1)} %bitcast.28, bf16[3,1,5120]{2,1,0:T(2,128)(2,1)S(1)} %broadcast_in_dim_reshape.4.refs_1_, f32[1,384]{1,0:T(1,128)S(1)} %get-tuple-element.32.refs_2_.refs_3_, bf16[640,320]{1,0:T(8,128)(2,1)S(1)} %bitcast.16, ...), custom_call_target="tpu_custom_call" | custom-call | flops 1000 | bytes 1000 | tf_op jit(solution)/shard_map/pallas_call | solution.py:131
  23.0 1.4 %collective-permute-start.5 = (bf16[32,5120]{1,0:T(8,128)(2,1)S(1)}, bf16[32,5120]{1,0:T(8,128)(2,1)S(1)}, u32[]{:S(2)}, u32[]{:S(2)}) collective-permute-start(bf16[32,5120]{1,0:T(8,128)(2,1)S(1)} %get-tuple-element.34), channel_id=1, source_target_pairs={{0,1},{1,0},{2,3},{3,2},{4,5},{5,4},{6,7},{7,6},{8,9},{9,8},{10,11... | collective-permute-start | bytes 983048 | tf_op jit(solution)/shard_map/ppermute | solution.py:26
  24.4 2.0 %collective-permute-start.8 = (bf16[32,5120]{1,0:T(8,128)(2,1)S(1)}, bf16[32,5120]{1,0:T(8,128)(2,1)S(1)}, u32[]{:S(2)}, u32[]{:S(2)}) collective-permute-start(bf16[32,5120]{1,0:T(8,128)(2,1)S(1)} %get-tuple-element.36), channel_id=1, source_target_pairs={{0,4},{1,5},{2,6},{3,7},{4,0},{5,1},{6,2},{7,3},{8,12},{9,13},{10,... | collective-permute-start | bytes 983048 | tf_op jit(solution)/shard_map/ppermute | solution.py:26
  26.4 1.9 %collective-permute-start.9 = (bf16[32,5120]{1,0:T(8,128)(2,1)S(1)}, bf16[32,5120]{1,0:T(8,128)(2,1)S(1)}, u32[]{:S(2)}, u32[]{:S(2)}) collective-permute-start(bf16[32,5120]{1,0:T(8,128)(2,1)S(1)} %get-tuple-element.37), channel_id=1, source_target_pairs={{0,196},{1,197},{2,198},{3,199},{4,64},{5,65},{6,66},{7,67},{8,204... | collective-permute-start | bytes 983048 | tf_op jit(solution)/shard_map/ppermute | solution.py:26
  28.3 1.1 %collective-permute-start.7 = (bf16[32,5120]{1,0:T(8,128)(2,1)S(1)}, bf16[32,5120]{1,0:T(8,128)(2,1)S(1)}, u32[]{:S(2)}, u32[]{:S(2)}) collective-permute-start(bf16[32,5120]{1,0:T(8,128)(2,1)S(1)} %get-tuple-element.35), channel_id=1, source_target_pairs={{0,3},{1,2},{2,1},{3,0},{4,7},{5,6},{6,5},{7,4},{8,11},{9,10},{10,... | collective-permute-start | bytes 983048 | tf_op jit(solution)/shard_map/ppermute | solution.py:26
  29.4 4.2 %collective-permute-done.4.refs_3_ = bf16[32,5120]{1,0:T(8,128)(2,1)S(1)} collective-permute-done((bf16[32,5120]{1,0:T(8,128)(2,1)S(1)}, bf16[32,5120]{1,0:T(8,128)(2,1)S(1)}, u32[]{:S(2)}, u32[]{:S(2)}) %collective-permute-start.4) | collective-permute-done | bytes 327712 | tf_op jit(solution)/shard_map/ppermute | solution.py:26
  33.6 1.4 %collective-permute-start.6 = (bf16[32,5120]{1,0:T(8,128)(2,1)S(1)}, bf16[32,5120]{1,0:T(8,128)(2,1)S(1)}, u32[]{:S(2)}, u32[]{:S(2)}) collective-permute-start(bf16[32,5120]{1,0:T(8,128)(2,1)S(1)} %get-tuple-element.35), channel_id=1, source_target_pairs={{0,1},{1,0},{2,3},{3,2},{4,5},{5,4},{6,7},{7,6},{8,9},{9,8},{10,11... | collective-permute-start | bytes 983048 | tf_op jit(solution)/shard_map/ppermute | solution.py:26
  35.1 2.0 %collective-permute-start.10 = (bf16[32,5120]{1,0:T(8,128)(2,1)S(1)}, bf16[32,5120]{1,0:T(8,128)(2,1)S(1)}, u32[]{:S(2)}, u32[]{:S(2)}) collective-permute-start(bf16[32,5120]{1,0:T(8,128)(2,1)S(1)} %collective-permute-done.4.refs_3_), channel_id=1, source_target_pairs={{0,4},{1,5},{2,6},{3,7},{4,0},{5,1},{6,2},{7,3},{8,12},{9,13},{10,... | collective-permute-start | bytes 983048 | tf_op jit(solution)/shard_map/ppermute | solution.py:26
  37.1 1.5 %collective-permute-start.11 = (bf16[32,5120]{1,0:T(8,128)(2,1)S(1)}, bf16[32,5120]{1,0:T(8,128)(2,1)S(1)}, u32[]{:S(2)}, u32[]{:S(2)}) collective-permute-start(bf16[32,5120]{1,0:T(8,128)(2,1)S(1)} %collective-permute-done.5.refs_4_), channel_id=1, source_target_pairs={{0,196},{1,197},{2,198},{3,199},{4,64},{5,65},{6,66},{7,67},{8,204... | collective-permute-start | bytes 983048 | tf_op jit(solution)/shard_map/ppermute | solution.py:26
  38.7 2.0 %collective-permute-done.6.refs_6_.refs_2_.refs_7_ = bf16[32,5120]{1,0:T(8,128)(2,1)S(1)} collective-permute-done((bf16[32,5120]{1,0:T(8,128)(2,1)S(1)}, bf16[32,5120]{1,0:T(8,128)(2,1)S(1)}, u32[]{:S(2)}, u32[]{:S(2)}) %collective-permute-start.6) | collective-permute-done | bytes 327712 | tf_op jit(solution)/shard_map/ppermute | solution.py:26
  40.7 1.9 %shard_map.94.refs_9_.refs_1_ = bf16[640,256]{1,0:T(8,128)(2,1)S(1)} custom-call(bf16[64,5120]{1,0:T(8,128)(2,1)S(1)} %copy-done, bf16[64,5120]{1,0:T(8,128)(2,1)S(1)} %collective-permute-done.refs_0_.refs_1_, bf16[64,5120]{1,0:T(8,128)(2,1)S(1)} %collective-permute-done.1.refs_1_.refs_2_, bf16[32,5120]{1,0:T(8,128)(2,1)S(1)} %collective-permute-done.4.refs_3_, ...), custom_call_target="tpu_custom_call" | custom-call | flops 1000 | bytes 1000 | tf_op jit(solution)/shard_map/pallas_call | solution.py:91
  42.6 2.8 %collective-permute-done.11.refs_7_.refs_12_ = bf16[32,5120]{1,0:T(8,128)(2,1)S(1)} collective-permute-done((bf16[32,5120]{1,0:T(8,128)(2,1)S(1)}, bf16[32,5120]{1,0:T(8,128)(2,1)S(1)}, u32[]{:S(2)}, u32[]{:S(2)}) %collective-permute-start.11) | collective-permute-done | bytes 327712 | tf_op jit(solution)/shard_map/ppermute | solution.py:26
  45.4 1.9 %shard_map.95.refs_2_ = bf16[640,256]{1,0:T(8,128)(2,1)S(1)} custom-call(bf16[32,5120]{1,0:T(8,128)(2,1)S(1)} %collective-permute-done.2.refs_2_.refs_0_.refs_5_, bf16[32,5120]{1,0:T(8,128)(2,1)S(1)} %collective-permute-done.3.refs_3_.refs_1_.refs_6_, bf16[32,5120]{1,0:T(8,128)(2,1)S(1)} %collective-permute-done.6.refs_6_.refs_2_.refs_7_, ...), custom_call_target="tpu_custom_call" | custom-call | flops 1000 | bytes 1000 | tf_op jit(solution)/shard_map/pallas_call | solution.py:91
  47.3 1.9 %shard_map.96.refs_8_ = bf16[320,960]{1,0:T(8,128)(2,1)S(1)} custom-call(s32[32]{0:T(128)S(1)} %dynamic-slice_bitcast_fusion.refs_0_, bf16[640,256]{1,0:T(8,128)(2,1)S(1)} %shard_map.94.refs_9_.refs_1_, bf16[640,256]{1,0:T(8,128)(2,1)S(1)} %shard_map.95.refs_2_, f32[1,384]{1,0:T(1,128)S(1)} %get-tuple-element.32.refs_2_.refs_3_, ...), custom_call_target="tpu_custom_call" | custom-call | flops 1000 | bytes 1000 | tf_op jit(solution)/shard_map/pallas_call | solution.py:91
  49.3 1.9 %shard_map.97.refs_1_ = f32[320,960]{1,0:T(8,128)S(1)} custom-call(s32[32]{0:T(128)S(1)} %dynamic-slice_bitcast_fusion.refs_0_, bf16[640,256]{1,0:T(8,128)(2,1)S(1)} %shard_map.94.refs_9_.refs_1_, bf16[640,256]{1,0:T(8,128)(2,1)S(1)} %shard_map.95.refs_2_, f32[1,384]{1,0:T(1,128)S(1)} %get-tuple-element.32.refs_2_.refs_3_, ...), custom_call_target="tpu_custom_call" | custom-call | flops 1000 | bytes 1000 | tf_op jit(solution)/shard_map/pallas_call | solution.py:91
  51.4 0.7 shard_map.98
  52.1 3.3 %collective-permute-start.14 = (bf16[80,960]{1,0:T(8,128)(2,1)S(1)}, bf16[80,960]{1,0:T(8,128)(2,1)S(1)}, u32[]{:S(2)}, u32[]{:S(2)}) collective-permute-start(bf16[80,960]{1,0:T(8,128)(2,1)S(1)} %get-tuple-element.41), channel_id=1, source_target_pairs={{0,32},{1,33},{2,34},{3,35},{4,36},{5,37},{6,38},{7,39},{8,40},{9,... | collective-permute-start | bytes 460808 | tf_op jit(solution)/shard_map/ppermute | solution.py:26
  55.4 1.1 collective-permute-start.16
  56.4 1.0 collective-permute-start.15
  57.4 2.0 %shard_map.99.refs_4_.refs_13_ = bf16[1,320,5120]{2,1,0:T(8,128)(2,1)S(1)} custom-call(bf16[3,320,5120]{2,1,0:T(8,128)(2,1)} %bitcast.29, bf16[3,1,5120]{2,1,0:T(2,128)(2,1)S(1)} %broadcast_in_dim_reshape.4.refs_1_, bf16[80,960]{1,0:T(8,128)(2,1)S(1)} %get-tuple-element.39.refs_2_), custom_call_target="tpu_custom_call" | custom-call | flops 1000 | bytes 1000 | tf_op jit(solution)/shard_map/pallas_call | solution.py:131
  59.4 1.3 %collective-permute-done.14.refs_1_ = bf16[80,960]{1,0:T(8,128)(2,1)S(1)} collective-permute-done((bf16[80,960]{1,0:T(8,128)(2,1)S(1)}, bf16[80,960]{1,0:T(8,128)(2,1)S(1)}, u32[]{:S(2)}, u32[]{:S(2)}) %collective-permute-start.14) | collective-permute-done | bytes 153632 | tf_op jit(solution)/shard_map/ppermute | solution.py:26
  60.7 3.3 %collective-permute-done.16.refs_3_ = bf16[80,960]{1,0:T(8,128)(2,1)S(1)} collective-permute-done((bf16[80,960]{1,0:T(8,128)(2,1)S(1)}, bf16[80,960]{1,0:T(8,128)(2,1)S(1)}, u32[]{:S(2)}, u32[]{:S(2)}) %collective-permute-start.16) | collective-permute-done | bytes 153632 | tf_op jit(solution)/shard_map/ppermute | solution.py:26
  64.1 0.8 collective-permute-start.18
  65.0 2.7 %collective-permute-start.17 = (bf16[40,960]{1,0:T(8,128)(2,1)S(1)}, bf16[40,960]{1,0:T(8,128)(2,1)S(1)}, u32[]{:S(2)}, u32[]{:S(2)}) collective-permute-start(bf16[40,960]{1,0:T(8,128)(2,1)S(1)} %get-tuple-element.43.refs_14_), channel_id=1, source_target_pairs={{0,64},{1,65},{2,66},{3,67},{4,68},{5,69},{6,70},{7,71},{8,72},{9,... | collective-permute-start | bytes 230408 | tf_op jit(solution)/shard_map/ppermute | solution.py:26
  67.6 1.9 %shard_map.101.refs_3_.refs_0_ = bf16[320,512]{1,0:T(8,128)(2,1)S(1)} custom-call(bf16[64,5120]{1,0:T(8,128)(2,1)S(1)} %copy-done, bf16[64,5120]{1,0:T(8,128)(2,1)S(1)} %collective-permute-done.refs_0_.refs_1_, bf16[64,5120]{1,0:T(8,128)(2,1)S(1)} %collective-permute-done.1.refs_1_.refs_2_, bf16[32,5120]{1,0:T(8,128)(2,1)S(1)} %collective-permute-done.4.refs_3_, ...), custom_call_target="tpu_custom_call" | custom-call | flops 1000 | bytes 1000 | tf_op jit(solution)/shard_map/pallas_call | solution.py:91
  69.5 2.5 %collective-permute-done.18.refs_2_ = bf16[40,960]{1,0:T(8,128)(2,1)S(1)} collective-permute-done((bf16[40,960]{1,0:T(8,128)(2,1)S(1)}, bf16[40,960]{1,0:T(8,128)(2,1)S(1)}, u32[]{:S(2)}, u32[]{:S(2)}) %collective-permute-start.18) | collective-permute-done | bytes 76832 | tf_op jit(solution)/shard_map/ppermute | solution.py:26
  72.1 1.7 %collective-permute-start.19 = (bf16[40,960]{1,0:T(8,128)(2,1)S(1)}, bf16[40,960]{1,0:T(8,128)(2,1)S(1)}, u32[]{:S(2)}, u32[]{:S(2)}) collective-permute-start(bf16[40,960]{1,0:T(8,128)(2,1)S(1)} %get-tuple-element.47), channel_id=1, source_target_pairs={{0,192},{1,193},{2,194},{3,195},{4,196},{5,197},{6,198},{7,199},{8... | collective-permute-start | bytes 230408 | tf_op jit(solution)/shard_map/ppermute | solution.py:26
  73.8 1.4 %collective-permute-start.20 = (bf16[40,960]{1,0:T(8,128)(2,1)S(1)}, bf16[40,960]{1,0:T(8,128)(2,1)S(1)}, u32[]{:S(2)}, u32[]{:S(2)}) collective-permute-start(bf16[40,960]{1,0:T(8,128)(2,1)S(1)} %get-tuple-element.48), channel_id=1, source_target_pairs={{0,64},{1,65},{2,66},{3,67},{4,68},{5,69},{6,70},{7,71},{8,72},{9,... | collective-permute-start | bytes 230408 | tf_op jit(solution)/shard_map/ppermute | solution.py:26
  75.2 3.5 %collective-permute-done.19.refs_2_ = bf16[40,960]{1,0:T(8,128)(2,1)S(1)} collective-permute-done((bf16[40,960]{1,0:T(8,128)(2,1)S(1)}, bf16[40,960]{1,0:T(8,128)(2,1)S(1)}, u32[]{:S(2)}, u32[]{:S(2)}) %collective-permute-start.19) | collective-permute-done | bytes 76832 | tf_op jit(solution)/shard_map/ppermute | solution.py:26
  78.8 0.4 collective-permute-done.20.refs_3_
  79.2 0.9 shard_map.103.refs_1_
  80.1 3.2 %collective-permute-start.23 = (bf16[80,960]{1,0:T(8,128)(2,1)S(1)}, bf16[80,960]{1,0:T(8,128)(2,1)S(1)}, u32[]{:S(2)}, u32[]{:S(2)}) collective-permute-start(bf16[80,960]{1,0:T(8,128)(2,1)S(1)} %shard_map.103.refs_1_), channel_id=1, source_target_pairs={{0,32},{1,33},{2,34},{3,35},{4,36},{5,37},{6,38},{7,39},{8,40},{9,... | collective-permute-start | bytes 460808 | tf_op jit(solution)/shard_map/ppermute | solution.py:26
  83.3 1.0 collective-permute-start.22
  84.3 1.0 collective-permute-start.21
  85.3 3.2 %collective-permute-done.23.refs_4_ = bf16[80,960]{1,0:T(8,128)(2,1)S(1)} collective-permute-done((bf16[80,960]{1,0:T(8,128)(2,1)S(1)}, bf16[80,960]{1,0:T(8,128)(2,1)S(1)}, u32[]{:S(2)}, u32[]{:S(2)}) %collective-permute-start.23) | collective-permute-done | bytes 153632 | tf_op jit(solution)/shard_map/ppermute | solution.py:26
  88.6 2.5 %collective-permute-done.22.refs_3_ = bf16[80,960]{1,0:T(8,128)(2,1)S(1)} collective-permute-done((bf16[80,960]{1,0:T(8,128)(2,1)S(1)}, bf16[80,960]{1,0:T(8,128)(2,1)S(1)}, u32[]{:S(2)}, u32[]{:S(2)}) %collective-permute-start.22) | collective-permute-done | bytes 153632 | tf_op jit(solution)/shard_map/ppermute | solution.py:26
  91.1 0.2 collective-permute-done.21.refs_2_
  91.3 0.3 collective-permute-start.25
  91.6 0.9 collective-permute-done.26.refs_7_
  92.5 0.2 collective-permute-done.25.refs_6_
  92.7 1.0 shard_map.104
  93.7 1.4 %collective-permute-start.29 = (bf16[64,640]{1,0:T(8,128)(2,1)S(1)}, bf16[64,640]{1,0:T(8,128)(2,1)S(1)}, u32[]{:S(2)}, u32[]{:S(2)}) collective-permute-start(bf16[64,640]{1,0:T(8,128)(2,1)S(1)} %get-tuple-element.50), channel_id=1, source_target_pairs={{0,196},{1,197},{2,198},{3,199},{4,64},{5,65},{6,66},{7,67},{8,204... | collective-permute-start | bytes 245768 | tf_op jit(solution)/shard_map/ppermute | solution.py:26
  95.1 0.8 collective-permute-start.28
  95.9 1.0 shard_map.105.refs_0_
  96.9 2.8 %collective-permute-done.29.refs_2_ = bf16[64,640]{1,0:T(8,128)(2,1)S(1)} collective-permute-done((bf16[64,640]{1,0:T(8,128)(2,1)S(1)}, bf16[64,640]{1,0:T(8,128)(2,1)S(1)}, u32[]{:S(2)}, u32[]{:S(2)}) %collective-permute-start.29) | collective-permute-done | bytes 81952 | tf_op jit(solution)/shard_map/ppermute | solution.py:26
  99.8 0.9 collective-permute-start.30
  100.7 1.1 collective-permute-start.31
  101.8 2.2 %collective-permute-start.32 = (bf16[64,640]{1,0:T(8,128)(2,1)S(1)}, bf16[64,640]{1,0:T(8,128)(2,1)S(1)}, u32[]{:S(2)}, u32[]{:S(2)}) collective-permute-start(bf16[64,640]{1,0:T(8,128)(2,1)S(1)} %get-tuple-element.54), channel_id=1, source_target_pairs={{0,2},{1,3},{2,0},{3,1},{4,6},{5,7},{6,4},{7,5},{8,10},{9,11},{10,... | collective-permute-start | bytes 245768 | tf_op jit(solution)/shard_map/ppermute | solution.py:26
  104.0 0.7 collective-permute-done.30.refs_2_
  104.7 1.4 %collective-permute-done.31.refs_3_ = bf16[64,640]{1,0:T(8,128)(2,1)S(1)} collective-permute-done((bf16[64,640]{1,0:T(8,128)(2,1)S(1)}, bf16[64,640]{1,0:T(8,128)(2,1)S(1)}, u32[]{:S(2)}, u32[]{:S(2)}) %collective-permute-start.31) | collective-permute-done | bytes 81952 | tf_op jit(solution)/shard_map/ppermute | solution.py:26
  106.0 1.7 %collective-permute-done.32.refs_4_ = bf16[64,640]{1,0:T(8,128)(2,1)S(1)} collective-permute-done((bf16[64,640]{1,0:T(8,128)(2,1)S(1)}, bf16[64,640]{1,0:T(8,128)(2,1)S(1)}, u32[]{:S(2)}, u32[]{:S(2)}) %collective-permute-start.32) | collective-permute-done | bytes 81952 | tf_op jit(solution)/shard_map/ppermute | solution.py:26
  107.7 1.5 %shard_map.107 = bf16[64,2560]{1,0:T(8,128)(2,1)} custom-call(s32[32]{0:T(128)S(1)} %dynamic-slice_bitcast_fusion.refs_0_, bf16[64,640]{1,0:T(8,128)(2,1)S(1)} %get-tuple-element.51.refs_1_, bf16[64,640]{1,0:T(8,128)(2,1)S(1)} %collective-permute-done.30.refs_2_, bf16[64,640]{1,0:T(8,128)(2,1)S(1)} %collective-permute-done.31.refs_3_, ...), custom_call_target="tpu_custom_call" | custom-call | flops 1000 | bytes 1000 | tf_op jit(solution)/shard_map/pallas_call | solution.py:91
  (33 shorter events, 1.1 us)
Async XLA Ops:
  0.0 22.8 %collective-permute-start.1 = (bf16[64,5120]{1,0:T(8,128)(2,1)}, bf16[64,5120]{1,0:T(8,128)(2,1)S(1)}, u32[]{:S(2)}, u32[]{:S(2)}) collective-permute-start(bf16[64,5120]{1,0:T(8,128)(2,1)} %refs_0_.3), channel_id=1, source_target_pairs={{0,3},{1,2},{2,1},{3,0},{4,7},{5,6},{6,5},{7,4},{8,11},{9,10},{10,... | collective-permute-start | bytes 1966088 | tf_op jit(solution)/shard_map/ppermute | solution.py:26
  1.5 21.3 %collective-permute-start = (bf16[64,5120]{1,0:T(8,128)(2,1)}, bf16[64,5120]{1,0:T(8,128)(2,1)S(1)}, u32[]{:S(2)}, u32[]{:S(2)}) collective-permute-start(bf16[64,5120]{1,0:T(8,128)(2,1)} %refs_0_.3), channel_id=1, source_target_pairs={{0,1},{1,0},{2,3},{3,2},{4,5},{5,4},{6,7},{7,6},{8,9},{9,8},{10,11... | collective-permute-start | bytes 1966088 | tf_op jit(solution)/shard_map/ppermute | solution.py:26
  5.9 16.8 %collective-permute-start.3 = (bf16[32,5120]{1,0:T(8,128)(2,1)}, bf16[32,5120]{1,0:T(8,128)(2,1)S(1)}, u32[]{:S(2)}, u32[]{:S(2)}) collective-permute-start(bf16[32,5120]{1,0:T(8,128)(2,1)} %get-tuple-element.55), channel_id=1, source_target_pairs={{0,196},{1,197},{2,198},{3,199},{4,64},{5,65},{6,66},{7,67},{8,204... | collective-permute-start | bytes 983048 | tf_op jit(solution)/shard_map/ppermute | solution.py:26
  11.8 11.0 %collective-permute-start.2 = (bf16[32,5120]{1,0:T(8,128)(2,1)}, bf16[32,5120]{1,0:T(8,128)(2,1)S(1)}, u32[]{:S(2)}, u32[]{:S(2)}) collective-permute-start(bf16[32,5120]{1,0:T(8,128)(2,1)} %get-tuple-element.56), channel_id=1, source_target_pairs={{0,4},{1,5},{2,6},{3,7},{4,0},{5,1},{6,2},{7,3},{8,12},{9,13},{10,... | collective-permute-start | bytes 983048 | tf_op jit(solution)/shard_map/ppermute | solution.py:26
  22.7 18.0 %copy-start = (bf16[64,5120]{1,0:T(8,128)(2,1)S(1)}, bf16[64,5120]{1,0:T(8,128)(2,1)}, u32[]{:S(2)}) copy-start(bf16[64,5120]{1,0:T(8,128)(2,1)} %refs_0_.3) | copy-start | bytes 1966084
  22.9 10.7 %collective-permute-start.4 = (bf16[32,5120]{1,0:T(8,128)(2,1)S(1)}, bf16[32,5120]{1,0:T(8,128)(2,1)S(1)}, u32[]{:S(2)}, u32[]{:S(2)}) collective-permute-start(bf16[32,5120]{1,0:T(8,128)(2,1)S(1)} %get-tuple-element.33), channel_id=1, source_target_pairs={{0,3},{1,2},{2,1},{3,0},{4,7},{5,6},{6,5},{7,4},{8,11},{9,10},{10,... | collective-permute-start | bytes 983048 | tf_op jit(solution)/shard_map/ppermute | solution.py:26
  23.0 12.1 %collective-permute-start.5 = (bf16[32,5120]{1,0:T(8,128)(2,1)S(1)}, bf16[32,5120]{1,0:T(8,128)(2,1)S(1)}, u32[]{:S(2)}, u32[]{:S(2)}) collective-permute-start(bf16[32,5120]{1,0:T(8,128)(2,1)S(1)} %get-tuple-element.34), channel_id=1, source_target_pairs={{0,1},{1,0},{2,3},{3,2},{4,5},{5,4},{6,7},{7,6},{8,9},{9,8},{10,11... | collective-permute-start | bytes 983048 | tf_op jit(solution)/shard_map/ppermute | solution.py:26
  24.4 12.8 %collective-permute-start.8 = (bf16[32,5120]{1,0:T(8,128)(2,1)S(1)}, bf16[32,5120]{1,0:T(8,128)(2,1)S(1)}, u32[]{:S(2)}, u32[]{:S(2)}) collective-permute-start(bf16[32,5120]{1,0:T(8,128)(2,1)S(1)} %get-tuple-element.36), channel_id=1, source_target_pairs={{0,4},{1,5},{2,6},{3,7},{4,0},{5,1},{6,2},{7,3},{8,12},{9,13},{10,... | collective-permute-start | bytes 983048 | tf_op jit(solution)/shard_map/ppermute | solution.py:26
  26.4 12.2 %collective-permute-start.9 = (bf16[32,5120]{1,0:T(8,128)(2,1)S(1)}, bf16[32,5120]{1,0:T(8,128)(2,1)S(1)}, u32[]{:S(2)}, u32[]{:S(2)}) collective-permute-start(bf16[32,5120]{1,0:T(8,128)(2,1)S(1)} %get-tuple-element.37), channel_id=1, source_target_pairs={{0,196},{1,197},{2,198},{3,199},{4,64},{5,65},{6,66},{7,67},{8,204... | collective-permute-start | bytes 983048 | tf_op jit(solution)/shard_map/ppermute | solution.py:26
  28.3 10.4 %collective-permute-start.7 = (bf16[32,5120]{1,0:T(8,128)(2,1)S(1)}, bf16[32,5120]{1,0:T(8,128)(2,1)S(1)}, u32[]{:S(2)}, u32[]{:S(2)}) collective-permute-start(bf16[32,5120]{1,0:T(8,128)(2,1)S(1)} %get-tuple-element.35), channel_id=1, source_target_pairs={{0,3},{1,2},{2,1},{3,0},{4,7},{5,6},{6,5},{7,4},{8,11},{9,10},{10,... | collective-permute-start | bytes 983048 | tf_op jit(solution)/shard_map/ppermute | solution.py:26
  33.6 7.1 %collective-permute-start.6 = (bf16[32,5120]{1,0:T(8,128)(2,1)S(1)}, bf16[32,5120]{1,0:T(8,128)(2,1)S(1)}, u32[]{:S(2)}, u32[]{:S(2)}) collective-permute-start(bf16[32,5120]{1,0:T(8,128)(2,1)S(1)} %get-tuple-element.35), channel_id=1, source_target_pairs={{0,1},{1,0},{2,3},{3,2},{4,5},{5,4},{6,7},{7,6},{8,9},{9,8},{10,11... | collective-permute-start | bytes 983048 | tf_op jit(solution)/shard_map/ppermute | solution.py:26
  35.1 7.5 %collective-permute-start.10 = (bf16[32,5120]{1,0:T(8,128)(2,1)S(1)}, bf16[32,5120]{1,0:T(8,128)(2,1)S(1)}, u32[]{:S(2)}, u32[]{:S(2)}) collective-permute-start(bf16[32,5120]{1,0:T(8,128)(2,1)S(1)} %collective-permute-done.4.refs_3_), channel_id=1, source_target_pairs={{0,4},{1,5},{2,6},{3,7},{4,0},{5,1},{6,2},{7,3},{8,12},{9,13},{10,... | collective-permute-start | bytes 983048 | tf_op jit(solution)/shard_map/ppermute | solution.py:26
  37.1 8.3 %collective-permute-start.11 = (bf16[32,5120]{1,0:T(8,128)(2,1)S(1)}, bf16[32,5120]{1,0:T(8,128)(2,1)S(1)}, u32[]{:S(2)}, u32[]{:S(2)}) collective-permute-start(bf16[32,5120]{1,0:T(8,128)(2,1)S(1)} %collective-permute-done.5.refs_4_), channel_id=1, source_target_pairs={{0,196},{1,197},{2,198},{3,199},{4,64},{5,65},{6,66},{7,67},{8,204... | collective-permute-start | bytes 983048 | tf_op jit(solution)/shard_map/ppermute | solution.py:26
  38.6 8.7 %collective-permute-start.12 = (f32[1,128]{1,0:T(1,128)S(1)}, f32[1,128]{1,0:T(1,128)S(1)}, u32[]{:S(2)}, u32[]{:S(2)}) collective-permute-start(f32[1,128]{1,0:T(1,128)S(1)} %get-tuple-element.38), channel_id=1, source_target_pairs={{0,64},{1,65},{2,66},{3,67},{4,196},{5,197},{6,198},{7,199},{8,72}... | collective-permute-start | bytes 1544 | tf_op jit(solution)/shard_map/ppermute | solution.py:26
  49.2 2.2 %collective-permute-start.13 = (bf16[320,960]{1,0:T(8,128)(2,1)S(1)}, bf16[320,960]{1,0:T(8,128)(2,1)S(1)}, u32[]{:S(2)}, u32[]{:S(2)}) collective-permute-start(bf16[320,960]{1,0:T(8,128)(2,1)S(1)} %shard_map.96.refs_8_), channel_id=1, source_target_pairs={{0,8},{1,9},{2,10},{3,11},{4,12},{5,13},{6,14},{7,15},{8,0},{9,1},... | collective-permute-start | bytes 1843208 | tf_op jit(solution)/shard_map/ppermute | solution.py:26
  52.1 8.6 %collective-permute-start.14 = (bf16[80,960]{1,0:T(8,128)(2,1)S(1)}, bf16[80,960]{1,0:T(8,128)(2,1)S(1)}, u32[]{:S(2)}, u32[]{:S(2)}) collective-permute-start(bf16[80,960]{1,0:T(8,128)(2,1)S(1)} %get-tuple-element.41), channel_id=1, source_target_pairs={{0,32},{1,33},{2,34},{3,35},{4,36},{5,37},{6,38},{7,39},{8,40},{9,... | collective-permute-start | bytes 460808 | tf_op jit(solution)/shard_map/ppermute | solution.py:26
  55.4 8.7 %collective-permute-start.16 = (bf16[80,960]{1,0:T(8,128)(2,1)S(1)}, bf16[80,960]{1,0:T(8,128)(2,1)S(1)}, u32[]{:S(2)}, u32[]{:S(2)}) collective-permute-start(bf16[80,960]{1,0:T(8,128)(2,1)S(1)} %get-tuple-element.42), channel_id=1, source_target_pairs={{0,48},{1,49},{2,50},{3,51},{4,52},{5,53},{6,54},{7,55},{8,56},{9,... | collective-permute-start | bytes 460808 | tf_op jit(solution)/shard_map/ppermute | solution.py:26
  56.4 7.6 %collective-permute-start.15 = (bf16[80,960]{1,0:T(8,128)(2,1)S(1)}, bf16[80,960]{1,0:T(8,128)(2,1)S(1)}, u32[]{:S(2)}, u32[]{:S(2)}) collective-permute-start(bf16[80,960]{1,0:T(8,128)(2,1)S(1)} %get-tuple-element.39.refs_2_), channel_id=1, source_target_pairs={{0,16},{1,17},{2,18},{3,19},{4,20},{5,21},{6,22},{7,23},{8,24},{9,... | collective-permute-start | bytes 460808 | tf_op jit(solution)/shard_map/ppermute | solution.py:26
  64.1 7.9 %collective-permute-start.18 = (bf16[40,960]{1,0:T(8,128)(2,1)S(1)}, bf16[40,960]{1,0:T(8,128)(2,1)S(1)}, u32[]{:S(2)}, u32[]{:S(2)}) collective-permute-start(bf16[40,960]{1,0:T(8,128)(2,1)S(1)} %get-tuple-element.45), channel_id=1, source_target_pairs={{0,192},{1,193},{2,194},{3,195},{4,196},{5,197},{6,198},{7,199},{8... | collective-permute-start | bytes 230408 | tf_op jit(solution)/shard_map/ppermute | solution.py:26
  65.0 7.1 %collective-permute-start.17 = (bf16[40,960]{1,0:T(8,128)(2,1)S(1)}, bf16[40,960]{1,0:T(8,128)(2,1)S(1)}, u32[]{:S(2)}, u32[]{:S(2)}) collective-permute-start(bf16[40,960]{1,0:T(8,128)(2,1)S(1)} %get-tuple-element.43.refs_14_), channel_id=1, source_target_pairs={{0,64},{1,65},{2,66},{3,67},{4,68},{5,69},{6,70},{7,71},{8,72},{9,... | collective-permute-start | bytes 230408 | tf_op jit(solution)/shard_map/ppermute | solution.py:26
  72.1 6.7 %collective-permute-start.19 = (bf16[40,960]{1,0:T(8,128)(2,1)S(1)}, bf16[40,960]{1,0:T(8,128)(2,1)S(1)}, u32[]{:S(2)}, u32[]{:S(2)}) collective-permute-start(bf16[40,960]{1,0:T(8,128)(2,1)S(1)} %get-tuple-element.47), channel_id=1, source_target_pairs={{0,192},{1,193},{2,194},{3,195},{4,196},{5,197},{6,198},{7,199},{8... | collective-permute-start | bytes 230408 | tf_op jit(solution)/shard_map/ppermute | solution.py:26
  73.8 5.4 %collective-permute-start.20 = (bf16[40,960]{1,0:T(8,128)(2,1)S(1)}, bf16[40,960]{1,0:T(8,128)(2,1)S(1)}, u32[]{:S(2)}, u32[]{:S(2)}) collective-permute-start(bf16[40,960]{1,0:T(8,128)(2,1)S(1)} %get-tuple-element.48), channel_id=1, source_target_pairs={{0,64},{1,65},{2,66},{3,67},{4,68},{5,69},{6,70},{7,71},{8,72},{9,... | collective-permute-start | bytes 230408 | tf_op jit(solution)/shard_map/ppermute | solution.py:26
  80.1 8.5 %collective-permute-start.23 = (bf16[80,960]{1,0:T(8,128)(2,1)S(1)}, bf16[80,960]{1,0:T(8,128)(2,1)S(1)}, u32[]{:S(2)}, u32[]{:S(2)}) collective-permute-start(bf16[80,960]{1,0:T(8,128)(2,1)S(1)} %shard_map.103.refs_1_), channel_id=1, source_target_pairs={{0,32},{1,33},{2,34},{3,35},{4,36},{5,37},{6,38},{7,39},{8,40},{9,... | collective-permute-start | bytes 460808 | tf_op jit(solution)/shard_map/ppermute | solution.py:26
  83.3 7.8 %collective-permute-start.22 = (bf16[80,960]{1,0:T(8,128)(2,1)S(1)}, bf16[80,960]{1,0:T(8,128)(2,1)S(1)}, u32[]{:S(2)}, u32[]{:S(2)}) collective-permute-start(bf16[80,960]{1,0:T(8,128)(2,1)S(1)} %shard_map.103.refs_1_), channel_id=1, source_target_pairs={{0,48},{1,49},{2,50},{3,51},{4,52},{5,53},{6,54},{7,55},{8,56},{9,... | collective-permute-start | bytes 460808 | tf_op jit(solution)/shard_map/ppermute | solution.py:26
  84.3 7.0 %collective-permute-start.21 = (bf16[80,960]{1,0:T(8,128)(2,1)S(1)}, bf16[80,960]{1,0:T(8,128)(2,1)S(1)}, u32[]{:S(2)}, u32[]{:S(2)}) collective-permute-start(bf16[80,960]{1,0:T(8,128)(2,1)S(1)} %shard_map.103.refs_1_), channel_id=1, source_target_pairs={{0,16},{1,17},{2,18},{3,19},{4,20},{5,21},{6,22},{7,23},{8,24},{9,... | collective-permute-start | bytes 460808 | tf_op jit(solution)/shard_map/ppermute | solution.py:26
  85.3 6.3 %collective-permute-start.24 = (bf16[80,960]{1,0:T(8,128)(2,1)S(1)}, bf16[80,960]{1,0:T(8,128)(2,1)S(1)}, u32[]{:S(2)}, u32[]{:S(2)}) collective-permute-start(bf16[80,960]{1,0:T(8,128)(2,1)S(1)} %shard_map.103.refs_1_), channel_id=1, source_target_pairs={{0,8},{1,9},{2,10},{3,11},{4,12},{5,13},{6,14},{7,15},{8,0},{9,1},... | collective-permute-start | bytes 460808 | tf_op jit(solution)/shard_map/ppermute | solution.py:26
  88.6 3.1 %collective-permute-start.27 = (bf16[80,960]{1,0:T(8,128)(2,1)S(1)}, bf16[80,960]{1,0:T(8,128)(2,1)S(1)}, u32[]{:S(2)}, u32[]{:S(2)}) collective-permute-start(bf16[80,960]{1,0:T(8,128)(2,1)S(1)} %collective-permute-done.23.refs_4_), channel_id=1, source_target_pairs={{0,8},{1,9},{2,10},{3,11},{4,12},{5,13},{6,14},{7,15},{8,0},{9,1},... | collective-permute-start | bytes 460808 | tf_op jit(solution)/shard_map/ppermute | solution.py:26
  91.1 1.4 %collective-permute-start.26 = (bf16[80,960]{1,0:T(8,128)(2,1)S(1)}, bf16[80,960]{1,0:T(8,128)(2,1)S(1)}, u32[]{:S(2)}, u32[]{:S(2)}) collective-permute-start(bf16[80,960]{1,0:T(8,128)(2,1)S(1)} %collective-permute-done.22.refs_3_), channel_id=1, source_target_pairs={{0,8},{1,9},{2,10},{3,11},{4,12},{5,13},{6,14},{7,15},{8,0},{9,1},... | collective-permute-start | bytes 460808 | tf_op jit(solution)/shard_map/ppermute | solution.py:26
  91.3 1.4 %collective-permute-start.25 = (bf16[80,960]{1,0:T(8,128)(2,1)S(1)}, bf16[80,960]{1,0:T(8,128)(2,1)S(1)}, u32[]{:S(2)}, u32[]{:S(2)}) collective-permute-start(bf16[80,960]{1,0:T(8,128)(2,1)S(1)} %collective-permute-done.21.refs_2_), channel_id=1, source_target_pairs={{0,8},{1,9},{2,10},{3,11},{4,12},{5,13},{6,14},{7,15},{8,0},{9,1},... | collective-permute-start | bytes 460808 | tf_op jit(solution)/shard_map/ppermute | solution.py:26
  93.7 5.9 %collective-permute-start.29 = (bf16[64,640]{1,0:T(8,128)(2,1)S(1)}, bf16[64,640]{1,0:T(8,128)(2,1)S(1)}, u32[]{:S(2)}, u32[]{:S(2)}) collective-permute-start(bf16[64,640]{1,0:T(8,128)(2,1)S(1)} %get-tuple-element.50), channel_id=1, source_target_pairs={{0,196},{1,197},{2,198},{3,199},{4,64},{5,65},{6,66},{7,67},{8,204... | collective-permute-start | bytes 245768 | tf_op jit(solution)/shard_map/ppermute | solution.py:26
  95.1 4.6 %collective-permute-start.28 = (bf16[64,640]{1,0:T(8,128)(2,1)S(1)}, bf16[64,640]{1,0:T(8,128)(2,1)S(1)}, u32[]{:S(2)}, u32[]{:S(2)}) collective-permute-start(bf16[64,640]{1,0:T(8,128)(2,1)S(1)} %get-tuple-element.49.refs_9_), channel_id=1, source_target_pairs={{0,4},{1,5},{2,6},{3,7},{4,0},{5,1},{6,2},{7,3},{8,12},{9,13},{10,... | collective-permute-start | bytes 245768 | tf_op jit(solution)/shard_map/ppermute | solution.py:26
  99.8 4.9 %collective-permute-start.30 = (bf16[64,640]{1,0:T(8,128)(2,1)S(1)}, bf16[64,640]{1,0:T(8,128)(2,1)S(1)}, u32[]{:S(2)}, u32[]{:S(2)}) collective-permute-start(bf16[64,640]{1,0:T(8,128)(2,1)S(1)} %get-tuple-element.52), channel_id=1, source_target_pairs={{0,1},{1,0},{2,3},{3,2},{4,5},{5,4},{6,7},{7,6},{8,9},{9,8},{10,11... | collective-permute-start | bytes 245768 | tf_op jit(solution)/shard_map/ppermute | solution.py:26
  100.7 5.3 %collective-permute-start.31 = (bf16[64,640]{1,0:T(8,128)(2,1)S(1)}, bf16[64,640]{1,0:T(8,128)(2,1)S(1)}, u32[]{:S(2)}, u32[]{:S(2)}) collective-permute-start(bf16[64,640]{1,0:T(8,128)(2,1)S(1)} %get-tuple-element.53), channel_id=1, source_target_pairs={{0,3},{1,2},{2,1},{3,0},{4,7},{5,6},{6,5},{7,4},{8,11},{9,10},{10,... | collective-permute-start | bytes 245768 | tf_op jit(solution)/shard_map/ppermute | solution.py:26
  101.8 5.9 %collective-permute-start.32 = (bf16[64,640]{1,0:T(8,128)(2,1)S(1)}, bf16[64,640]{1,0:T(8,128)(2,1)S(1)}, u32[]{:S(2)}, u32[]{:S(2)}) collective-permute-start(bf16[64,640]{1,0:T(8,128)(2,1)S(1)} %get-tuple-element.54), channel_id=1, source_target_pairs={{0,2},{1,3},{2,0},{3,1},{4,6},{5,7},{6,4},{7,5},{8,10},{9,11},{10,... | collective-permute-start | bytes 245768 | tf_op jit(solution)/shard_map/ppermute | solution.py:26

commit v12 on v11

--- a/solution.py
+++ b/solution.py
@@ -152,11 +152,14 @@
     return call(functools.partial(project_kernel, cuts), like(shape), *tiles, weff, after=after)
 
 
-def grads_kernel(which, my, kv1, kv2, weight, moved, gate_t, up_t, down_t, out):
+def grads_kernel(which, planes, my, kv, weight, gate_t, up_t, down_t, *refs):
     half = pl.ds(pl.multiple_of(my[which], 16), 320)
-    weight = jnp.concatenate([weight[...], moved[...]], axis=1)
-    keys = jnp.concatenate([kv1[:320, :], kv2[:320, :]], axis=1)
-    values = jnp.concatenate([kv1[320:, :], kv2[320:, :]], axis=1)
+    out = refs[-1]
+    keys, values = kv[:320, :], kv[320:, :]
+    if planes:
+        weight = weight[:, :256]
+    else:
+        weight = jnp.concatenate([weight[:, 256:], refs[0][...]], axis=1)
     gate = jnp.dot(gate_t[half, :], keys, preferred_element_type=F32)
     upper = jnp.dot(up_t[half, :], keys, preferred_element_type=F32)
     sigma = jax.nn.sigmoid(gate)
@@ -169,7 +172,10 @@
     pairs = ((d_gate, keys), (d_upper, keys), (hidden, weighted))
     for i, (left, right) in enumerate(pairs):
         grad = lax.dot_general(left, right, BY_ROW, preferred_element_type=F32)
-        out[:, i * 320 : (i + 1) * 320] = grad.astype(out.dtype)
+        at = slice(i * 320, (i + 1) * 320)
+        if not planes:
+            grad += refs[1][:, at]
+        out[:, at] = grad.astype(out.dtype)
 
 
 def halves_kernel(my, own, got, to1, to2, to3, mine):
@@ -321,20 +327,17 @@
     weff = load(w_t, factor, 1, 2, after=(weight, *old_t))
     plane, others = gather(tokens, same_tokens, (weff,))
     kv1 = project(plane, PLANE, weff, after=others[2:6])
-    kv2 = project(others, OTHERS, weff, after=(kv1,))
-
-    grads = (my, kv1, kv2, weight, moved, *old_t)
-    sent = call(
-        functools.partial(grads_kernel, OTHER_HALF), like((320, 960)), *grads, scalars=1
-    )
+
+    def grads(which, planes, *args, dtype=F32, after=()):
+        kernel = functools.partial(grads_kernel, which, planes)
+        args = (my, args[0], weight, *old_t, *args[1:])
+        return call(kernel, like((320, 960), dtype), *args, scalars=1, after=after)
+
+    base_other, base_own = grads(OTHER_HALF, True, kv1), grads(OWN_HALF, True, kv1)
+    kv2 = project(others, OTHERS, weff, after=(kv1, base_other, base_own))
+    sent = grads(OTHER_HALF, False, kv2, moved, base_other, dtype=BF16)
     got = to_core(sent)
-    own = call(
-        functools.partial(grads_kernel, OWN_HALF),
-        like((320, 960), F32),
-        *grads,
-        scalars=1,
-        after=(sent,),
-    )
+    own = grads(OWN_HALF, False, kv2, moved, base_own, after=(sent,))
     to1, to2, to3, mine = call(
         halves_kernel, [like((80, 960))] * 3 + [like((80, 960), F32)], my, own, got, scalars=1
     )

time: 110 us -> 112 us (1.018)
  starting transfers between devices: 44.5 us -> 47.6 us
  waiting for transfers between devices: 34.1 us -> 31.2 us
  Pallas kernels: 20.5 us -> 22.5 us
    ppermute x33, starting transfers between devices: 44.5 us -> 47.6 us  [permute(): return lax.ppermute(value, AXES, pairs)]
    ppermute x33, waiting for transfers between devices: 34.1 us -> 31.2 us  [permute(): return lax.ppermute(value, AXES, pairs)]
    pallas_call x15 -> x17, Pallas kernels: 15.5 us -> 17.5 us  [call(): pl.pallas_call(run, out_shape=out_shape, in_specs=[SMEM] * scalars + [VME...]
  transfers between devices with their start and end apart: 33 -> 33, of which waited for: 19 -> 18; matrix products, arithmetic and copies ran while one was open for 8% -> 8% of each run, Pallas kernels for 13% -> 15%
where the time goes in v12:
time: 112 us
  starting transfers between devices  47.6 us (42%)
  waiting for transfers between devices  31.2 us (28%)
  Pallas kernels  22.5 us (20%)
  local copies, waits for them, and re-layouts  7.2 us (6%)
  other arithmetic  2.06 us (2%)
    ppermute x33, starting transfers between devices, permute(): return lax.ppermute(value, AXES, pairs)  47.6 us
    ppermute x33, waiting for transfers between devices, permute(): return lax.ppermute(value, AXES, pairs)  31.2 us
    pallas_call x17, Pallas kernels, call(): pl.pallas_call(run, out_shape=out_shape, in_specs=[SMEM] * scalars + [VME...  17.5 us
    pallas_call x2, Pallas kernels, load(): pl.pallas_call(run, out_shape=like((count, *w_t.shape[1:])), in_specs=[pl...  5 us
    unnamed x7, local copies, waits for them, and re-layouts  4.37 us
  transfers between devices with their start and end apart: 33, of which 18 were waited for; matrix products, arithmetic and copies ran while one was open for 8% of the time, Pallas kernels for 15%

profile of v12, /device:TPU:2, one launch (start us, length us, event | category | flops | bytes accessed | tf_op | source)
XLA Modules:
  0.0 111.5 jit_solution(12812151763504999332)
XLA Ops:
  0.0 1.5 %collective-permute-start.1 = (bf16[64,5120]{1,0:T(8,128)(2,1)}, bf16[64,5120]{1,0:T(8,128)(2,1)S(1)}, u32[]{:S(2)}, u32[]{:S(2)}) collective-permute-start(bf16[64,5120]{1,0:T(8,128)(2,1)} %refs_0_.3), channel_id=1, source_target_pairs={{0,3},{1,2},{2,1},{3,0},{4,7},{5,6},{6,5},{7,4},{8,11},{9,10},{10,... | collective-permute-start | bytes 1966088 | tf_op jit(solution)/shard_map/ppermute | solution.py:26
  1.5 1.8 %collective-permute-start = (bf16[64,5120]{1,0:T(8,128)(2,1)}, bf16[64,5120]{1,0:T(8,128)(2,1)S(1)}, u32[]{:S(2)}, u32[]{:S(2)}) collective-permute-start(bf16[64,5120]{1,0:T(8,128)(2,1)} %refs_0_.3), channel_id=1, source_target_pairs={{0,1},{1,0},{2,3},{3,2},{4,5},{5,4},{6,7},{7,6},{8,9},{9,8},{10,11... | collective-permute-start | bytes 1966088 | tf_op jit(solution)/shard_map/ppermute | solution.py:26
  3.3 0.7 dynamic-slice_bitcast_fusion.refs_0_
  4.0 1.9 %fusion = (bf16[32,5120]{1,0:T(8,128)(2,1)}, bf16[32,5120]{1,0:T(8,128)(2,1)}) fusion(bf16[64,5120]{1,0:T(8,128)(2,1)} %refs_0_.3), kind=kLoop, calls=%fused_computation.3 | loop fusion | bytes 1310720 | tf_op jit(solution)/shard_map/slice | solution.py:239
  5.9 5.9 %collective-permute-start.3 = (bf16[32,5120]{1,0:T(8,128)(2,1)}, bf16[32,5120]{1,0:T(8,128)(2,1)S(1)}, u32[]{:S(2)}, u32[]{:S(2)}) collective-permute-start(bf16[32,5120]{1,0:T(8,128)(2,1)} %get-tuple-element.55), channel_id=1, source_target_pairs={{0,196},{1,197},{2,198},{3,199},{4,64},{5,65},{6,66},{7,67},{8,204... | collective-permute-start | bytes 983048 | tf_op jit(solution)/shard_map/ppermute | solution.py:26
  12.4 0.6 broadcast.3
  13.0 1.4 %reduce.3 = s32[512]{0:T(512)S(1)} reduce(s32[512,1]{0,1:T(1,128)} %param.12, s32[]{:T(128)} %broadcast.3), dimensions={1}, to_apply=%param.12.reduce_sub_computation.3 | reduce | bytes 4100 | tf_op args[3]
  14.5 0.6 shard_map.91
  15.1 0.7 exponential_convert_fusion
  15.9 1.3 %copy.13 = bf16[1,320,640]{1,2,0:T(8,128)(2,1)S(1)} copy(bf16[1,320,640]{2,1,0:T(8,128)(2,1)} %param.14) | data formatting | bytes 819200 | tf_op args[5]
  17.2 1.3 %copy.14 = bf16[1,320,640]{1,2,0:T(8,128)(2,1)S(1)} copy(bf16[1,320,640]{2,1,0:T(8,128)(2,1)} %param.15) | data formatting | bytes 819200 | tf_op args[6]
  18.4 1.3 %copy.15 = bf16[1,320,640]{1,2,0:T(8,128)(2,1)S(1)} copy(bf16[1,320,640]{2,1,0:T(8,128)(2,1)} %param.16) | data formatting | bytes 819200 | tf_op args[7]
  19.7 3.0 %shard_map.92.refs_4_.refs_5_.refs_8_ = bf16[2,320,5120]{2,1,0:T(8,128)(2,1)S(1)} custom-call(bf16[3,320,5120]{2,1,0:T(8,128)(2,1)} %bitcast.34, bf16[3,1,5120]{2,1,0:T(2,128)(2,1)S(1)} %broadcast_in_dim_reshape.4.refs_1_, f32[1,384]{1,0:T(1,128)S(1)} %get-tuple-element.32.refs_2_, bf16[640,320]{1,0:T(8,128)(2,1)S(1)} %bitcast.16, ...), custom_call_target="tpu_custom_call" | custom-call | flops 1000 | bytes 1000 | tf_op jit(solution)/shard_map/pallas_call | solution.py:131
  23.0 1.4 %collective-permute-start.5 = (bf16[32,5120]{1,0:T(8,128)(2,1)S(1)}, bf16[32,5120]{1,0:T(8,128)(2,1)S(1)}, u32[]{:S(2)}, u32[]{:S(2)}) collective-permute-start(bf16[32,5120]{1,0:T(8,128)(2,1)S(1)} %get-tuple-element.34), channel_id=1, source_target_pairs={{0,1},{1,0},{2,3},{3,2},{4,5},{5,4},{6,7},{7,6},{8,9},{9,8},{10,11... | collective-permute-start | bytes 983048 | tf_op jit(solution)/shard_map/ppermute | solution.py:26
  24.4 2.0 %collective-permute-start.8 = (bf16[32,5120]{1,0:T(8,128)(2,1)S(1)}, bf16[32,5120]{1,0:T(8,128)(2,1)S(1)}, u32[]{:S(2)}, u32[]{:S(2)}) collective-permute-start(bf16[32,5120]{1,0:T(8,128)(2,1)S(1)} %get-tuple-element.36), channel_id=1, source_target_pairs={{0,4},{1,5},{2,6},{3,7},{4,0},{5,1},{6,2},{7,3},{8,12},{9,13},{10,... | collective-permute-start | bytes 983048 | tf_op jit(solution)/shard_map/ppermute | solution.py:26
  26.4 1.9 %collective-permute-start.9 = (bf16[32,5120]{1,0:T(8,128)(2,1)S(1)}, bf16[32,5120]{1,0:T(8,128)(2,1)S(1)}, u32[]{:S(2)}, u32[]{:S(2)}) collective-permute-start(bf16[32,5120]{1,0:T(8,128)(2,1)S(1)} %get-tuple-element.37), channel_id=1, source_target_pairs={{0,196},{1,197},{2,198},{3,199},{4,64},{5,65},{6,66},{7,67},{8,204... | collective-permute-start | bytes 983048 | tf_op jit(solution)/shard_map/ppermute | solution.py:26
  28.3 1.1 %collective-permute-start.7 = (bf16[32,5120]{1,0:T(8,128)(2,1)S(1)}, bf16[32,5120]{1,0:T(8,128)(2,1)S(1)}, u32[]{:S(2)}, u32[]{:S(2)}) collective-permute-start(bf16[32,5120]{1,0:T(8,128)(2,1)S(1)} %get-tuple-element.35), channel_id=1, source_target_pairs={{0,3},{1,2},{2,1},{3,0},{4,7},{5,6},{6,5},{7,4},{8,11},{9,10},{10,... | collective-permute-start | bytes 983048 | tf_op jit(solution)/shard_map/ppermute | solution.py:26
  29.4 4.2 %collective-permute-done.4.refs_3_ = bf16[32,5120]{1,0:T(8,128)(2,1)S(1)} collective-permute-done((bf16[32,5120]{1,0:T(8,128)(2,1)S(1)}, bf16[32,5120]{1,0:T(8,128)(2,1)S(1)}, u32[]{:S(2)}, u32[]{:S(2)}) %collective-permute-start.4) | collective-permute-done | bytes 327712 | tf_op jit(solution)/shard_map/ppermute | solution.py:26
  33.6 1.4 %collective-permute-start.6 = (bf16[32,5120]{1,0:T(8,128)(2,1)S(1)}, bf16[32,5120]{1,0:T(8,128)(2,1)S(1)}, u32[]{:S(2)}, u32[]{:S(2)}) collective-permute-start(bf16[32,5120]{1,0:T(8,128)(2,1)S(1)} %get-tuple-element.35), channel_id=1, source_target_pairs={{0,1},{1,0},{2,3},{3,2},{4,5},{5,4},{6,7},{7,6},{8,9},{9,8},{10,11... | collective-permute-start | bytes 983048 | tf_op jit(solution)/shard_map/ppermute | solution.py:26
  35.1 2.0 %collective-permute-start.10 = (bf16[32,5120]{1,0:T(8,128)(2,1)S(1)}, bf16[32,5120]{1,0:T(8,128)(2,1)S(1)}, u32[]{:S(2)}, u32[]{:S(2)}) collective-permute-start(bf16[32,5120]{1,0:T(8,128)(2,1)S(1)} %collective-permute-done.4.refs_3_), channel_id=1, source_target_pairs={{0,4},{1,5},{2,6},{3,7},{4,0},{5,1},{6,2},{7,3},{8,12},{9,13},{10,... | collective-permute-start | bytes 983048 | tf_op jit(solution)/shard_map/ppermute | solution.py:26
  37.1 1.5 %collective-permute-start.11 = (bf16[32,5120]{1,0:T(8,128)(2,1)S(1)}, bf16[32,5120]{1,0:T(8,128)(2,1)S(1)}, u32[]{:S(2)}, u32[]{:S(2)}) collective-permute-start(bf16[32,5120]{1,0:T(8,128)(2,1)S(1)} %collective-permute-done.5.refs_4_), channel_id=1, source_target_pairs={{0,196},{1,197},{2,198},{3,199},{4,64},{5,65},{6,66},{7,67},{8,204... | collective-permute-start | bytes 983048 | tf_op jit(solution)/shard_map/ppermute | solution.py:26
  38.7 2.0 %collective-permute-done.6.refs_6_.refs_2_.refs_7_ = bf16[32,5120]{1,0:T(8,128)(2,1)S(1)} collective-permute-done((bf16[32,5120]{1,0:T(8,128)(2,1)S(1)}, bf16[32,5120]{1,0:T(8,128)(2,1)S(1)}, u32[]{:S(2)}, u32[]{:S(2)}) %collective-permute-start.6) | collective-permute-done | bytes 327712 | tf_op jit(solution)/shard_map/ppermute | solution.py:26
  40.7 1.9 %shard_map.94.refs_1_.refs_9_ = bf16[640,256]{1,0:T(8,128)(2,1)S(1)} custom-call(bf16[64,5120]{1,0:T(8,128)(2,1)S(1)} %copy-done, bf16[64,5120]{1,0:T(8,128)(2,1)S(1)} %collective-permute-done.refs_0_.refs_1_, bf16[64,5120]{1,0:T(8,128)(2,1)S(1)} %collective-permute-done.1.refs_1_.refs_2_, bf16[32,5120]{1,0:T(8,128)(2,1)S(1)} %collective-permute-done.4.refs_3_, ...), custom_call_target="tpu_custom_call" | custom-call | flops 1000 | bytes 1000 | tf_op jit(solution)/shard_map/pallas_call | solution.py:91
  42.6 1.4 %shard_map.96.refs_11_.refs_7_ = f32[320,960]{1,0:T(8,128)S(1)} custom-call(s32[32]{0:T(128)S(1)} %dynamic-slice_bitcast_fusion.refs_0_, bf16[640,256]{1,0:T(8,128)(2,1)S(1)} %shard_map.94.refs_1_.refs_9_, f32[1,384]{1,0:T(1,128)S(1)} %get-tuple-element.32.refs_2_, bf16[640,320]{1,0:T(8,128)(2,1)S(1)} %bitcast.17, bf16[640,320]{1,0:T(8,128)(2,1)S(1)} %bitcast.23, ...), custom_call_target="tpu_custom_call" | custom-call | flops 1000 | bytes 1000 | tf_op jit(solution)/shard_map/pallas_call | solution.py:91
  44.1 1.5 %shard_map.95.refs_10_.refs_7_ = f32[320,960]{1,0:T(8,128)S(1)} custom-call(s32[32]{0:T(128)S(1)} %dynamic-slice_bitcast_fusion.refs_0_, bf16[640,256]{1,0:T(8,128)(2,1)S(1)} %shard_map.94.refs_1_.refs_9_, f32[1,384]{1,0:T(1,128)S(1)} %get-tuple-element.32.refs_2_, bf16[640,320]{1,0:T(8,128)(2,1)S(1)} %bitcast.18, bf16[640,320]{1,0:T(8,128)(2,1)S(1)} %bitcast.24, ...), custom_call_target="tpu_custom_call" | custom-call | flops 1000 | bytes 1000 | tf_op jit(solution)/shard_map/pallas_call | solution.py:91
  45.6 1.9 %shard_map.97.refs_1_ = bf16[640,256]{1,0:T(8,128)(2,1)S(1)} custom-call(bf16[32,5120]{1,0:T(8,128)(2,1)S(1)} %collective-permute-done.2.refs_2_.refs_0_.refs_5_, bf16[32,5120]{1,0:T(8,128)(2,1)S(1)} %collective-permute-done.3.refs_3_.refs_1_.refs_6_, bf16[32,5120]{1,0:T(8,128)(2,1)S(1)} %collective-permute-done.6.refs_6_.refs_2_.refs_7_, ...), custom_call_target="tpu_custom_call" | custom-call | flops 1000 | bytes 1000 | tf_op jit(solution)/shard_map/pallas_call | solution.py:91
  47.5 1.5 %shard_map.98.refs_8_ = bf16[320,960]{1,0:T(8,128)(2,1)S(1)} custom-call(s32[32]{0:T(128)S(1)} %dynamic-slice_bitcast_fusion.refs_0_, bf16[640,256]{1,0:T(8,128)(2,1)S(1)} %shard_map.97.refs_1_, f32[1,384]{1,0:T(1,128)S(1)} %get-tuple-element.32.refs_2_, bf16[640,320]{1,0:T(8,128)(2,1)S(1)} %bitcast.19, bf16[640,320]{1,0:T(8,128)(2,1)S(1)} %bitcast.25, ...), custom_call_target="tpu_custom_call" | custom-call | flops 1000 | bytes 1000 | tf_op jit(solution)/shard_map/pallas_call | solution.py:91
  49.0 1.5 %shard_map.99.refs_1_ = f32[320,960]{1,0:T(8,128)S(1)} custom-call(s32[32]{0:T(128)S(1)} %dynamic-slice_bitcast_fusion.refs_0_, bf16[640,256]{1,0:T(8,128)(2,1)S(1)} %shard_map.97.refs_1_, f32[1,384]{1,0:T(1,128)S(1)} %get-tuple-element.32.refs_2_, bf16[640,320]{1,0:T(8,128)(2,1)S(1)} %bitcast.20, bf16[640,320]{1,0:T(8,128)(2,1)S(1)} %bitcast.26, ...), custom_call_target="tpu_custom_call" | custom-call | flops 1000 | bytes 1000 | tf_op jit(solution)/shard_map/pallas_call | solution.py:91
  50.5 0.6 collective-permute-done.13.refs_2_
  51.1 0.7 shard_map.100
  51.8 3.3 %collective-permute-start.14 = (bf16[80,960]{1,0:T(8,128)(2,1)S(1)}, bf16[80,960]{1,0:T(8,128)(2,1)S(1)}, u32[]{:S(2)}, u32[]{:S(2)}) collective-permute-start(bf16[80,960]{1,0:T(8,128)(2,1)S(1)} %get-tuple-element.41), channel_id=1, source_target_pairs={{0,32},{1,33},{2,34},{3,35},{4,36},{5,37},{6,38},{7,39},{8,40},{9,... | collective-permute-start | bytes 460808 | tf_op jit(solution)/shard_map/ppermute | solution.py:26
  55.1 1.1 collective-permute-start.16
  56.2 1.0 collective-permute-start.15
  57.1 2.0 %shard_map.101.refs_4_.refs_13_ = bf16[1,320,5120]{2,1,0:T(8,128)(2,1)S(1)} custom-call(bf16[3,320,5120]{2,1,0:T(8,128)(2,1)} %bitcast.35, bf16[3,1,5120]{2,1,0:T(2,128)(2,1)S(1)} %broadcast_in_dim_reshape.4.refs_1_, bf16[80,960]{1,0:T(8,128)(2,1)S(1)} %get-tuple-element.39.refs_2_), custom_call_target="tpu_custom_call" | custom-call | flops 1000 | bytes 1000 | tf_op jit(solution)/shard_map/pallas_call | solution.py:131
  59.1 1.3 %collective-permute-done.14.refs_1_ = bf16[80,960]{1,0:T(8,128)(2,1)S(1)} collective-permute-done((bf16[80,960]{1,0:T(8,128)(2,1)S(1)}, bf16[80,960]{1,0:T(8,128)(2,1)S(1)}, u32[]{:S(2)}, u32[]{:S(2)}) %collective-permute-start.14) | collective-permute-done | bytes 153632 | tf_op jit(solution)/shard_map/ppermute | solution.py:26
  60.4 3.1 %collective-permute-done.16.refs_3_ = bf16[80,960]{1,0:T(8,128)(2,1)S(1)} collective-permute-done((bf16[80,960]{1,0:T(8,128)(2,1)S(1)}, bf16[80,960]{1,0:T(8,128)(2,1)S(1)}, u32[]{:S(2)}, u32[]{:S(2)}) %collective-permute-start.16) | collective-permute-done | bytes 153632 | tf_op jit(solution)/shard_map/ppermute | solution.py:26
  63.6 2.5 %collective-permute-start.18 = (bf16[40,960]{1,0:T(8,128)(2,1)S(1)}, bf16[40,960]{1,0:T(8,128)(2,1)S(1)}, u32[]{:S(2)}, u32[]{:S(2)}) collective-permute-start(bf16[40,960]{1,0:T(8,128)(2,1)S(1)} %get-tuple-element.45), channel_id=1, source_target_pairs={{0,192},{1,193},{2,194},{3,195},{4,196},{5,197},{6,198},{7,199},{8... | collective-permute-start | bytes 230408 | tf_op jit(solution)/shard_map/ppermute | solution.py:26
  66.1 1.5 %collective-permute-start.17 = (bf16[40,960]{1,0:T(8,128)(2,1)S(1)}, bf16[40,960]{1,0:T(8,128)(2,1)S(1)}, u32[]{:S(2)}, u32[]{:S(2)}) collective-permute-start(bf16[40,960]{1,0:T(8,128)(2,1)S(1)} %get-tuple-element.43.refs_14_), channel_id=1, source_target_pairs={{0,64},{1,65},{2,66},{3,67},{4,68},{5,69},{6,70},{7,71},{8,72},{9,... | collective-permute-start | bytes 230408 | tf_op jit(solution)/shard_map/ppermute | solution.py:26
  67.6 1.9 %shard_map.103.refs_3_.refs_0_ = bf16[320,512]{1,0:T(8,128)(2,1)S(1)} custom-call(bf16[64,5120]{1,0:T(8,128)(2,1)S(1)} %copy-done, bf16[64,5120]{1,0:T(8,128)(2,1)S(1)} %collective-permute-done.refs_0_.refs_1_, bf16[64,5120]{1,0:T(8,128)(2,1)S(1)} %collective-permute-done.1.refs_1_.refs_2_, bf16[32,5120]{1,0:T(8,128)(2,1)S(1)} %collective-permute-done.4.refs_3_, ...), custom_call_target="tpu_custom_call" | custom-call | flops 1000 | bytes 1000 | tf_op jit(solution)/shard_map/pallas_call | solution.py:91
  69.5 0.7 collective-permute-done.18.refs_2_
  70.3 1.8 %collective-permute-done.17.refs_1_ = bf16[40,960]{1,0:T(8,128)(2,1)S(1)} collective-permute-done((bf16[40,960]{1,0:T(8,128)(2,1)S(1)}, bf16[40,960]{1,0:T(8,128)(2,1)S(1)}, u32[]{:S(2)}, u32[]{:S(2)}) %collective-permute-start.17) | collective-permute-done | bytes 76832 | tf_op jit(solution)/shard_map/ppermute | solution.py:26
  72.1 2.1 %collective-permute-start.19 = (bf16[40,960]{1,0:T(8,128)(2,1)S(1)}, bf16[40,960]{1,0:T(8,128)(2,1)S(1)}, u32[]{:S(2)}, u32[]{:S(2)}) collective-permute-start(bf16[40,960]{1,0:T(8,128)(2,1)S(1)} %get-tuple-element.47), channel_id=1, source_target_pairs={{0,192},{1,193},{2,194},{3,195},{4,196},{5,197},{6,198},{7,199},{8... | collective-permute-start | bytes 230408 | tf_op jit(solution)/shard_map/ppermute | solution.py:26
  74.2 2.4 %collective-permute-start.20 = (bf16[40,960]{1,0:T(8,128)(2,1)S(1)}, bf16[40,960]{1,0:T(8,128)(2,1)S(1)}, u32[]{:S(2)}, u32[]{:S(2)}) collective-permute-start(bf16[40,960]{1,0:T(8,128)(2,1)S(1)} %get-tuple-element.48), channel_id=1, source_target_pairs={{0,64},{1,65},{2,66},{3,67},{4,68},{5,69},{6,70},{7,71},{8,72},{9,... | collective-permute-start | bytes 230408 | tf_op jit(solution)/shard_map/ppermute | solution.py:26
  76.6 2.7 %collective-permute-done.19.refs_2_ = bf16[40,960]{1,0:T(8,128)(2,1)S(1)} collective-permute-done((bf16[40,960]{1,0:T(8,128)(2,1)S(1)}, bf16[40,960]{1,0:T(8,128)(2,1)S(1)}, u32[]{:S(2)}, u32[]{:S(2)}) %collective-permute-start.19) | collective-permute-done | bytes 76832 | tf_op jit(solution)/shard_map/ppermute | solution.py:26
  79.5 0.9 shard_map.105.refs_1_
  80.4 3.8 %collective-permute-start.23 = (bf16[80,960]{1,0:T(8,128)(2,1)S(1)}, bf16[80,960]{1,0:T(8,128)(2,1)S(1)}, u32[]{:S(2)}, u32[]{:S(2)}) collective-permute-start(bf16[80,960]{1,0:T(8,128)(2,1)S(1)} %shard_map.105.refs_1_), channel_id=1, source_target_pairs={{0,32},{1,33},{2,34},{3,35},{4,36},{5,37},{6,38},{7,39},{8,40},{9,... | collective-permute-start | bytes 460808 | tf_op jit(solution)/shard_map/ppermute | solution.py:26
  84.3 1.3 %collective-permute-start.22 = (bf16[80,960]{1,0:T(8,128)(2,1)S(1)}, bf16[80,960]{1,0:T(8,128)(2,1)S(1)}, u32[]{:S(2)}, u32[]{:S(2)}) collective-permute-start(bf16[80,960]{1,0:T(8,128)(2,1)S(1)} %shard_map.105.refs_1_), channel_id=1, source_target_pairs={{0,48},{1,49},{2,50},{3,51},{4,52},{5,53},{6,54},{7,55},{8,56},{9,... | collective-permute-start | bytes 460808 | tf_op jit(solution)/shard_map/ppermute | solution.py:26
  85.5 0.7 collective-permute-start.21
  86.3 2.0 %collective-permute-done.23.refs_4_ = bf16[80,960]{1,0:T(8,128)(2,1)S(1)} collective-permute-done((bf16[80,960]{1,0:T(8,128)(2,1)S(1)}, bf16[80,960]{1,0:T(8,128)(2,1)S(1)}, u32[]{:S(2)}, u32[]{:S(2)}) %collective-permute-start.23) | collective-permute-done | bytes 153632 | tf_op jit(solution)/shard_map/ppermute | solution.py:26
  88.3 1.7 %collective-permute-done.22.refs_3_ = bf16[80,960]{1,0:T(8,128)(2,1)S(1)} collective-permute-done((bf16[80,960]{1,0:T(8,128)(2,1)S(1)}, bf16[80,960]{1,0:T(8,128)(2,1)S(1)}, u32[]{:S(2)}, u32[]{:S(2)}) %collective-permute-start.22) | collective-permute-done | bytes 153632 | tf_op jit(solution)/shard_map/ppermute | solution.py:26
  90.0 2.1 %collective-permute-done.21.refs_2_ = bf16[80,960]{1,0:T(8,128)(2,1)S(1)} collective-permute-done((bf16[80,960]{1,0:T(8,128)(2,1)S(1)}, bf16[80,960]{1,0:T(8,128)(2,1)S(1)}, u32[]{:S(2)}, u32[]{:S(2)}) %collective-permute-start.21) | collective-permute-done | bytes 153632 | tf_op jit(solution)/shard_map/ppermute | solution.py:26
  92.1 1.4 %collective-permute-done.25.refs_6_ = bf16[80,960]{1,0:T(8,128)(2,1)S(1)} collective-permute-done((bf16[80,960]{1,0:T(8,128)(2,1)S(1)}, bf16[80,960]{1,0:T(8,128)(2,1)S(1)}, u32[]{:S(2)}, u32[]{:S(2)}) %collective-permute-start.25) | collective-permute-done | bytes 153632 | tf_op jit(solution)/shard_map/ppermute | solution.py:26
  93.5 1.0 shard_map.106
  94.4 2.6 %collective-permute-start.29 = (bf16[64,640]{1,0:T(8,128)(2,1)S(1)}, bf16[64,640]{1,0:T(8,128)(2,1)S(1)}, u32[]{:S(2)}, u32[]{:S(2)}) collective-permute-start(bf16[64,640]{1,0:T(8,128)(2,1)S(1)} %get-tuple-element.50), channel_id=1, source_target_pairs={{0,196},{1,197},{2,198},{3,199},{4,64},{5,65},{6,66},{7,67},{8,204... | collective-permute-start | bytes 245768 | tf_op jit(solution)/shard_map/ppermute | solution.py:26
  97.0 0.4 collective-permute-start.28
  97.4 1.0 shard_map.107.refs_0_
  98.4 1.8 %collective-permute-done.29.refs_2_ = bf16[64,640]{1,0:T(8,128)(2,1)S(1)} collective-permute-done((bf16[64,640]{1,0:T(8,128)(2,1)S(1)}, bf16[64,640]{1,0:T(8,128)(2,1)S(1)}, u32[]{:S(2)}, u32[]{:S(2)}) %collective-permute-start.29) | collective-permute-done | bytes 81952 | tf_op jit(solution)/shard_map/ppermute | solution.py:26
  100.2 1.2 %collective-permute-done.28.refs_1_ = bf16[64,640]{1,0:T(8,128)(2,1)S(1)} collective-permute-done((bf16[64,640]{1,0:T(8,128)(2,1)S(1)}, bf16[64,640]{1,0:T(8,128)(2,1)S(1)}, u32[]{:S(2)}, u32[]{:S(2)}) %collective-permute-start.28) | collective-permute-done | bytes 81952 | tf_op jit(solution)/shard_map/ppermute | solution.py:26
  101.6 2.0 %collective-permute-start.30 = (bf16[64,640]{1,0:T(8,128)(2,1)S(1)}, bf16[64,640]{1,0:T(8,128)(2,1)S(1)}, u32[]{:S(2)}, u32[]{:S(2)}) collective-permute-start(bf16[64,640]{1,0:T(8,128)(2,1)S(1)} %get-tuple-element.52), channel_id=1, source_target_pairs={{0,1},{1,0},{2,3},{3,2},{4,5},{5,4},{6,7},{7,6},{8,9},{9,8},{10,11... | collective-permute-start | bytes 245768 | tf_op jit(solution)/shard_map/ppermute | solution.py:26
  103.6 0.4 collective-permute-start.31
  104.0 1.8 %collective-permute-start.32 = (bf16[64,640]{1,0:T(8,128)(2,1)S(1)}, bf16[64,640]{1,0:T(8,128)(2,1)S(1)}, u32[]{:S(2)}, u32[]{:S(2)}) collective-permute-start(bf16[64,640]{1,0:T(8,128)(2,1)S(1)} %get-tuple-element.54), channel_id=1, source_target_pairs={{0,2},{1,3},{2,0},{3,1},{4,6},{5,7},{6,4},{7,5},{8,10},{9,11},{10,... | collective-permute-start | bytes 245768 | tf_op jit(solution)/shard_map/ppermute | solution.py:26
  106.1 2.2 %collective-permute-done.31.refs_3_ = bf16[64,640]{1,0:T(8,128)(2,1)S(1)} collective-permute-done((bf16[64,640]{1,0:T(8,128)(2,1)S(1)}, bf16[64,640]{1,0:T(8,128)(2,1)S(1)}, u32[]{:S(2)}, u32[]{:S(2)}) %collective-permute-start.31) | collective-permute-done | bytes 81952 | tf_op jit(solution)/shard_map/ppermute | solution.py:26
  108.3 1.6 %collective-permute-done.32.refs_4_ = bf16[64,640]{1,0:T(8,128)(2,1)S(1)} collective-permute-done((bf16[64,640]{1,0:T(8,128)(2,1)S(1)}, bf16[64,640]{1,0:T(8,128)(2,1)S(1)}, u32[]{:S(2)}, u32[]{:S(2)}) %collective-permute-start.32) | collective-permute-done | bytes 81952 | tf_op jit(solution)/shard_map/ppermute | solution.py:26
  110.0 1.5 %shard_map.109 = bf16[64,2560]{1,0:T(8,128)(2,1)} custom-call(s32[32]{0:T(128)S(1)} %dynamic-slice_bitcast_fusion.refs_0_, bf16[64,640]{1,0:T(8,128)(2,1)S(1)} %get-tuple-element.51.refs_1_, bf16[64,640]{1,0:T(8,128)(2,1)S(1)} %collective-permute-done.30.refs_2_, bf16[64,640]{1,0:T(8,128)(2,1)S(1)} %collective-permute-done.31.refs_3_, ...), custom_call_target="tpu_custom_call" | custom-call | flops 1000 | bytes 1000 | tf_op jit(solution)/shard_map/pallas_call | solution.py:91
  (35 shorter events, 1.4 us)
Async XLA Ops:
  0.0 22.8 %collective-permute-start.1 = (bf16[64,5120]{1,0:T(8,128)(2,1)}, bf16[64,5120]{1,0:T(8,128)(2,1)S(1)}, u32[]{:S(2)}, u32[]{:S(2)}) collective-permute-start(bf16[64,5120]{1,0:T(8,128)(2,1)} %refs_0_.3), channel_id=1, source_target_pairs={{0,3},{1,2},{2,1},{3,0},{4,7},{5,6},{6,5},{7,4},{8,11},{9,10},{10,... | collective-permute-start | bytes 1966088 | tf_op jit(solution)/shard_map/ppermute | solution.py:26
  1.5 21.3 %collective-permute-start = (bf16[64,5120]{1,0:T(8,128)(2,1)}, bf16[64,5120]{1,0:T(8,128)(2,1)S(1)}, u32[]{:S(2)}, u32[]{:S(2)}) collective-permute-start(bf16[64,5120]{1,0:T(8,128)(2,1)} %refs_0_.3), channel_id=1, source_target_pairs={{0,1},{1,0},{2,3},{3,2},{4,5},{5,4},{6,7},{7,6},{8,9},{9,8},{10,11... | collective-permute-start | bytes 1966088 | tf_op jit(solution)/shard_map/ppermute | solution.py:26
  5.9 16.8 %collective-permute-start.3 = (bf16[32,5120]{1,0:T(8,128)(2,1)}, bf16[32,5120]{1,0:T(8,128)(2,1)S(1)}, u32[]{:S(2)}, u32[]{:S(2)}) collective-permute-start(bf16[32,5120]{1,0:T(8,128)(2,1)} %get-tuple-element.55), channel_id=1, source_target_pairs={{0,196},{1,197},{2,198},{3,199},{4,64},{5,65},{6,66},{7,67},{8,204... | collective-permute-start | bytes 983048 | tf_op jit(solution)/shard_map/ppermute | solution.py:26
  11.8 11.0 %collective-permute-start.2 = (bf16[32,5120]{1,0:T(8,128)(2,1)}, bf16[32,5120]{1,0:T(8,128)(2,1)S(1)}, u32[]{:S(2)}, u32[]{:S(2)}) collective-permute-start(bf16[32,5120]{1,0:T(8,128)(2,1)} %get-tuple-element.56), channel_id=1, source_target_pairs={{0,4},{1,5},{2,6},{3,7},{4,0},{5,1},{6,2},{7,3},{8,12},{9,13},{10,... | collective-permute-start | bytes 983048 | tf_op jit(solution)/shard_map/ppermute | solution.py:26
  22.7 18.0 %copy-start = (bf16[64,5120]{1,0:T(8,128)(2,1)S(1)}, bf16[64,5120]{1,0:T(8,128)(2,1)}, u32[]{:S(2)}) copy-start(bf16[64,5120]{1,0:T(8,128)(2,1)} %refs_0_.3) | copy-start | bytes 1966084
  22.9 10.7 %collective-permute-start.4 = (bf16[32,5120]{1,0:T(8,128)(2,1)S(1)}, bf16[32,5120]{1,0:T(8,128)(2,1)S(1)}, u32[]{:S(2)}, u32[]{:S(2)}) collective-permute-start(bf16[32,5120]{1,0:T(8,128)(2,1)S(1)} %get-tuple-element.33), channel_id=1, source_target_pairs={{0,3},{1,2},{2,1},{3,0},{4,7},{5,6},{6,5},{7,4},{8,11},{9,10},{10,... | collective-permute-start | bytes 983048 | tf_op jit(solution)/shard_map/ppermute | solution.py:26
  23.0 12.1 %collective-permute-start.5 = (bf16[32,5120]{1,0:T(8,128)(2,1)S(1)}, bf16[32,5120]{1,0:T(8,128)(2,1)S(1)}, u32[]{:S(2)}, u32[]{:S(2)}) collective-permute-start(bf16[32,5120]{1,0:T(8,128)(2,1)S(1)} %get-tuple-element.34), channel_id=1, source_target_pairs={{0,1},{1,0},{2,3},{3,2},{4,5},{5,4},{6,7},{7,6},{8,9},{9,8},{10,11... | collective-permute-start | bytes 983048 | tf_op jit(solution)/shard_map/ppermute | solution.py:26
  24.4 12.8 %collective-permute-start.8 = (bf16[32,5120]{1,0:T(8,128)(2,1)S(1)}, bf16[32,5120]{1,0:T(8,128)(2,1)S(1)}, u32[]{:S(2)}, u32[]{:S(2)}) collective-permute-start(bf16[32,5120]{1,0:T(8,128)(2,1)S(1)} %get-tuple-element.36), channel_id=1, source_target_pairs={{0,4},{1,5},{2,6},{3,7},{4,0},{5,1},{6,2},{7,3},{8,12},{9,13},{10,... | collective-permute-start | bytes 983048 | tf_op jit(solution)/shard_map/ppermute | solution.py:26
  26.4 12.2 %collective-permute-start.9 = (bf16[32,5120]{1,0:T(8,128)(2,1)S(1)}, bf16[32,5120]{1,0:T(8,128)(2,1)S(1)}, u32[]{:S(2)}, u32[]{:S(2)}) collective-permute-start(bf16[32,5120]{1,0:T(8,128)(2,1)S(1)} %get-tuple-element.37), channel_id=1, source_target_pairs={{0,196},{1,197},{2,198},{3,199},{4,64},{5,65},{6,66},{7,67},{8,204... | collective-permute-start | bytes 983048 | tf_op jit(solution)/shard_map/ppermute | solution.py:26
  28.3 10.4 %collective-permute-start.7 = (bf16[32,5120]{1,0:T(8,128)(2,1)S(1)}, bf16[32,5120]{1,0:T(8,128)(2,1)S(1)}, u32[]{:S(2)}, u32[]{:S(2)}) collective-permute-start(bf16[32,5120]{1,0:T(8,128)(2,1)S(1)} %get-tuple-element.35), channel_id=1, source_target_pairs={{0,3},{1,2},{2,1},{3,0},{4,7},{5,6},{6,5},{7,4},{8,11},{9,10},{10,... | collective-permute-start | bytes 983048 | tf_op jit(solution)/shard_map/ppermute | solution.py:26
  33.6 7.1 %collective-permute-start.6 = (bf16[32,5120]{1,0:T(8,128)(2,1)S(1)}, bf16[32,5120]{1,0:T(8,128)(2,1)S(1)}, u32[]{:S(2)}, u32[]{:S(2)}) collective-permute-start(bf16[32,5120]{1,0:T(8,128)(2,1)S(1)} %get-tuple-element.35), channel_id=1, source_target_pairs={{0,1},{1,0},{2,3},{3,2},{4,5},{5,4},{6,7},{7,6},{8,9},{9,8},{10,11... | collective-permute-start | bytes 983048 | tf_op jit(solution)/shard_map/ppermute | solution.py:26
  35.1 10.5 %collective-permute-start.10 = (bf16[32,5120]{1,0:T(8,128)(2,1)S(1)}, bf16[32,5120]{1,0:T(8,128)(2,1)S(1)}, u32[]{:S(2)}, u32[]{:S(2)}) collective-permute-start(bf16[32,5120]{1,0:T(8,128)(2,1)S(1)} %collective-permute-done.4.refs_3_), channel_id=1, source_target_pairs={{0,4},{1,5},{2,6},{3,7},{4,0},{5,1},{6,2},{7,3},{8,12},{9,13},{10,... | collective-permute-start | bytes 983048 | tf_op jit(solution)/shard_map/ppermute | solution.py:26
  37.1 8.4 %collective-permute-start.11 = (bf16[32,5120]{1,0:T(8,128)(2,1)S(1)}, bf16[32,5120]{1,0:T(8,128)(2,1)S(1)}, u32[]{:S(2)}, u32[]{:S(2)}) collective-permute-start(bf16[32,5120]{1,0:T(8,128)(2,1)S(1)} %collective-permute-done.5.refs_4_), channel_id=1, source_target_pairs={{0,196},{1,197},{2,198},{3,199},{4,64},{5,65},{6,66},{7,67},{8,204... | collective-permute-start | bytes 983048 | tf_op jit(solution)/shard_map/ppermute | solution.py:26
  38.6 8.8 %collective-permute-start.12 = (f32[1,128]{1,0:T(1,128)S(1)}, f32[1,128]{1,0:T(1,128)S(1)}, u32[]{:S(2)}, u32[]{:S(2)}) collective-permute-start(f32[1,128]{1,0:T(1,128)S(1)} %get-tuple-element.38), channel_id=1, source_target_pairs={{0,64},{1,65},{2,66},{3,67},{4,196},{5,197},{6,198},{7,199},{8,72}... | collective-permute-start | bytes 1544 | tf_op jit(solution)/shard_map/ppermute | solution.py:26
  48.9 2.2 %collective-permute-start.13 = (bf16[320,960]{1,0:T(8,128)(2,1)S(1)}, bf16[320,960]{1,0:T(8,128)(2,1)S(1)}, u32[]{:S(2)}, u32[]{:S(2)}) collective-permute-start(bf16[320,960]{1,0:T(8,128)(2,1)S(1)} %shard_map.98.refs_8_), channel_id=1, source_target_pairs={{0,8},{1,9},{2,10},{3,11},{4,12},{5,13},{6,14},{7,15},{8,0},{9,1},... | collective-permute-start | bytes 1843208 | tf_op jit(solution)/shard_map/ppermute | solution.py:26
  51.8 8.6 %collective-permute-start.14 = (bf16[80,960]{1,0:T(8,128)(2,1)S(1)}, bf16[80,960]{1,0:T(8,128)(2,1)S(1)}, u32[]{:S(2)}, u32[]{:S(2)}) collective-permute-start(bf16[80,960]{1,0:T(8,128)(2,1)S(1)} %get-tuple-element.41), channel_id=1, source_target_pairs={{0,32},{1,33},{2,34},{3,35},{4,36},{5,37},{6,38},{7,39},{8,40},{9,... | collective-permute-start | bytes 460808 | tf_op jit(solution)/shard_map/ppermute | solution.py:26
  55.1 8.4 %collective-permute-start.16 = (bf16[80,960]{1,0:T(8,128)(2,1)S(1)}, bf16[80,960]{1,0:T(8,128)(2,1)S(1)}, u32[]{:S(2)}, u32[]{:S(2)}) collective-permute-start(bf16[80,960]{1,0:T(8,128)(2,1)S(1)} %get-tuple-element.42), channel_id=1, source_target_pairs={{0,48},{1,49},{2,50},{3,51},{4,52},{5,53},{6,54},{7,55},{8,56},{9,... | collective-permute-start | bytes 460808 | tf_op jit(solution)/shard_map/ppermute | solution.py:26
  56.2 7.4 %collective-permute-start.15 = (bf16[80,960]{1,0:T(8,128)(2,1)S(1)}, bf16[80,960]{1,0:T(8,128)(2,1)S(1)}, u32[]{:S(2)}, u32[]{:S(2)}) collective-permute-start(bf16[80,960]{1,0:T(8,128)(2,1)S(1)} %get-tuple-element.39.refs_2_), channel_id=1, source_target_pairs={{0,16},{1,17},{2,18},{3,19},{4,20},{5,21},{6,22},{7,23},{8,24},{9,... | collective-permute-start | bytes 460808 | tf_op jit(solution)/shard_map/ppermute | solution.py:26
  63.6 6.6 %collective-permute-start.18 = (bf16[40,960]{1,0:T(8,128)(2,1)S(1)}, bf16[40,960]{1,0:T(8,128)(2,1)S(1)}, u32[]{:S(2)}, u32[]{:S(2)}) collective-permute-start(bf16[40,960]{1,0:T(8,128)(2,1)S(1)} %get-tuple-element.45), channel_id=1, source_target_pairs={{0,192},{1,193},{2,194},{3,195},{4,196},{5,197},{6,198},{7,199},{8... | collective-permute-start | bytes 230408 | tf_op jit(solution)/shard_map/ppermute | solution.py:26
  66.1 6.0 %collective-permute-start.17 = (bf16[40,960]{1,0:T(8,128)(2,1)S(1)}, bf16[40,960]{1,0:T(8,128)(2,1)S(1)}, u32[]{:S(2)}, u32[]{:S(2)}) collective-permute-start(bf16[40,960]{1,0:T(8,128)(2,1)S(1)} %get-tuple-element.43.refs_14_), channel_id=1, source_target_pairs={{0,64},{1,65},{2,66},{3,67},{4,68},{5,69},{6,70},{7,71},{8,72},{9,... | collective-permute-start | bytes 230408 | tf_op jit(solution)/shard_map/ppermute | solution.py:26
  72.1 7.2 %collective-permute-start.19 = (bf16[40,960]{1,0:T(8,128)(2,1)S(1)}, bf16[40,960]{1,0:T(8,128)(2,1)S(1)}, u32[]{:S(2)}, u32[]{:S(2)}) collective-permute-start(bf16[40,960]{1,0:T(8,128)(2,1)S(1)} %get-tuple-element.47), channel_id=1, source_target_pairs={{0,192},{1,193},{2,194},{3,195},{4,196},{5,197},{6,198},{7,199},{8... | collective-permute-start | bytes 230408 | tf_op jit(solution)/shard_map/ppermute | solution.py:26
  74.2 5.3 %collective-permute-start.20 = (bf16[40,960]{1,0:T(8,128)(2,1)S(1)}, bf16[40,960]{1,0:T(8,128)(2,1)S(1)}, u32[]{:S(2)}, u32[]{:S(2)}) collective-permute-start(bf16[40,960]{1,0:T(8,128)(2,1)S(1)} %get-tuple-element.48), channel_id=1, source_target_pairs={{0,64},{1,65},{2,66},{3,67},{4,68},{5,69},{6,70},{7,71},{8,72},{9,... | collective-permute-start | bytes 230408 | tf_op jit(solution)/shard_map/ppermute | solution.py:26
  80.4 7.9 %collective-permute-start.23 = (bf16[80,960]{1,0:T(8,128)(2,1)S(1)}, bf16[80,960]{1,0:T(8,128)(2,1)S(1)}, u32[]{:S(2)}, u32[]{:S(2)}) collective-permute-start(bf16[80,960]{1,0:T(8,128)(2,1)S(1)} %shard_map.105.refs_1_), channel_id=1, source_target_pairs={{0,32},{1,33},{2,34},{3,35},{4,36},{5,37},{6,38},{7,39},{8,40},{9,... | collective-permute-start | bytes 460808 | tf_op jit(solution)/shard_map/ppermute | solution.py:26
  84.3 5.7 %collective-permute-start.22 = (bf16[80,960]{1,0:T(8,128)(2,1)S(1)}, bf16[80,960]{1,0:T(8,128)(2,1)S(1)}, u32[]{:S(2)}, u32[]{:S(2)}) collective-permute-start(bf16[80,960]{1,0:T(8,128)(2,1)S(1)} %shard_map.105.refs_1_), channel_id=1, source_target_pairs={{0,48},{1,49},{2,50},{3,51},{4,52},{5,53},{6,54},{7,55},{8,56},{9,... | collective-permute-start | bytes 460808 | tf_op jit(solution)/shard_map/ppermute | solution.py:26
  85.5 6.5 %collective-permute-start.21 = (bf16[80,960]{1,0:T(8,128)(2,1)S(1)}, bf16[80,960]{1,0:T(8,128)(2,1)S(1)}, u32[]{:S(2)}, u32[]{:S(2)}) collective-permute-start(bf16[80,960]{1,0:T(8,128)(2,1)S(1)} %shard_map.105.refs_1_), channel_id=1, source_target_pairs={{0,16},{1,17},{2,18},{3,19},{4,20},{5,21},{6,22},{7,23},{8,24},{9,... | collective-permute-start | bytes 460808 | tf_op jit(solution)/shard_map/ppermute | solution.py:26
  86.3 5.8 %collective-permute-start.24 = (bf16[80,960]{1,0:T(8,128)(2,1)S(1)}, bf16[80,960]{1,0:T(8,128)(2,1)S(1)}, u32[]{:S(2)}, u32[]{:S(2)}) collective-permute-start(bf16[80,960]{1,0:T(8,128)(2,1)S(1)} %shard_map.105.refs_1_), channel_id=1, source_target_pairs={{0,8},{1,9},{2,10},{3,11},{4,12},{5,13},{6,14},{7,15},{8,0},{9,1},... | collective-permute-start | bytes 460808 | tf_op jit(solution)/shard_map/ppermute | solution.py:26
  88.3 3.8 %collective-permute-start.27 = (bf16[80,960]{1,0:T(8,128)(2,1)S(1)}, bf16[80,960]{1,0:T(8,128)(2,1)S(1)}, u32[]{:S(2)}, u32[]{:S(2)}) collective-permute-start(bf16[80,960]{1,0:T(8,128)(2,1)S(1)} %collective-permute-done.23.refs_4_), channel_id=1, source_target_pairs={{0,8},{1,9},{2,10},{3,11},{4,12},{5,13},{6,14},{7,15},{8,0},{9,1},... | collective-permute-start | bytes 460808 | tf_op jit(solution)/shard_map/ppermute | solution.py:26
  90.0 2.1 %collective-permute-start.26 = (bf16[80,960]{1,0:T(8,128)(2,1)S(1)}, bf16[80,960]{1,0:T(8,128)(2,1)S(1)}, u32[]{:S(2)}, u32[]{:S(2)}) collective-permute-start(bf16[80,960]{1,0:T(8,128)(2,1)S(1)} %collective-permute-done.22.refs_3_), channel_id=1, source_target_pairs={{0,8},{1,9},{2,10},{3,11},{4,12},{5,13},{6,14},{7,15},{8,0},{9,1},... | collective-permute-start | bytes 460808 | tf_op jit(solution)/shard_map/ppermute | solution.py:26
  92.1 1.4 %collective-permute-start.25 = (bf16[80,960]{1,0:T(8,128)(2,1)S(1)}, bf16[80,960]{1,0:T(8,128)(2,1)S(1)}, u32[]{:S(2)}, u32[]{:S(2)}) collective-permute-start(bf16[80,960]{1,0:T(8,128)(2,1)S(1)} %collective-permute-done.21.refs_2_), channel_id=1, source_target_pairs={{0,8},{1,9},{2,10},{3,11},{4,12},{5,13},{6,14},{7,15},{8,0},{9,1},... | collective-permute-start | bytes 460808 | tf_op jit(solution)/shard_map/ppermute | solution.py:26
  94.4 5.8 %collective-permute-start.29 = (bf16[64,640]{1,0:T(8,128)(2,1)S(1)}, bf16[64,640]{1,0:T(8,128)(2,1)S(1)}, u32[]{:S(2)}, u32[]{:S(2)}) collective-permute-start(bf16[64,640]{1,0:T(8,128)(2,1)S(1)} %get-tuple-element.50), channel_id=1, source_target_pairs={{0,196},{1,197},{2,198},{3,199},{4,64},{5,65},{6,66},{7,67},{8,204... | collective-permute-start | bytes 245768 | tf_op jit(solution)/shard_map/ppermute | solution.py:26
  97.0 4.4 %collective-permute-start.28 = (bf16[64,640]{1,0:T(8,128)(2,1)S(1)}, bf16[64,640]{1,0:T(8,128)(2,1)S(1)}, u32[]{:S(2)}, u32[]{:S(2)}) collective-permute-start(bf16[64,640]{1,0:T(8,128)(2,1)S(1)} %get-tuple-element.49.refs_9_), channel_id=1, source_target_pairs={{0,4},{1,5},{2,6},{3,7},{4,0},{5,1},{6,2},{7,3},{8,12},{9,13},{10,... | collective-permute-start | bytes 245768 | tf_op jit(solution)/shard_map/ppermute | solution.py:26
  101.6 4.5 %collective-permute-start.30 = (bf16[64,640]{1,0:T(8,128)(2,1)S(1)}, bf16[64,640]{1,0:T(8,128)(2,1)S(1)}, u32[]{:S(2)}, u32[]{:S(2)}) collective-permute-start(bf16[64,640]{1,0:T(8,128)(2,1)S(1)} %get-tuple-element.52), channel_id=1, source_target_pairs={{0,1},{1,0},{2,3},{3,2},{4,5},{5,4},{6,7},{7,6},{8,9},{9,8},{10,11... | collective-permute-start | bytes 245768 | tf_op jit(solution)/shard_map/ppermute | solution.py:26
  103.6 4.7 %collective-permute-start.31 = (bf16[64,640]{1,0:T(8,128)(2,1)S(1)}, bf16[64,640]{1,0:T(8,128)(2,1)S(1)}, u32[]{:S(2)}, u32[]{:S(2)}) collective-permute-start(bf16[64,640]{1,0:T(8,128)(2,1)S(1)} %get-tuple-element.53), channel_id=1, source_target_pairs={{0,3},{1,2},{2,1},{3,0},{4,7},{5,6},{6,5},{7,4},{8,11},{9,10},{10,... | collective-permute-start | bytes 245768 | tf_op jit(solution)/shard_map/ppermute | solution.py:26
  104.0 5.9 %collective-permute-start.32 = (bf16[64,640]{1,0:T(8,128)(2,1)S(1)}, bf16[64,640]{1,0:T(8,128)(2,1)S(1)}, u32[]{:S(2)}, u32[]{:S(2)}) collective-permute-start(bf16[64,640]{1,0:T(8,128)(2,1)S(1)} %get-tuple-element.54), channel_id=1, source_target_pairs={{0,2},{1,3},{2,0},{3,1},{4,6},{5,7},{6,4},{7,5},{8,10},{9,11},{10,... | collective-permute-start | bytes 245768 | tf_op jit(solution)/shard_map/ppermute | solution.py:26
